TPU v7x, 32 devices: a whole 2x2x4 slice. The times are simulated.
32 devices in a mesh: fsdp: 16 (over z, y, x), dp: 2 (over core).
Axes of the slice: x: 2, y: 2, z: 4, core: 2. Of those that a mesh axis runs over, the one named last changes fastest.
Arguments:
- image_states: bfloat16 [32, 325, 768], P(('fsdp', 'dp')), may hold values from -6 to 6
- text_states: bfloat16 [32, 513, 768], P(('fsdp', 'dp')), may hold values from -6 to 6
- size_group: int32 [32], P(('fsdp', 'dp')), may hold values from 0 to 1
- caption_len: int32 [32], P(('fsdp', 'dp')), may hold values from 16 to 512, as said below
- cotangent: bfloat16 [32, 839, 768], P(('fsdp', 'dp')), may hold values from -6 to 6
- image_proj: bfloat16 [768, 768], P('fsdp'), may hold values from -0.21875 to 0.21875
- image_bias: bfloat16 [768], P('fsdp'), may hold values from -1.75 to 1.75
- text_proj: bfloat16 [768, 768], P('fsdp'), may hold values from -0.21875 to 0.21875
- text_bias: bfloat16 [768], P('fsdp'), may hold values from -1.75 to 1.75
- cls_token: bfloat16 [768], P('fsdp'), may hold values from -6 to 6
- first_gain: bfloat16 [768], P('fsdp'), may hold values from 0.5 to 1.5
- first_shift: bfloat16 [768], P('fsdp'), may hold values from -1.75 to 1.75
- query_proj: bfloat16 [768, 768], P('fsdp'), may hold values from -0.21875 to 0.21875
- query_bias: bfloat16 [768], P('fsdp'), may hold values from -1.75 to 1.75
- key_proj: bfloat16 [768, 768], P('fsdp'), may hold values from -0.21875 to 0.21875
- value_proj: bfloat16 [768, 768], P('fsdp'), may hold values from -0.21875 to 0.21875
- value_bias: bfloat16 [768], P('fsdp'), may hold values from -0.1875 to 0.1875
- output_proj: bfloat16 [768, 768], P('fsdp'), may hold values from -4 to 4
- output_bias: bfloat16 [768], P('fsdp'), may hold values from -1.75 to 1.75
- second_gain: bfloat16 [768], P('fsdp'), may hold values from 0.5 to 1.5
- second_shift: bfloat16 [768], P('fsdp'), may hold values from -1.75 to 1.75
- hidden_proj: bfloat16 [768, 3072], P('fsdp'), may hold values from -0.21875 to 0.21875
- hidden_bias: bfloat16 [3072], P('fsdp'), may hold values from -1.75 to 1.75
- return_proj: bfloat16 [3072, 768], P('fsdp'), may hold values from -0.109375 to 0.109375
- return_bias: bfloat16 [768], P('fsdp'), may hold values from -1.75 to 1.75
Outputs:
- layer_out: bfloat16 [32, 839, 768], P(('fsdp', 'dp'))
- image_grad: float32 [32, 325, 768], P(('fsdp', 'dp'))
- text_grad: float32 [32, 513, 768], P(('fsdp', 'dp'))
- grad_image_proj: float32 [768, 768], P('fsdp')
- grad_image_bias: float32 [768], P('fsdp')
- grad_text_proj: float32 [768, 768], P('fsdp')
- grad_text_bias: float32 [768], P('fsdp')
- grad_cls_token: float32 [768], P('fsdp')
- grad_first_gain: float32 [768], P('fsdp')
- grad_first_shift: float32 [768], P('fsdp')
- grad_query_proj: float32 [768, 768], P('fsdp')
- grad_query_bias: float32 [768], P('fsdp')
- grad_key_proj: float32 [768, 768], P('fsdp')
- grad_value_proj: float32 [768, 768], P('fsdp')
- grad_value_bias: float32 [768], P('fsdp')
- grad_output_proj: float32 [768, 768], P('fsdp')
- grad_output_bias: float32 [768], P('fsdp')
- grad_second_gain: float32 [768], P('fsdp')
- grad_second_shift: float32 [768], P('fsdp')
- grad_hidden_proj: float32 [768, 3072], P('fsdp')
- grad_hidden_bias: float32 [3072], P('fsdp')
- grad_return_proj: float32 [3072, 768], P('fsdp')
- grad_return_bias: float32 [768], P('fsdp')
Inputs may be any that keep to these rules, and one draw needn't show every extreme that they name: `size_group`: 1 marks an item with 325 image rows in use, 0 one with the first 197. The caption tokens of each item fill its first caption_len text slots.
All inputs are finite; a program needn't handle non-finite values.
Results may differ from a plain program's by a relative error of at most 0.014.
Values may be sent and summed in bfloat16 or wider, within the bound.
No kernel may reach another device: no remote copies, remote signals or barrier semaphores. Data moves between devices by JAX's collectives and lax.ppermute only.
A program may use at most 192 MiB of HBM per device.

v0:
```python
import math

import jax
import jax.numpy as jnp
from jax import lax
from jax.sharding import PartitionSpec as P

HEADS = 12
HEAD_DIM = 64
PATCH_BIG = 325
PATCH_SMALL = 197


EPSILON = 1e-06
NEGATIVE = -1e30


def matmul(left, right):
    return jnp.dot(left, right, preferred_element_type=jnp.float32)


def left_product(left, right):
    return lax.dot_general(
        left, right, (((0,), (0,)), ((), ())), preferred_element_type=jnp.float32
    )


def right_product(left, right):
    return lax.dot_general(
        left, right, (((1,), (1,)), ((), ())), preferred_element_type=jnp.float32
    )


def to_low(values):
    return values.astype(jnp.bfloat16)


def column_sum(values):
    return jnp.sum(values.astype(jnp.float32), 0)


def gelu_exact(values):
    return jax.nn.gelu(values, approximate=False)


def layer_norm(values, gain, shift):
    centered = values - jnp.mean(values, -1, keepdims=True)
    scaled = centered * lax.rsqrt(jnp.mean(centered * centered, -1, keepdims=True) + EPSILON)
    return scaled * gain + shift


def key_mask(size_code, length, row_count):
    position = jnp.arange(row_count, dtype=jnp.int32)
    patches = jnp.where(size_code == 1, PATCH_BIG, PATCH_SMALL).astype(jnp.int32)
    image_live = (position >= 1) & (position <= patches)
    text_live = (position >= 1 + PATCH_BIG) & (position < 1 + PATCH_BIG + length)
    return (position == 0) | image_live | text_live


def head_slice(source, offset, span_width, per_group):
    part = lax.dynamic_slice_in_dim(source, offset, span_width, 1)
    return part.reshape(source.shape[0], per_group, HEAD_DIM)


def attend_forward(queries, keys_all, values_all, key_live):
    row_count = queries.shape[0]
    per_group = math.gcd(HEADS, 4)
    span_width = per_group * HEAD_DIM
    factor = HEAD_DIM ** (-0.5)

    def one_group(group_index, running):
        attended, totals = running
        offset = group_index * span_width
        query_part = head_slice(queries, offset, span_width, per_group)
        key_part = head_slice(keys_all, offset, span_width, per_group)
        value_part = head_slice(values_all, offset, span_width, per_group)
        scores = (
            jnp.einsum("qhd,khd->hqk", query_part, key_part, preferred_element_type=jnp.float32)
            * factor
        )
        scores = jnp.where(key_live, scores, NEGATIVE)
        row_top = jnp.max(scores, -1, keepdims=True)
        exps = jnp.exp(scores - row_top)
        row_total = jnp.sum(exps, -1, keepdims=True)
        prob_rows = to_low(exps / row_total)
        mixed_heads = jnp.einsum(
            "hqk,khd->qhd", prob_rows, value_part, preferred_element_type=jnp.float32
        )
        attended = lax.dynamic_update_slice_in_dim(
            attended, to_low(mixed_heads.reshape(row_count, span_width)), offset, 1
        )
        log_total = (row_top + jnp.log(row_total))[:, :, 0]
        totals = lax.dynamic_update_slice_in_dim(totals, log_total, group_index * per_group, 0)
        return (attended, totals)

    initial = (
        jnp.zeros((row_count, HEADS * HEAD_DIM), jnp.bfloat16),
        jnp.zeros((HEADS, row_count), jnp.float32),
    )
    return lax.fori_loop(0, HEADS // per_group, one_group, initial)


def attend_backward(queries, keys_all, values_all, key_live, totals, incoming):
    row_count = queries.shape[0]
    per_group = math.gcd(HEADS, 4)
    span_width = per_group * HEAD_DIM
    factor = HEAD_DIM ** (-0.5)

    def one_group(group_index, running):
        query_grad, key_grad, value_grad = running
        offset = group_index * span_width
        query_part = head_slice(queries, offset, span_width, per_group)
        key_part = head_slice(keys_all, offset, span_width, per_group)
        value_part = head_slice(values_all, offset, span_width, per_group)
        incoming_part = head_slice(incoming, offset, span_width, per_group)
        log_total = lax.dynamic_slice_in_dim(totals, group_index * per_group, per_group, 0)
        scores = (
            jnp.einsum("qhd,khd->hqk", query_part, key_part, preferred_element_type=jnp.float32)
            * factor
        )
        scores = jnp.where(key_live, scores, NEGATIVE)
        prob_rows = jnp.exp(scores - log_total[:, :, None])
        value_part_grad = jnp.einsum(
            "hqk,qhd->khd", to_low(prob_rows), incoming_part, preferred_element_type=jnp.float32
        )
        prob_grad = jnp.einsum(
            "qhd,khd->hqk", incoming_part, value_part, preferred_element_type=jnp.float32
        )
        score_grad = to_low(
            prob_rows * (prob_grad - jnp.sum(prob_rows * prob_grad, -1, keepdims=True))
        )
        query_part_grad = (
            jnp.einsum("hqk,khd->qhd", score_grad, key_part, preferred_element_type=jnp.float32)
            * factor
        )
        key_part_grad = (
            jnp.einsum("hqk,qhd->khd", score_grad, query_part, preferred_element_type=jnp.float32)
            * factor
        )
        query_grad = lax.dynamic_update_slice_in_dim(
            query_grad, to_low(query_part_grad.reshape(row_count, span_width)), offset, 1
        )
        key_grad = lax.dynamic_update_slice_in_dim(
            key_grad, to_low(key_part_grad.reshape(row_count, span_width)), offset, 1
        )
        value_grad = lax.dynamic_update_slice_in_dim(
            value_grad, to_low(value_part_grad.reshape(row_count, span_width)), offset, 1
        )
        return (query_grad, key_grad, value_grad)

    empty_grad = jnp.zeros((row_count, HEADS * HEAD_DIM), jnp.bfloat16)
    return lax.fori_loop(0, HEADS // per_group, one_group, (empty_grad, empty_grad, empty_grad))


def item_forward(weights, image_rows, text_rows, size_code, length):
    (
        image_proj,
        image_bias,
        text_proj,
        text_bias,
        cls_token,
        first_gain,
        first_shift,
        query_proj,
        query_bias,
        key_proj,
        value_proj,
        value_bias,
        output_proj,
        output_bias,
        second_gain,
        second_shift,
        hidden_proj,
        hidden_bias,
        return_proj,
        return_bias,
    ) = weights
    image_part = matmul(image_rows, image_proj) + image_bias.astype(jnp.float32)
    text_part = matmul(text_rows, text_proj) + text_bias.astype(jnp.float32)
    embedded = jnp.concatenate([cls_token.astype(jnp.float32)[None, :], image_part, text_part], 0)
    normed = to_low(
        layer_norm(embedded, first_gain.astype(jnp.float32), first_shift.astype(jnp.float32))
    )
    queries = to_low(matmul(normed, query_proj) + query_bias.astype(jnp.float32))
    keys_all = to_low(matmul(normed, key_proj))
    values_all = to_low(matmul(normed, value_proj) + value_bias.astype(jnp.float32))
    key_live = key_mask(size_code, length, embedded.shape[0])
    attended, totals = attend_forward(queries, keys_all, values_all, key_live)
    middle = embedded + matmul(attended, output_proj) + output_bias.astype(jnp.float32)
    second = to_low(
        layer_norm(middle, second_gain.astype(jnp.float32), second_shift.astype(jnp.float32))
    )
    inner_pre = matmul(second, hidden_proj) + hidden_bias.astype(jnp.float32)
    activated = to_low(gelu_exact(inner_pre))
    result = middle + matmul(activated, return_proj) + return_bias.astype(jnp.float32)
    kept_rows = (
        embedded,
        normed,
        queries,
        keys_all,
        values_all,
        attended,
        totals,
        middle,
        second,
        inner_pre,
        activated,
    )
    return (to_low(result), kept_rows)


def item_backward(weights, image_rows, text_rows, size_code, length, kept_rows, out_grad):
    (
        image_proj,
        image_bias,
        text_proj,
        text_bias,
        cls_token,
        first_gain,
        first_shift,
        query_proj,
        query_bias,
        key_proj,
        value_proj,
        value_bias,
        output_proj,
        output_bias,
        second_gain,
        second_shift,
        hidden_proj,
        hidden_bias,
        return_proj,
        return_bias,
    ) = weights
    (
        embedded,
        normed,
        queries,
        keys_all,
        values_all,
        attended,
        totals,
        middle,
        second,
        inner_pre,
        activated,
    ) = kept_rows
    grad_return_proj = left_product(activated, out_grad)
    grad_return_bias = column_sum(out_grad)
    activated_grad = right_product(out_grad, return_proj)
    unused_value, gelu_pull = jax.vjp(gelu_exact, inner_pre)
    inner_grad = to_low(gelu_pull(activated_grad)[0])
    grad_hidden_proj = left_product(second, inner_grad)
    grad_hidden_bias = column_sum(inner_grad)
    second_grad = right_product(inner_grad, hidden_proj)
    unused_norm, second_pull = jax.vjp(
        layer_norm, middle, second_gain.astype(jnp.float32), second_shift.astype(jnp.float32)
    )
    middle_part, grad_second_gain, grad_second_shift = second_pull(second_grad)
    middle_grad = out_grad.astype(jnp.float32) + middle_part
    branch_grad = to_low(middle_grad)
    grad_output_proj = left_product(attended, branch_grad)
    grad_output_bias = column_sum(branch_grad)
    attended_grad = to_low(right_product(branch_grad, output_proj))
    key_live = key_mask(size_code, length, embedded.shape[0])
    query_grad, key_grad, value_grad = attend_backward(
        queries, keys_all, values_all, key_live, totals, attended_grad
    )
    grad_query_proj = left_product(normed, query_grad)
    grad_query_bias = column_sum(query_grad)
    grad_key_proj = left_product(normed, key_grad)
    grad_value_proj = left_product(normed, value_grad)
    grad_value_bias = column_sum(value_grad)
    normed_grad = (
        right_product(query_grad, query_proj)
        + right_product(key_grad, key_proj)
        + right_product(value_grad, value_proj)
    )
    unused_first, first_pull = jax.vjp(
        layer_norm, embedded, first_gain.astype(jnp.float32), first_shift.astype(jnp.float32)
    )
    embedded_part, grad_first_gain, grad_first_shift = first_pull(normed_grad)
    embedded_grad = middle_grad + embedded_part
    grad_cls_token = embedded_grad[0]
    image_low = to_low(embedded_grad[1 : 1 + PATCH_BIG])
    text_low = to_low(embedded_grad[1 + PATCH_BIG :])
    image_grad = right_product(image_low, image_proj)
    text_grad = right_product(text_low, text_proj)
    grad_image_proj = left_product(image_rows, image_low)
    grad_image_bias = column_sum(image_low)
    grad_text_proj = left_product(text_rows, text_low)
    grad_text_bias = column_sum(text_low)
    grads = (
        grad_image_proj,
        grad_image_bias,
        grad_text_proj,
        grad_text_bias,
        grad_cls_token,
        grad_first_gain,
        grad_first_shift,
        grad_query_proj,
        grad_query_bias,
        grad_key_proj,
        grad_value_proj,
        grad_value_bias,
        grad_output_proj,
        grad_output_bias,
        grad_second_gain,
        grad_second_shift,
        grad_hidden_proj,
        grad_hidden_bias,
        grad_return_proj,
        grad_return_bias,
    )
    return (image_grad, text_grad, grads)


def on_device(
    image_states,
    text_states,
    size_group,
    caption_len,
    cotangent,
    image_proj,
    image_bias,
    text_proj,
    text_bias,
    cls_token,
    first_gain,
    first_shift,
    query_proj,
    query_bias,
    key_proj,
    value_proj,
    value_bias,
    output_proj,
    output_bias,
    second_gain,
    second_shift,
    hidden_proj,
    hidden_bias,
    return_proj,
    return_bias,
):
    gathered = (
        lax.all_gather(image_proj, "fsdp", axis=0, tiled=True),
        lax.all_gather(image_bias, "fsdp", axis=0, tiled=True),
        lax.all_gather(text_proj, "fsdp", axis=0, tiled=True),
        lax.all_gather(text_bias, "fsdp", axis=0, tiled=True),
        lax.all_gather(cls_token, "fsdp", axis=0, tiled=True),
        lax.all_gather(first_gain, "fsdp", axis=0, tiled=True),
        lax.all_gather(first_shift, "fsdp", axis=0, tiled=True),
        lax.all_gather(query_proj, "fsdp", axis=0, tiled=True),
        lax.all_gather(query_bias, "fsdp", axis=0, tiled=True),
        lax.all_gather(key_proj, "fsdp", axis=0, tiled=True),
        lax.all_gather(value_proj, "fsdp", axis=0, tiled=True),
        lax.all_gather(value_bias, "fsdp", axis=0, tiled=True),
        lax.all_gather(output_proj, "fsdp", axis=0, tiled=True),
        lax.all_gather(output_bias, "fsdp", axis=0, tiled=True),
        lax.all_gather(second_gain, "fsdp", axis=0, tiled=True),
        lax.all_gather(second_shift, "fsdp", axis=0, tiled=True),
        lax.all_gather(hidden_proj, "fsdp", axis=0, tiled=True),
        lax.all_gather(hidden_bias, "fsdp", axis=0, tiled=True),
        lax.all_gather(return_proj, "fsdp", axis=0, tiled=True),
        lax.all_gather(return_bias, "fsdp", axis=0, tiled=True),
    )

    def forward_step(running, item_data):
        image_rows, text_rows, size_code, length = item_data
        result, kept_rows = item_forward(gathered, image_rows, text_rows, size_code, length)
        return (running, (result, kept_rows))

    unused_carry, (layer_out, kept_all) = lax.scan(
        forward_step, None, (image_states, text_states, size_group, caption_len)
    )
    initial = tuple((jnp.zeros(weight.shape, jnp.float32) for weight in gathered))

    def backward_step(running, item_data):
        image_rows, text_rows, size_code, length, kept_rows, out_grad = item_data
        image_grad, text_grad, grads = item_backward(
            gathered, image_rows, text_rows, size_code, length, kept_rows, out_grad
        )
        return (jax.tree.map(jnp.add, running, grads), (image_grad, text_grad))

    summed, (image_grads, text_grads) = lax.scan(
        backward_step,
        initial,
        (image_states, text_states, size_group, caption_len, kept_all, cotangent),
    )
    pieces = (
        lax.psum_scatter(summed[0], "fsdp", scatter_dimension=0, tiled=True),
        lax.psum_scatter(summed[1], "fsdp", scatter_dimension=0, tiled=True),
        lax.psum_scatter(summed[2], "fsdp", scatter_dimension=0, tiled=True),
        lax.psum_scatter(summed[3], "fsdp", scatter_dimension=0, tiled=True),
        lax.psum_scatter(summed[4], "fsdp", scatter_dimension=0, tiled=True),
        lax.psum_scatter(summed[5], "fsdp", scatter_dimension=0, tiled=True),
        lax.psum_scatter(summed[6], "fsdp", scatter_dimension=0, tiled=True),
        lax.psum_scatter(summed[7], "fsdp", scatter_dimension=0, tiled=True),
        lax.psum_scatter(summed[8], "fsdp", scatter_dimension=0, tiled=True),
        lax.psum_scatter(summed[9], "fsdp", scatter_dimension=0, tiled=True),
        lax.psum_scatter(summed[10], "fsdp", scatter_dimension=0, tiled=True),
        lax.psum_scatter(summed[11], "fsdp", scatter_dimension=0, tiled=True),
        lax.psum_scatter(summed[12], "fsdp", scatter_dimension=0, tiled=True),
        lax.psum_scatter(summed[13], "fsdp", scatter_dimension=0, tiled=True),
        lax.psum_scatter(summed[14], "fsdp", scatter_dimension=0, tiled=True),
        lax.psum_scatter(summed[15], "fsdp", scatter_dimension=0, tiled=True),
        lax.psum_scatter(summed[16], "fsdp", scatter_dimension=0, tiled=True),
        lax.psum_scatter(summed[17], "fsdp", scatter_dimension=0, tiled=True),
        lax.psum_scatter(summed[18], "fsdp", scatter_dimension=0, tiled=True),
        lax.psum_scatter(summed[19], "fsdp", scatter_dimension=0, tiled=True),
    )
    owned_grads = (
        lax.psum(pieces[0].astype(jnp.bfloat16), "dp").astype(jnp.float32),
        lax.psum(pieces[1].astype(jnp.bfloat16), "dp").astype(jnp.float32),
        lax.psum(pieces[2].astype(jnp.bfloat16), "dp").astype(jnp.float32),
        lax.psum(pieces[3].astype(jnp.bfloat16), "dp").astype(jnp.float32),
        lax.psum(pieces[4].astype(jnp.bfloat16), "dp").astype(jnp.float32),
        lax.psum(pieces[5].astype(jnp.bfloat16), "dp").astype(jnp.float32),
        lax.psum(pieces[6].astype(jnp.bfloat16), "dp").astype(jnp.float32),
        lax.psum(pieces[7].astype(jnp.bfloat16), "dp").astype(jnp.float32),
        lax.psum(pieces[8].astype(jnp.bfloat16), "dp").astype(jnp.float32),
        lax.psum(pieces[9].astype(jnp.bfloat16), "dp").astype(jnp.float32),
        lax.psum(pieces[10].astype(jnp.bfloat16), "dp").astype(jnp.float32),
        lax.psum(pieces[11].astype(jnp.bfloat16), "dp").astype(jnp.float32),
        lax.psum(pieces[12].astype(jnp.bfloat16), "dp").astype(jnp.float32),
        lax.psum(pieces[13].astype(jnp.bfloat16), "dp").astype(jnp.float32),
        lax.psum(pieces[14].astype(jnp.bfloat16), "dp").astype(jnp.float32),
        lax.psum(pieces[15].astype(jnp.bfloat16), "dp").astype(jnp.float32),
        lax.psum(pieces[16].astype(jnp.bfloat16), "dp").astype(jnp.float32),
        lax.psum(pieces[17].astype(jnp.bfloat16), "dp").astype(jnp.float32),
        lax.psum(pieces[18].astype(jnp.bfloat16), "dp").astype(jnp.float32),
        lax.psum(pieces[19].astype(jnp.bfloat16), "dp").astype(jnp.float32),
    )
    return (
        layer_out,
        image_grads,
        text_grads,
        owned_grads[0],
        owned_grads[1],
        owned_grads[2],
        owned_grads[3],
        owned_grads[4],
        owned_grads[5],
        owned_grads[6],
        owned_grads[7],
        owned_grads[8],
        owned_grads[9],
        owned_grads[10],
        owned_grads[11],
        owned_grads[12],
        owned_grads[13],
        owned_grads[14],
        owned_grads[15],
        owned_grads[16],
        owned_grads[17],
        owned_grads[18],
        owned_grads[19],
    )


def solution(mesh):
    placed = (
        P(("fsdp", "dp"), None, None),
        P(("fsdp", "dp"), None, None),
        P(("fsdp", "dp")),
        P(("fsdp", "dp")),
        P(("fsdp", "dp"), None, None),
        P("fsdp", None),
        P("fsdp"),
        P("fsdp", None),
        P("fsdp"),
        P("fsdp"),
        P("fsdp"),
        P("fsdp"),
        P("fsdp", None),
        P("fsdp"),
        P("fsdp", None),
        P("fsdp", None),
        P("fsdp"),
        P("fsdp", None),
        P("fsdp"),
        P("fsdp"),
        P("fsdp"),
        P("fsdp", None),
        P("fsdp"),
        P("fsdp", None),
        P("fsdp"),
    )
    return jax.shard_map(
        on_device,
        mesh=mesh,
        in_specs=placed,
        out_specs=(
            P(("fsdp", "dp"), None, None),
            P(("fsdp", "dp"), None, None),
            P(("fsdp", "dp"), None, None),
            P("fsdp", None),
            P("fsdp"),
            P("fsdp", None),
            P("fsdp"),
            P("fsdp"),
            P("fsdp"),
            P("fsdp"),
            P("fsdp", None),
            P("fsdp"),
            P("fsdp", None),
            P("fsdp", None),
            P("fsdp"),
            P("fsdp", None),
            P("fsdp"),
            P("fsdp"),
            P("fsdp"),
            P("fsdp", None),
            P("fsdp"),
            P("fsdp", None),
            P("fsdp"),
        ),
        check_vma=False,
    )
```

profile of v0, /device:TPU:0, one launch (start us, length us, event | category | flops | bytes accessed | tf_op | source)
XLA Modules:
  0.0 1739.5 jit_solution(14928153283874079700)
XLA Ops:
  26.7 79.0 %all-reduce.25 = (bf16[768]{0:T(1024)(128)(2,1)S(1)}, bf16[768]{0:T(1024)(128)(2,1)S(1)}, bf16[768]{0:T(1024)(128)(2,1)S(1)}, bf16[768]{0:T(1024)(128)(2,1)S(1)}...) all-reduce(bf16[768]{0:T(1024)(128)(2,1)S(1)} %dynamic-update-slice, ...), channel_id=1, replica_groups=mesh['fsdp'=16,'dp'=2] {'fsdp'}, use_global_device_ids=true, to_apply=%add.4 | all-reduce | flops 11520 | bytes 46080
  110.1 17.7 %all-gather.11.cloned.1.call-done = bf16[768,768]{1,0:T(8,128)(2,1)} async-done(((bf16[48,768]{1,0:T(8,128)(2,1)}), bf16[768,768]{1,0:T(8,128)(2,1)}) %all-gather.11.cloned.1.call-update) | async-done | bytes 1179664 | tf_op jit(solution)/shard_map/all_gather | solution.py:348
  131.6 54.0 %all-gather.15.cloned.1.call-done = bf16[768,768]{1,0:T(8,128)(2,1)} async-done(((bf16[48,768]{1,0:T(8,128)(2,1)}), bf16[768,768]{1,0:T(8,128)(2,1)}) %all-gather.15.cloned.1.call-update) | async-done | bytes 1179664 | tf_op jit(solution)/shard_map/all_gather | solution.py:353
  185.6 3.5 add_convert_fusion.3
  190.9 52.4 %all-gather.13.cloned.1.call-done = bf16[768,768]{1,0:T(8,128)(2,1)} async-done(((bf16[48,768]{1,0:T(8,128)(2,1)}), bf16[768,768]{1,0:T(8,128)(2,1)}) %all-gather.13.cloned.1.call-update) | async-done | bytes 1179664 | tf_op jit(solution)/shard_map/all_gather | solution.py:356
  243.3 3.5 add_convert_fusion.4
  248.6 52.4 %all-gather.17.cloned.1.call-done = bf16[768,768]{1,0:T(8,128)(2,1)} async-done(((bf16[48,768]{1,0:T(8,128)(2,1)}), bf16[768,768]{1,0:T(8,128)(2,1)}) %all-gather.17.cloned.1.call-update) | async-done | bytes 1179664 | tf_op jit(solution)/shard_map/all_gather | solution.py:355
  301.0 3.9 convolution_convert_fusion.1
  304.9 2.5 copy.69
  309.2 34.8 %while.43 = (s32[]{:T(128)}, bf16[839,768]{0,1:T(8,128)(2,1)}, f32[12,839]{1,0:T(8,128)}, bf16[839,768]{0,1:T(8,128)(2,1)S(1)}, bf16[839,768]{0,1:T(8,128)(2,1)S...) while((s32[]{:T(128)}, bf16[839,768]{0,1:T(8,128)(2,1)}, ...), condition=%wide.region_5.6_spmd.clone, body=%wide.region_2.0_spmd.clone.sunk | while | flops 754822272 | bytes 39084124 | solution.py:100
  311.0 2.4 fusion.144
  313.4 3.0 fusion.145
  316.4 3.4 fusion.146
  322.4 2.4 fusion.144
  324.8 3.0 fusion.145
  327.8 3.4 fusion.146
  333.8 2.4 fusion.144
  336.2 3.0 fusion.145
  339.2 3.4 fusion.146
  344.0 14.7 all-gather.19.cloned.1.call-done
  358.7 4.0 fusion.62
  363.3 77.6 %all-gather.21.cloned.1.call-done = bf16[768,3072]{1,0:T(8,128)(2,1)} async-done(((bf16[48,3072]{1,0:T(8,128)(2,1)}), bf16[768,3072]{1,0:T(8,128)(2,1)}) %all-gather.21.cloned.1.call-update) | async-done | bytes 4718608 | tf_op jit(solution)/shard_map/all_gather | solution.py:362
  440.9 30.3 %multiply_convert_fusion.1 = (bf16[839,3072]{1,0:T(8,128)(2,1)}, f32[839,3072]{1,0:T(8,128)}, f32[839,3072]{1,0:T(8,128)}) fusion(f32[3072]{0:T(1024)S(1)} %copy-done.46, bf16[768,3072]{1,0:T(8,128)(2,1)} %all-gather.21.cloned.1.call-done, f32[839,768]{1,0:T(8,128)S(1)} %get-tuple-element.843, f32[768]{0:T(1024)S(1)} %copy-done.30, f32[768]{0:T(1024)S(1)} %copy-done.28, ...), kind=kOutput, calls=%fused_computation.59 | convolution fusion | flops 4132229376 | bytes 33095224 | tf_op jit(solution)/shard_map/while/body/eval_jaxpr/dot_general | solution.py:19
  471.2 51.6 %all-gather.23.cloned.1.call-done = bf16[3072,768]{1,0:T(8,128)(2,1)} async-done(((bf16[192,768]{1,0:T(8,128)(2,1)}), bf16[3072,768]{1,0:T(8,128)(2,1)}) %all-gather.23.cloned.1.call-update) | async-done | bytes 4718608 | tf_op jit(solution)/shard_map/all_gather | solution.py:364
  522.8 14.8 convert_reduce_fusion
  537.6 9.5 multiply_reduce_fusion.1
  550.4 2.8 fusion.69
  553.3 2.3 convolution_convert_fusion
  558.1 84.2 %while.44 = (s32[]{:T(128)}, bf16[839,768]{0,1:T(8,128)(2,1)}, bf16[839,768]{0,1:T(8,128)(2,1)}, bf16[839,768]{0,1:T(8,128)(2,1)S(1)}, bf16[839,768]{0,1:T(8,128...) while((s32[]{:T(128)}, bf16[839,768]{0,1:T(8,128)(2,1)}, ...), condition=%wide.region_12.13_spmd.clone, body=%wide.region_10.12_spmd.clone.sunk | while | flops 1845351040 | bytes 95882832 | solution.py:152
  565.7 2.8 fusion.160
  568.5 6.4 multiply_reduce_fusion.8
  574.9 6.8 multiply_convert_fusion.3
  593.7 2.8 fusion.160
  596.5 6.4 multiply_reduce_fusion.8
  602.9 6.8 multiply_convert_fusion.3
  621.6 2.8 fusion.160
  624.4 6.3 multiply_reduce_fusion.8
  630.8 6.8 multiply_convert_fusion.3
  642.2 5.1 fusion.67
  647.6 4.6 fusion.66
  652.3 4.2 fusion.68
  656.6 3.2 fusion.65
  661.9 2.4 multiply_reduce_fusion.2
  666.5 2.1 fusion.57
  668.6 2.3 convolution_bitcast_fusion.1
  670.9 3.1 copy.82
  674.0 2.6 convolution_bitcast_fusion
  676.6 3.2 copy.84
  680.2 10.4 fusion.53
  690.6 9.6 fusion.37
  701.7 2.2 convolution_bitcast_fusion.3
  707.5 75.2 %all-reduce.24 = (bf16[768]{0:T(1024)(128)(2,1)S(1)}, bf16[768]{0:T(1024)(128)(2,1)S(1)}, bf16[768]{0:T(1024)(128)(2,1)S(1)}, bf16[768]{0:T(1024)(128)(2,1)S(1)}...) all-reduce(f32[768]{0:T(1024)S(1)} %convert_reduce_fusion.6, ...), channel_id=3, replica_groups=mesh['fsdp'=16,'dp'=2] {'fsdp'}, use_global_device_ids=true, to_apply=%region_18.19.clone | all-reduce | flops 11520 | bytes 69120
  783.6 2.7 all-reduce.26
  792.6 2.4 convolution_bitcast_fusion.2
  794.9 2.8 copy.75
  799.2 14.2 reduce-scatter.15.cloned.1.call-done
  815.0 131.0 %reduce-scatter.13.cloned.1.call-done = f32[48,768]{1,0:T(8,128)} async-done(((f32[768,768]{1,0:T(8,128)}), f32[48,768]{1,0:T(8,128)}) %reduce-scatter.13.cloned.1.call-update) | async-done | bytes 147472 | tf_op jit(solution)/shard_map/reduce_scatter | solution.py:398
  947.6 131.5 %reduce-scatter.17.cloned.1.call-done = f32[48,768]{1,0:T(8,128)} async-done(((f32[768,768]{1,0:T(8,128)}), f32[48,768]{1,0:T(8,128)}) %reduce-scatter.17.cloned.1.call-update) | async-done | bytes 147472 | tf_op jit(solution)/shard_map/reduce_scatter | solution.py:401
  1080.6 130.8 %reduce-scatter.25.cloned.1.call-done = f32[48,768]{1,0:T(8,128)} async-done(((f32[768,768]{1,0:T(8,128)}), f32[48,768]{1,0:T(8,128)}) %reduce-scatter.25.cloned.1.call-update) | async-done | bytes 147472
  1213.2 131.4 %reduce-scatter.27.cloned.1.call-done = f32[48,768]{1,0:T(8,128)} async-done(((f32[768,768]{1,0:T(8,128)}), f32[48,768]{1,0:T(8,128)}) %reduce-scatter.27.cloned.1.call-update) | async-done | bytes 147472
  1346.3 174.0 %reduce-scatter.21.cloned.1.call-done = f32[48,3072]{1,0:T(8,128)} async-done(((f32[768,3072]{1,0:T(8,128)}), f32[48,3072]{1,0:T(8,128)}) %reduce-scatter.21.cloned.1.call-update) | async-done | bytes 589840 | tf_op jit(solution)/shard_map/reduce_scatter | solution.py:407
  1522.1 174.9 %reduce-scatter.23.cloned.1.call-done = f32[192,768]{1,0:T(8,128)} async-done(((f32[3072,768]{1,0:T(8,128)}), f32[192,768]{1,0:T(8,128)}) %reduce-scatter.23.cloned.1.call-update) | async-done | bytes 589840 | tf_op jit(solution)/shard_map/reduce_scatter | solution.py:409
  1698.9 9.1 fusion.36
  1708.0 12.1 all-reduce.30.cloned.1.call-done
  (300 shorter events, 121.6 us)
Async XLA Ops:
  7.2 120.6 %copy-start = (bf16[1,513,768]{2,1,0:T(8,128)(2,1)S(1)}, bf16[1,513,768]{2,1,0:T(8,128)(2,1)}, u32[]{:S(2)}) copy-start(bf16[1,513,768]{2,1,0:T(8,128)(2,1)} %param.30) | copy-start | bytes 2363908
  7.2 100.9 %all-gather.9.cloned.1.call-start = ((), (), s32[]{:S(2)}) async-start(), calls=%async_computation.8 | async-start | bytes 1253376 | tf_op jit(solution)/shard_map/all_gather | solution.py:346
  7.9 119.9 %all-gather.11.cloned.1.call-start = ((), (), s32[]{:S(2)}) async-start(), calls=%async_computation.9 | async-start | bytes 1253376 | tf_op jit(solution)/shard_map/all_gather | solution.py:348
  8.7 176.9 %all-gather.15.cloned.1.call-start = ((), (), s32[]{:S(2)}) async-start(), calls=%async_computation.11 | async-start | bytes 1253376 | tf_op jit(solution)/shard_map/all_gather | solution.py:353
  9.4 233.9 %all-gather.13.cloned.1.call-start = ((), (), s32[]{:S(2)}) async-start(), calls=%async_computation.10 | async-start | bytes 1253376 | tf_op jit(solution)/shard_map/all_gather | solution.py:356
  10.0 291.0 %all-gather.17.cloned.1.call-start = ((), (), s32[]{:S(2)}) async-start(), calls=%async_computation.12 | async-start | bytes 1253376 | tf_op jit(solution)/shard_map/all_gather | solution.py:355
  10.6 348.1 %all-gather.19.cloned.1.call-start = ((), (), s32[]{:S(2)}) async-start(), calls=%async_computation.13 | async-start | bytes 1253376 | tf_op jit(solution)/shard_map/all_gather | solution.py:358
  11.2 429.7 %all-gather.21.cloned.1.call-start = ((), (), s32[]{:S(2)}) async-start(), calls=%async_computation.14 | async-start | bytes 5013504 | tf_op jit(solution)/shard_map/all_gather | solution.py:362
  11.9 510.9 %all-gather.23.cloned.1.call-start = ((), (), s32[]{:S(2)}) async-start(), calls=%async_computation.15 | async-start | bytes 5013504 | tf_op jit(solution)/shard_map/all_gather | solution.py:364
  12.7 785.0 %reduce-scatter.19.cloned.1.call-start = ((), (), s32[]{:S(2)}) async-start(), calls=%async_computation.19 | async-start | bytes 2506752 | tf_op jit(solution)/shard_map/reduce_scatter | solution.py:403
  105.7 253.0 %copy-start.32 = (f32[1,768]{1,0:T(1,128)}, f32[1,768]{1,0:T(1,128)S(1)}, u32[]{:S(2)}) copy-start(f32[1,768]{1,0:T(1,128)S(1)} %reshape.247) | copy-start | bytes 9220
  106.3 24.6 %copy-start.36 = (f32[768]{0:T(1024)}, f32[768]{0:T(1024)S(1)}, u32[]{:S(2)}) copy-start(f32[768]{0:T(1024)S(1)} %convert_element_type.318) | copy-start | bytes 9220
  110.1 20.8 %copy-start.9 = (f32[325,768]{1,0:T(8,128)}, f32[325,768]{1,0:T(8,128)S(1)}, u32[]{:S(2)}) copy-start(f32[325,768]{1,0:T(8,128)S(1)} %convolution_add_fusion.1) | copy-start | bytes 2995204
  130.9 58.3 %copy-start.42 = (f32[839]{0:T(1024)}, f32[839]{0:T(1024)S(1)}, u32[]{:S(2)}) copy-start(f32[839]{0:T(1024)S(1)} %multiply_reduce_fusion.6) | copy-start | bytes 10072
  131.0 58.1 %copy-start.38 = (f32[839]{0:T(1024)}, f32[839]{0:T(1024)S(1)}, u32[]{:S(2)}) copy-start(f32[839]{0:T(1024)S(1)} %fusion.51) | copy-start | bytes 10072
  131.6 111.7 %copy-start.21 = (bf16[839,768]{1,0:T(8,128)(2,1)}, bf16[839,768]{1,0:T(8,128)(2,1)S(1)}, u32[]{:S(2)}) copy-start(bf16[839,768]{1,0:T(8,128)(2,1)S(1)} %add_convert_fusion.5) | copy-start | bytes 3866116
  344.0 14.7 copy-start.3
  344.0 14.7 copy-start.4
  362.7 184.4 %copy-start.1 = (f32[839,768]{1,0:T(8,128)}, f32[839,768]{1,0:T(8,128)S(1)}, u32[]{:S(2)}) copy-start(f32[839,768]{1,0:T(8,128)S(1)} %get-tuple-element.843) | copy-start | bytes 7732228
  362.7 78.2 %copy-start.28 = (f32[768]{0:T(1024)S(1)}, f32[768]{0:T(1024)}, u32[]{:S(2)}) copy-start(f32[768]{0:T(1024)} %convert_element_type.327) | copy-start | bytes 9220
  362.7 78.2 %copy-start.30 = (f32[768]{0:T(1024)S(1)}, f32[768]{0:T(1024)}, u32[]{:S(2)}) copy-start(f32[768]{0:T(1024)} %convert_element_type.328) | copy-start | bytes 9220
  362.7 78.2 %copy-start.46 = (f32[3072]{0:T(1024)S(1)}, f32[3072]{0:T(1024)}, u32[]{:S(2)}) copy-start(f32[3072]{0:T(1024)} %convert_element_type.330) | copy-start | bytes 36868
  362.8 184.3 %copy-start.23 = (f32[839]{0:T(1024)}, f32[839]{0:T(1024)S(1)}, u32[]{:S(2)}) copy-start(f32[839]{0:T(1024)S(1)} %broadcast_multiply_fusion) | copy-start | bytes 10072
  363.3 183.9 %copy-start.25 = (f32[839]{0:T(1024)}, f32[839]{0:T(1024)S(1)}, u32[]{:S(2)}) copy-start(f32[839]{0:T(1024)S(1)} %fusion.52) | copy-start | bytes 10072
  537.6 9.5 copy-start.13
  548.1 1.5 copy-start.7
  548.4 2.0 copy-start.20
  550.4 2.9 copy-start.52
  553.2 260.2 %reduce-scatter.15.cloned.1.call-start = ((), (), s32[]{:S(2)}) async-start(), calls=%async_computation.17 | async-start | bytes 2506752 | tf_op jit(solution)/shard_map/reduce_scatter | solution.py:400
  642.2 19.0 %copy-start.14 = (bf16[839,768]{0,1:T(8,128)(2,1)}, bf16[839,768]{0,1:T(8,128)(2,1)S(1)}, u32[]{:S(2)}) copy-start(bf16[839,768]{0,1:T(8,128)(2,1)S(1)} %get-tuple-element.602) | copy-start | bytes 3866116
  647.3 298.7 %reduce-scatter.13.cloned.1.call-start = ((), (), s32[]{:S(2)}) async-start(), calls=%async_computation.16 | async-start | bytes 2506752 | tf_op jit(solution)/shard_map/reduce_scatter | solution.py:398
  652.2 426.9 %reduce-scatter.17.cloned.1.call-start = ((), (), s32[]{:S(2)}) async-start(), calls=%async_computation.18 | async-start | bytes 2506752 | tf_op jit(solution)/shard_map/reduce_scatter | solution.py:401
  656.5 555.0 %reduce-scatter.25.cloned.1.call-start = ((), (), s32[]{:S(2)}) async-start(), calls=%async_computation.22 | async-start | bytes 2506752
  656.6 3.2 copy-start.16
  656.6 3.2 copy-start.50
  659.8 1.7 copy-start.10
  659.8 1.7 copy-start.33
  659.8 1.7 copy-start.35
  659.8 1.7 copy-start.37
  659.8 1.7 copy-start.39
  659.9 2.1 copy-start.51
  661.9 2.5 copy-start.43
  664.4 1.7 copy-start.8
  664.4 2.1 copy-start.19
  664.4 2.1 copy-start.41
  666.5 2.1 copy-start.22
  668.6 5.4 copy-start.11
  674.0 670.7 %reduce-scatter.27.cloned.1.call-start = ((), (), s32[]{:S(2)}) async-start(), calls=%async_computation.23 | async-start | bytes 2506752
  676.6 3.5 copy-start.2
  676.6 3.5 copy-start.24
  676.6 3.5 copy-start.26
  676.6 3.6 copy-start.29
  676.6 3.6 copy-start.31
  679.9 840.5 %reduce-scatter.21.cloned.1.call-start = ((), (), s32[]{:S(2)}) async-start(), calls=%async_computation.20 | async-start | bytes 10027008 | tf_op jit(solution)/shard_map/reduce_scatter | solution.py:407
  690.6 1006.5 %reduce-scatter.23.cloned.1.call-start = ((), (), s32[]{:S(2)}) async-start(), calls=%async_computation.21 | async-start | bytes 10027008 | tf_op jit(solution)/shard_map/reduce_scatter | solution.py:409
  700.3 1019.9 %all-reduce.30.cloned.1.call-start = ((), (), s32[]{:S(2)}) async-start(), calls=%async_computation.24 | async-start | bytes 2555904 | tf_op jit(solution)/shard_map/psum | solution.py:413
  701.6 5.0 copy-start.12
  701.6 5.4 copy-start.15
  701.6 5.4 copy-start.17
  703.9 3.7 copy-start.44
  703.9 3.7 copy-start.45
  703.9 3.7 copy-start.47
  703.9 3.6 copy-start.48
  1720.1 11.5 copy-start.27
  (6 other events, 8.1 us)
Sparse Core Ops, SparseCore 0:
  10.8 59.0 all-gather.8
  72.7 55.0 all-gather.10
  130.6 54.9 all-gather.14
  188.3 54.9 all-gather.12
  246.0 54.9 all-gather.16
  303.7 55.0 all-gather.18
  361.5 79.3 all-gather.20
  443.7 79.0 all-gather.22
  553.4 126.9 reduce-scatter.18
  685.9 127.5 reduce-scatter.14
  818.4 127.6 reduce-scatter.12
  951.6 127.4 reduce-scatter.16
  1084.0 127.4 reduce-scatter.24
  1217.0 127.5 reduce-scatter.26
  1350.1 170.1 reduce-scatter.20
  1526.8 170.2 reduce-scatter.22
  1700.9 19.1 all-reduce.29
where the time goes:
time: 1750 us; the launch traced here: 1740 us
  waiting for transfers between devices  1230 us (70%)
  matrix products  198 us (11%)
  blocking collectives  157 us (9%)
  local copies, waits for them, and re-layouts  71 us (4%)
  other arithmetic  66.9 us (4%)
  between operations  19 us (1%)
    unnamed x19, waiting for transfers between devices  267 us
    reduce_scatter x1, waiting for transfers between devices, on_device(): lax.psum_scatter(summed[18], 'fsdp', scatter_dimension=0, tiled=True)  175 us
    reduce_scatter x1, waiting for transfers between devices, on_device(): lax.psum_scatter(summed[16], 'fsdp', scatter_dimension=0, tiled=True)  174 us
    unnamed x2, blocking collectives  154 us
    reduce_scatter x1, waiting for transfers between devices, on_device(): lax.psum_scatter(summed[10], 'fsdp', scatter_dimension=0, tiled=True)  131 us
    reduce_scatter x1, waiting for transfers between devices, on_device(): lax.psum_scatter(summed[7], 'fsdp', scatter_dimension=0, tiled=True)  131 us
    all_gather x1, waiting for transfers between devices, on_device(): lax.all_gather(hidden_proj, 'fsdp', axis=0, tiled=True)  77.6 us
    dot_general x8, matrix products, matmul(): return jnp.dot(left, right, preferred_element_type=jnp.float32)  58.4 us
  transfers between devices with their start and end apart: 17, of which 15 were waited for; matrix products, arithmetic and copies ran while one was open for 17% of the time, Pallas kernels for 0%

commit v1 on v0

--- a/solution.py
+++ b/solution.py
@@ -1,8 +1,11 @@
+import functools
 import math
 
 import jax
 import jax.numpy as jnp
 from jax import lax
+from jax.experimental import pallas as pl
+from jax.experimental.pallas import tpu as pltpu
 from jax.sharding import PartitionSpec as P
 
 HEADS = 12
@@ -315,7 +318,243 @@
     return (image_grad, text_grad, grads)
 
 
+MATRICES = (0, 2, 7, 9, 10, 12, 16, 18)
+VECTORS = (1, 3, 4, 5, 6, 8, 11, 13, 14, 15, 19, 17)
+LANES = 384
+VEC_ROWS = 16
+GATHER_CHUNKS = ((0, 2, "vec"), (7, 9, 10), (12, 16), (18,))
+SCATTER_CHUNKS = ((18,), (16,), (12, 7, 9, 10), (0, 2, "vec"))
+BOTH = ("fsdp", "dp")
+
+
+class Place:
+    def __init__(self):
+        self.core = lax.axis_index("dp")
+        chip = lax.axis_index("fsdp")
+        self.x, self.y, self.z = chip & 1, (chip >> 1) & 1, chip >> 2
+
+    def scalars(self):
+        return jnp.stack([self.core, self.x, self.y, self.z]).astype(jnp.int32)
+
+
+def swap_cores(values):
+    return lax.ppermute(values, "dp", [(0, 1), (1, 0)])
+
+
+def to_chip(values, mask_zero, mask_one):
+    pairs = []
+    for chip in range(16):
+        pairs.append((chip * 2, (chip ^ mask_zero) * 2))
+        pairs.append((chip * 2 + 1, (chip ^ mask_one) * 2 + 1))
+    return lax.ppermute(values, BOTH, pairs)
+
+
+def sub_blocks(weight_index):
+    return 4 if weight_index == 16 else 1
+
+
+def block_rows(shards, weight_index):
+    if weight_index == "vec":
+        return VEC_ROWS
+    return shards[weight_index].shape[0] * sub_blocks(weight_index)
+
+
+def half_of(shard, core, weight_index):
+    count = sub_blocks(weight_index)
+    width = count * LANES
+    half = lax.dynamic_slice_in_dim(shard, core * width, width, 1)
+    if count > 1:
+        half = jnp.concatenate([half[:, s * LANES : (s + 1) * LANES] for s in range(count)], 0)
+    return half
+
+
+def assemble_kernel(layout, place_ref, s8, r8, s8p, r8p, *outs):
+    core, x, y = place_ref[0], place_ref[1], place_ref[2]
+
+    def fill(zero_s, zero_r, one_s, one_r):
+        for (offset, rows, count, is_vec), out in zip(layout, outs):
+            for s in range(count):
+                first = slice(offset + s * rows, offset + (s + 1) * rows)
+                columns = slice(s * LANES, (s + 1) * LANES)
+                for z in range(4):
+                    for b in range(2):
+                        out[z, y, b, :, columns] = zero_s[z, b, first, :]
+                        out[z, 1 - y, b, :, columns] = zero_r[z, b, first, :]
+                if is_vec:
+                    continue
+                columns = slice((count + s) * LANES, (count + s + 1) * LANES)
+                for z in range(4):
+                    for b in range(2):
+                        out[z, b, x, :, columns] = one_s[z, b, first, :]
+                        out[z, b, 1 - x, :, columns] = one_r[z, b, first, :]
+
+    @pl.when(core == 0)
+    def _():
+        fill(s8, r8, s8p, r8p)
+
+    @pl.when(core == 1)
+    def _():
+        fill(s8p, r8p, s8, r8)
+
+
+def assemble(place, pieces, shards, chunk):
+    layout, shapes, offset = [], [], 0
+    for index in chunk:
+        if index == "vec":
+            rows, count, columns = VEC_ROWS, 1, LANES
+        else:
+            rows, columns = shards[index].shape
+            count = sub_blocks(index)
+        layout.append((offset, rows, count, index == "vec"))
+        offset += rows * count
+        shapes.append(jax.ShapeDtypeStruct((4, 2, 2, rows, columns), jnp.bfloat16))
+    fast = pl.BlockSpec(memory_space=pltpu.VMEM)
+    return pl.pallas_call(
+        functools.partial(assemble_kernel, tuple(layout)),
+        out_shape=tuple(shapes),
+        in_specs=[pl.BlockSpec(memory_space=pltpu.SMEM)] + [fast] * 4,
+        out_specs=tuple(fast for _ in shapes),
+        compiler_params=pltpu.CompilerParams(vmem_limit_bytes=48 * 2**20),
+    )(place.scalars(), *pieces)
+
+
+def gather_chunk(place, shards, chunk, vec):
+    parts = [vec if i == "vec" else half_of(shards[i], place.core, i) for i in chunk]
+    own = jnp.concatenate(parts, 0) if len(parts) > 1 else parts[0]
+    others = [to_chip(own, 4 * step, 4 * step) for step in (1, 2, 3)]
+    along_z = in_order([own] + others, place.z)
+    beside = to_chip(along_z, 1, 2)
+    mine = jnp.where(place.core == 0, place.x, place.y)
+    s8 = jnp.where(mine == 0, jnp.stack([along_z, beside], 1), jnp.stack([beside, along_z], 1))
+    r8 = to_chip(s8, 2, 1)
+    s8p, r8p = swap_cores(s8), swap_cores(r8)
+    outs = assemble(place, (s8, r8, s8p, r8p), shards, chunk)
+    return {i: out.reshape(-1, out.shape[-1]) for i, out in zip(chunk, outs)}
+
+
+def in_order(relative, z):
+    a, b, c, d = relative
+    low = z & 1
+    e, f = jnp.where(low == 0, a, b), jnp.where(low == 0, b, a)
+    g, h = jnp.where(low == 0, c, d), jnp.where(low == 0, d, c)
+    high = (z >> 1) == 0
+    return jnp.stack(
+        [jnp.where(high, e, g), jnp.where(high, f, h), jnp.where(high, g, e), jnp.where(high, h, f)]
+    )
+
+
+def gather_fast(shards):
+    place = Place()
+    flat = jnp.concatenate([shards[i] for i in VECTORS])
+    vec = jnp.pad(flat, (0, VEC_ROWS * LANES - flat.shape[0])).reshape(VEC_ROWS, LANES)
+    whole = {}
+    for chunk in GATHER_CHUNKS:
+        whole.update(gather_chunk(place, shards, chunk, vec))
+    vectors = whole["vec"].reshape(16, VEC_ROWS * LANES)
+    at = 0
+    for i in VECTORS:
+        width = shards[i].shape[0]
+        whole[i] = vectors[:, at : at + width].reshape(-1)
+        at += width
+    return tuple(whole[i] for i in range(20))
+
+
+def halves(place, grad, index, shards):
+    grad = to_low(grad)
+    if index == "vec":
+        return grad, grad
+    count = sub_blocks(index)
+    width = count * LANES
+    made = []
+    for core in (place.core, 1 - place.core):
+        half = lax.dynamic_slice_in_dim(grad, core * width, width, 1)
+        half = half.reshape(16, shards[index].shape[0], width)
+        if count > 1:
+            half = jnp.concatenate([half[:, :, s * LANES : (s + 1) * LANES] for s in range(count)], 1)
+        made.append(half)
+    return tuple(made)
+
+
+def add_low(*values):
+    total = values[0].astype(jnp.float32)
+    for value in values[1:]:
+        total = total + value.astype(jnp.float32)
+    return to_low(total)
+
+
+def pick(values, at, axis):
+    return lax.dynamic_index_in_dim(values, at, axis, keepdims=False)
+
+
+def scatter_chunk(place, grads, chunk, shards):
+    pairs = [halves(place, grads[i], i, shards) for i in chunk]
+    keep = jnp.concatenate([p[0] for p in pairs], 1) if len(pairs) > 1 else pairs[0][0]
+    send = jnp.concatenate([p[1] for p in pairs], 1) if len(pairs) > 1 else pairs[0][1]
+    got = swap_cores(send)
+    rows = keep.shape[1]
+    keep, got = (v.reshape(4, 4, rows, LANES) for v in (keep, got))
+    zero = place.core == 0
+    x, y = place.x, place.y
+    near = [jnp.where(zero, 2 * y + s, 2 * s + x) for s in (0, 1)]
+    far = [jnp.where(zero, 2 * (1 - y) + s, 2 * s + (1 - x)) for s in (0, 1)]
+    sent = jnp.stack([add_low(pick(keep, q, 1), pick(got, q, 1)) for q in far], 1)
+    kept = jnp.stack([add_low(pick(keep, q, 1), pick(got, q, 1)) for q in near], 1)
+    got = to_chip(sent, 2, 1)
+    mine = jnp.where(zero, x, y)
+    sent = add_low(pick(kept, 1 - mine, 1), pick(got, 1 - mine, 1))
+    kept = add_low(pick(kept, mine, 1), pick(got, mine, 1))
+    got = to_chip(sent, 1, 2)
+    total = add_low(kept, got)
+    arrived = [to_chip(pick(total, place.z ^ s, 0), 4 * s, 4 * s) for s in (1, 2, 3)]
+    final = add_low(pick(total, place.z, 0), *arrived)
+    other = swap_cores(final)
+    left = jnp.where(zero, final, other).astype(jnp.float32)
+    right = jnp.where(zero, other, final).astype(jnp.float32)
+    result, at = {}, 0
+    for index in chunk:
+        if index == "vec":
+            result[index] = left[at : at + VEC_ROWS].reshape(-1)
+            at += VEC_ROWS
+            continue
+        rows, count = shards[index].shape[0], sub_blocks(index)
+        pieces = []
+        for side in (left, right):
+            for s in range(count):
+                pieces.append(side[at + s * rows : at + (s + 1) * rows])
+        result[index] = jnp.concatenate(pieces, 1)
+        at += rows * count
+    return result
+
+
+def scatter_fast(grads, shards):
+    place = Place()
+    grads = dict(enumerate(grads))
+    flat = jnp.concatenate([grads[i].reshape(16, -1) for i in VECTORS], 1)
+    flat = jnp.pad(flat, ((0, 0), (0, VEC_ROWS * LANES - flat.shape[1])))
+    grads["vec"] = flat.reshape(16, VEC_ROWS, LANES)
+    owned = {}
+    for chunk in SCATTER_CHUNKS:
+        owned.update(scatter_chunk(place, grads, chunk, shards))
+    at = 0
+    for i in VECTORS:
+        width = shards[i].shape[0]
+        owned[i] = owned["vec"][at : at + width]
+        at += width
+    return tuple(owned[i] for i in range(20))
+
+
+def gather_any(shards):
+    return tuple(lax.all_gather(shard, "fsdp", axis=0, tiled=True) for shard in shards)
+
+
+def scatter_any(grads):
+    pieces = [lax.psum_scatter(g, "fsdp", scatter_dimension=0, tiled=True) for g in grads]
+    return tuple(lax.psum(to_low(p), "dp").astype(jnp.float32) for p in pieces)
+
+
 def on_device(
+    chips,
+    cores,
     image_states,
     text_states,
     size_group,
@@ -342,120 +581,42 @@
     return_proj,
     return_bias,
 ):
-    gathered = (
-        lax.all_gather(image_proj, "fsdp", axis=0, tiled=True),
-        lax.all_gather(image_bias, "fsdp", axis=0, tiled=True),
-        lax.all_gather(text_proj, "fsdp", axis=0, tiled=True),
-        lax.all_gather(text_bias, "fsdp", axis=0, tiled=True),
-        lax.all_gather(cls_token, "fsdp", axis=0, tiled=True),
-        lax.all_gather(first_gain, "fsdp", axis=0, tiled=True),
-        lax.all_gather(first_shift, "fsdp", axis=0, tiled=True),
-        lax.all_gather(query_proj, "fsdp", axis=0, tiled=True),
-        lax.all_gather(query_bias, "fsdp", axis=0, tiled=True),
-        lax.all_gather(key_proj, "fsdp", axis=0, tiled=True),
-        lax.all_gather(value_proj, "fsdp", axis=0, tiled=True),
-        lax.all_gather(value_bias, "fsdp", axis=0, tiled=True),
-        lax.all_gather(output_proj, "fsdp", axis=0, tiled=True),
-        lax.all_gather(output_bias, "fsdp", axis=0, tiled=True),
-        lax.all_gather(second_gain, "fsdp", axis=0, tiled=True),
-        lax.all_gather(second_shift, "fsdp", axis=0, tiled=True),
-        lax.all_gather(hidden_proj, "fsdp", axis=0, tiled=True),
-        lax.all_gather(hidden_bias, "fsdp", axis=0, tiled=True),
-        lax.all_gather(return_proj, "fsdp", axis=0, tiled=True),
-        lax.all_gather(return_bias, "fsdp", axis=0, tiled=True),
-    )
-
-    def forward_step(running, item_data):
-        image_rows, text_rows, size_code, length = item_data
-        result, kept_rows = item_forward(gathered, image_rows, text_rows, size_code, length)
-        return (running, (result, kept_rows))
-
-    unused_carry, (layer_out, kept_all) = lax.scan(
-        forward_step, None, (image_states, text_states, size_group, caption_len)
-    )
-    initial = tuple((jnp.zeros(weight.shape, jnp.float32) for weight in gathered))
-
-    def backward_step(running, item_data):
-        image_rows, text_rows, size_code, length, kept_rows, out_grad = item_data
+    shards = (
+        image_proj,
+        image_bias,
+        text_proj,
+        text_bias,
+        cls_token,
+        first_gain,
+        first_shift,
+        query_proj,
+        query_bias,
+        key_proj,
+        value_proj,
+        value_bias,
+        output_proj,
+        output_bias,
+        second_gain,
+        second_shift,
+        hidden_proj,
+        hidden_bias,
+        return_proj,
+        return_bias,
+    )
+    by_permutes = chips == 16 and cores == 2
+    weights = gather_fast(shards) if by_permutes else gather_any(shards)
+    results, summed = [], None
+    for item in range(image_states.shape[0]):
+        image_rows, text_rows = image_states[item], text_states[item]
+        code, length = size_group[item], caption_len[item]
+        result, kept_rows = item_forward(weights, image_rows, text_rows, code, length)
         image_grad, text_grad, grads = item_backward(
-            gathered, image_rows, text_rows, size_code, length, kept_rows, out_grad
-        )
-        return (jax.tree.map(jnp.add, running, grads), (image_grad, text_grad))
-
-    summed, (image_grads, text_grads) = lax.scan(
-        backward_step,
-        initial,
-        (image_states, text_states, size_group, caption_len, kept_all, cotangent),
-    )
-    pieces = (
-        lax.psum_scatter(summed[0], "fsdp", scatter_dimension=0, tiled=True),
-        lax.psum_scatter(summed[1], "fsdp", scatter_dimension=0, tiled=True),
-        lax.psum_scatter(summed[2], "fsdp", scatter_dimension=0, tiled=True),
-        lax.psum_scatter(summed[3], "fsdp", scatter_dimension=0, tiled=True),
-        lax.psum_scatter(summed[4], "fsdp", scatter_dimension=0, tiled=True),
-        lax.psum_scatter(summed[5], "fsdp", scatter_dimension=0, tiled=True),
-        lax.psum_scatter(summed[6], "fsdp", scatter_dimension=0, tiled=True),
-        lax.psum_scatter(summed[7], "fsdp", scatter_dimension=0, tiled=True),
-        lax.psum_scatter(summed[8], "fsdp", scatter_dimension=0, tiled=True),
-        lax.psum_scatter(summed[9], "fsdp", scatter_dimension=0, tiled=True),
-        lax.psum_scatter(summed[10], "fsdp", scatter_dimension=0, tiled=True),
-        lax.psum_scatter(summed[11], "fsdp", scatter_dimension=0, tiled=True),
-        lax.psum_scatter(summed[12], "fsdp", scatter_dimension=0, tiled=True),
-        lax.psum_scatter(summed[13], "fsdp", scatter_dimension=0, tiled=True),
-        lax.psum_scatter(summed[14], "fsdp", scatter_dimension=0, tiled=True),
-        lax.psum_scatter(summed[15], "fsdp", scatter_dimension=0, tiled=True),
-        lax.psum_scatter(summed[16], "fsdp", scatter_dimension=0, tiled=True),
-        lax.psum_scatter(summed[17], "fsdp", scatter_dimension=0, tiled=True),
-        lax.psum_scatter(summed[18], "fsdp", scatter_dimension=0, tiled=True),
-        lax.psum_scatter(summed[19], "fsdp", scatter_dimension=0, tiled=True),
-    )
-    owned_grads = (
-        lax.psum(pieces[0].astype(jnp.bfloat16), "dp").astype(jnp.float32),
-        lax.psum(pieces[1].astype(jnp.bfloat16), "dp").astype(jnp.float32),
-        lax.psum(pieces[2].astype(jnp.bfloat16), "dp").astype(jnp.float32),
-        lax.psum(pieces[3].astype(jnp.bfloat16), "dp").astype(jnp.float32),
-        lax.psum(pieces[4].astype(jnp.bfloat16), "dp").astype(jnp.float32),
-        lax.psum(pieces[5].astype(jnp.bfloat16), "dp").astype(jnp.float32),
-        lax.psum(pieces[6].astype(jnp.bfloat16), "dp").astype(jnp.float32),
-        lax.psum(pieces[7].astype(jnp.bfloat16), "dp").astype(jnp.float32),
-        lax.psum(pieces[8].astype(jnp.bfloat16), "dp").astype(jnp.float32),
-        lax.psum(pieces[9].astype(jnp.bfloat16), "dp").astype(jnp.float32),
-        lax.psum(pieces[10].astype(jnp.bfloat16), "dp").astype(jnp.float32),
-        lax.psum(pieces[11].astype(jnp.bfloat16), "dp").astype(jnp.float32),
-        lax.psum(pieces[12].astype(jnp.bfloat16), "dp").astype(jnp.float32),
-        lax.psum(pieces[13].astype(jnp.bfloat16), "dp").astype(jnp.float32),
-        lax.psum(pieces[14].astype(jnp.bfloat16), "dp").astype(jnp.float32),
-        lax.psum(pieces[15].astype(jnp.bfloat16), "dp").astype(jnp.float32),
-        lax.psum(pieces[16].astype(jnp.bfloat16), "dp").astype(jnp.float32),
-        lax.psum(pieces[17].astype(jnp.bfloat16), "dp").astype(jnp.float32),
-        lax.psum(pieces[18].astype(jnp.bfloat16), "dp").astype(jnp.float32),
-        lax.psum(pieces[19].astype(jnp.bfloat16), "dp").astype(jnp.float32),
-    )
-    return (
-        layer_out,
-        image_grads,
-        text_grads,
-        owned_grads[0],
-        owned_grads[1],
-        owned_grads[2],
-        owned_grads[3],
-        owned_grads[4],
-        owned_grads[5],
-        owned_grads[6],
-        owned_grads[7],
-        owned_grads[8],
-        owned_grads[9],
-        owned_grads[10],
-        owned_grads[11],
-        owned_grads[12],
-        owned_grads[13],
-        owned_grads[14],
-        owned_grads[15],
-        owned_grads[16],
-        owned_grads[17],
-        owned_grads[18],
-        owned_grads[19],
-    )
+            weights, image_rows, text_rows, code, length, kept_rows, cotangent[item]
+        )
+        results.append((result, image_grad, text_grad))
+        summed = grads if summed is None else jax.tree.map(jnp.add, summed, grads)
+    owned = scatter_fast(summed, shards) if by_permutes else scatter_any(summed)
+    return tuple(jnp.stack(parts) for parts in zip(*results)) + owned
 
 
 def solution(mesh):
@@ -486,8 +647,9 @@
         P("fsdp", None),
         P("fsdp"),
     )
+    chips, cores = mesh.shape["fsdp"], mesh.shape["dp"]
     return jax.shard_map(
-        on_device,
+        functools.partial(on_device, chips, cores),
         mesh=mesh,
         in_specs=placed,
         out_specs=(

time: 1750 us -> 538 us (0.31)
  waiting for transfers between devices: 1230 us -> 102 us
  blocking collectives: 157 us -> 0 us
  starting transfers between devices: 1.06 us -> 65.9 us
  matrix products: 198 us -> 178 us
    reduce_scatter x6 -> x0, waiting for transfers between devices: 626 us -> none  [the longest x1 175 us: on_device(): lax.psum_scatter(summed[18], 'fsdp', scatter_dimension=0, tiled=True)]
    all_gather x8 -> x0, waiting for transfers between devices: 320 us -> none  [the longest x1 77.6 us: on_device(): lax.all_gather(hidden_proj, 'fsdp', axis=0, tiled=True)]
    unnamed x19 -> x0, waiting for transfers between devices: 267 us -> none
    unnamed x2 -> x0, blocking collectives: 154 us -> none
    ppermute x0 -> x56, waiting for transfers between devices: none -> 102 us  [the longest x40 102 us: to_chip(): return lax.ppermute(values, BOTH, pairs)]
    ppermute x0 -> x56, starting transfers between devices: none -> 65.9 us  [the longest x40 62.8 us: to_chip(): return lax.ppermute(values, BOTH, pairs)]
    convert_element_type x33 -> x3, other arithmetic: 26.7 us -> 0.12 us  [the longest x2 0.07 us: scatter_chunk(): left = jnp.where(zero, final, other).astype(jnp.float32)]
    convert_element_type x4 -> x21, other arithmetic: 20.9 us -> 35.6 us  [to_low(): return values.astype(jnp.bfloat16)]
  transfers between devices with their start and end apart: 17 -> 56, of which waited for: 15 -> 15; matrix products, arithmetic and copies ran while one was open for 17% -> 22% of each run, Pallas kernels for 0% -> 2%
where the time goes in v1:
time: 538 us; the launch traced here: 529 us
  matrix products  178 us (33%)
  waiting for transfers between devices  102 us (19%)
  local copies, waits for them, and re-layouts  88.3 us (16%)
  other arithmetic  75.1 us (14%)
  starting transfers between devices  65.9 us (12%)
  Pallas kernels  15.4 us (3%)
    ppermute x40, waiting for transfers between devices, to_chip(): return lax.ppermute(values, BOTH, pairs)  102 us
    ppermute x40, starting transfers between devices, to_chip(): return lax.ppermute(values, BOTH, pairs)  62.8 us
    dot_general x8, matrix products, matmul(): return jnp.dot(left, right, preferred_element_type=jnp.float32)  53.7 us
    convert_element_type x21, other arithmetic, to_low(): return values.astype(jnp.bfloat16)  35.6 us
    dot_general x8, matrix products, right_product(): lax.dot_general(left, right, (((1,), (1,)), ((), ())), preferred_element_...  34.2 us
    dot_general x8, matrix products, left_product(): lax.dot_general(left, right, (((0,), (0,)), ((), ())), preferred_element_...  30.4 us
    unnamed x176, local copies, waits for them, and re-layouts  30.3 us
    dynamic_slice x21, local copies, waits for them, and re-layouts, head_slice(): part = lax.dynamic_slice_in_dim(source, offset, span_width, 1)  20.3 us
  transfers between devices with their start and end apart: 56, of which 15 were waited for; matrix products, arithmetic and copies ran while one was open for 22% of the time, Pallas kernels for 2%

profile of v1, /device:TPU:0, one launch (start us, length us, event | category | flops | bytes accessed | tf_op | source)
XLA Modules:
  0.0 529.0 jit_solution(13848710952917467529)
XLA Ops:
  0.7 8.2 %concatenate.77 = bf16[720]{0:T(1024)(128)(2,1)S(1)} concatenate(bf16[48]{0:T(256)(128)(2,1)} %param.35, bf16[48]{0:T(256)(128)(2,1)} %param.37, bf16[48]{0:T(256)(128)(2,1)} %param.38, bf16[48]{0:T(256)(128)(2,1)} %param.39, bf16[48]{0:T(256)(128)(2,1)} %param.40, bf16[48]{0:T(256)(128)(2,1)} %param.42, bf16[48]{0:T(256)(128)(2,1)} %param.45, bf16[48]{0:T(256)(128)(2,1)} %param.47, ...), dimensions={0} | concatenate | bytes 2880 | tf_op jit(solution)/shard_map/concatenate | solution.py:448
  10.5 4.1 collective-permute-start.1
  18.5 2.9 collective-permute-start.8
  27.6 3.0 collective-permute-start.22
  32.3 2.5 collective-permute-start.16
  36.5 9.5 %collective-permute-done.22 = bf16[192,384]{1,0:T(8,128)(2,1)S(1)} collective-permute-done((bf16[192,384]{1,0:T(8,128)(2,1)S(1)}, bf16[192,384]{1,0:T(8,128)(2,1)S(1)}, u32[]{:S(2)}, u32[]{:S(2)}) %collective-permute-start.22) | collective-permute-done | bytes 147488 | tf_op jit(solution)/shard_map/ppermute | solution.py:349
  46.0 7.6 %collective-permute-start.14 = (bf16[240,384]{1,0:T(8,128)(2,1)S(1)}, bf16[240,384]{1,0:T(8,128)(2,1)S(1)}, u32[]{:S(2)}, u32[]{:S(2)}) collective-permute-start(bf16[240,384]{1,0:T(8,128)(2,1)S(1)} %dynamic-slice_dynamic-update-slice_fusion), channel_id=1, source_target_pairs={{0,8},{1,9},{2,10},{3,11},{4,12},{5,13},{6,14},{7,15},{8,0},{9,1},... | collective-permute-start | bytes 552968 | tf_op jit(solution)/shard_map/ppermute | solution.py:349
  57.8 2.9 collective-permute-done.15
  66.5 2.6 collective-permute-start.11
  72.8 20.2 %collective-permute-done.24 = bf16[4,192,384]{2,1,0:T(8,128)(2,1)S(1)} collective-permute-done((bf16[4,192,384]{2,1,0:T(8,128)(2,1)S(1)}, bf16[4,192,384]{2,1,0:T(8,128)(2,1)S(1)}, u32[]{:S(2)}, u32[]{:S(2)}) %collective-permute-start.24) | collective-permute-done | bytes 589856 | tf_op jit(solution)/shard_map/ppermute | solution.py:349
  105.7 3.0 fusion.44
  119.1 3.5 shard_map.417
  126.8 2.5 copy.68
  129.4 3.9 add_convert_fusion.3
  133.2 2.5 copy.67
  135.8 3.9 convolution_convert_fusion.3
  139.7 2.5 copy.69
  143.8 35.8 %while.34 = (s32[]{:T(128)}, bf16[839,768]{0,1:T(8,128)(2,1)}, f32[12,839]{1,0:T(8,128)S(1)}, bf16[839,768]{0,1:T(8,128)(2,1)}, bf16[839,768]{0,1:T(8,128)(2,1)}...) while((s32[]{:T(128)}, bf16[839,768]{0,1:T(8,128)(2,1)}, ...), condition=%wide.region_5.6_spmd.clone, body=%wide.region_2.5_spmd.clone.sunk | while | flops 754822272 | bytes 39085948 | solution.py:103
  146.1 2.4 fusion.191
  148.5 3.0 fusion.192
  151.5 3.4 fusion.193
  158.0 2.4 fusion.191
  160.4 3.0 fusion.192
  163.4 3.4 fusion.193
  172.3 3.0 fusion.192
  175.3 3.4 fusion.193
  179.6 4.6 shard_map.419
  184.2 5.3 %shard_map.418 = (bf16[4,2,2,48,768]{4,3,2,1,0:T(8,128)(2,1)S(1)}, bf16[4,2,2,48,3072]{4,3,2,1,0:T(8,128)(2,1)}) custom-call(s32[4]{0:T(128)S(1)} %pad_add_fusion.place_ref, bf16[4,2,240,384]{3,2,1,0:T(8,128)(2,1)S(1)} %maximum_select_fusion.s8, bf16[4,2,240,384]{3,2,1,0:T(8,128)(2,1)} %collective-permute-done.18.r8, ...), custom_call_target="tpu_custom_call" | custom-call | tf_op jit(solution)/shard_map/pallas_call | solution.py:412
  192.0 29.4 %multiply_convert_fusion.1 = (bf16[839,3072]{1,0:T(8,128)(2,1)}, f32[839,3072]{1,0:T(8,128)}, f32[839,3072]{1,0:T(8,128)}) fusion(f32[3072]{0:T(1024)S(1)} %copy-done.58, bf16[768,3072]{1,0:T(8,128)(2,1)S(1)} %bitcast.462, f32[839,768]{1,0:T(8,128)S(1)} %get-tuple-element.652, f32[768]{0:T(1024)S(1)} %copy-done.63, f32[768]{0:T(1024)S(1)} %copy-done.57, ...), kind=kOutput, calls=%fused_computation.67 | convolution fusion | flops 4132229376 | bytes 33095224 | tf_op jit(solution)/shard_map/dot_general | solution.py:22
  221.4 13.9 %convert_reduce_fusion = (bf16[3072]{0:T(1024)(128)(2,1)}, bf16[839,3072]{1,0:T(8,128)(2,1)}) fusion(f32[839,3072]{1,0:T(8,128)} %get-tuple-element.524, bf16[3072,768]{1,0:T(8,128)(2,1)S(1)} %bitcast.426, bf16[1,839,768]{2,1,0:T(8,128)(2,1)S(1)} %copy-done.23, f32[839,3072]{1,0:T(8,128)} %get-tuple-element.653, f32[3072]{0:T(1024)S(1)} %copy-done.58), kind=kOutput, calls=%fused_computation.66 | convolution fusion | flops 4002711552 | bytes 31799808 | tf_op jit(solution)/shard_map/dot_general | solution.py:32
  235.3 9.3 %multiply_reduce_fusion.1 = (bf16[768]{0:T(1024)(128)(2,1)}, f32[839]{0:T(1024)S(1)}, bf16[768]{0:T(1024)(128)(2,1)}, f32[839,768]{1,0:T(8,128)S(1)}) fusion(f32[839,768]{1,0:T(8,128)S(1)} %get-tuple-element.652, f32[839]{0:T(1024)S(1)} %fusion.94, f32[839]{0:T(1024)S(1)} %broadcast_multiply_fusion, f32[768]{0:T(1024)S(1)} %copy-done.57, ...), kind=kOutput, calls=%fused_computation.90 | convolution fusion | flops 3964051200 | bytes 15044436 | tf_op jit(solution)/shard_map/dot_general | solution.py:32
  244.6 7.5 %convolution_convert_fusion.1 = bf16[768,3072]{1,0:T(8,128)(2,1)} fusion(bf16[839,3072]{1,0:T(8,128)(2,1)S(1)} %copy-done.68, f32[839,768]{1,0:T(8,128)S(1)} %get-tuple-element.652, f32[768]{0:T(1024)S(1)} %copy-done.63, f32[768]{0:T(1024)S(1)} %copy-done.57, f32[839]{0:T(1024)S(1)} %fusion.94, f32[839]{0:T(1024)S(1)} %broadcast_multiply_fusion), kind=kOutput, calls=%fused_computation.82 | convolution fusion | flops 3964479744 | bytes 12463672 | tf_op jit(solution)/shard_map/dot_general | solution.py:26
  254.5 2.4 convolution_convert_fusion.8
  261.6 82.0 %while.35 = (s32[]{:T(128)}, bf16[839,768]{0,1:T(8,128)(2,1)}, bf16[839,768]{0,1:T(8,128)(2,1)}, bf16[839,768]{0,1:T(8,128)(2,1)S(1)}, bf16[839,768]{0,1:T(8,128...) while((s32[]{:T(128)}, bf16[839,768]{0,1:T(8,128)(2,1)}, ...), condition=%wide.region_12.13_spmd.clone, body=%wide.region_10.12_spmd.clone.sunk | while | flops 1845351040 | bytes 95882832 | solution.py:155
  268.3 2.8 fusion.207
  271.1 6.4 %multiply_reduce_fusion.8 = (f32[4,839]{1,0:T(4,128)S(1)}, f32[4,839,839]{1,2,0:T(8,128)}) fusion(f32[4,839,839]{1,2,0:T(8,128)S(1)} %fusion.204, f32[4,839]{1,0:T(4,128)S(1)} %constant_dynamic-slice_fusion.41, pred[839]{0:T(1024)(128)(4,1)S(1)} %fusion.205, bf16[839,4,64]{0,2,1:T(8,128)(2,1)S(1)} %bitcast.413, bf16[839,4,64]{0,2,1:T(8,128)(2,1)S(1)} %bitcast.414), kind=kOutput, calls=%fused_computation.26.clone.1 | convolution fusion | flops 374482592 | bytes 23412296 | tf_op jit(solution)/shard_map/while/body/eval_jaxpr/qhd,khd->hqk/dot_general | solution.py:129
  277.5 6.7 %multiply_convert_fusion.3 = bf16[4,839,839]{1,2,0:T(8,128)(2,1)S(1)} fusion(f32[4,839,839]{1,2,0:T(8,128)} %get-tuple-element.797, f32[4,839,839]{1,2,0:T(8,128)S(1)} %fusion.204, f32[4,839]{1,0:T(4,128)S(1)} %get-tuple-element.798, f32[4,839]{1,0:T(4,128)S(1)} %constant_dynamic-slice_fusion.41, pred[839]{0:T(1024)(128)(4,1)S(1)} %fusion.205), kind=kLoop, calls=%fused_computation.25.clone.1 | loop fusion | flops 16894104 | bytes 28184528 | tf_op jit(solution)/shard_map/while/body/eval_jaxpr/convert_element_type | solution.py:38
  295.5 2.8 fusion.207
  298.3 6.4 %multiply_reduce_fusion.8 = (f32[4,839]{1,0:T(4,128)S(1)}, f32[4,839,839]{1,2,0:T(8,128)}) fusion(f32[4,839,839]{1,2,0:T(8,128)S(1)} %fusion.204, f32[4,839]{1,0:T(4,128)S(1)} %constant_dynamic-slice_fusion.41, pred[839]{0:T(1024)(128)(4,1)S(1)} %fusion.205, bf16[839,4,64]{0,2,1:T(8,128)(2,1)S(1)} %bitcast.413, bf16[839,4,64]{0,2,1:T(8,128)(2,1)S(1)} %bitcast.414), kind=kOutput, calls=%fused_computation.26.clone.1 | convolution fusion | flops 374482592 | bytes 23412296 | tf_op jit(solution)/shard_map/while/body/eval_jaxpr/qhd,khd->hqk/dot_general | solution.py:129
  304.7 6.7 %multiply_convert_fusion.3 = bf16[4,839,839]{1,2,0:T(8,128)(2,1)S(1)} fusion(f32[4,839,839]{1,2,0:T(8,128)} %get-tuple-element.797, f32[4,839,839]{1,2,0:T(8,128)S(1)} %fusion.204, f32[4,839]{1,0:T(4,128)S(1)} %get-tuple-element.798, f32[4,839]{1,0:T(4,128)S(1)} %constant_dynamic-slice_fusion.41, pred[839]{0:T(1024)(128)(4,1)S(1)} %fusion.205), kind=kLoop, calls=%fused_computation.25.clone.1 | loop fusion | flops 16894104 | bytes 28184528 | tf_op jit(solution)/shard_map/while/body/eval_jaxpr/convert_element_type | solution.py:38
  322.6 2.8 fusion.207
  325.4 6.4 %multiply_reduce_fusion.8 = (f32[4,839]{1,0:T(4,128)S(1)}, f32[4,839,839]{1,2,0:T(8,128)}) fusion(f32[4,839,839]{1,2,0:T(8,128)S(1)} %fusion.204, f32[4,839]{1,0:T(4,128)S(1)} %constant_dynamic-slice_fusion.41, pred[839]{0:T(1024)(128)(4,1)S(1)} %fusion.205, bf16[839,4,64]{0,2,1:T(8,128)(2,1)S(1)} %bitcast.413, bf16[839,4,64]{0,2,1:T(8,128)(2,1)S(1)} %bitcast.414), kind=kOutput, calls=%fused_computation.26.clone.1 | convolution fusion | flops 374482592 | bytes 23412296 | tf_op jit(solution)/shard_map/while/body/eval_jaxpr/qhd,khd->hqk/dot_general | solution.py:129
  331.8 6.7 %multiply_convert_fusion.3 = bf16[4,839,839]{1,2,0:T(8,128)(2,1)S(1)} fusion(f32[4,839,839]{1,2,0:T(8,128)} %get-tuple-element.797, f32[4,839,839]{1,2,0:T(8,128)S(1)} %fusion.204, f32[4,839]{1,0:T(4,128)S(1)} %get-tuple-element.798, f32[4,839]{1,0:T(4,128)S(1)} %constant_dynamic-slice_fusion.41, pred[839]{0:T(1024)(128)(4,1)S(1)} %fusion.205), kind=kLoop, calls=%fused_computation.25.clone.1 | loop fusion | flops 16894104 | bytes 28184528 | tf_op jit(solution)/shard_map/while/body/eval_jaxpr/convert_element_type | solution.py:38
  343.6 4.4 convolution_convert_fusion.6
  349.4 2.5 convolution_convert_fusion.5
  352.3 2.5 convolution_convert_fusion.7
  371.8 7.2 %convolution_convert_fusion = bf16[3072,768]{1,0:T(8,128)(2,1)} fusion(bf16[839,3072]{1,0:T(8,128)(2,1)S(1)} %bitcast.466, bf16[1,839,768]{2,1,0:T(8,128)(2,1)S(1)} %copy-done.24), kind=kOutput, calls=%fused_computation.81 | convolution fusion | flops 3961257984 | bytes 11162112 | tf_op jit(solution)/shard_map/dot_general | solution.py:26
  381.5 3.2 copy.106
  386.1 4.2 copy.107
  390.3 3.0 constant_dynamic-slice_fusion.21
  400.7 7.7 %fusion.43 = bf16[1,839,768]{2,1,0:T(8,128)(2,1)} fusion(f32[839,768]{1,0:T(8,128)S(1)} %copy-done.19, bf16[839,3072]{1,0:T(8,128)(2,1)} %get-tuple-element.523, bf16[3072,768]{1,0:T(8,128)(2,1)S(1)} %bitcast.429, f32[768]{0:T(1024)S(1)} %copy-done.62), kind=kOutput, calls=%fused_computation.122 | convolution fusion | flops 3960831744 | bytes 13742592 | tf_op jit(solution)/shard_map/dot_general | solution.py:22
  411.4 8.4 %collective-permute-done.29 = bf16[4,2,112,384]{3,2,1,0:T(8,128)(2,1)S(1)} collective-permute-done((bf16[4,2,112,384]{3,2,1,0:T(8,128)(2,1)S(1)}, bf16[4,2,112,384]{3,2,1,0:T(8,128)(2,1)S(1)}, u32[]{:S(2)}, u32[]{:S(2)}) %collective-permute-start.29) | collective-permute-done | bytes 688160 | tf_op jit(solution)/shard_map/ppermute | solution.py:349
  424.7 4.6 add_convert_fusion.8
  431.3 3.5 collective-permute-start.33
  439.0 2.9 collective-permute-done.32
  448.9 5.4 %collective-permute-done.43 = bf16[4,2,192,384]{3,2,0,1:T(8,128)(2,1)} collective-permute-done((bf16[4,2,192,384]{3,2,0,1:T(8,128)(2,1)}, bf16[4,2,192,384]{3,2,0,1:T(8,128)(2,1)}, u32[]{:S(2)}, u32[]{:S(2)}) %collective-permute-start.43) | collective-permute-done | bytes 1179680 | tf_op jit(solution)/shard_map/ppermute | solution.py:349
  456.6 21.0 %collective-permute-done.50 = bf16[4,2,192,384]{3,2,0,1:T(8,128)(2,1)} collective-permute-done((bf16[4,2,192,384]{3,2,0,1:T(8,128)(2,1)}, bf16[4,2,192,384]{3,2,0,1:T(8,128)(2,1)}, u32[]{:S(2)}, u32[]{:S(2)}) %collective-permute-start.50) | collective-permute-done | bytes 1179680 | tf_op jit(solution)/shard_map/ppermute | solution.py:349
  481.2 3.4 collective-permute-start.40
  488.9 3.4 collective-permute-start.47
  493.9 2.8 collective-permute-start.52
  496.7 9.0 %collective-permute-done.39 = bf16[192,384]{1,0:T(8,128)(2,1)S(1)} collective-permute-done((bf16[192,384]{1,0:T(8,128)(2,1)S(1)}, bf16[192,384]{1,0:T(8,128)(2,1)S(1)}, u32[]{:S(2)}, u32[]{:S(2)}) %collective-permute-start.39) | collective-permute-done | bytes 147488 | tf_op jit(solution)/shard_map/ppermute | solution.py:349
  505.6 2.9 collective-permute-start.54
  508.8 9.4 %collective-permute-done.46 = bf16[192,384]{1,0:T(8,128)(2,1)S(1)} collective-permute-done((bf16[192,384]{1,0:T(8,128)(2,1)S(1)}, bf16[192,384]{1,0:T(8,128)(2,1)S(1)}, u32[]{:S(2)}, u32[]{:S(2)}) %collective-permute-start.46) | collective-permute-done | bytes 147488 | tf_op jit(solution)/shard_map/ppermute | solution.py:349
  518.6 6.0 %collective-permute-done.53 = bf16[192,384]{1,0:T(8,128)(2,1)S(1)} collective-permute-done((bf16[192,384]{1,0:T(8,128)(2,1)S(1)}, bf16[192,384]{1,0:T(8,128)(2,1)S(1)}, u32[]{:S(2)}, u32[]{:S(2)}) %collective-permute-start.53) | collective-permute-done | bytes 147488 | tf_op jit(solution)/shard_map/ppermute | solution.py:349
  (464 shorter events, 178.2 us)
Async XLA Ops:
  0.7 108.1 %copy-start = (bf16[1,513,768]{2,1,0:T(8,128)(2,1)S(1)}, bf16[1,513,768]{2,1,0:T(8,128)(2,1)}, u32[]{:S(2)}) copy-start(bf16[1,513,768]{2,1,0:T(8,128)(2,1)} %param.30) | copy-start | bytes 2363908
  10.4 44.7 %copy-start.44 = (bf16[192,768]{1,0:T(8,128)(2,1)S(1)}, bf16[192,768]{1,0:T(8,128)(2,1)}, u32[]{:S(2)}) copy-start(bf16[192,768]{1,0:T(8,128)(2,1)} %param.52) | copy-start | bytes 884740
  10.5 17.1 %collective-permute-start.1 = (bf16[112,384]{1,0:T(8,128)(2,1)S(1)}, bf16[112,384]{1,0:T(8,128)(2,1)S(1)}, u32[]{:S(2)}, u32[]{:S(2)}) collective-permute-start(bf16[112,384]{1,0:T(8,128)(2,1)S(1)} %pad_maximum_fusion.22), channel_id=1, source_target_pairs={{0,16},{1,17},{2,18},{3,19},{4,20},{5,21},{6,22},{7,23},{8,24},{9,... | collective-permute-start | bytes 258056 | tf_op jit(solution)/shard_map/ppermute | solution.py:349
  14.6 13.0 %collective-permute-start.2 = (bf16[112,384]{1,0:T(8,128)(2,1)S(1)}, bf16[112,384]{1,0:T(8,128)(2,1)S(1)}, u32[]{:S(2)}, u32[]{:S(2)}) collective-permute-start(bf16[112,384]{1,0:T(8,128)(2,1)S(1)} %pad_maximum_fusion.22), channel_id=1, source_target_pairs={{0,24},{1,25},{2,26},{3,27},{4,28},{5,29},{6,30},{7,31},{8,16},{9,... | collective-permute-start | bytes 258056 | tf_op jit(solution)/shard_map/ppermute | solution.py:349
  15.9 14.7 %collective-permute-start = (bf16[112,384]{1,0:T(8,128)(2,1)S(1)}, bf16[112,384]{1,0:T(8,128)(2,1)S(1)}, u32[]{:S(2)}, u32[]{:S(2)}) collective-permute-start(bf16[112,384]{1,0:T(8,128)(2,1)S(1)} %pad_maximum_fusion.22), channel_id=1, source_target_pairs={{0,8},{1,9},{2,10},{3,11},{4,12},{5,13},{6,14},{7,15},{8,0},{9,1},... | collective-permute-start | bytes 258056 | tf_op jit(solution)/shard_map/ppermute | solution.py:349
  18.5 13.7 %collective-permute-start.8 = (bf16[144,384]{1,0:T(8,128)(2,1)S(1)}, bf16[144,384]{1,0:T(8,128)(2,1)S(1)}, u32[]{:S(2)}, u32[]{:S(2)}) collective-permute-start(bf16[144,384]{1,0:T(8,128)(2,1)S(1)} %pad_maximum_fusion.21), channel_id=1, source_target_pairs={{0,16},{1,17},{2,18},{3,19},{4,20},{5,21},{6,22},{7,23},{8,24},{9,... | collective-permute-start | bytes 331784 | tf_op jit(solution)/shard_map/ppermute | solution.py:349
  21.3 10.9 %collective-permute-start.9 = (bf16[144,384]{1,0:T(8,128)(2,1)S(1)}, bf16[144,384]{1,0:T(8,128)(2,1)S(1)}, u32[]{:S(2)}, u32[]{:S(2)}) collective-permute-start(bf16[144,384]{1,0:T(8,128)(2,1)S(1)} %pad_maximum_fusion.21), channel_id=1, source_target_pairs={{0,24},{1,25},{2,26},{3,27},{4,28},{5,29},{6,30},{7,31},{8,16},{9,... | collective-permute-start | bytes 331784 | tf_op jit(solution)/shard_map/ppermute | solution.py:349
  27.5 7.3 %collective-permute-start.7 = (bf16[144,384]{1,0:T(8,128)(2,1)S(1)}, bf16[144,384]{1,0:T(8,128)(2,1)S(1)}, u32[]{:S(2)}, u32[]{:S(2)}) collective-permute-start(bf16[144,384]{1,0:T(8,128)(2,1)S(1)} %pad_maximum_fusion.21), channel_id=1, source_target_pairs={{0,8},{1,9},{2,10},{3,11},{4,12},{5,13},{6,14},{7,15},{8,0},{9,1},... | collective-permute-start | bytes 331784 | tf_op jit(solution)/shard_map/ppermute | solution.py:349
  27.6 18.4 %collective-permute-start.22 = (bf16[192,384]{1,0:T(8,128)(2,1)S(1)}, bf16[192,384]{1,0:T(8,128)(2,1)S(1)}, u32[]{:S(2)}, u32[]{:S(2)}) collective-permute-start(bf16[192,384]{1,0:T(8,128)(2,1)S(1)} %constant_dynamic-slice_fusion.24), channel_id=1, source_target_pairs={{0,16},{1,17},{2,18},{3,19},{4,20},{5,21},{6,22},{7,23},{8,24},{9,... | collective-permute-start | bytes 442376 | tf_op jit(solution)/shard_map/ppermute | solution.py:349
  30.6 15.4 %collective-permute-start.23 = (bf16[192,384]{1,0:T(8,128)(2,1)S(1)}, bf16[192,384]{1,0:T(8,128)(2,1)S(1)}, u32[]{:S(2)}, u32[]{:S(2)}) collective-permute-start(bf16[192,384]{1,0:T(8,128)(2,1)S(1)} %constant_dynamic-slice_fusion.24), channel_id=1, source_target_pairs={{0,24},{1,25},{2,26},{3,27},{4,28},{5,29},{6,30},{7,31},{8,16},{9,... | collective-permute-start | bytes 442376 | tf_op jit(solution)/shard_map/ppermute | solution.py:349
  32.2 21.5 %collective-permute-start.21 = (bf16[192,384]{1,0:T(8,128)(2,1)S(1)}, bf16[192,384]{1,0:T(8,128)(2,1)S(1)}, u32[]{:S(2)}, u32[]{:S(2)}) collective-permute-start(bf16[192,384]{1,0:T(8,128)(2,1)S(1)} %constant_dynamic-slice_fusion.24), channel_id=1, source_target_pairs={{0,8},{1,9},{2,10},{3,11},{4,12},{5,13},{6,14},{7,15},{8,0},{9,1},... | collective-permute-start | bytes 442376 | tf_op jit(solution)/shard_map/ppermute | solution.py:349
  32.3 25.5 %collective-permute-start.16 = (bf16[240,384]{1,0:T(8,128)(2,1)S(1)}, bf16[240,384]{1,0:T(8,128)(2,1)S(1)}, u32[]{:S(2)}, u32[]{:S(2)}) collective-permute-start(bf16[240,384]{1,0:T(8,128)(2,1)S(1)} %dynamic-slice_dynamic-update-slice_fusion), channel_id=1, source_target_pairs={{0,24},{1,25},{2,26},{3,27},{4,28},{5,29},{6,30},{7,31},{8,16},{9,... | collective-permute-start | bytes 552968 | tf_op jit(solution)/shard_map/ppermute | solution.py:349
  34.8 20.5 %collective-permute-start.3 = (bf16[4,112,384]{2,1,0:T(8,128)(2,1)S(1)}, bf16[4,112,384]{2,1,0:T(8,128)(2,1)S(1)}, u32[]{:S(2)}, u32[]{:S(2)}) collective-permute-start(bf16[4,112,384]{2,1,0:T(8,128)(2,1)S(1)} %get-tuple-element.604), channel_id=1, source_target_pairs={{0,2},{1,5},{2,0},{3,7},{4,6},{5,1},{6,4},{7,3},{8,10},{9,13},{10,... | collective-permute-start | bytes 1032200 | tf_op jit(solution)/shard_map/ppermute | solution.py:349
  46.0 14.6 %collective-permute-start.15 = (bf16[240,384]{1,0:T(8,128)(2,1)S(1)}, bf16[240,384]{1,0:T(8,128)(2,1)S(1)}, u32[]{:S(2)}, u32[]{:S(2)}) collective-permute-start(bf16[240,384]{1,0:T(8,128)(2,1)S(1)} %dynamic-slice_dynamic-update-slice_fusion), channel_id=1, source_target_pairs={{0,16},{1,17},{2,18},{3,19},{4,20},{5,21},{6,22},{7,23},{8,24},{9,... | collective-permute-start | bytes 552968 | tf_op jit(solution)/shard_map/ppermute | solution.py:349
  46.0 16.1 %collective-permute-start.14 = (bf16[240,384]{1,0:T(8,128)(2,1)S(1)}, bf16[240,384]{1,0:T(8,128)(2,1)S(1)}, u32[]{:S(2)}, u32[]{:S(2)}) collective-permute-start(bf16[240,384]{1,0:T(8,128)(2,1)S(1)} %dynamic-slice_dynamic-update-slice_fusion), channel_id=1, source_target_pairs={{0,8},{1,9},{2,10},{3,11},{4,12},{5,13},{6,14},{7,15},{8,0},{9,1},... | collective-permute-start | bytes 552968 | tf_op jit(solution)/shard_map/ppermute | solution.py:349
  53.6 11.9 %collective-permute-start.10 = (bf16[4,144,384]{2,1,0:T(8,128)(2,1)S(1)}, bf16[4,144,384]{2,1,0:T(8,128)(2,1)S(1)}, u32[]{:S(2)}, u32[]{:S(2)}) collective-permute-start(bf16[4,144,384]{2,1,0:T(8,128)(2,1)S(1)} %get-tuple-element.595), channel_id=1, source_target_pairs={{0,2},{1,5},{2,0},{3,7},{4,6},{5,1},{6,4},{7,3},{8,10},{9,13},{10,... | collective-permute-start | bytes 1327112 | tf_op jit(solution)/shard_map/ppermute | solution.py:349
  56.3 14.5 %collective-permute-start.4 = (bf16[4,2,112,384]{3,2,1,0:T(8,128)(2,1)}, bf16[4,2,112,384]{3,2,1,0:T(8,128)(2,1)}, u32[]{:S(2)}, u32[]{:S(2)}) collective-permute-start(bf16[4,2,112,384]{3,2,1,0:T(8,128)(2,1)} %maximum_select_fusion.3.s8), channel_id=1, source_target_pairs={{0,4},{1,3},{2,6},{3,1},{4,0},{5,7},{6,2},{7,5},{8,12},{9,11},{10,... | collective-permute-start | bytes 2064392 | tf_op jit(solution)/shard_map/ppermute | solution.py:349
  63.5 31.8 %collective-permute-start.17 = (bf16[4,240,384]{2,1,0:T(8,128)(2,1)}, bf16[4,240,384]{2,1,0:T(8,128)(2,1)S(1)}, u32[]{:S(2)}, u32[]{:S(2)}) collective-permute-start(bf16[4,240,384]{2,1,0:T(8,128)(2,1)} %get-tuple-element.574), channel_id=1, source_target_pairs={{0,2},{1,5},{2,0},{3,7},{4,6},{5,1},{6,4},{7,3},{8,10},{9,13},{10,... | collective-permute-start | bytes 2211848 | tf_op jit(solution)/shard_map/ppermute | solution.py:349
  66.5 33.7 %collective-permute-start.11 = (bf16[4,2,144,384]{3,2,1,0:T(8,128)(2,1)}, bf16[4,2,144,384]{3,2,1,0:T(8,128)(2,1)}, u32[]{:S(2)}, u32[]{:S(2)}) collective-permute-start(bf16[4,2,144,384]{3,2,1,0:T(8,128)(2,1)} %maximum_select_fusion.2.s8), channel_id=1, source_target_pairs={{0,4},{1,3},{2,6},{3,1},{4,0},{5,7},{6,2},{7,5},{8,12},{9,11},{10,... | collective-permute-start | bytes 2654216 | tf_op jit(solution)/shard_map/ppermute | solution.py:349
  69.2 23.8 %collective-permute-start.24 = (bf16[4,192,384]{2,1,0:T(8,128)(2,1)S(1)}, bf16[4,192,384]{2,1,0:T(8,128)(2,1)S(1)}, u32[]{:S(2)}, u32[]{:S(2)}) collective-permute-start(bf16[4,192,384]{2,1,0:T(8,128)(2,1)S(1)} %get-tuple-element.589), channel_id=1, source_target_pairs={{0,2},{1,5},{2,0},{3,7},{4,6},{5,1},{6,4},{7,3},{8,10},{9,13},{10,... | collective-permute-start | bytes 1769480 | tf_op jit(solution)/shard_map/ppermute | solution.py:349
  70.8 27.9 %collective-permute-start.5 = (bf16[4,2,112,384]{3,2,1,0:T(8,128)(2,1)}, bf16[4,2,112,384]{3,2,1,0:T(8,128)(2,1)}, u32[]{:S(2)}, u32[]{:S(2)}) collective-permute-start(bf16[4,2,112,384]{3,2,1,0:T(8,128)(2,1)} %maximum_select_fusion.3.s8), channel_id=1, source_target_pairs={{0,1},{1,0},{2,3},{3,2},{4,5},{5,4},{6,7},{7,6},{8,9},{9,8},{10,11... | collective-permute-start | bytes 2064392 | tf_op jit(solution)/shard_map/ppermute | solution.py:341
  70.8 30.0 %collective-permute-start.6 = (bf16[4,2,112,384]{3,2,1,0:T(8,128)(2,1)}, bf16[4,2,112,384]{3,2,1,0:T(8,128)(2,1)}, u32[]{:S(2)}, u32[]{:S(2)}) collective-permute-start(bf16[4,2,112,384]{3,2,1,0:T(8,128)(2,1)} %collective-permute-done.4.r8), channel_id=1, source_target_pairs={{0,1},{1,0},{2,3},{3,2},{4,5},{5,4},{6,7},{7,6},{8,9},{9,8},{10,11... | collective-permute-start | bytes 2064392 | tf_op jit(solution)/shard_map/ppermute | solution.py:341
  93.0 25.4 %collective-permute-start.12 = (bf16[4,2,144,384]{3,2,1,0:T(8,128)(2,1)}, bf16[4,2,144,384]{3,2,1,0:T(8,128)(2,1)}, u32[]{:S(2)}, u32[]{:S(2)}) collective-permute-start(bf16[4,2,144,384]{3,2,1,0:T(8,128)(2,1)} %maximum_select_fusion.2.s8), channel_id=1, source_target_pairs={{0,1},{1,0},{2,3},{3,2},{4,5},{5,4},{6,7},{7,6},{8,9},{9,8},{10,11... | collective-permute-start | bytes 2654216 | tf_op jit(solution)/shard_map/ppermute | solution.py:341
  95.4 84.2 %collective-permute-start.26 = (bf16[4,2,192,384]{3,2,1,0:T(8,128)(2,1)S(1)}, bf16[4,2,192,384]{3,2,1,0:T(8,128)(2,1)}, u32[]{:S(2)}, u32[]{:S(2)}) collective-permute-start(bf16[4,2,192,384]{3,2,1,0:T(8,128)(2,1)S(1)} %maximum_select_fusion.1.s8), channel_id=1, source_target_pairs={{0,1},{1,0},{2,3},{3,2},{4,5},{5,4},{6,7},{7,6},{8,9},{9,8},{10,11... | collective-permute-start | bytes 3538952 | tf_op jit(solution)/shard_map/ppermute | solution.py:341
  98.6 20.4 %collective-permute-start.25 = (bf16[4,2,192,384]{3,2,1,0:T(8,128)(2,1)S(1)}, bf16[4,2,192,384]{3,2,1,0:T(8,128)(2,1)}, u32[]{:S(2)}, u32[]{:S(2)}) collective-permute-start(bf16[4,2,192,384]{3,2,1,0:T(8,128)(2,1)S(1)} %maximum_select_fusion.1.s8), channel_id=1, source_target_pairs={{0,4},{1,3},{2,6},{3,1},{4,0},{5,7},{6,2},{7,5},{8,12},{9,11},{10,... | collective-permute-start | bytes 3538952 | tf_op jit(solution)/shard_map/ppermute | solution.py:349
  100.2 41.9 %collective-permute-start.18 = (bf16[4,2,240,384]{3,2,1,0:T(8,128)(2,1)S(1)}, bf16[4,2,240,384]{3,2,1,0:T(8,128)(2,1)}, u32[]{:S(2)}, u32[]{:S(2)}) collective-permute-start(bf16[4,2,240,384]{3,2,1,0:T(8,128)(2,1)S(1)} %maximum_select_fusion.s8), channel_id=1, source_target_pairs={{0,4},{1,3},{2,6},{3,1},{4,0},{5,7},{6,2},{7,5},{8,12},{9,11},{10,... | collective-permute-start | bytes 4423688 | tf_op jit(solution)/shard_map/ppermute | solution.py:349
  100.7 18.4 %collective-permute-start.13 = (bf16[4,2,144,384]{3,2,1,0:T(8,128)(2,1)}, bf16[4,2,144,384]{3,2,1,0:T(8,128)(2,1)}, u32[]{:S(2)}, u32[]{:S(2)}) collective-permute-start(bf16[4,2,144,384]{3,2,1,0:T(8,128)(2,1)} %collective-permute-done.11.r8), channel_id=1, source_target_pairs={{0,1},{1,0},{2,3},{3,2},{4,5},{5,4},{6,7},{7,6},{8,9},{9,8},{10,11... | collective-permute-start | bytes 2654216 | tf_op jit(solution)/shard_map/ppermute | solution.py:341
  112.9 76.6 %copy-start.45 = (f32[1,768]{1,0:T(1,128)}, f32[1,768]{1,0:T(1,128)S(1)}, u32[]{:S(2)}) copy-start(f32[1,768]{1,0:T(1,128)S(1)} %reshape.512) | copy-start | bytes 9220
  118.4 65.8 %collective-permute-start.19 = (bf16[4,2,240,384]{3,2,1,0:T(8,128)(2,1)S(1)}, bf16[4,2,240,384]{3,2,1,0:T(8,128)(2,1)}, u32[]{:S(2)}, u32[]{:S(2)}) collective-permute-start(bf16[4,2,240,384]{3,2,1,0:T(8,128)(2,1)S(1)} %maximum_select_fusion.s8), channel_id=1, source_target_pairs={{0,1},{1,0},{2,3},{3,2},{4,5},{5,4},{6,7},{7,6},{8,9},{9,8},{10,11... | collective-permute-start | bytes 4423688 | tf_op jit(solution)/shard_map/ppermute | solution.py:341
  119.0 60.6 %collective-permute-start.27 = (bf16[4,2,192,384]{3,2,1,0:T(8,128)(2,1)}, bf16[4,2,192,384]{3,2,1,0:T(8,128)(2,1)}, u32[]{:S(2)}, u32[]{:S(2)}) collective-permute-start(bf16[4,2,192,384]{3,2,1,0:T(8,128)(2,1)} %collective-permute-done.25.r8), channel_id=1, source_target_pairs={{0,1},{1,0},{2,3},{3,2},{4,5},{5,4},{6,7},{7,6},{8,9},{9,8},{10,11... | collective-permute-start | bytes 3538952 | tf_op jit(solution)/shard_map/ppermute | solution.py:341
  142.2 42.0 %collective-permute-start.20 = (bf16[4,2,240,384]{3,2,1,0:T(8,128)(2,1)}, bf16[4,2,240,384]{3,2,1,0:T(8,128)(2,1)}, u32[]{:S(2)}, u32[]{:S(2)}) collective-permute-start(bf16[4,2,240,384]{3,2,1,0:T(8,128)(2,1)} %collective-permute-done.18.r8), channel_id=1, source_target_pairs={{0,1},{1,0},{2,3},{3,2},{4,5},{5,4},{6,7},{7,6},{8,9},{9,8},{10,11... | collective-permute-start | bytes 4423688 | tf_op jit(solution)/shard_map/ppermute | solution.py:341
  189.6 31.8 %slice-start = ((s8[4718592]{0:T(1024)(128)(4,1)}), s8[524288]{0:T(1024)(128)(4,1)S(1)}, s32[]{:S(2)}) async-start(s8[4718592]{0:T(1024)(128)(4,1)} %bitcast.424), calls=%async_computation | async-start | bytes 1048576
  191.1 60.9 %copy-start.18 = (f32[839,768]{1,0:T(8,128)}, f32[839,768]{1,0:T(8,128)S(1)}, u32[]{:S(2)}) copy-start(f32[839,768]{1,0:T(8,128)S(1)} %get-tuple-element.652) | copy-start | bytes 7732228
  192.0 29.4 %copy-start.23 = (bf16[1,839,768]{2,1,0:T(8,128)(2,1)S(1)}, bf16[1,839,768]{2,1,0:T(8,128)(2,1)}, u32[]{:S(2)}) copy-start(bf16[1,839,768]{2,1,0:T(8,128)(2,1)} %param.33) | copy-start | bytes 3866116
  192.0 29.4 %slice-start.1 = ((s8[4718592]{0:T(1024)(128)(4,1)}), s8[4194304]{0:T(1024)(128)(4,1)S(1)}, s32[]{:S(2)}) async-start(s8[4718592]{0:T(1024)(128)(4,1)} %bitcast.424), calls=%async_computation.1 | async-start | bytes 8388608
  394.9 13.5 %collective-permute-start.28 = (bf16[16,112,384]{2,1,0:T(8,128)(2,1)}, bf16[16,112,384]{2,1,0:T(8,128)(2,1)S(1)}, u32[]{:S(2)}, u32[]{:S(2)}) collective-permute-start(bf16[16,112,384]{2,1,0:T(8,128)(2,1)} %pad_maximum_fusion.6), channel_id=1, source_target_pairs={{0,1},{1,0},{2,3},{3,2},{4,5},{5,4},{6,7},{7,6},{8,9},{9,8},{10,11... | collective-permute-start | bytes 4128776 | tf_op jit(solution)/shard_map/ppermute | solution.py:341
  397.3 24.3 %collective-permute-start.35 = (bf16[16,192,384]{2,1,0:T(8,128)(2,1)S(1)}, bf16[16,192,384]{2,1,0:T(8,128)(2,1)S(1)}, u32[]{:S(2)}, u32[]{:S(2)}) collective-permute-start(bf16[16,192,384]{2,1,0:T(8,128)(2,1)S(1)} %pad_maximum_fusion.2), channel_id=1, source_target_pairs={{0,1},{1,0},{2,3},{3,2},{4,5},{5,4},{6,7},{7,6},{8,9},{9,8},{10,11... | collective-permute-start | bytes 7077896 | tf_op jit(solution)/shard_map/ppermute | solution.py:341
  397.5 27.2 %collective-permute-start.49 = (bf16[16,192,384]{2,1,0:T(8,128)(2,1)S(1)}, bf16[16,192,384]{2,1,0:T(8,128)(2,1)S(1)}, u32[]{:S(2)}, u32[]{:S(2)}) collective-permute-start(bf16[16,192,384]{2,1,0:T(8,128)(2,1)S(1)} %bitcast.440), channel_id=1, source_target_pairs={{0,1},{1,0},{2,3},{3,2},{4,5},{5,4},{6,7},{7,6},{8,9},{9,8},{10,11... | collective-permute-start | bytes 7077896 | tf_op jit(solution)/shard_map/ppermute | solution.py:341
  399.1 25.6 %collective-permute-start.42 = (bf16[16,192,384]{2,1,0:T(8,128)(2,1)S(1)}, bf16[16,192,384]{2,1,0:T(8,128)(2,1)}, u32[]{:S(2)}, u32[]{:S(2)}) collective-permute-start(bf16[16,192,384]{2,1,0:T(8,128)(2,1)S(1)} %pad_maximum_fusion.4), channel_id=1, source_target_pairs={{0,1},{1,0},{2,3},{3,2},{4,5},{5,4},{6,7},{7,6},{8,9},{9,8},{10,11... | collective-permute-start | bytes 7077896 | tf_op jit(solution)/shard_map/ppermute | solution.py:341
  408.9 11.0 %collective-permute-start.29 = (bf16[4,2,112,384]{3,2,1,0:T(8,128)(2,1)S(1)}, bf16[4,2,112,384]{3,2,1,0:T(8,128)(2,1)S(1)}, u32[]{:S(2)}, u32[]{:S(2)}) collective-permute-start(bf16[4,2,112,384]{3,2,1,0:T(8,128)(2,1)S(1)} %pad_maximum_fusion.11), channel_id=1, source_target_pairs={{0,4},{1,3},{2,6},{3,1},{4,0},{5,7},{6,2},{7,5},{8,12},{9,11},{10,... | collective-permute-start | bytes 2064392 | tf_op jit(solution)/shard_map/ppermute | solution.py:349
  420.1 10.9 %collective-permute-start.30 = (bf16[4,112,384]{2,1,0:T(8,128)(2,1)S(1)}, bf16[4,112,384]{2,1,0:T(8,128)(2,1)S(1)}, u32[]{:S(2)}, u32[]{:S(2)}) collective-permute-start(bf16[4,112,384]{2,1,0:T(8,128)(2,1)S(1)} %fusion.77), channel_id=1, source_target_pairs={{0,2},{1,5},{2,0},{3,7},{4,6},{5,1},{6,4},{7,3},{8,10},{9,13},{10,... | collective-permute-start | bytes 1032200 | tf_op jit(solution)/shard_map/ppermute | solution.py:349
  423.1 22.3 %collective-permute-start.36 = (bf16[4,2,192,384]{3,2,1,0:T(8,128)(2,1)}, bf16[4,2,192,384]{3,2,1,0:T(8,128)(2,1)}, u32[]{:S(2)}, u32[]{:S(2)}) collective-permute-start(bf16[4,2,192,384]{3,2,1,0:T(8,128)(2,1)} %pad_maximum_fusion.7), channel_id=1, source_target_pairs={{0,4},{1,3},{2,6},{3,1},{4,0},{5,7},{6,2},{7,5},{8,12},{9,11},{10,... | collective-permute-start | bytes 3538952 | tf_op jit(solution)/shard_map/ppermute | solution.py:349
  430.5 23.8 %collective-permute-start.43 = (bf16[4,2,192,384]{3,2,0,1:T(8,128)(2,1)}, bf16[4,2,192,384]{3,2,0,1:T(8,128)(2,1)}, u32[]{:S(2)}, u32[]{:S(2)}) collective-permute-start(bf16[4,2,192,384]{3,2,0,1:T(8,128)(2,1)} %pad_maximum_fusion.8), channel_id=1, source_target_pairs={{0,4},{1,3},{2,6},{3,1},{4,0},{5,7},{6,2},{7,5},{8,12},{9,11},{10,... | collective-permute-start | bytes 3538952 | tf_op jit(solution)/shard_map/ppermute | solution.py:349
  431.3 5.8 %collective-permute-start.31 = (bf16[112,384]{1,0:T(8,128)(2,1)S(1)}, bf16[112,384]{1,0:T(8,128)(2,1)S(1)}, u32[]{:S(2)}, u32[]{:S(2)}) collective-permute-start(bf16[112,384]{1,0:T(8,128)(2,1)S(1)} %get-tuple-element.600), channel_id=1, source_target_pairs={{0,8},{1,9},{2,10},{3,11},{4,12},{5,13},{6,14},{7,15},{8,0},{9,1},... | collective-permute-start | bytes 258056 | tf_op jit(solution)/shard_map/ppermute | solution.py:349
  431.3 7.7 %collective-permute-start.33 = (bf16[112,384]{1,0:T(8,128)(2,1)S(1)}, bf16[112,384]{1,0:T(8,128)(2,1)S(1)}, u32[]{:S(2)}, u32[]{:S(2)}) collective-permute-start(bf16[112,384]{1,0:T(8,128)(2,1)S(1)} %get-tuple-element.601), channel_id=1, source_target_pairs={{0,24},{1,25},{2,26},{3,27},{4,28},{5,29},{6,30},{7,31},{8,16},{9,... | collective-permute-start | bytes 258056 | tf_op jit(solution)/shard_map/ppermute | solution.py:349
  434.8 7.1 %collective-permute-start.32 = (bf16[112,384]{1,0:T(8,128)(2,1)S(1)}, bf16[112,384]{1,0:T(8,128)(2,1)S(1)}, u32[]{:S(2)}, u32[]{:S(2)}) collective-permute-start(bf16[112,384]{1,0:T(8,128)(2,1)S(1)} %get-tuple-element.602), channel_id=1, source_target_pairs={{0,16},{1,17},{2,18},{3,19},{4,20},{5,21},{6,22},{7,23},{8,24},{9,... | collective-permute-start | bytes 258056 | tf_op jit(solution)/shard_map/ppermute | solution.py:349
  442.0 2.0 collective-permute-start.34
  443.3 34.2 %collective-permute-start.50 = (bf16[4,2,192,384]{3,2,0,1:T(8,128)(2,1)}, bf16[4,2,192,384]{3,2,0,1:T(8,128)(2,1)}, u32[]{:S(2)}, u32[]{:S(2)}) collective-permute-start(bf16[4,2,192,384]{3,2,0,1:T(8,128)(2,1)} %pad_maximum_fusion.9), channel_id=1, source_target_pairs={{0,4},{1,3},{2,6},{3,1},{4,0},{5,7},{6,2},{7,5},{8,12},{9,11},{10,... | collective-permute-start | bytes 3538952 | tf_op jit(solution)/shard_map/ppermute | solution.py:349
  444.1 10.2 %copy-start.21 = (bf16[4,1,192,384]{3,2,0,1:T(8,128)(2,1)S(1)}, bf16[4,1,192,384]{3,2,0,1:T(8,128)(2,1)}, u32[]{:S(2)}) copy-start(bf16[4,1,192,384]{3,2,0,1:T(8,128)(2,1)} %get-tuple-element.666) | copy-start | bytes 1769476
  446.8 32.8 %collective-permute-start.37 = (bf16[4,192,384]{2,1,0:T(8,128)(2,1)S(1)}, bf16[4,192,384]{2,1,0:T(8,128)(2,1)S(1)}, u32[]{:S(2)}, u32[]{:S(2)}) collective-permute-start(bf16[4,192,384]{2,1,0:T(8,128)(2,1)S(1)} %fusion.63), channel_id=1, source_target_pairs={{0,2},{1,5},{2,0},{3,7},{4,6},{5,1},{6,4},{7,3},{8,10},{9,13},{10,... | collective-permute-start | bytes 1769480 | tf_op jit(solution)/shard_map/ppermute | solution.py:349
  455.6 29.5 %collective-permute-start.44 = (bf16[4,192,384]{2,1,0:T(8,128)(2,1)S(1)}, bf16[4,192,384]{2,1,0:T(8,128)(2,1)S(1)}, u32[]{:S(2)}, u32[]{:S(2)}) collective-permute-start(bf16[4,192,384]{2,1,0:T(8,128)(2,1)S(1)} %fusion.60), channel_id=1, source_target_pairs={{0,2},{1,5},{2,0},{3,7},{4,6},{5,1},{6,4},{7,3},{8,10},{9,13},{10,... | collective-permute-start | bytes 1769480 | tf_op jit(solution)/shard_map/ppermute | solution.py:349
  479.0 9.9 %collective-permute-start.51 = (bf16[4,192,384]{2,1,0:T(8,128)(2,1)S(1)}, bf16[4,192,384]{2,1,0:T(8,128)(2,1)S(1)}, u32[]{:S(2)}, u32[]{:S(2)}) collective-permute-start(bf16[4,192,384]{2,1,0:T(8,128)(2,1)S(1)} %fusion.62), channel_id=1, source_target_pairs={{0,2},{1,5},{2,0},{3,7},{4,6},{5,1},{6,4},{7,3},{8,10},{9,13},{10,... | collective-permute-start | bytes 1769480 | tf_op jit(solution)/shard_map/ppermute | solution.py:349
  481.1 12.7 %collective-permute-start.38 = (bf16[192,384]{1,0:T(8,128)(2,1)S(1)}, bf16[192,384]{1,0:T(8,128)(2,1)S(1)}, u32[]{:S(2)}, u32[]{:S(2)}) collective-permute-start(bf16[192,384]{1,0:T(8,128)(2,1)S(1)} %get-tuple-element.585), channel_id=1, source_target_pairs={{0,8},{1,9},{2,10},{3,11},{4,12},{5,13},{6,14},{7,15},{8,0},{9,1},... | collective-permute-start | bytes 442376 | tf_op jit(solution)/shard_map/ppermute | solution.py:349
  481.2 12.7 %collective-permute-start.40 = (bf16[192,384]{1,0:T(8,128)(2,1)S(1)}, bf16[192,384]{1,0:T(8,128)(2,1)S(1)}, u32[]{:S(2)}, u32[]{:S(2)}) collective-permute-start(bf16[192,384]{1,0:T(8,128)(2,1)S(1)} %get-tuple-element.586), channel_id=1, source_target_pairs={{0,24},{1,25},{2,26},{3,27},{4,28},{5,29},{6,30},{7,31},{8,16},{9,... | collective-permute-start | bytes 442376 | tf_op jit(solution)/shard_map/ppermute | solution.py:349
  484.6 21.0 %collective-permute-start.39 = (bf16[192,384]{1,0:T(8,128)(2,1)S(1)}, bf16[192,384]{1,0:T(8,128)(2,1)S(1)}, u32[]{:S(2)}, u32[]{:S(2)}) collective-permute-start(bf16[192,384]{1,0:T(8,128)(2,1)S(1)} %get-tuple-element.587), channel_id=1, source_target_pairs={{0,16},{1,17},{2,18},{3,19},{4,20},{5,21},{6,22},{7,23},{8,24},{9,... | collective-permute-start | bytes 442376 | tf_op jit(solution)/shard_map/ppermute | solution.py:349
  486.6 22.0 %collective-permute-start.45 = (bf16[192,384]{1,0:T(8,128)(2,1)S(1)}, bf16[192,384]{1,0:T(8,128)(2,1)S(1)}, u32[]{:S(2)}, u32[]{:S(2)}) collective-permute-start(bf16[192,384]{1,0:T(8,128)(2,1)S(1)} %get-tuple-element.582), channel_id=1, source_target_pairs={{0,8},{1,9},{2,10},{3,11},{4,12},{5,13},{6,14},{7,15},{8,0},{9,1},... | collective-permute-start | bytes 442376 | tf_op jit(solution)/shard_map/ppermute | solution.py:349
  488.9 19.8 %collective-permute-start.47 = (bf16[192,384]{1,0:T(8,128)(2,1)S(1)}, bf16[192,384]{1,0:T(8,128)(2,1)S(1)}, u32[]{:S(2)}, u32[]{:S(2)}) collective-permute-start(bf16[192,384]{1,0:T(8,128)(2,1)S(1)} %get-tuple-element.583), channel_id=1, source_target_pairs={{0,24},{1,25},{2,26},{3,27},{4,28},{5,29},{6,30},{7,31},{8,16},{9,... | collective-permute-start | bytes 442376 | tf_op jit(solution)/shard_map/ppermute | solution.py:349
  493.8 24.5 %collective-permute-start.46 = (bf16[192,384]{1,0:T(8,128)(2,1)S(1)}, bf16[192,384]{1,0:T(8,128)(2,1)S(1)}, u32[]{:S(2)}, u32[]{:S(2)}) collective-permute-start(bf16[192,384]{1,0:T(8,128)(2,1)S(1)} %get-tuple-element.584), channel_id=1, source_target_pairs={{0,16},{1,17},{2,18},{3,19},{4,20},{5,21},{6,22},{7,23},{8,24},{9,... | collective-permute-start | bytes 442376 | tf_op jit(solution)/shard_map/ppermute | solution.py:349
  493.9 24.6 %collective-permute-start.52 = (bf16[192,384]{1,0:T(8,128)(2,1)S(1)}, bf16[192,384]{1,0:T(8,128)(2,1)S(1)}, u32[]{:S(2)}, u32[]{:S(2)}) collective-permute-start(bf16[192,384]{1,0:T(8,128)(2,1)S(1)} %get-tuple-element.579), channel_id=1, source_target_pairs={{0,8},{1,9},{2,10},{3,11},{4,12},{5,13},{6,14},{7,15},{8,0},{9,1},... | collective-permute-start | bytes 442376 | tf_op jit(solution)/shard_map/ppermute | solution.py:349
  505.6 12.9 %collective-permute-start.54 = (bf16[192,384]{1,0:T(8,128)(2,1)S(1)}, bf16[192,384]{1,0:T(8,128)(2,1)S(1)}, u32[]{:S(2)}, u32[]{:S(2)}) collective-permute-start(bf16[192,384]{1,0:T(8,128)(2,1)S(1)} %get-tuple-element.580), channel_id=1, source_target_pairs={{0,24},{1,25},{2,26},{3,27},{4,28},{5,29},{6,30},{7,31},{8,16},{9,... | collective-permute-start | bytes 442376 | tf_op jit(solution)/shard_map/ppermute | solution.py:349
  508.7 15.9 %collective-permute-start.53 = (bf16[192,384]{1,0:T(8,128)(2,1)S(1)}, bf16[192,384]{1,0:T(8,128)(2,1)S(1)}, u32[]{:S(2)}, u32[]{:S(2)}) collective-permute-start(bf16[192,384]{1,0:T(8,128)(2,1)S(1)} %get-tuple-element.581), channel_id=1, source_target_pairs={{0,16},{1,17},{2,18},{3,19},{4,20},{5,21},{6,22},{7,23},{8,24},{9,... | collective-permute-start | bytes 442376 | tf_op jit(solution)/shard_map/ppermute | solution.py:349
  508.8 16.1 %collective-permute-start.41 = (bf16[192,384]{1,0:T(8,128)(2,1)S(1)}, bf16[192,384]{1,0:T(8,128)(2,1)S(1)}, u32[]{:S(2)}, u32[]{:S(2)}) collective-permute-start(bf16[192,384]{1,0:T(8,128)(2,1)S(1)} %fusion.89), channel_id=1, source_target_pairs={{0,1},{1,0},{2,3},{3,2},{4,5},{5,4},{6,7},{7,6},{8,9},{9,8},{10,11... | collective-permute-start | bytes 442376 | tf_op jit(solution)/shard_map/ppermute | solution.py:341
  518.4 6.6 %collective-permute-start.48 = (bf16[192,384]{1,0:T(8,128)(2,1)S(1)}, bf16[192,384]{1,0:T(8,128)(2,1)S(1)}, u32[]{:S(2)}, u32[]{:S(2)}) collective-permute-start(bf16[192,384]{1,0:T(8,128)(2,1)S(1)} %fusion.86), channel_id=1, source_target_pairs={{0,1},{1,0},{2,3},{3,2},{4,5},{5,4},{6,7},{7,6},{8,9},{9,8},{10,11... | collective-permute-start | bytes 442376 | tf_op jit(solution)/shard_map/ppermute | solution.py:341
  524.7 3.2 collective-permute-start.55
  (71 other events, 191.3 us)

commit v2 on v1

--- a/solution.py
+++ b/solution.py
@@ -318,13 +318,30 @@
     return (image_grad, text_grad, grads)
 
 
-MATRICES = (0, 2, 7, 9, 10, 12, 16, 18)
 VECTORS = (1, 3, 4, 5, 6, 8, 11, 13, 14, 15, 19, 17)
 LANES = 384
 VEC_ROWS = 16
-GATHER_CHUNKS = ((0, 2, "vec"), (7, 9, 10), (12, 16), (18,))
-SCATTER_CHUNKS = ((18,), (16,), (12, 7, 9, 10), (0, 2, "vec"))
+GATHER_CHUNKS = ((0, 2, "vec"), (7, 9, 10), (12, 16, 18))
+SCATTER_CHUNKS = ((18, 16), (12, 7, 9, 10), (0, 2, "vec"))
 BOTH = ("fsdp", "dp")
+WIDTH = 768
+HIDDEN = 3072
+IMAGE = 325
+TEXTS = 513
+ROWS = 839
+KEYS = 848
+PADDED = 896
+LOW = jnp.bfloat16
+FULL = jnp.float32
+COST_SCALE = 0.3
+FAST = pl.BlockSpec(memory_space=pltpu.VMEM)
+SCALARS = pl.BlockSpec(memory_space=pltpu.SMEM)
+
+
+def cost(micros):
+    return pl.CostEstimate(
+        flops=int(micros * COST_SCALE * 1e9), bytes_accessed=1024, transcendentals=0
+    )
 
 
 class Place:
@@ -332,13 +349,37 @@
         self.core = lax.axis_index("dp")
         chip = lax.axis_index("fsdp")
         self.x, self.y, self.z = chip & 1, (chip >> 1) & 1, chip >> 2
-
-    def scalars(self):
-        return jnp.stack([self.core, self.x, self.y, self.z]).astype(jnp.int32)
+        self.scalars = jnp.stack([self.core, self.x, self.y, self.z]).astype(jnp.int32)
+
+
+def shape(dims, kind=LOW):
+    return jax.ShapeDtypeStruct(dims, kind)
+
+
+def call(kernel, micros, outs, *args, scratch=(), limit=60):
+    specs = [SCALARS if a.dtype == jnp.int32 else FAST for a in args]
+    return pl.pallas_call(
+        kernel,
+        out_shape=tuple(outs),
+        in_specs=specs,
+        out_specs=tuple(FAST for _ in outs),
+        scratch_shapes=list(scratch),
+        compiler_params=pltpu.CompilerParams(vmem_limit_bytes=limit * 2**20),
+        cost_estimate=cost(micros),
+    )(*args)
+
+
+def after(values, *others):
+    return lax.optimization_barrier((values, others))[0]
+
+
+def settle(*values):
+    return lax.optimization_barrier(values)
 
 
 def swap_cores(values):
-    return lax.ppermute(values, "dp", [(0, 1), (1, 0)])
+    with jax.named_scope("between_cores"):
+        return lax.ppermute(values, "dp", [(0, 1), (1, 0)])
 
 
 def to_chip(values, mask_zero, mask_one):
@@ -346,47 +387,82 @@
     for chip in range(16):
         pairs.append((chip * 2, (chip ^ mask_zero) * 2))
         pairs.append((chip * 2 + 1, (chip ^ mask_one) * 2 + 1))
-    return lax.ppermute(values, BOTH, pairs)
-
-
-def sub_blocks(weight_index):
-    return 4 if weight_index == 16 else 1
-
-
-def block_rows(shards, weight_index):
-    if weight_index == "vec":
-        return VEC_ROWS
-    return shards[weight_index].shape[0] * sub_blocks(weight_index)
-
-
-def half_of(shard, core, weight_index):
-    count = sub_blocks(weight_index)
-    width = count * LANES
-    half = lax.dynamic_slice_in_dim(shard, core * width, width, 1)
-    if count > 1:
-        half = jnp.concatenate([half[:, s * LANES : (s + 1) * LANES] for s in range(count)], 0)
-    return half
-
-
-def assemble_kernel(layout, place_ref, s8, r8, s8p, r8p, *outs):
-    core, x, y = place_ref[0], place_ref[1], place_ref[2]
+    with jax.named_scope(f"chips_{mask_zero}_{mask_one}"):
+        return lax.ppermute(values, BOTH, pairs)
+
+
+def sub_blocks(index):
+    return 4 if index == 16 else 1
+
+
+def block_rows(index):
+    return {"vec": VEC_ROWS, 16: 192, 18: 192}.get(index, 48)
+
+
+def layout_of(chunk):
+    made, offset = {}, 0
+    for index in chunk:
+        made[index] = offset
+        offset += block_rows(index)
+    return made, offset
+
+
+def pack_kernel(chunk, at_ref, *refs):
+    core = at_ref[0]
+    out, ins = refs[len(chunk) if "vec" not in chunk else len(chunk) - 1 + 12], refs
+    offset = 0
+    for place, index in enumerate(chunk):
+        if index == "vec":
+            rows = refs[-1]
+            rows[...] = jnp.zeros_like(rows)
+            for row in range(12):
+                source = ins[place + row]
+                rows[row : row + 1, 0 : source.shape[1]] = source[...].astype(FULL)
+            out[offset : offset + VEC_ROWS, :] = rows[...].astype(LOW)
+            continue
+        count = sub_blocks(index)
+        rows = ins[place].shape[0]
+        for s in range(count):
+            first = pl.multiple_of((core * count + s) * LANES, LANES)
+            out[offset : offset + rows, :] = ins[place][:, pl.ds(first, LANES)]
+            offset += rows
+
+
+def pack(place, shards, chunk):
+    rows = sum(block_rows(i) for i in chunk)
+    ins = [shards[i] for i in chunk if i != "vec"]
+    scratch = ()
+    if "vec" in chunk:
+        ins += [shards[i].reshape(1, -1) for i in VECTORS]
+        scratch = (pltpu.VMEM((VEC_ROWS, LANES), FULL),)
+    kernel = functools.partial(pack_kernel, chunk)
+    return call(kernel, 1, [shape((rows, LANES))], place.scalars, *ins, scratch=scratch)[0]
+
+
+def all_z(own):
+    return [own] + [to_chip(own, 4 * s, 4 * s) for s in (1, 2, 3)]
+
+
+def unpack(at_ref, pieces, targets):
+    core, x, y, z = at_ref[0], at_ref[1], at_ref[2], at_ref[3]
 
     def fill(zero_s, zero_r, one_s, one_r):
-        for (offset, rows, count, is_vec), out in zip(layout, outs):
+        for offset, count, is_vec, out in targets:
+            rows = out.shape[3]
             for s in range(count):
                 first = slice(offset + s * rows, offset + (s + 1) * rows)
-                columns = slice(s * LANES, (s + 1) * LANES)
-                for z in range(4):
+                left = slice(s * LANES, (s + 1) * LANES)
+                right = slice((count + s) * LANES, (count + s + 1) * LANES)
+                for far in range(4):
+                    plane = z ^ far
                     for b in range(2):
-                        out[z, y, b, :, columns] = zero_s[z, b, first, :]
-                        out[z, 1 - y, b, :, columns] = zero_r[z, b, first, :]
-                if is_vec:
-                    continue
-                columns = slice((count + s) * LANES, (count + s + 1) * LANES)
-                for z in range(4):
-                    for b in range(2):
-                        out[z, b, x, :, columns] = one_s[z, b, first, :]
-                        out[z, b, 1 - x, :, columns] = one_r[z, b, first, :]
+                        out[plane, y, x ^ b, :, left] = zero_s[b, far, first, :]
+                        out[plane, 1 - y, x ^ b, :, left] = zero_r[b, far, first, :]
+                        if not is_vec:
+                            out[plane, y ^ b, x, :, right] = one_s[b, far, first, :]
+                            out[plane, y ^ b, 1 - x, :, right] = one_r[b, far, first, :]
+
+    s8, r8, s8p, r8p = pieces
 
     @pl.when(core == 0)
     def _():
@@ -397,88 +473,472 @@
         fill(s8p, r8p, s8, r8)
 
 
-def assemble(place, pieces, shards, chunk):
-    layout, shapes, offset = [], [], 0
-    for index in chunk:
-        if index == "vec":
-            rows, count, columns = VEC_ROWS, 1, LANES
-        else:
-            rows, columns = shards[index].shape
-            count = sub_blocks(index)
-        layout.append((offset, rows, count, index == "vec"))
-        offset += rows * count
-        shapes.append(jax.ShapeDtypeStruct((4, 2, 2, rows, columns), jnp.bfloat16))
-    fast = pl.BlockSpec(memory_space=pltpu.VMEM)
+def square(ref):
+    return ref[...].reshape(16 * ref.shape[3], ref.shape[4])
+
+
+def row_chunks(step, total=ROWS):
+    return [slice(a, min(a + step, total)) for a in range(0, total, step)]
+
+
+def standard(values):
+    centered = values - jnp.mean(values, -1, keepdims=True)
+    scale = lax.rsqrt(jnp.mean(centered * centered, -1, keepdims=True) + EPSILON)
+    return centered * scale, scale
+
+
+def norm_back(values, gain, incoming):
+    unit, scale = standard(values)
+    f = incoming * gain
+    back = (f - jnp.mean(f, -1, keepdims=True) - unit * jnp.mean(f * unit, -1, keepdims=True)) * scale
+    return back, unit
+
+
+def sum_rows(values):
+    return jnp.sum(values.astype(FULL), 0, keepdims=True)
+
+
+def embed_kernel(at, image, text, s8, r8, s8p, r8p, w_image, w_text, vec, hid, embedded, normed, small):
+    unpack(
+        at,
+        (s8, r8, s8p, r8p),
+        ((0, 1, False, w_image), (48, 1, False, w_text), (96, 1, True, small)),
+    )
+    for f in range(16):
+        piece = small[f >> 2, (f >> 1) & 1, f & 1].astype(FULL)
+        vec[:, f * 48 : (f + 1) * 48] = piece[:, :48]
+        hid[:, f * 192 : (f + 1) * 192] = piece[11:12, :192]
+    embedded[0:1, :] = vec[2:3, :]
+    embedded[1 : 1 + IMAGE, :] = matmul(image[...], square(w_image)) + vec[0:1, :]
+    embedded[1 + IMAGE : ROWS, :] = matmul(text[...], square(w_text)) + vec[1:2, :]
+    for rows in row_chunks(64):
+        unit, unused_scale = standard(embedded[rows, :])
+        normed[rows, :] = to_low(unit * vec[3:4, :] + vec[4:5, :])
+
+
+def embed(place, image, text, pieces):
+    block = (4, 2, 2, 48, WIDTH)
+    outs = [
+        shape(block),
+        shape(block),
+        shape((VEC_ROWS, WIDTH), FULL),
+        shape((1, HIDDEN), FULL),
+        shape((ROWS, WIDTH), FULL),
+        shape((ROWS, WIDTH)),
+    ]
+    scratch = (pltpu.VMEM((4, 2, 2, VEC_ROWS, LANES), LOW),)
+    return call(embed_kernel, 5.5, outs, place.scalars, image, text, *pieces, scratch=scratch)
+
+
+def qkv_kernel(at, normed, vec, s8, r8, s8p, r8p, wq, wk, wv, q, k, v):
+    unpack(
+        at,
+        (s8, r8, s8p, r8p),
+        ((0, 1, False, wq), (48, 1, False, wk), (96, 1, False, wv)),
+    )
+    rows = normed[...]
+    for out in (q, k, v):
+        out[832:PADDED, :] = jnp.zeros((PADDED - 832, WIDTH), LOW)
+    low = to_low(matmul(rows, square(wq)) + vec[5:6, :])
+    q[0:ROWS, :] = to_low(low.astype(FULL) * HEAD_DIM**-0.5)
+    k[0:ROWS, :] = to_low(matmul(rows, square(wk)))
+    v[0:ROWS, :] = to_low(matmul(rows, square(wv)) + vec[6:7, :])
+
+
+def qkv(place, normed, vec, pieces):
+    outs = [shape((4, 2, 2, 48, WIDTH))] * 3 + [shape((PADDED, WIDTH))] * 3
+    return call(qkv_kernel, 7, outs, place.scalars, normed, vec, *pieces)
+
+
+def mask_column(live):
+    position = lax.broadcasted_iota(jnp.int32, (KEYS, 1), 0)
+    patches = jnp.where(live[0] == 1, PATCH_BIG, PATCH_SMALL).astype(jnp.int32)
+    image_live = (position >= 1) & (position <= patches)
+    text_live = (position >= 1 + PATCH_BIG) & (position < 1 + PATCH_BIG + live[1])
+    return jnp.where((position == 0) | image_live | text_live, 0.0, NEGATIVE).astype(FULL)
+
+
+QUERY_CHUNKS = ((0, 256), (256, 256), (512, 256), (768, 128))
+
+
+def one_head(ref_value, head):
+    lane = lax.broadcasted_iota(jnp.int32, ref_value.shape, 1)
+    keep = (lane < HEAD_DIM) if head == 0 else (lane >= HEAD_DIM)
+    return jnp.where(keep, ref_value, jnp.zeros_like(ref_value))
+
+
+def attend_kernel(live, q, k, v, attended, totals):
+    bias = mask_column(live)
+    keys = [one_head(k[0:KEYS, :], h) for h in range(2)]
+    values_t = jnp.transpose(v[0:KEYS, :].astype(FULL)).astype(LOW)
+    totals[...] = jnp.zeros_like(totals)
+    for start, width in QUERY_CHUNKS:
+        part = q[start : start + width, :]
+        mixed = []
+        for h in range(2):
+            scores = right_product(keys[h], part) + bias
+            top = jnp.max(scores, 0, keepdims=True)
+            exps = jnp.exp(scores - top)
+            total = jnp.sum(exps, 0, keepdims=True)
+            out = matmul(values_t[h * HEAD_DIM : (h + 1) * HEAD_DIM, :], to_low(exps))
+            mixed.append(out * (1.0 / total))
+            totals[0, h : h + 1, start : start + width] = top + jnp.log(total)
+        attended[start : start + width, :] = to_low(jnp.transpose(jnp.concatenate(mixed, 0)))
+
+
+def attend(live, q, k, v, first, count, earlier=()):
+    spec = pl.BlockSpec((PADDED, 2 * HEAD_DIM), lambda i: (0, i + first))
+    anywhere = pl.BlockSpec(memory_space=pl.ANY)
+
+    def kernel(live, q, k, v, *refs):
+        attend_kernel(live, q, k, v, *refs[-2:])
+
     return pl.pallas_call(
-        functools.partial(assemble_kernel, tuple(layout)),
-        out_shape=tuple(shapes),
-        in_specs=[pl.BlockSpec(memory_space=pltpu.SMEM)] + [fast] * 4,
-        out_specs=tuple(fast for _ in shapes),
-        compiler_params=pltpu.CompilerParams(vmem_limit_bytes=48 * 2**20),
-    )(place.scalars(), *pieces)
-
-
-def gather_chunk(place, shards, chunk, vec):
-    parts = [vec if i == "vec" else half_of(shards[i], place.core, i) for i in chunk]
-    own = jnp.concatenate(parts, 0) if len(parts) > 1 else parts[0]
-    others = [to_chip(own, 4 * step, 4 * step) for step in (1, 2, 3)]
-    along_z = in_order([own] + others, place.z)
-    beside = to_chip(along_z, 1, 2)
-    mine = jnp.where(place.core == 0, place.x, place.y)
-    s8 = jnp.where(mine == 0, jnp.stack([along_z, beside], 1), jnp.stack([beside, along_z], 1))
-    r8 = to_chip(s8, 2, 1)
-    s8p, r8p = swap_cores(s8), swap_cores(r8)
-    outs = assemble(place, (s8, r8, s8p, r8p), shards, chunk)
-    return {i: out.reshape(-1, out.shape[-1]) for i, out in zip(chunk, outs)}
-
-
-def in_order(relative, z):
-    a, b, c, d = relative
-    low = z & 1
-    e, f = jnp.where(low == 0, a, b), jnp.where(low == 0, b, a)
-    g, h = jnp.where(low == 0, c, d), jnp.where(low == 0, d, c)
-    high = (z >> 1) == 0
-    return jnp.stack(
-        [jnp.where(high, e, g), jnp.where(high, f, h), jnp.where(high, g, e), jnp.where(high, h, f)]
-    )
-
-
-def gather_fast(shards):
-    place = Place()
-    flat = jnp.concatenate([shards[i] for i in VECTORS])
-    vec = jnp.pad(flat, (0, VEC_ROWS * LANES - flat.shape[0])).reshape(VEC_ROWS, LANES)
-    whole = {}
-    for chunk in GATHER_CHUNKS:
-        whole.update(gather_chunk(place, shards, chunk, vec))
-    vectors = whole["vec"].reshape(16, VEC_ROWS * LANES)
-    at = 0
-    for i in VECTORS:
-        width = shards[i].shape[0]
-        whole[i] = vectors[:, at : at + width].reshape(-1)
-        at += width
-    return tuple(whole[i] for i in range(20))
-
-
-def halves(place, grad, index, shards):
-    grad = to_low(grad)
-    if index == "vec":
-        return grad, grad
-    count = sub_blocks(index)
-    width = count * LANES
-    made = []
-    for core in (place.core, 1 - place.core):
-        half = lax.dynamic_slice_in_dim(grad, core * width, width, 1)
-        half = half.reshape(16, shards[index].shape[0], width)
-        if count > 1:
-            half = jnp.concatenate([half[:, :, s * LANES : (s + 1) * LANES] for s in range(count)], 1)
-        made.append(half)
-    return tuple(made)
+        kernel,
+        grid=(count,),
+        out_shape=(shape((PADDED, WIDTH)), shape((HEADS // 2, 8, PADDED), FULL)),
+        in_specs=[SCALARS] + [spec] * 3 + [anywhere] * len(earlier),
+        out_specs=(spec, pl.BlockSpec((1, 8, PADDED), lambda i: (i + first, 0, 0))),
+        input_output_aliases={4 + n: n for n in range(len(earlier))},
+        compiler_params=pltpu.CompilerParams(vmem_limit_bytes=32 * 2**20),
+        cost_estimate=cost(5 * count),
+    )(live, q, k, v, *earlier)
+
+
+def attend_back_kernel(live, q, k, v, incoming, totals, q_grad, k_grad, v_grad):
+    bias = mask_column(live)
+    keys = [one_head(k[0:KEYS, :], h) for h in range(2)]
+    values = [one_head(v[0:KEYS, :], h) for h in range(2)]
+    keys_t = jnp.transpose(k[0:KEYS, :].astype(FULL)).astype(LOW)
+    k_sum, v_sum = [None, None], [None, None]
+    for start, width in QUERY_CHUNKS:
+        part = q[start : start + width, :]
+        grad = incoming[start : start + width, :]
+        mixed = []
+        for h in range(2):
+            scores = right_product(keys[h], part) + bias
+            probs = jnp.exp(scores - totals[0, h : h + 1, start : start + width])
+            prob_grad = right_product(values[h], grad)
+            along = jnp.sum(probs * prob_grad, 0, keepdims=True)
+            score_grad = to_low(probs * (prob_grad - along))
+            v_part = matmul(to_low(probs), grad)
+            k_part = matmul(score_grad, part)
+            v_sum[h] = v_part if v_sum[h] is None else v_sum[h] + v_part
+            k_sum[h] = k_part if k_sum[h] is None else k_sum[h] + k_part
+            mixed.append(matmul(keys_t[h * HEAD_DIM : (h + 1) * HEAD_DIM, :], score_grad))
+        back = jnp.transpose(jnp.concatenate(mixed, 0)) * HEAD_DIM**-0.5
+        q_grad[start : start + width, :] = to_low(back)
+    lane = lax.broadcasted_iota(jnp.int32, (KEYS, 2 * HEAD_DIM), 1) < HEAD_DIM
+    k_grad[0:KEYS, :] = to_low(jnp.where(lane, k_sum[0], k_sum[1]))
+    v_grad[0:KEYS, :] = to_low(jnp.where(lane, v_sum[0], v_sum[1]))
+
+
+def attend_back(live, q, k, v, incoming, totals, first, count, earlier=()):
+    spec = pl.BlockSpec((PADDED, 2 * HEAD_DIM), lambda i: (0, i + first))
+    anywhere = pl.BlockSpec(memory_space=pl.ANY)
+
+    def kernel(live, q, k, v, incoming, totals, *refs):
+        attend_back_kernel(live, q, k, v, incoming, totals, *refs[-3:])
+
+    return pl.pallas_call(
+        kernel,
+        grid=(count,),
+        out_shape=(shape((PADDED, WIDTH)),) * 3,
+        in_specs=[SCALARS]
+        + [spec] * 4
+        + [pl.BlockSpec((1, 8, PADDED), lambda i: (i + first, 0, 0))]
+        + [anywhere] * len(earlier),
+        out_specs=(spec,) * 3,
+        input_output_aliases={6 + n: n for n in range(len(earlier))},
+        compiler_params=pltpu.CompilerParams(vmem_limit_bytes=32 * 2**20),
+        cost_estimate=cost(6.5 * count),
+    )(live, q, k, v, incoming, totals, *earlier)
+
+
+def middle_kernel(at, attended, embedded, vec, s8, r8, s8p, r8p, w_out, w_hid, middle, second):
+    unpack(at, (s8, r8, s8p, r8p), ((0, 1, False, w_out), (48, 4, False, w_hid)))
+    middle[...] = embedded[...] + matmul(attended[0:ROWS, :], square(w_out)) + vec[7:8, :]
+    for rows in row_chunks(64):
+        unit, unused_scale = standard(middle[rows, :])
+        second[rows, :] = to_low(unit * vec[8:9, :] + vec[9:10, :])
+
+
+def middle_of(place, attended, embedded, vec, pieces):
+    outs = [
+        shape((4, 2, 2, 48, WIDTH)),
+        shape((4, 2, 2, 48, HIDDEN)),
+        shape((ROWS, WIDTH), FULL),
+        shape((ROWS, WIDTH)),
+    ]
+    return call(middle_kernel, 8, outs, place.scalars, attended, embedded, vec, *pieces)
+
+
+def gelu_parts(u):
+    cumulative = 0.5 * (1.0 + lax.erf(u * (2.0**-0.5)))
+    slope = cumulative + u * (jnp.exp(-0.5 * u * u) * (2.0 * math.pi) ** -0.5)
+    return u * cumulative, slope
+
+
+def feed_kernel(
+    at, second, cot, middle, vec, w_hid, hid, s8, r8, s8p, r8p,
+    layer_out, second_grad, ret_keep, ret_send, hid_keep, hid_send, hid_sum, ret_sum,
+    w_ret, act, inner, total,
+):
+    step = pl.program_id(0)
+    core, x, y = at[0], at[1], at[2]
+
+    def fill(zero_s, zero_r, one_s, one_r):
+        for b in range(2):
+            w_ret[y, x ^ b, :, 0:LANES] = zero_s[b, 0]
+            w_ret[1 - y, x ^ b, :, 0:LANES] = zero_r[b, 0]
+            w_ret[y ^ b, x, :, LANES:] = one_s[b, 0]
+            w_ret[y ^ b, 1 - x, :, LANES:] = one_r[b, 0]
+
+    @pl.when(core == 0)
+    def _():
+        fill(s8, r8, s8p, r8p)
+
+    @pl.when(core == 1)
+    def _():
+        fill(s8p, r8p, s8, r8)
+
+    ret = w_ret[...].reshape(WIDTH, WIDTH)
+    inward = w_hid[...]
+    for rows in row_chunks(432):
+        pre = matmul(second[rows, :], inward) + hid[...]
+        back = right_product(cot[rows, :], ret)
+        value, slope = gelu_parts(pre)
+        act[rows, :] = to_low(value)
+        inner[rows, :] = to_low(back * slope)
+        out = matmul(act[rows, :], ret)
+        back = right_product(inner[rows, :], inward)
+
+        @pl.when(step == 0)
+        def _():
+            total[rows, :] = out
+            second_grad[rows, :] = back
+
+        @pl.when(step > 0)
+        def _():
+            total[rows, :] += out
+            second_grad[rows, :] += back
+
+    hid_sum[...] = sum_rows(inner[...])
+    ret_grad = to_low(left_product(act[...], cot[...])).reshape(4, 192, WIDTH)
+    hid_grad = to_low(left_product(second[...], inner[...])).reshape(16, 48, WIDTH)
+
+    @pl.when(core == 0)
+    def _():
+        ret_keep[...] = ret_grad[:, :, 0:LANES]
+        ret_send[...] = ret_grad[:, :, LANES:]
+
+    @pl.when(core == 1)
+    def _():
+        ret_keep[...] = ret_grad[:, :, LANES:]
+        ret_send[...] = ret_grad[:, :, 0:LANES]
+
+    @pl.when(step < 2)
+    def _():
+        hid_send[:, 0:48, :] = hid_grad[:, :, 0:LANES]
+        hid_send[:, 48:96, :] = hid_grad[:, :, LANES:]
+
+    @pl.when(step >= 2)
+    def _():
+        hid_keep[:, 0:48, :] = hid_grad[:, :, 0:LANES]
+        hid_keep[:, 48:96, :] = hid_grad[:, :, LANES:]
+
+    @pl.when(step == 3)
+    def _():
+        layer_out[...] = to_low(middle[...] + total[...] + vec[10:11, :])
+        ret_sum[...] = sum_rows(cot[...])
+
+
+def feed(place, second, cot, middle, vec, w_hid, hid, pieces):
+    def column(i, at):
+        half = jnp.where(i < 2, 1 - at[0], at[0])
+        return 2 * half + lax.rem(i, 2)
+
+    def whole(dims):
+        return pl.BlockSpec(dims, lambda i, at: (0,) * len(dims))
+
+    piece = pl.BlockSpec((2, 1, 192, LANES), lambda i, at: (0, column(i, at) ^ at[3], 0, 0))
+    ret_spec = pl.BlockSpec((4, 192, LANES), lambda i, at: (column(i, at), 0, 0))
+    outs = (
+        shape((ROWS, WIDTH)),
+        shape((ROWS, WIDTH), FULL),
+        shape((16, 192, LANES)),
+        shape((16, 192, LANES)),
+        shape((16, 192, LANES)),
+        shape((16, 192, LANES)),
+        shape((1, HIDDEN), FULL),
+        shape((1, WIDTH), FULL),
+    )
+    grid = pltpu.PrefetchScalarGridSpec(
+        num_scalar_prefetch=1,
+        grid=(4,),
+        in_specs=[
+            whole((ROWS, WIDTH)),
+            whole((ROWS, WIDTH)),
+            whole((ROWS, WIDTH)),
+            whole((VEC_ROWS, WIDTH)),
+            pl.BlockSpec((WIDTH, WIDTH), lambda i, at: (0, column(i, at))),
+            pl.BlockSpec((1, WIDTH), lambda i, at: (0, column(i, at))),
+            piece,
+            piece,
+            piece,
+            piece,
+        ],
+        out_specs=(
+            whole((ROWS, WIDTH)),
+            whole((ROWS, WIDTH)),
+            ret_spec,
+            ret_spec,
+            pl.BlockSpec((16, 96, LANES), lambda i, at: (0, jnp.maximum(i - 2, 0), 0)),
+            pl.BlockSpec((16, 96, LANES), lambda i, at: (0, jnp.minimum(i, 1), 0)),
+            pl.BlockSpec((1, WIDTH), lambda i, at: (0, column(i, at))),
+            whole((1, WIDTH)),
+        ),
+        scratch_shapes=[
+            pltpu.VMEM((2, 2, 192, WIDTH), LOW),
+            pltpu.VMEM((ROWS, WIDTH), LOW),
+            pltpu.VMEM((ROWS, WIDTH), LOW),
+            pltpu.VMEM((ROWS, WIDTH), FULL),
+        ],
+    )
+    return pl.pallas_call(
+        feed_kernel,
+        grid_spec=grid,
+        out_shape=outs,
+        compiler_params=pltpu.CompilerParams(vmem_limit_bytes=56 * 2**20),
+        cost_estimate=cost(40),
+    )(place.scalars, second, cot, middle, vec, w_hid, hid, *pieces)
+
+
+def branch_kernel(middle, second_grad, cot, vec, w_out, middle_grad, branch, incoming, sums):
+    parts = [jnp.zeros((1, WIDTH), FULL)] * 3
+    for rows in row_chunks(64):
+        e = second_grad[rows, :]
+        back, unit = norm_back(middle[rows, :], vec[8:9, :], e)
+        grad = cot[rows, :].astype(FULL) + back
+        middle_grad[rows, :] = grad
+        branch[rows, :] = to_low(grad)
+        for n, term in enumerate((e * unit, e, to_low(grad))):
+            parts[n] = parts[n] + sum_rows(term)
+    for n in range(3):
+        sums[n : n + 1, :] = parts[n]
+    incoming[832:PADDED, :] = jnp.zeros((PADDED - 832, WIDTH), LOW)
+    incoming[0:ROWS, :] = to_low(right_product(branch[...], square(w_out)))
+
+
+def branch_of(middle, second_grad, cot, vec, w_out):
+    outs = [
+        shape((ROWS, WIDTH), FULL),
+        shape((ROWS, WIDTH)),
+        shape((PADDED, WIDTH)),
+        shape((8, WIDTH), FULL),
+    ]
+    return call(branch_kernel, 8, outs, middle, second_grad, cot, vec, w_out)
+
+
+def both_halves(core, left, right_ref, first, keep, send, offset, rows):
+    for half, out in ((core, keep), (1 - core, send)):
+        columns = pl.ds(pl.multiple_of(half * LANES, LANES), LANES)
+        grad = left_product(left, right_ref[first, columns])
+        out[:, offset : offset + 48, :] = to_low(grad).reshape(16, 48, LANES)
+
+
+def square_grads_kernel(at, attended, branch, normed, dq, dk, dv, keep, send):
+    rows = slice(0, ROWS)
+    both_halves(at[0], attended[rows, :], branch, rows, keep, send, 0, 48)
+    left = normed[...]
+    for n, ref in enumerate((dq, dk, dv)):
+        both_halves(at[0], left, ref, rows, keep, send, 48 * (n + 1), 48)
+
+
+def square_grads(place, attended, branch, normed, grads):
+    outs = [shape((16, 192, LANES))] * 2
+    return call(
+        square_grads_kernel, 11, outs, place.scalars, attended, branch, normed, *grads
+    )
+
+
+def norm_one_kernel(
+    dq, dk, dv, wq, wk, wv, embedded, middle_grad, vec, image_low, text_low, late, grad
+):
+    rows = slice(0, ROWS)
+    grad[...] = (
+        right_product(dq[rows, :], square(wq))
+        + right_product(dk[rows, :], square(wk))
+        + right_product(dv[rows, :], square(wv))
+    )
+    parts = [jnp.zeros((1, WIDTH), FULL)] * 4
+    for piece in row_chunks(64):
+        e = grad[piece, :]
+        back, unit = norm_back(embedded[piece, :], vec[3:4, :], e)
+        for n, term in enumerate((e * unit, e, dq[piece, :], dv[piece, :])):
+            parts[n] = parts[n] + sum_rows(term)
+        grad[piece, :] = middle_grad[piece, :] + back
+    image_low[...] = to_low(grad[1 : 1 + IMAGE, :])
+    text_low[...] = to_low(grad[1 + IMAGE : ROWS, :])
+    late[...] = jnp.zeros_like(late)
+    late[0:1, :] = grad[0:1, :]
+    for n in range(4):
+        late[n + 1 : n + 2, :] = parts[n]
+
+
+def norm_one(grads, projs, embedded, middle_grad, vec):
+    outs = [shape((IMAGE, WIDTH)), shape((TEXTS, WIDTH)), shape((8, WIDTH), FULL)]
+    scratch = (pltpu.VMEM((ROWS, WIDTH), FULL),)
+    return call(
+        norm_one_kernel, 11, outs, *grads, *projs, embedded, middle_grad, vec, scratch=scratch
+    )
+
+
+def last_kernel(
+    at, image, text, image_low, text_low, sums, hid_sum, ret_sum, late,
+    keep, send, rows16, packed,
+):
+    both_halves(at[0], image[...], image_low, slice(0, IMAGE), keep, send, 0, 48)
+    both_halves(at[0], text[...], text_low, slice(0, TEXTS), keep, send, 48, 48)
+    rows16[...] = jnp.zeros_like(rows16)
+    found = (
+        sum_rows(image_low[...]), sum_rows(text_low[...]), late[0:1, :], late[1:2, :], late[2:3, :],
+        late[3:4, :], late[4:5, :], sums[2:3, :], sums[0:1, :], sums[1:2, :], ret_sum[...],
+    )
+    for n, value in enumerate(found):
+        rows16[n : n + 1, :] = value
+    packed[...] = jnp.zeros_like(packed)
+    for f in range(16):
+        packed[f, :, 0:48] = rows16[:, f * 48 : (f + 1) * 48]
+        packed[f, 11:12, 0:192] = hid_sum[:, f * 192 : (f + 1) * 192]
+    low = to_low(packed[...])
+    keep[:, 96:112, :] = low
+    send[:, 96:112, :] = low
+
+
+def last(place, image, text, image_low, text_low, sums, hid_sum, ret_sum, late):
+    outs = [shape((16, 112, LANES)), shape((16, 112, LANES))]
+    scratch = (pltpu.VMEM((VEC_ROWS, WIDTH), FULL), pltpu.VMEM((16, VEC_ROWS, LANES), FULL))
+    return call(
+        last_kernel, 5.5, outs, place.scalars, image, text, image_low, text_low, sums, hid_sum, ret_sum,
+        late, scratch=scratch,
+    )
+
+
+def inputs_kernel(image_low, text_low, w_image, w_text, image_grad, text_grad):
+    image_grad[...] = right_product(image_low[...], square(w_image))
+    text_grad[...] = right_product(text_low[...], square(w_text))
+
+
+def input_grads(image_low, text_low, w_image, w_text):
+    outs = [shape((IMAGE, WIDTH), FULL), shape((TEXTS, WIDTH), FULL)]
+    return call(inputs_kernel, 4.4, outs, image_low, text_low, w_image, w_text)
 
 
 def add_low(*values):
-    total = values[0].astype(jnp.float32)
+    total = values[0].astype(FULL)
     for value in values[1:]:
-        total = total + value.astype(jnp.float32)
+        total = total + value.astype(FULL)
     return to_low(total)
 
 
@@ -486,61 +946,212 @@
     return lax.dynamic_index_in_dim(values, at, axis, keepdims=False)
 
 
-def scatter_chunk(place, grads, chunk, shards):
-    pairs = [halves(place, grads[i], i, shards) for i in chunk]
-    keep = jnp.concatenate([p[0] for p in pairs], 1) if len(pairs) > 1 else pairs[0][0]
-    send = jnp.concatenate([p[1] for p in pairs], 1) if len(pairs) > 1 else pairs[0][1]
-    got = swap_cores(send)
-    rows = keep.shape[1]
-    keep, got = (v.reshape(4, 4, rows, LANES) for v in (keep, got))
-    zero = place.core == 0
-    x, y = place.x, place.y
-    near = [jnp.where(zero, 2 * y + s, 2 * s + x) for s in (0, 1)]
-    far = [jnp.where(zero, 2 * (1 - y) + s, 2 * s + (1 - x)) for s in (0, 1)]
-    sent = jnp.stack([add_low(pick(keep, q, 1), pick(got, q, 1)) for q in far], 1)
-    kept = jnp.stack([add_low(pick(keep, q, 1), pick(got, q, 1)) for q in near], 1)
-    got = to_chip(sent, 2, 1)
-    mine = jnp.where(zero, x, y)
-    sent = add_low(pick(kept, 1 - mine, 1), pick(got, 1 - mine, 1))
-    kept = add_low(pick(kept, mine, 1), pick(got, mine, 1))
-    got = to_chip(sent, 1, 2)
-    total = add_low(kept, got)
-    arrived = [to_chip(pick(total, place.z ^ s, 0), 4 * s, 4 * s) for s in (1, 2, 3)]
-    final = add_low(pick(total, place.z, 0), *arrived)
-    other = swap_cores(final)
-    left = jnp.where(zero, final, other).astype(jnp.float32)
-    right = jnp.where(zero, other, final).astype(jnp.float32)
+class Scatter:
+    def __init__(self, place, pairs):
+        self.place = place
+        self.kept = [keep for keep, unused_send in pairs]
+        self.sent = [send for unused_keep, send in pairs]
+        self.got = None
+
+    def state(self):
+        return self.kept, self.got
+
+    def first(self):
+        zero, x, y = self.place.core == 0, self.place.x, self.place.y
+        near = [jnp.where(zero, 2 * y + s, 2 * s + x) for s in (0, 1)]
+        far = [jnp.where(zero, 2 * (1 - y) + s, 2 * s + (1 - x)) for s in (0, 1)]
+
+        def summed(places):
+            parts = []
+            for keep, more in zip(self.kept, self.got):
+                keep, more = (v.reshape(4, 4, v.shape[1], LANES) for v in (keep, more))
+                added = [add_low(pick(keep, q, 1), pick(more, q, 1)) for q in places]
+                parts.append(jnp.stack(added, 1))
+            return jnp.concatenate(parts, 2) if len(parts) > 1 else parts[0]
+
+        self.sent, self.kept = summed(far), summed(near)
+
+    def second(self):
+        mine = jnp.where(self.place.core == 0, self.place.x, self.place.y)
+        kept, got = self.kept, self.got
+        self.sent = add_low(pick(kept, 1 - mine, 1), pick(got, 1 - mine, 1))
+        self.kept = add_low(pick(kept, mine, 1), pick(got, mine, 1))
+
+    def third(self):
+        z = self.place.z
+        total = add_low(self.kept, self.got)
+        self.kept = pick(total, z, 0)
+        self.sent = [pick(total, z ^ s, 0) for s in (1, 2, 3)]
+
+    def fourth(self):
+        self.sent = self.kept = add_low(self.kept, *self.got)
+
+    def swap(self):
+        self.got = jax.tree.map(swap_cores, self.sent)
+
+    def send_first(self):
+        self.got = to_chip(self.sent, 2, 1)
+
+    def send_second(self):
+        self.got = to_chip(self.sent, 1, 2)
+
+    def send_third(self):
+        self.got = [to_chip(part, 4 * s, 4 * s) for s, part in zip((1, 2, 3), self.sent)]
+
+    def sides(self):
+        zero = self.place.core == 0
+        mine, other = self.kept, self.got
+        return jnp.where(zero, mine, other).astype(FULL), jnp.where(zero, other, mine).astype(FULL)
+
+
+def owned_rows(chunk, left, right):
     result, at = {}, 0
     for index in chunk:
+        rows = block_rows(index)
         if index == "vec":
-            result[index] = left[at : at + VEC_ROWS].reshape(-1)
-            at += VEC_ROWS
-            continue
-        rows, count = shards[index].shape[0], sub_blocks(index)
-        pieces = []
-        for side in (left, right):
-            for s in range(count):
-                pieces.append(side[at + s * rows : at + (s + 1) * rows])
-        result[index] = jnp.concatenate(pieces, 1)
-        at += rows * count
+            for n, vector in enumerate(VECTORS):
+                result[vector] = left[at + n, : 192 if vector == 17 else 48]
+        else:
+            count = sub_blocks(index)
+            step = rows // count
+            sides = [
+                side[at + s * step : at + (s + 1) * step] for side in (left, right) for s in range(count)
+            ]
+            result[index] = jnp.concatenate(sides, 1)
+        at += rows
     return result
 
 
-def scatter_fast(grads, shards):
+def by_kernels(shards, image, text, size_code, length, cot):
     place = Place()
-    grads = dict(enumerate(grads))
-    flat = jnp.concatenate([grads[i].reshape(16, -1) for i in VECTORS], 1)
-    flat = jnp.pad(flat, ((0, 0), (0, VEC_ROWS * LANES - flat.shape[1])))
-    grads["vec"] = flat.reshape(16, VEC_ROWS, LANES)
-    owned = {}
-    for chunk in SCATTER_CHUNKS:
-        owned.update(scatter_chunk(place, grads, chunk, shards))
-    at = 0
-    for i in VECTORS:
-        width = shards[i].shape[0]
-        owned[i] = owned["vec"][at : at + width]
-        at += width
-    return tuple(owned[i] for i in range(20))
+    live = jnp.concatenate([size_code, length]).astype(jnp.int32)
+    own_one = pack(place, shards, GATHER_CHUNKS[0])
+
+    z_one = all_z(own_one)
+    own_two, own_rest = (pack(place, shards, chunk) for chunk in GATHER_CHUNKS[1:])
+    z_one, own_two, own_rest = settle(z_one, own_two, own_rest)
+
+    z_one = jnp.stack(z_one)
+    owns = [own_rest[n * 144 : (n + 1) * 144] for n in range(3)]
+    b_one, z_two = to_chip(z_one, 1, 2), all_z(own_two)
+    b_one, z_two, z_one, owns = settle(b_one, z_two, z_one, owns)
+
+    s_one, z_two = jnp.stack([z_one, b_one]), jnp.stack(z_two)
+    r_one, sp_one, z_a = to_chip(s_one, 2, 1), swap_cores(s_one), all_z(owns[0])
+    r_one, sp_one, s_one, z_a, z_two = settle(r_one, sp_one, s_one, z_a, z_two)
+
+    b_two, z_b, rp_one = to_chip(z_two, 1, 2), all_z(owns[1]), swap_cores(r_one)
+    w_image, w_text, vec, hid, embedded, normed = embed(
+        place, image, text, (s_one, r_one, sp_one, rp_one)
+    )
+    b_two, z_b, z_two, normed = settle(b_two, z_b, z_two, normed)
+
+    s_two = jnp.stack([z_two, b_two])
+    r_two, sp_two, z_c = to_chip(s_two, 2, 1), swap_cores(s_two), all_z(owns[2])
+    z_ab = [jnp.concatenate(pair, 0) for pair in zip(z_a, z_b)]
+    r_two, sp_two, z_c, s_two, z_ab = settle(r_two, sp_two, z_c, s_two, z_ab)
+
+    z_rest = jnp.stack([jnp.concatenate(pair, 0) for pair in zip(z_ab, z_c)])
+    b_rest, rp_two = to_chip(z_rest, 1, 2), swap_cores(r_two)
+    wq, wk, wv, q, k, v = qkv(place, after(normed, z_rest), vec, (s_two, r_two, sp_two, rp_two))
+    both = attend(live, q, k, v, 0, 2)
+    b_rest, z_rest, both = settle(b_rest, z_rest, both)
+
+    s_three = jnp.stack([z_rest[:, :240], b_rest[:, :240]])
+    s_four = jnp.stack([z_rest[:, 240:], b_rest[:, 240:]])
+    r_three, r_four = to_chip(s_three, 2, 1), to_chip(s_four, 2, 1)
+    sp_three, sp_four = swap_cores(s_three), swap_cores(s_four)
+    both = attend(live, after(q, s_three, s_four), k, v, 2, 2, both)
+    attended, totals = attend(live, q, k, v, 4, 2, both)
+    r_three, r_four, sp_three, sp_four, attended = settle(
+        r_three, r_four, sp_three, sp_four, attended
+    )
+
+    rp_three, rp_four = swap_cores(r_three), swap_cores(r_four)
+    w_out, w_hid, middle, second = middle_of(
+        place, attended, embedded, vec, (s_three, r_three, sp_three, rp_three)
+    )
+    layer_out, second_grad, ret_keep, ret_send, hid_keep, hid_send, hid_sum, ret_sum = feed(
+        place, second, cot, middle, vec, w_hid.reshape(WIDTH, HIDDEN), hid,
+        (s_four, r_four, sp_four, rp_four),
+    )
+
+    feeding = Scatter(place, ((ret_keep, ret_send), (hid_keep, hid_send)))
+    feeding.swap()
+    middle_grad, branch, incoming, sums = branch_of(middle, second_grad, cot, vec, w_out)
+    feeding.got, feeding.kept, incoming = settle(feeding.got, feeding.kept, incoming)
+
+    feeding.first()
+    feeding.send_first()
+    ready = after(incoming, feeding.sent, feeding.kept)
+    grads = attend_back(live, q, k, v, ready, totals, 0, 2)
+    grads = attend_back(live, q, k, v, ready, totals, 2, 2, grads)
+    feeding.got, feeding.kept, incoming, grads = settle(feeding.got, feeding.kept, ready, grads)
+
+    feeding.second()
+    feeding.send_second()
+    ready = after(incoming, feeding.sent, feeding.kept)
+    grads = attend_back(live, q, k, v, ready, totals, 4, 2, grads)
+    feeding.got, feeding.kept, grads, normed = settle(feeding.got, feeding.kept, grads, normed)
+
+    feeding.third()
+    feeding.send_third()
+    normed, grads = after((normed, grads), feeding.sent, feeding.kept)
+    pair = square_grads(place, attended, branch, normed, grads)
+    image_low, text_low, late = norm_one(grads, (wq, wk, wv), embedded, middle_grad, vec)
+    feeding.got, feeding.kept, pair, image_low, text_low = settle(
+        feeding.got, feeding.kept, pair, image_low, text_low
+    )
+
+    feeding.fourth()
+    feeding.swap()
+    squares = Scatter(place, (pair,))
+    squares.swap()
+    pair = last(
+        place, image, text, after(image_low, feeding.sent), text_low, sums, hid_sum, ret_sum, late
+    )
+    feeding.got, squares.got, squares.kept, pair, image_low = settle(
+        feeding.got, squares.got, squares.kept, pair, image_low
+    )
+
+    squares.first()
+    squares.send_first()
+    ending = Scatter(place, (pair,))
+    ending.swap()
+    ready = after(image_low, squares.sent, squares.kept)
+    image_grad, text_grad = input_grads(ready, text_low, w_image, w_text)
+    squares.got, squares.kept, ending.got, ending.kept, image_grad, text_grad = settle(
+        squares.got, squares.kept, ending.got, ending.kept, image_grad, text_grad
+    )
+
+    squares.second()
+    squares.send_second()
+    ending.first()
+    ending.send_first()
+    owned = owned_rows(SCATTER_CHUNKS[0], *feeding.sides())
+    squares.got, squares.kept, ending.got, ending.kept, owned = settle(
+        squares.got, squares.kept, ending.got, ending.kept, owned
+    )
+
+    squares.third()
+    squares.send_third()
+    ending.second()
+    ending.send_second()
+    squares.got, squares.kept, ending.got, ending.kept = settle(
+        squares.got, squares.kept, ending.got, ending.kept
+    )
+
+    ending.third()
+    ending.send_third()
+    squares.fourth()
+    squares.swap()
+    ending.got, ending.kept, squares.got = settle(ending.got, ending.kept, squares.got)
+
+    ending.fourth()
+    ending.swap()
+    owned.update(owned_rows(SCATTER_CHUNKS[1], *squares.sides()))
+    owned.update(owned_rows(SCATTER_CHUNKS[2], *ending.sides()))
+    return (layer_out[None], image_grad[None], text_grad[None]) + tuple(owned[i] for i in range(20))
 
 
 def gather_any(shards):
@@ -603,8 +1214,11 @@
         return_proj,
         return_bias,
     )
-    by_permutes = chips == 16 and cores == 2
-    weights = gather_fast(shards) if by_permutes else gather_any(shards)
+    fits = chips == 16 and cores == 2 and image_states.shape == (1, IMAGE, WIDTH)
+    if fits and text_states.shape == (1, TEXTS, WIDTH) and hidden_proj.shape == (48, HIDDEN):
+        image, text, cot = image_states[0], text_states[0], cotangent[0]
+        return by_kernels(shards, image, text, size_group, caption_len, cot)
+    weights = gather_any(shards)
     results, summed = [], None
     for item in range(image_states.shape[0]):
         image_rows, text_rows = image_states[item], text_states[item]
@@ -615,7 +1229,7 @@
         )
         results.append((result, image_grad, text_grad))
         summed = grads if summed is None else jax.tree.map(jnp.add, summed, grads)
-    owned = scatter_fast(summed, shards) if by_permutes else scatter_any(summed)
+    owned = scatter_any(summed)
     return tuple(jnp.stack(parts) for parts in zip(*results)) + owned
 
 

time: 538 us -> 377 us (0.70)
  matrix products: 178 us -> 0 us
  Pallas kernels: 15.4 us -> 176 us
  local copies, waits for them, and re-layouts: 88.3 us -> 30.1 us
  other arithmetic: 75.1 us -> 30.5 us
  waiting for transfers between devices: 102 us -> 76.3 us
  starting transfers between devices: 65.9 us -> 56.1 us
    dot_general x45 -> x0, matrix products: 178 us -> none  [the longest x8 53.7 us: matmul(): return jnp.dot(left, right, preferred_element_type=jnp.float32)]
    pallas_call x4 -> x18, Pallas kernels: 15.4 us -> 176 us  [the longest x11 66 us: call(): pl.pallas_call(kernel, out_shape=tuple(outs), in_specs=specs, out_specs=t...]
    ppermute x40 -> x37, waiting for transfers between devices: 102 us -> 71.8 us  [to_chip(): return lax.ppermute(values, BOTH, pairs)]
    dynamic_slice x34 -> x0, local copies, waits for them, and re-layouts: 29.3 us -> none  [the longest x21 20.3 us: head_slice(): part = lax.dynamic_slice_in_dim(source, offset, span_width, 1)]
    reduce_sum x12 -> x0, other arithmetic: 16.6 us -> none  [the longest x3 8.98 us: one_group(): row_total = jnp.sum(exps, -1, keepdims=True)]
    convert_element_type x21 -> x20, other arithmetic: 35.6 us -> 20.3 us  [to_low(): return values.astype(jnp.bfloat16)]
    ppermute x40 -> x37, starting transfers between devices: 62.8 us -> 53.5 us  [to_chip(): return lax.ppermute(values, BOTH, pairs)]
    concatenate x4 -> x1, local copies, waits for them, and re-layouts: 9.06 us -> 0.01 us  [owned_rows(): result[index] = jnp.concatenate(sides, 1)]
  transfers between devices with their start and end apart: 56 -> 52, of which waited for: 15 -> 16; matrix products, arithmetic and copies ran while one was open for 22% -> 5% of each run, Pallas kernels for 2% -> 36%
where the time goes in v2:
time: 377 us; the launch traced here: 372 us
  Pallas kernels  176 us (47%)
  waiting for transfers between devices  76.3 us (20%)
  starting transfers between devices  56.1 us (15%)
  other arithmetic  30.5 us (8%)
  local copies, waits for them, and re-layouts  30.1 us (8%)
    ppermute x37, waiting for transfers between devices, to_chip(): return lax.ppermute(values, BOTH, pairs)  71.8 us
    pallas_call x11, Pallas kernels, call(): pl.pallas_call(kernel, out_shape=tuple(outs), in_specs=specs, out_specs=t...  66 us
    ppermute x37, starting transfers between devices, to_chip(): return lax.ppermute(values, BOTH, pairs)  53.5 us
    pallas_call x1, Pallas kernels, feed(): pl.pallas_call(feed_kernel, grid_spec=grid, out_shape=outs, compiler_para...  39.7 us
    pallas_call x3, Pallas kernels, attend_back(): pl.pallas_call(kernel, grid=(count,), out_shape=(shape((PADDED, WIDTH)),)...  39.1 us
    pallas_call x3, Pallas kernels, attend(): pl.pallas_call(kernel, grid=(count,), out_shape=(shape((PADDED, WIDTH)),...  30.9 us
    unnamed x99, local copies, waits for them, and re-layouts  27.1 us
    convert_element_type x20, other arithmetic, to_low(): return values.astype(jnp.bfloat16)  20.3 us
  transfers between devices with their start and end apart: 52, of which 16 were waited for; matrix products, arithmetic and copies ran while one was open for 5% of the time, Pallas kernels for 36%

profile of v2, /device:TPU:0, one launch (start us, length us, event | category | flops | bytes accessed | tf_op | source)
XLA Modules:
  0.0 371.6 jit_solution(354623274318417538)
XLA Ops:
  2.5 1.7 shard_map.416
  4.2 3.0 collective-permute-start
  7.2 2.6 collective-permute-start.1
  9.8 1.9 shard_map.418
  11.6 1.7 shard_map.417
  13.3 3.6 collective-permute-done.1
  17.0 1.6 collective-permute-start.3
  18.5 1.5 collective-permute-start.4
  20.0 1.5 collective-permute-start.5
  21.6 1.4 collective-permute-start.6
  24.1 6.1 %collective-permute-done.5 = bf16[144,384]{1,0:T(8,128)(2,1)S(1)} collective-permute-done((bf16[144,384]{1,0:T(8,128)(2,1)}, bf16[144,384]{1,0:T(8,128)(2,1)S(1)}, u32[]{:S(2)}, u32[]{:S(2)}) %collective-permute-start.5) | collective-permute-done | bytes 110624 | tf_op jit(solution)/shard_map/chips_8_8/ppermute | solution.py:391
  31.0 2.6 collective-permute-start.10
  33.6 1.5 collective-permute-start.11
  35.2 7.4 %collective-permute-done.10 = bf16[144,384]{1,0:T(8,128)(2,1)S(1)} collective-permute-done((bf16[144,384]{1,0:T(8,128)(2,1)S(1)}, bf16[144,384]{1,0:T(8,128)(2,1)S(1)}, u32[]{:S(2)}, u32[]{:S(2)}) %collective-permute-start.10) | collective-permute-done | bytes 110624 | tf_op jit(solution)/shard_map/chips_8_8/ppermute | solution.py:391
  43.6 1.5 collective-permute-start.12
  45.1 1.6 collective-permute-start.13
  47.7 1.8 collective-permute-start.15
  50.4 5.7 %shard_map.419 = (bf16[4,2,2,48,768]{4,3,2,1,0:T(8,128)(2,1)}, bf16[4,2,2,48,768]{4,3,2,1,0:T(8,128)(2,1)}, f32[16,768]{1,0:T(8,128)}, f32[1,3072]{1,0:T(1,128)}...) custom-call(s32[4]{0:T(128)} %pad_add_fusion.at_ref.at, bf16[325,768]{1,0:T(8,128)(2,1)} %bitcast.190, ...), custom_call_target="tpu_custom_call" | custom-call | flops 1650000000 | bytes 1024 | tf_op jit(solution)/shard_map/pallas_call | solution.py:361
  56.1 2.2 collective-permute-done.14
  59.2 2.2 collective-permute-start.19
  61.9 1.9 collective-permute-start.21
  64.8 8.1 %collective-permute-done.20 = bf16[144,384]{1,0:T(8,128)(2,1)S(1)} collective-permute-done((bf16[144,384]{1,0:T(8,128)(2,1)S(1)}, bf16[144,384]{1,0:T(8,128)(2,1)S(1)}, u32[]{:S(2)}, u32[]{:S(2)}) %collective-permute-start.20) | collective-permute-done | bytes 110624 | tf_op jit(solution)/shard_map/chips_8_8/ppermute | solution.py:391
  77.7 7.2 %shard_map.420 = (bf16[4,2,2,48,768]{4,3,2,1,0:T(8,128)(2,1)}, bf16[4,2,2,48,768]{4,3,2,1,0:T(8,128)(2,1)}, bf16[4,2,2,48,768]{4,3,2,1,0:T(8,128)(2,1)}, bf16[89...) custom-call(s32[4]{0:T(128)} %pad_add_fusion.at_ref.at, ...), custom_call_target="tpu_custom_call" | custom-call | flops 2100000000 | bytes 1024 | tf_op jit(solution)/shard_map/pallas_call | solution.py:361
  88.9 10.1 %shard_map.421 = (bf16[896,768]{1,0:T(8,128)(2,1)S(1)}, f32[6,8,896]{2,1,0:T(8,128)S(1)}) custom-call(s32[2]{0:T(128)S(1)} %pad_add_fusion.1.live, bf16[896,768]{1,0:T(8,128)(2,1)S(1)} %copy-done.8, bf16[896,768]{1,0:T(8,128)(2,1)S(1)} %copy-done.11, bf16[896,768]{1,0:T(8,128)(2,1)S(1)} %copy-done.14), custom_call_target="tpu_custom_call" | custom-call | flops 3000000000 | bytes 1024 | tf_op jit(solution)/shard_map/pallas_call | solution.py:596
  99.5 1.5 collective-permute-start.24
  102.2 10.1 %shard_map.422 = (bf16[896,768]{1,0:T(8,128)(2,1)S(1)}, f32[6,8,896]{2,1,0:T(8,128)S(1)}) custom-call(s32[2]{0:T(128)S(1)} %pad_add_fusion.1.live, bf16[896,768]{1,0:T(8,128)(2,1)S(1)} %copy-done.8, bf16[896,768]{1,0:T(8,128)(2,1)S(1)} %copy-done.11, bf16[896,768]{1,0:T(8,128)(2,1)S(1)} %copy-done.14, ...), custom_call_target="tpu_custom_call", output_to_operand_aliasing={{0}: (4, {}), {1}: (5, {})} | custom-call | flops 3000000000 | bytes 1024 | tf_op jit(solution)/shard_map/pallas_call | solution.py:596
  112.4 10.6 %shard_map.423 = (bf16[896,768]{1,0:T(8,128)(2,1)S(1)}, f32[6,8,896]{2,1,0:T(8,128)S(1)}) custom-call(s32[2]{0:T(128)S(1)} %pad_add_fusion.1.live, bf16[896,768]{1,0:T(8,128)(2,1)S(1)} %copy-done.8, bf16[896,768]{1,0:T(8,128)(2,1)S(1)} %copy-done.11, bf16[896,768]{1,0:T(8,128)(2,1)S(1)} %copy-done.14, ...), custom_call_target="tpu_custom_call", output_to_operand_aliasing={{0}: (4, {}), {1}: (5, {})} | custom-call | flops 3000000000 | bytes 1024 | tf_op jit(solution)/shard_map/pallas_call | solution.py:596
  124.1 7.6 %collective-permute-done.25.r8 = bf16[2,4,192,384]{3,2,1,0:T(8,128)(2,1)} collective-permute-done((bf16[2,4,192,384]{3,2,1,0:T(8,128)(2,1)S(1)}, bf16[2,4,192,384]{3,2,1,0:T(8,128)(2,1)}, u32[]{:S(2)}, u32[]{:S(2)}) %collective-permute-start.25) | collective-permute-done | bytes 1179680 | tf_op jit(solution)/shard_map/chips_2_1/ppermute | solution.py:391
  133.2 4.4 %collective-permute-done.28.r8p = bf16[2,4,240,384]{3,2,1,0:T(8,128)(2,1)S(1)} collective-permute-done((bf16[2,4,240,384]{3,2,1,0:T(8,128)(2,1)S(1)}, bf16[2,4,240,384]{3,2,1,0:T(8,128)(2,1)S(1)}, u32[]{:S(2)}, u32[]{:S(2)}) %collective-permute-start.28) | collective-permute-done | bytes 1474592 | tf_op jit(solution)/shard_map/between_cores/ppermute | solution.py:382
  138.8 8.1 %shard_map.424 = (bf16[4,2,2,48,768]{4,3,2,1,0:T(8,128)(2,1)}, bf16[4,2,2,48,3072]{4,3,2,1,0:T(8,128)(2,1)}, f32[839,768]{1,0:T(8,128)}, bf16[839,768]{1,0:T(8,128)(2,1)}) custom-call(s32[4]{0:T(128)} %pad_add_fusion.at_ref.at, bf16[896,768]{1,0:T(8,128)(2,1)} %copy-done.5, f32[839,768]{1,0:T(8,128)} %get-tuple-element.247.embedded, ...), custom_call_target="tpu_custom_call" | custom-call | flops 2400000000 | bytes 1024 | tf_op jit(solution)/shard_map/pallas_call | solution.py:361
  147.9 39.7 %shard_map.425 = (bf16[839,768]{1,0:T(8,128)(2,1)}, f32[839,768]{1,0:T(8,128)}, bf16[16,192,384]{2,1,0:T(8,128)(2,1)}, bf16[16,192,384]{2,1,0:T(8,128)(2,1)}, bf...) custom-call(s32[4]{0:T(128)} %pad_add_fusion.at_ref.at, ...), custom_call_target="tpu_custom_call" | custom-call | flops 12000000000 | bytes 1024 | tf_op jit(solution)/shard_map/pallas_call | solution.py:808
  188.3 7.8 %shard_map.426 = (f32[839,768]{1,0:T(8,128)}, bf16[839,768]{1,0:T(8,128)(2,1)}, bf16[896,768]{1,0:T(8,128)(2,1)}, f32[8,768]{1,0:T(8,128)}) custom-call(f32[839,768]{1,0:T(8,128)} %get-tuple-element.251.middle, f32[839,768]{1,0:T(8,128)} %get-tuple-element.261.second_grad, bf16[839,768]{1,0:T(8,128)(2,1)} %bitcast.187, f32[16,768]{1,0:T(8,128)} %get-tuple-element.229.vec, ...), custom_call_target="tpu_custom_call" | custom-call | flops 2400000000 | bytes 1024 | tf_op jit(solution)/shard_map/pallas_call | solution.py:361
  196.1 1.4 copy-done.20
  197.5 2.0 add_convert_fusion.15
  199.9 1.6 add_convert_fusion.13
  201.4 1.7 maximum_maximum_fusion
  203.1 1.5 collective-permute-start.32
  204.6 2.0 add_convert_fusion.11
  210.5 12.8 %shard_map.427 = (bf16[896,768]{1,0:T(8,128)(2,1)S(1)}, bf16[896,768]{1,0:T(8,128)(2,1)S(1)}, bf16[896,768]{1,0:T(8,128)(2,1)S(1)}) custom-call(s32[2]{0:T(128)S(1)} %pad_add_fusion.1.live, bf16[896,768]{1,0:T(8,128)(2,1)S(1)} %copy-done.9, bf16[896,768]{1,0:T(8,128)(2,1)S(1)} %copy-done.12, bf16[896,768]{1,0:T(8,128)(2,1)S(1)} %copy-done.15, ...), custom_call_target="tpu_custom_call" | custom-call | flops 3900000000 | bytes 1024 | tf_op jit(solution)/shard_map/pallas_call | solution.py:643
  223.4 13.1 %shard_map.428 = (bf16[896,768]{1,0:T(8,128)(2,1)S(1)}, bf16[896,768]{1,0:T(8,128)(2,1)S(1)}, bf16[896,768]{1,0:T(8,128)(2,1)S(1)}) custom-call(s32[2]{0:T(128)S(1)} %pad_add_fusion.1.live, bf16[896,768]{1,0:T(8,128)(2,1)S(1)} %copy-done.9, bf16[896,768]{1,0:T(8,128)(2,1)S(1)} %copy-done.12, ...), custom_call_target="tpu_custom_call", output_to_operand_aliasing={{0}: (6, {}), {1}: (7, {}), {2}: (8, {})} | custom-call | flops 3900000000 | bytes 1024 | tf_op jit(solution)/shard_map/pallas_call | solution.py:643
  236.5 3.1 fusion.1
  240.2 2.1 fusion.2
  246.7 13.2 %shard_map.429 = (bf16[896,768]{1,0:T(8,128)(2,1)S(1)}, bf16[896,768]{1,0:T(8,128)(2,1)S(1)}, bf16[896,768]{1,0:T(8,128)(2,1)S(1)}) custom-call(s32[2]{0:T(128)S(1)} %pad_add_fusion.1.live, bf16[896,768]{1,0:T(8,128)(2,1)S(1)} %copy-done.10, bf16[896,768]{1,0:T(8,128)(2,1)S(1)} %copy-done.13, ...), custom_call_target="tpu_custom_call", output_to_operand_aliasing={{0}: (6, {}), {1}: (7, {}), {2}: (8, {})} | custom-call | flops 3900000000 | bytes 1024 | tf_op jit(solution)/shard_map/pallas_call | solution.py:643
  261.0 2.4 add_convert_fusion
  263.6 2.3 collective-permute-start.34
  266.5 1.8 collective-permute-start.36
  268.3 11.1 %shard_map.430 = (bf16[16,192,384]{2,1,0:T(8,128)(2,1)}, bf16[16,192,384]{2,1,0:T(8,128)(2,1)}) custom-call(s32[4]{0:T(128)} %pad_add_fusion.at_ref.at, bf16[896,768]{1,0:T(8,128)(2,1)} %copy-done.5, bf16[839,768]{1,0:T(8,128)(2,1)} %get-tuple-element.289.branch, bf16[839,768]{1,0:T(8,128)(2,1)} %get-tuple-element.294.normed, bf16[896,768]{1,0:T(8,128)(2,1)} %copy-done, ...), custom_call_target="tpu_custom_call" | custom-call | flops 3300000000 | bytes 1024 | tf_op jit(solution)/shard_map/pallas_call | solution.py:361
  279.5 10.8 %shard_map.431 = (bf16[325,768]{1,0:T(8,128)(2,1)}, bf16[513,768]{1,0:T(8,128)(2,1)}, f32[8,768]{1,0:T(8,128)}) custom-call(bf16[896,768]{1,0:T(8,128)(2,1)} %copy-done, bf16[896,768]{1,0:T(8,128)(2,1)} %copy-done.1, bf16[896,768]{1,0:T(8,128)(2,1)} %copy-done.4, bf16[4,2,2,48,768]{4,3,2,1,0:T(8,128)(2,1)} %get-tuple-element.300.wq, ...), custom_call_target="tpu_custom_call" | custom-call | flops 3300000000 | bytes 1024 | tf_op jit(solution)/shard_map/pallas_call | solution.py:361
  291.1 5.6 %shard_map.432 = (bf16[16,112,384]{2,1,0:T(8,128)(2,1)}, bf16[16,112,384]{2,1,0:T(8,128)(2,1)}) custom-call(s32[4]{0:T(128)} %pad_add_fusion.at_ref.at, bf16[325,768]{1,0:T(8,128)(2,1)} %bitcast.191, bf16[513,768]{1,0:T(8,128)(2,1)} %bitcast.189, bf16[325,768]{1,0:T(8,128)(2,1)} %get-tuple-element.326.image_low, ...), custom_call_target="tpu_custom_call" | custom-call | flops 1650000000 | bytes 1024 | tf_op jit(solution)/shard_map/pallas_call | solution.py:361
  301.7 4.4 %shard_map.433 = (f32[325,768]{1,0:T(8,128)}, f32[513,768]{1,0:T(8,128)}) custom-call(bf16[325,768]{1,0:T(8,128)(2,1)} %get-tuple-element.326.image_low, bf16[513,768]{1,0:T(8,128)(2,1)} %get-tuple-element.314.text_low, bf16[4,2,2,48,768]{4,3,2,1,0:T(8,128)(2,1)} %get-tuple-element.327.w_image, bf16[4,2,2,48,768]{4,3,2,1,0:T(8,128)(2,1)} %get-tuple-element.328.w_text), custom_call_target="tpu_custom_call" | custom-call | flops 1320000000 | bytes 1024 | tf_op jit(solution)/shard_map/pallas_call | solution.py:361
  306.2 9.6 %collective-permute-done.39 = bf16[4,2,192,384]{3,2,0,1:T(8,128)(2,1)} collective-permute-done((bf16[4,2,192,384]{3,2,0,1:T(8,128)(2,1)S(1)}, bf16[4,2,192,384]{3,2,0,1:T(8,128)(2,1)}, u32[]{:S(2)}, u32[]{:S(2)}) %collective-permute-start.39) | collective-permute-done | bytes 1179680 | tf_op jit(solution)/shard_map/chips_2_1/ppermute | solution.py:391
  315.8 1.5 add_convert_fusion.21
  320.6 1.4 fusion.6
  323.4 9.4 %collective-permute-done.41 = bf16[4,192,384]{2,1,0:T(8,128)(2,1)S(1)} collective-permute-done((bf16[4,192,384]{2,1,0:T(8,128)(2,1)S(1)}, bf16[4,192,384]{2,1,0:T(8,128)(2,1)S(1)}, u32[]{:S(2)}, u32[]{:S(2)}) %collective-permute-start.41) | collective-permute-done | bytes 589856 | tf_op jit(solution)/shard_map/chips_1_2/ppermute | solution.py:391
  332.8 1.8 collective-permute-done.42
  336.2 4.3 %collective-permute-start.43 = (bf16[192,384]{1,0:T(8,128)(2,1)S(1)}, bf16[192,384]{1,0:T(8,128)(2,1)S(1)}, u32[]{:S(2)}, u32[]{:S(2)}) collective-permute-start(bf16[192,384]{1,0:T(8,128)(2,1)S(1)} %get-tuple-element.401), channel_id=1, source_target_pairs={{0,8},{1,9},{2,10},{3,11},{4,12},{5,13},{6,14},{7,15},{8,0},{9,1},... | collective-permute-start | bytes 442376 | tf_op jit(solution)/shard_map/chips_4_4/ppermute | solution.py:391
  341.2 1.8 collective-permute-start.45
  343.1 2.0 collective-permute-done.43
  345.1 8.3 %collective-permute-done.44 = bf16[192,384]{1,0:T(8,128)(2,1)S(1)} collective-permute-done((bf16[192,384]{1,0:T(8,128)(2,1)S(1)}, bf16[192,384]{1,0:T(8,128)(2,1)S(1)}, u32[]{:S(2)}, u32[]{:S(2)}) %collective-permute-start.44) | collective-permute-done | bytes 147488 | tf_op jit(solution)/shard_map/chips_8_8/ppermute | solution.py:391
  353.7 2.4 collective-permute-start.47
  356.6 1.8 collective-permute-start.49
  358.5 2.8 copy.81
  361.2 2.0 copy.80
  363.2 2.8 collective-permute-done.48
  (226 shorter events, 53.8 us)
Async XLA Ops:
  4.2 12.8 %copy-start.35 = (bf16[112,384]{1,0:T(8,128)(2,1)S(1)}, bf16[112,384]{1,0:T(8,128)(2,1)}, u32[]{:S(2)}) copy-start(bf16[112,384]{1,0:T(8,128)(2,1)} %shard_map.416) | copy-start | bytes 258052
  4.2 9.1 %collective-permute-start = (bf16[112,384]{1,0:T(8,128)(2,1)}, bf16[112,384]{1,0:T(8,128)(2,1)S(1)}, u32[]{:S(2)}, u32[]{:S(2)}) collective-permute-start(bf16[112,384]{1,0:T(8,128)(2,1)} %shard_map.416), channel_id=1, source_target_pairs={{0,8},{1,9},{2,10},{3,11},{4,12},{5,13},{6,14},{7,15},{8,0},{9,1},... | collective-permute-start | bytes 258056 | tf_op jit(solution)/shard_map/chips_4_4/ppermute | solution.py:391
  7.2 9.7 %collective-permute-start.1 = (bf16[112,384]{1,0:T(8,128)(2,1)}, bf16[112,384]{1,0:T(8,128)(2,1)S(1)}, u32[]{:S(2)}, u32[]{:S(2)}) collective-permute-start(bf16[112,384]{1,0:T(8,128)(2,1)} %shard_map.416), channel_id=1, source_target_pairs={{0,16},{1,17},{2,18},{3,19},{4,20},{5,21},{6,22},{7,23},{8,24},{9,... | collective-permute-start | bytes 258056 | tf_op jit(solution)/shard_map/chips_8_8/ppermute | solution.py:391
  9.8 7.1 %collective-permute-start.2 = (bf16[112,384]{1,0:T(8,128)(2,1)}, bf16[112,384]{1,0:T(8,128)(2,1)S(1)}, u32[]{:S(2)}, u32[]{:S(2)}) collective-permute-start(bf16[112,384]{1,0:T(8,128)(2,1)} %shard_map.416), channel_id=1, source_target_pairs={{0,24},{1,25},{2,26},{3,27},{4,28},{5,29},{6,30},{7,31},{8,16},{9,... | collective-permute-start | bytes 258056 | tf_op jit(solution)/shard_map/chips_12_12/ppermute | solution.py:391
  11.6 11.3 %copy-start.32 = (bf16[432,384]{1,0:T(8,128)(2,1)S(1)}, bf16[432,384]{1,0:T(8,128)(2,1)}, u32[]{:S(2)}) copy-start(bf16[432,384]{1,0:T(8,128)(2,1)} %shard_map.418) | copy-start | bytes 995332
  16.9 18.2 %copy-start.34 = (bf16[144,384]{1,0:T(8,128)(2,1)S(1)}, bf16[144,384]{1,0:T(8,128)(2,1)}, u32[]{:S(2)}) copy-start(bf16[144,384]{1,0:T(8,128)(2,1)} %shard_map.417) | copy-start | bytes 331780
  17.0 13.3 %collective-permute-start.3 = (bf16[4,112,384]{2,1,0:T(8,128)(2,1)S(1)}, bf16[4,112,384]{2,1,0:T(8,128)(2,1)S(1)}, u32[]{:S(2)}, u32[]{:S(2)}) collective-permute-start(bf16[4,112,384]{2,1,0:T(8,128)(2,1)S(1)} %pad_maximum_fusion.11), channel_id=1, source_target_pairs={{0,2},{1,5},{2,0},{3,7},{4,6},{5,1},{6,4},{7,3},{8,10},{9,13},{10,... | collective-permute-start | bytes 1032200 | tf_op jit(solution)/shard_map/chips_1_2/ppermute | solution.py:391
  18.5 5.6 %collective-permute-start.4 = (bf16[144,384]{1,0:T(8,128)(2,1)}, bf16[144,384]{1,0:T(8,128)(2,1)S(1)}, u32[]{:S(2)}, u32[]{:S(2)}) collective-permute-start(bf16[144,384]{1,0:T(8,128)(2,1)} %shard_map.417), channel_id=1, source_target_pairs={{0,8},{1,9},{2,10},{3,11},{4,12},{5,13},{6,14},{7,15},{8,0},{9,1},... | collective-permute-start | bytes 331784 | tf_op jit(solution)/shard_map/chips_4_4/ppermute | solution.py:391
  20.0 10.2 %collective-permute-start.5 = (bf16[144,384]{1,0:T(8,128)(2,1)}, bf16[144,384]{1,0:T(8,128)(2,1)S(1)}, u32[]{:S(2)}, u32[]{:S(2)}) collective-permute-start(bf16[144,384]{1,0:T(8,128)(2,1)} %shard_map.417), channel_id=1, source_target_pairs={{0,16},{1,17},{2,18},{3,19},{4,20},{5,21},{6,22},{7,23},{8,24},{9,... | collective-permute-start | bytes 331784 | tf_op jit(solution)/shard_map/chips_8_8/ppermute | solution.py:391
  21.6 8.7 %collective-permute-start.6 = (bf16[144,384]{1,0:T(8,128)(2,1)}, bf16[144,384]{1,0:T(8,128)(2,1)S(1)}, u32[]{:S(2)}, u32[]{:S(2)}) collective-permute-start(bf16[144,384]{1,0:T(8,128)(2,1)} %shard_map.417), channel_id=1, source_target_pairs={{0,24},{1,25},{2,26},{3,27},{4,28},{5,29},{6,30},{7,31},{8,16},{9,... | collective-permute-start | bytes 331784 | tf_op jit(solution)/shard_map/chips_12_12/ppermute | solution.py:391
  30.3 20.0 %copy-start.31 = (bf16[2,4,112,384]{3,2,1,0:T(8,128)(2,1)}, bf16[2,4,112,384]{3,2,1,0:T(8,128)(2,1)S(1)}, u32[]{:S(2)}) copy-start(bf16[2,4,112,384]{3,2,1,0:T(8,128)(2,1)S(1)} %pad_maximum_fusion.6.s8) | copy-start | bytes 2064388
  30.4 13.1 %collective-permute-start.7 = (bf16[2,4,112,384]{3,2,1,0:T(8,128)(2,1)S(1)}, bf16[2,4,112,384]{3,2,1,0:T(8,128)(2,1)S(1)}, u32[]{:S(2)}, u32[]{:S(2)}) collective-permute-start(bf16[2,4,112,384]{3,2,1,0:T(8,128)(2,1)S(1)} %pad_maximum_fusion.6.s8), channel_id=1, source_target_pairs={{0,4},{1,3},{2,6},{3,1},{4,0},{5,7},{6,2},{7,5},{8,12},{9,11},{10,... | collective-permute-start | bytes 2064392 | tf_op jit(solution)/shard_map/chips_2_1/ppermute | solution.py:391
  31.0 12.5 %collective-permute-start.8 = (bf16[2,4,112,384]{3,2,1,0:T(8,128)(2,1)S(1)}, bf16[2,4,112,384]{3,2,1,0:T(8,128)(2,1)S(1)}, u32[]{:S(2)}, u32[]{:S(2)}) collective-permute-start(bf16[2,4,112,384]{3,2,1,0:T(8,128)(2,1)S(1)} %pad_maximum_fusion.6.s8), channel_id=1, source_target_pairs={{0,1},{1,0},{2,3},{3,2},{4,5},{5,4},{6,7},{7,6},{8,9},{9,8},{10,11... | collective-permute-start | bytes 2064392 | tf_op jit(solution)/shard_map/between_cores/ppermute | solution.py:382
  31.0 11.5 %collective-permute-start.10 = (bf16[144,384]{1,0:T(8,128)(2,1)S(1)}, bf16[144,384]{1,0:T(8,128)(2,1)S(1)}, u32[]{:S(2)}, u32[]{:S(2)}) collective-permute-start(bf16[144,384]{1,0:T(8,128)(2,1)S(1)} %get-tuple-element.211), channel_id=1, source_target_pairs={{0,16},{1,17},{2,18},{3,19},{4,20},{5,21},{6,22},{7,23},{8,24},{9,... | collective-permute-start | bytes 331784 | tf_op jit(solution)/shard_map/chips_8_8/ppermute | solution.py:391
  33.6 9.0 %collective-permute-start.11 = (bf16[144,384]{1,0:T(8,128)(2,1)S(1)}, bf16[144,384]{1,0:T(8,128)(2,1)S(1)}, u32[]{:S(2)}, u32[]{:S(2)}) collective-permute-start(bf16[144,384]{1,0:T(8,128)(2,1)S(1)} %get-tuple-element.211), channel_id=1, source_target_pairs={{0,24},{1,25},{2,26},{3,27},{4,28},{5,29},{6,30},{7,31},{8,16},{9,... | collective-permute-start | bytes 331784 | tf_op jit(solution)/shard_map/chips_12_12/ppermute | solution.py:391
  35.1 8.4 %collective-permute-start.9 = (bf16[144,384]{1,0:T(8,128)(2,1)S(1)}, bf16[144,384]{1,0:T(8,128)(2,1)S(1)}, u32[]{:S(2)}, u32[]{:S(2)}) collective-permute-start(bf16[144,384]{1,0:T(8,128)(2,1)S(1)} %get-tuple-element.211), channel_id=1, source_target_pairs={{0,8},{1,9},{2,10},{3,11},{4,12},{5,13},{6,14},{7,15},{8,0},{9,1},... | collective-permute-start | bytes 331784 | tf_op jit(solution)/shard_map/chips_4_4/ppermute | solution.py:391
  43.5 6.9 %copy-start.42 = (bf16[2,4,112,384]{3,2,1,0:T(8,128)(2,1)}, bf16[2,4,112,384]{3,2,1,0:T(8,128)(2,1)S(1)}, u32[]{:S(2)}) copy-start(bf16[2,4,112,384]{3,2,1,0:T(8,128)(2,1)S(1)} %collective-permute-done.7.r8) | copy-start | bytes 2064388
  43.5 6.9 %copy-start.43 = (bf16[2,4,112,384]{3,2,1,0:T(8,128)(2,1)}, bf16[2,4,112,384]{3,2,1,0:T(8,128)(2,1)S(1)}, u32[]{:S(2)}) copy-start(bf16[2,4,112,384]{3,2,1,0:T(8,128)(2,1)S(1)} %collective-permute-done.8.s8p) | copy-start | bytes 2064388
  43.5 6.0 %collective-permute-start.16 = (bf16[2,4,112,384]{3,2,1,0:T(8,128)(2,1)S(1)}, bf16[2,4,112,384]{3,2,1,0:T(8,128)(2,1)S(1)}, u32[]{:S(2)}, u32[]{:S(2)}) collective-permute-start(bf16[2,4,112,384]{3,2,1,0:T(8,128)(2,1)S(1)} %collective-permute-done.7.r8), channel_id=1, source_target_pairs={{0,1},{1,0},{2,3},{3,2},{4,5},{5,4},{6,7},{7,6},{8,9},{9,8},{10,11... | collective-permute-start | bytes 2064392 | tf_op jit(solution)/shard_map/between_cores/ppermute | solution.py:382
  43.6 14.7 %collective-permute-start.12 = (bf16[4,144,384]{2,1,0:T(8,128)(2,1)S(1)}, bf16[4,144,384]{2,1,0:T(8,128)(2,1)S(1)}, u32[]{:S(2)}, u32[]{:S(2)}) collective-permute-start(bf16[4,144,384]{2,1,0:T(8,128)(2,1)S(1)} %pad_maximum_fusion.10), channel_id=1, source_target_pairs={{0,2},{1,5},{2,0},{3,7},{4,6},{5,1},{6,4},{7,3},{8,10},{9,13},{10,... | collective-permute-start | bytes 1327112 | tf_op jit(solution)/shard_map/chips_1_2/ppermute | solution.py:391
  45.1 11.0 %collective-permute-start.13 = (bf16[144,384]{1,0:T(8,128)(2,1)S(1)}, bf16[144,384]{1,0:T(8,128)(2,1)S(1)}, u32[]{:S(2)}, u32[]{:S(2)}) collective-permute-start(bf16[144,384]{1,0:T(8,128)(2,1)S(1)} %get-tuple-element.212), channel_id=1, source_target_pairs={{0,8},{1,9},{2,10},{3,11},{4,12},{5,13},{6,14},{7,15},{8,0},{9,1},... | collective-permute-start | bytes 331784 | tf_op jit(solution)/shard_map/chips_4_4/ppermute | solution.py:391
  46.7 11.6 %collective-permute-start.14 = (bf16[144,384]{1,0:T(8,128)(2,1)S(1)}, bf16[144,384]{1,0:T(8,128)(2,1)S(1)}, u32[]{:S(2)}, u32[]{:S(2)}) collective-permute-start(bf16[144,384]{1,0:T(8,128)(2,1)S(1)} %get-tuple-element.212), channel_id=1, source_target_pairs={{0,16},{1,17},{2,18},{3,19},{4,20},{5,21},{6,22},{7,23},{8,24},{9,... | collective-permute-start | bytes 331784 | tf_op jit(solution)/shard_map/chips_8_8/ppermute | solution.py:391
  47.7 10.6 %collective-permute-start.15 = (bf16[144,384]{1,0:T(8,128)(2,1)S(1)}, bf16[144,384]{1,0:T(8,128)(2,1)S(1)}, u32[]{:S(2)}, u32[]{:S(2)}) collective-permute-start(bf16[144,384]{1,0:T(8,128)(2,1)S(1)} %get-tuple-element.212), channel_id=1, source_target_pairs={{0,24},{1,25},{2,26},{3,27},{4,28},{5,29},{6,30},{7,31},{8,16},{9,... | collective-permute-start | bytes 331784 | tf_op jit(solution)/shard_map/chips_12_12/ppermute | solution.py:391
  58.4 14.8 %copy-start.30 = (bf16[2,4,144,384]{3,2,1,0:T(8,128)(2,1)}, bf16[2,4,144,384]{3,2,1,0:T(8,128)(2,1)S(1)}, u32[]{:S(2)}) copy-start(bf16[2,4,144,384]{3,2,1,0:T(8,128)(2,1)S(1)} %pad_maximum_fusion.5.s8) | copy-start | bytes 2654212
  58.4 14.5 %collective-permute-start.17 = (bf16[2,4,144,384]{3,2,1,0:T(8,128)(2,1)S(1)}, bf16[2,4,144,384]{3,2,1,0:T(8,128)(2,1)S(1)}, u32[]{:S(2)}, u32[]{:S(2)}) collective-permute-start(bf16[2,4,144,384]{3,2,1,0:T(8,128)(2,1)S(1)} %pad_maximum_fusion.5.s8), channel_id=1, source_target_pairs={{0,4},{1,3},{2,6},{3,1},{4,0},{5,7},{6,2},{7,5},{8,12},{9,11},{10,... | collective-permute-start | bytes 2654216 | tf_op jit(solution)/shard_map/chips_2_1/ppermute | solution.py:391
  59.2 13.8 %collective-permute-start.18 = (bf16[2,4,144,384]{3,2,1,0:T(8,128)(2,1)S(1)}, bf16[2,4,144,384]{3,2,1,0:T(8,128)(2,1)S(1)}, u32[]{:S(2)}, u32[]{:S(2)}) collective-permute-start(bf16[2,4,144,384]{3,2,1,0:T(8,128)(2,1)S(1)} %pad_maximum_fusion.5.s8), channel_id=1, source_target_pairs={{0,1},{1,0},{2,3},{3,2},{4,5},{5,4},{6,7},{7,6},{8,9},{9,8},{10,11... | collective-permute-start | bytes 2654216 | tf_op jit(solution)/shard_map/between_cores/ppermute | solution.py:382
  59.2 5.7 %collective-permute-start.19 = (bf16[144,384]{1,0:T(8,128)(2,1)S(1)}, bf16[144,384]{1,0:T(8,128)(2,1)S(1)}, u32[]{:S(2)}, u32[]{:S(2)}) collective-permute-start(bf16[144,384]{1,0:T(8,128)(2,1)S(1)} %get-tuple-element.220), channel_id=1, source_target_pairs={{0,8},{1,9},{2,10},{3,11},{4,12},{5,13},{6,14},{7,15},{8,0},{9,1},... | collective-permute-start | bytes 331784 | tf_op jit(solution)/shard_map/chips_4_4/ppermute | solution.py:391
  61.4 11.5 %collective-permute-start.20 = (bf16[144,384]{1,0:T(8,128)(2,1)S(1)}, bf16[144,384]{1,0:T(8,128)(2,1)S(1)}, u32[]{:S(2)}, u32[]{:S(2)}) collective-permute-start(bf16[144,384]{1,0:T(8,128)(2,1)S(1)} %get-tuple-element.220), channel_id=1, source_target_pairs={{0,16},{1,17},{2,18},{3,19},{4,20},{5,21},{6,22},{7,23},{8,24},{9,... | collective-permute-start | bytes 331784 | tf_op jit(solution)/shard_map/chips_8_8/ppermute | solution.py:391
  61.9 11.0 %collective-permute-start.21 = (bf16[144,384]{1,0:T(8,128)(2,1)S(1)}, bf16[144,384]{1,0:T(8,128)(2,1)S(1)}, u32[]{:S(2)}, u32[]{:S(2)}) collective-permute-start(bf16[144,384]{1,0:T(8,128)(2,1)S(1)} %get-tuple-element.220), channel_id=1, source_target_pairs={{0,24},{1,25},{2,26},{3,27},{4,28},{5,29},{6,30},{7,31},{8,16},{9,... | collective-permute-start | bytes 331784 | tf_op jit(solution)/shard_map/chips_12_12/ppermute | solution.py:391
  73.0 3.8 %collective-permute-start.23 = (bf16[2,4,144,384]{3,2,1,0:T(8,128)(2,1)S(1)}, bf16[2,4,144,384]{3,2,1,0:T(8,128)(2,1)S(1)}, u32[]{:S(2)}, u32[]{:S(2)}) collective-permute-start(bf16[2,4,144,384]{3,2,1,0:T(8,128)(2,1)S(1)} %collective-permute-done.17.r8), channel_id=1, source_target_pairs={{0,1},{1,0},{2,3},{3,2},{4,5},{5,4},{6,7},{7,6},{8,9},{9,8},{10,11... | collective-permute-start | bytes 2654216 | tf_op jit(solution)/shard_map/between_cores/ppermute | solution.py:382
  74.3 24.7 %collective-permute-start.22 = (bf16[4,432,384]{2,1,0:T(8,128)(2,1)S(1)}, bf16[4,432,384]{2,1,0:T(8,128)(2,1)S(1)}, u32[]{:S(2)}, u32[]{:S(2)}) collective-permute-start(bf16[4,432,384]{2,1,0:T(8,128)(2,1)S(1)} %pad_maximum_fusion.1), channel_id=1, source_target_pairs={{0,2},{1,5},{2,0},{3,7},{4,6},{5,1},{6,4},{7,3},{8,10},{9,13},{10,... | collective-permute-start | bytes 3981320 | tf_op jit(solution)/shard_map/chips_1_2/ppermute | solution.py:391
  99.5 32.2 %collective-permute-start.24 = (bf16[2,4,240,384]{3,2,1,0:T(8,128)(2,1)S(1)}, bf16[2,4,240,384]{3,2,1,0:T(8,128)(2,1)S(1)}, u32[]{:S(2)}, u32[]{:S(2)}) collective-permute-start(bf16[2,4,240,384]{3,2,1,0:T(8,128)(2,1)S(1)} %pad_maximum_fusion.s8), channel_id=1, source_target_pairs={{0,4},{1,3},{2,6},{3,1},{4,0},{5,7},{6,2},{7,5},{8,12},{9,11},{10,... | collective-permute-start | bytes 4423688 | tf_op jit(solution)/shard_map/chips_2_1/ppermute | solution.py:391
  101.1 30.7 %collective-permute-start.26 = (bf16[2,4,240,384]{3,2,1,0:T(8,128)(2,1)S(1)}, bf16[2,4,240,384]{3,2,1,0:T(8,128)(2,1)S(1)}, u32[]{:S(2)}, u32[]{:S(2)}) collective-permute-start(bf16[2,4,240,384]{3,2,1,0:T(8,128)(2,1)S(1)} %pad_maximum_fusion.s8), channel_id=1, source_target_pairs={{0,1},{1,0},{2,3},{3,2},{4,5},{5,4},{6,7},{7,6},{8,9},{9,8},{10,11... | collective-permute-start | bytes 4423688 | tf_op jit(solution)/shard_map/between_cores/ppermute | solution.py:382
  101.3 11.1 %copy-start.28 = (bf16[2,4,192,384]{3,2,1,0:T(8,128)(2,1)}, bf16[2,4,192,384]{3,2,1,0:T(8,128)(2,1)S(1)}, u32[]{:S(2)}) copy-start(bf16[2,4,192,384]{3,2,1,0:T(8,128)(2,1)S(1)} %pad_maximum_fusion.2.s8) | copy-start | bytes 3538948
  101.3 30.4 %collective-permute-start.25 = (bf16[2,4,192,384]{3,2,1,0:T(8,128)(2,1)S(1)}, bf16[2,4,192,384]{3,2,1,0:T(8,128)(2,1)}, u32[]{:S(2)}, u32[]{:S(2)}) collective-permute-start(bf16[2,4,192,384]{3,2,1,0:T(8,128)(2,1)S(1)} %pad_maximum_fusion.2.s8), channel_id=1, source_target_pairs={{0,4},{1,3},{2,6},{3,1},{4,0},{5,7},{6,2},{7,5},{8,12},{9,11},{10,... | collective-permute-start | bytes 3538952 | tf_op jit(solution)/shard_map/chips_2_1/ppermute | solution.py:391
  102.1 29.6 %collective-permute-start.27 = (bf16[2,4,192,384]{3,2,1,0:T(8,128)(2,1)S(1)}, bf16[2,4,192,384]{3,2,1,0:T(8,128)(2,1)S(1)}, u32[]{:S(2)}, u32[]{:S(2)}) collective-permute-start(bf16[2,4,192,384]{3,2,1,0:T(8,128)(2,1)S(1)} %pad_maximum_fusion.2.s8), channel_id=1, source_target_pairs={{0,1},{1,0},{2,3},{3,2},{4,5},{5,4},{6,7},{7,6},{8,9},{9,8},{10,11... | collective-permute-start | bytes 3538952 | tf_op jit(solution)/shard_map/between_cores/ppermute | solution.py:382
  131.7 7.1 %copy-start.24 = (bf16[2,4,240,384]{3,2,1,0:T(8,128)(2,1)}, bf16[2,4,240,384]{3,2,1,0:T(8,128)(2,1)S(1)}, u32[]{:S(2)}) copy-start(bf16[2,4,240,384]{3,2,1,0:T(8,128)(2,1)S(1)} %collective-permute-done.24.r8) | copy-start | bytes 4423684
  132.7 5.0 %copy-start.25 = (bf16[2,4,240,384]{3,2,1,0:T(8,128)(2,1)}, bf16[2,4,240,384]{3,2,1,0:T(8,128)(2,1)S(1)}, u32[]{:S(2)}) copy-start(bf16[2,4,240,384]{3,2,1,0:T(8,128)(2,1)S(1)} %collective-permute-done.26.s8p) | copy-start | bytes 4423684
  132.7 5.0 %collective-permute-start.28 = (bf16[2,4,240,384]{3,2,1,0:T(8,128)(2,1)S(1)}, bf16[2,4,240,384]{3,2,1,0:T(8,128)(2,1)S(1)}, u32[]{:S(2)}, u32[]{:S(2)}) collective-permute-start(bf16[2,4,240,384]{3,2,1,0:T(8,128)(2,1)S(1)} %collective-permute-done.24.r8), channel_id=1, source_target_pairs={{0,1},{1,0},{2,3},{3,2},{4,5},{5,4},{6,7},{7,6},{8,9},{9,8},{10,11... | collective-permute-start | bytes 4423688 | tf_op jit(solution)/shard_map/between_cores/ppermute | solution.py:382
  132.7 14.2 %collective-permute-start.29 = (bf16[2,4,192,384]{3,2,1,0:T(8,128)(2,1)}, bf16[2,4,192,384]{3,2,1,0:T(8,128)(2,1)S(1)}, u32[]{:S(2)}, u32[]{:S(2)}) collective-permute-start(bf16[2,4,192,384]{3,2,1,0:T(8,128)(2,1)} %collective-permute-done.25.r8), channel_id=1, source_target_pairs={{0,1},{1,0},{2,3},{3,2},{4,5},{5,4},{6,7},{7,6},{8,9},{9,8},{10,11... | collective-permute-start | bytes 3538952 | tf_op jit(solution)/shard_map/between_cores/ppermute | solution.py:382
  187.7 8.4 %collective-permute-start.30 = (bf16[16,192,384]{2,1,0:T(8,128)(2,1)}, bf16[16,192,384]{2,1,0:T(8,128)(2,1)}, u32[]{:S(2)}, u32[]{:S(2)}) collective-permute-start(bf16[16,192,384]{2,1,0:T(8,128)(2,1)} %get-tuple-element.257), channel_id=1, source_target_pairs={{0,1},{1,0},{2,3},{3,2},{4,5},{5,4},{6,7},{7,6},{8,9},{9,8},{10,11... | collective-permute-start | bytes 7077896 | tf_op jit(solution)/shard_map/between_cores/ppermute | solution.py:382
  187.9 8.2 %collective-permute-start.31 = (bf16[16,192,384]{2,1,0:T(8,128)(2,1)}, bf16[16,192,384]{2,1,0:T(8,128)(2,1)S(1)}, u32[]{:S(2)}, u32[]{:S(2)}) collective-permute-start(bf16[16,192,384]{2,1,0:T(8,128)(2,1)} %get-tuple-element.258), channel_id=1, source_target_pairs={{0,1},{1,0},{2,3},{3,2},{4,5},{5,4},{6,7},{7,6},{8,9},{9,8},{10,11... | collective-permute-start | bytes 7077896 | tf_op jit(solution)/shard_map/between_cores/ppermute | solution.py:382
  203.1 33.3 %collective-permute-start.32 = (bf16[4,2,384,384]{3,2,0,1:T(8,128)(2,1)}, bf16[4,2,384,384]{3,2,0,1:T(8,128)(2,1)}, u32[]{:S(2)}, u32[]{:S(2)}) collective-permute-start(bf16[4,2,384,384]{3,2,0,1:T(8,128)(2,1)} %maximum_maximum_fusion), channel_id=1, source_target_pairs={{0,4},{1,3},{2,6},{3,1},{4,0},{5,7},{6,2},{7,5},{8,12},{9,11},{10,... | collective-permute-start | bytes 7077896 | tf_op jit(solution)/shard_map/chips_2_1/ppermute | solution.py:391
  207.6 28.8 %copy-start.17 = (bf16[4,2,384,384]{3,2,1,0:T(8,128)(2,1)}, bf16[4,2,384,384]{3,2,1,0:T(8,128)(2,1)S(1)}, u32[]{:S(2)}) copy-start(bf16[4,2,384,384]{3,2,1,0:T(8,128)(2,1)S(1)} %maximum_maximum_fusion.1) | copy-start | bytes 7077892
  239.6 21.4 %collective-permute-start.33 = (bf16[4,384,384]{2,1,0:T(8,128)(2,1)}, bf16[4,384,384]{2,1,0:T(8,128)(2,1)}, u32[]{:S(2)}, u32[]{:S(2)}) collective-permute-start(bf16[4,384,384]{2,1,0:T(8,128)(2,1)} %fusion.1), channel_id=1, source_target_pairs={{0,2},{1,5},{2,0},{3,7},{4,6},{5,1},{6,4},{7,3},{8,10},{9,13},{10,... | collective-permute-start | bytes 3538952 | tf_op jit(solution)/shard_map/chips_1_2/ppermute | solution.py:391
  263.6 26.6 %collective-permute-start.34 = (bf16[384,384]{1,0:T(8,128)(2,1)S(1)}, bf16[384,384]{1,0:T(8,128)(2,1)S(1)}, u32[]{:S(2)}, u32[]{:S(2)}) collective-permute-start(bf16[384,384]{1,0:T(8,128)(2,1)S(1)} %get-tuple-element.397), channel_id=1, source_target_pairs={{0,8},{1,9},{2,10},{3,11},{4,12},{5,13},{6,14},{7,15},{8,0},{9,1},... | collective-permute-start | bytes 884744 | tf_op jit(solution)/shard_map/chips_4_4/ppermute | solution.py:391
  265.9 24.4 %collective-permute-start.35 = (bf16[384,384]{1,0:T(8,128)(2,1)S(1)}, bf16[384,384]{1,0:T(8,128)(2,1)S(1)}, u32[]{:S(2)}, u32[]{:S(2)}) collective-permute-start(bf16[384,384]{1,0:T(8,128)(2,1)S(1)} %get-tuple-element.396), channel_id=1, source_target_pairs={{0,16},{1,17},{2,18},{3,19},{4,20},{5,21},{6,22},{7,23},{8,24},{9,... | collective-permute-start | bytes 884744 | tf_op jit(solution)/shard_map/chips_8_8/ppermute | solution.py:391
  266.5 23.7 %collective-permute-start.36 = (bf16[384,384]{1,0:T(8,128)(2,1)S(1)}, bf16[384,384]{1,0:T(8,128)(2,1)S(1)}, u32[]{:S(2)}, u32[]{:S(2)}) collective-permute-start(bf16[384,384]{1,0:T(8,128)(2,1)S(1)} %get-tuple-element.395), channel_id=1, source_target_pairs={{0,24},{1,25},{2,26},{3,27},{4,28},{5,29},{6,30},{7,31},{8,16},{9,... | collective-permute-start | bytes 884744 | tf_op jit(solution)/shard_map/chips_12_12/ppermute | solution.py:391
  290.3 6.4 %collective-permute-start.38 = (bf16[16,192,384]{2,1,0:T(8,128)(2,1)}, bf16[16,192,384]{2,1,0:T(8,128)(2,1)S(1)}, u32[]{:S(2)}, u32[]{:S(2)}) collective-permute-start(bf16[16,192,384]{2,1,0:T(8,128)(2,1)} %get-tuple-element.310), channel_id=1, source_target_pairs={{0,1},{1,0},{2,3},{3,2},{4,5},{5,4},{6,7},{7,6},{8,9},{9,8},{10,11... | collective-permute-start | bytes 7077896 | tf_op jit(solution)/shard_map/between_cores/ppermute | solution.py:382
  290.5 6.1 %collective-permute-start.37 = (bf16[384,384]{1,0:T(8,128)(2,1)S(1)}, bf16[384,384]{1,0:T(8,128)(2,1)S(1)}, u32[]{:S(2)}, u32[]{:S(2)}) collective-permute-start(bf16[384,384]{1,0:T(8,128)(2,1)S(1)} %add_convert_fusion.22), channel_id=1, source_target_pairs={{0,1},{1,0},{2,3},{3,2},{4,5},{5,4},{6,7},{7,6},{8,9},{9,8},{10,11... | collective-permute-start | bytes 884744 | tf_op jit(solution)/shard_map/between_cores/ppermute | solution.py:382
  299.4 16.4 %collective-permute-start.39 = (bf16[4,2,192,384]{3,2,0,1:T(8,128)(2,1)S(1)}, bf16[4,2,192,384]{3,2,0,1:T(8,128)(2,1)}, u32[]{:S(2)}, u32[]{:S(2)}) collective-permute-start(bf16[4,2,192,384]{3,2,0,1:T(8,128)(2,1)S(1)} %pad_maximum_fusion.3), channel_id=1, source_target_pairs={{0,4},{1,3},{2,6},{3,1},{4,0},{5,7},{6,2},{7,5},{8,12},{9,11},{10,... | collective-permute-start | bytes 3538952 | tf_op jit(solution)/shard_map/chips_2_1/ppermute | solution.py:391
  300.3 15.5 %collective-permute-start.40 = (bf16[16,112,384]{2,1,0:T(8,128)(2,1)}, bf16[16,112,384]{2,1,0:T(8,128)(2,1)}, u32[]{:S(2)}, u32[]{:S(2)}) collective-permute-start(bf16[16,112,384]{2,1,0:T(8,128)(2,1)} %get-tuple-element.323), channel_id=1, source_target_pairs={{0,1},{1,0},{2,3},{3,2},{4,5},{5,4},{6,7},{7,6},{8,9},{9,8},{10,11... | collective-permute-start | bytes 4128776 | tf_op jit(solution)/shard_map/between_cores/ppermute | solution.py:382
  317.3 17.3 %collective-permute-start.42 = (bf16[4,2,112,384]{3,2,0,1:T(8,128)(2,1)S(1)}, bf16[4,2,112,384]{3,2,0,1:T(8,128)(2,1)S(1)}, u32[]{:S(2)}, u32[]{:S(2)}) collective-permute-start(bf16[4,2,112,384]{3,2,0,1:T(8,128)(2,1)S(1)} %pad_maximum_fusion.7), channel_id=1, source_target_pairs={{0,4},{1,3},{2,6},{3,1},{4,0},{5,7},{6,2},{7,5},{8,12},{9,11},{10,... | collective-permute-start | bytes 2064392 | tf_op jit(solution)/shard_map/chips_2_1/ppermute | solution.py:391
  319.3 13.5 %collective-permute-start.41 = (bf16[4,192,384]{2,1,0:T(8,128)(2,1)S(1)}, bf16[4,192,384]{2,1,0:T(8,128)(2,1)S(1)}, u32[]{:S(2)}, u32[]{:S(2)}) collective-permute-start(bf16[4,192,384]{2,1,0:T(8,128)(2,1)S(1)} %fusion.5), channel_id=1, source_target_pairs={{0,2},{1,5},{2,0},{3,7},{4,6},{5,1},{6,4},{7,3},{8,10},{9,13},{10,... | collective-permute-start | bytes 1769480 | tf_op jit(solution)/shard_map/chips_1_2/ppermute | solution.py:391
  334.7 18.6 %collective-permute-start.46 = (bf16[4,112,384]{2,1,0:T(8,128)(2,1)S(1)}, bf16[4,112,384]{2,1,0:T(8,128)(2,1)S(1)}, u32[]{:S(2)}, u32[]{:S(2)}) collective-permute-start(bf16[4,112,384]{2,1,0:T(8,128)(2,1)S(1)} %fusion.7), channel_id=1, source_target_pairs={{0,2},{1,5},{2,0},{3,7},{4,6},{5,1},{6,4},{7,3},{8,10},{9,13},{10,... | collective-permute-start | bytes 1032200 | tf_op jit(solution)/shard_map/chips_1_2/ppermute | solution.py:391
  336.2 8.8 %collective-permute-start.43 = (bf16[192,384]{1,0:T(8,128)(2,1)S(1)}, bf16[192,384]{1,0:T(8,128)(2,1)S(1)}, u32[]{:S(2)}, u32[]{:S(2)}) collective-permute-start(bf16[192,384]{1,0:T(8,128)(2,1)S(1)} %get-tuple-element.401), channel_id=1, source_target_pairs={{0,8},{1,9},{2,10},{3,11},{4,12},{5,13},{6,14},{7,15},{8,0},{9,1},... | collective-permute-start | bytes 442376 | tf_op jit(solution)/shard_map/chips_4_4/ppermute | solution.py:391
  340.6 12.8 %collective-permute-start.44 = (bf16[192,384]{1,0:T(8,128)(2,1)S(1)}, bf16[192,384]{1,0:T(8,128)(2,1)S(1)}, u32[]{:S(2)}, u32[]{:S(2)}) collective-permute-start(bf16[192,384]{1,0:T(8,128)(2,1)S(1)} %get-tuple-element.400), channel_id=1, source_target_pairs={{0,16},{1,17},{2,18},{3,19},{4,20},{5,21},{6,22},{7,23},{8,24},{9,... | collective-permute-start | bytes 442376 | tf_op jit(solution)/shard_map/chips_8_8/ppermute | solution.py:391
  341.2 12.1 %collective-permute-start.45 = (bf16[192,384]{1,0:T(8,128)(2,1)S(1)}, bf16[192,384]{1,0:T(8,128)(2,1)S(1)}, u32[]{:S(2)}, u32[]{:S(2)}) collective-permute-start(bf16[192,384]{1,0:T(8,128)(2,1)S(1)} %get-tuple-element.399), channel_id=1, source_target_pairs={{0,24},{1,25},{2,26},{3,27},{4,28},{5,29},{6,30},{7,31},{8,16},{9,... | collective-permute-start | bytes 442376 | tf_op jit(solution)/shard_map/chips_12_12/ppermute | solution.py:391
  343.1 15.4 %copy-start.23 = (f32[513,768]{1,0:T(8,128)S(1)}, f32[513,768]{1,0:T(8,128)}, u32[]{:S(2)}) copy-start(f32[513,768]{1,0:T(8,128)} %get-tuple-element.332) | copy-start | bytes 4727812
  353.4 12.6 %collective-permute-start.50 = (bf16[192,384]{1,0:T(8,128)(2,1)S(1)}, bf16[192,384]{1,0:T(8,128)(2,1)S(1)}, u32[]{:S(2)}, u32[]{:S(2)}) collective-permute-start(bf16[192,384]{1,0:T(8,128)(2,1)S(1)} %add_convert_fusion.23), channel_id=1, source_target_pairs={{0,1},{1,0},{2,3},{3,2},{4,5},{5,4},{6,7},{7,6},{8,9},{9,8},{10,11... | collective-permute-start | bytes 442376 | tf_op jit(solution)/shard_map/between_cores/ppermute | solution.py:382
  353.7 9.6 %collective-permute-start.47 = (bf16[112,384]{1,0:T(8,128)(2,1)S(1)}, bf16[112,384]{1,0:T(8,128)(2,1)S(1)}, u32[]{:S(2)}, u32[]{:S(2)}) collective-permute-start(bf16[112,384]{1,0:T(8,128)(2,1)S(1)} %get-tuple-element.407), channel_id=1, source_target_pairs={{0,8},{1,9},{2,10},{3,11},{4,12},{5,13},{6,14},{7,15},{8,0},{9,1},... | collective-permute-start | bytes 258056 | tf_op jit(solution)/shard_map/chips_4_4/ppermute | solution.py:391
  356.0 9.9 %collective-permute-start.48 = (bf16[112,384]{1,0:T(8,128)(2,1)S(1)}, bf16[112,384]{1,0:T(8,128)(2,1)S(1)}, u32[]{:S(2)}, u32[]{:S(2)}) collective-permute-start(bf16[112,384]{1,0:T(8,128)(2,1)S(1)} %get-tuple-element.406), channel_id=1, source_target_pairs={{0,16},{1,17},{2,18},{3,19},{4,20},{5,21},{6,22},{7,23},{8,24},{9,... | collective-permute-start | bytes 258056 | tf_op jit(solution)/shard_map/chips_8_8/ppermute | solution.py:391
  356.6 9.3 %collective-permute-start.49 = (bf16[112,384]{1,0:T(8,128)(2,1)S(1)}, bf16[112,384]{1,0:T(8,128)(2,1)S(1)}, u32[]{:S(2)}, u32[]{:S(2)}) collective-permute-start(bf16[112,384]{1,0:T(8,128)(2,1)S(1)} %get-tuple-element.405), channel_id=1, source_target_pairs={{0,24},{1,25},{2,26},{3,27},{4,28},{5,29},{6,30},{7,31},{8,16},{9,... | collective-permute-start | bytes 258056 | tf_op jit(solution)/shard_map/chips_12_12/ppermute | solution.py:391
  366.2 2.8 collective-permute-start.51
  (33 other events, 58.1 us)

commit v3 on v2

--- a/solution.py
+++ b/solution.py
@@ -321,7 +321,7 @@
 VECTORS = (1, 3, 4, 5, 6, 8, 11, 13, 14, 15, 19, 17)
 LANES = 384
 VEC_ROWS = 16
-GATHER_CHUNKS = ((0, 2, "vec"), (7, 9, 10), (12, 16, 18))
+GATHER_CHUNKS = ((0, 2, "vec"), (7, 9, 10), (12, "low"), ("high",), (18,))
 SCATTER_CHUNKS = ((18, 16), (12, 7, 9, 10), (0, 2, "vec"))
 BOTH = ("fsdp", "dp")
 WIDTH = 768
@@ -396,20 +396,13 @@
 
 
 def block_rows(index):
-    return {"vec": VEC_ROWS, 16: 192, 18: 192}.get(index, 48)
-
-
-def layout_of(chunk):
-    made, offset = {}, 0
-    for index in chunk:
-        made[index] = offset
-        offset += block_rows(index)
-    return made, offset
+    return {"vec": VEC_ROWS, 16: 192, 18: 192, "low": 96, "high": 96}.get(index, 48)
 
 
 def pack_kernel(chunk, at_ref, *refs):
     core = at_ref[0]
-    out, ins = refs[len(chunk) if "vec" not in chunk else len(chunk) - 1 + 12], refs
+    count = len(chunk) + (11 if "vec" in chunk else 0)
+    ins, out = refs[:count], refs[count]
     offset = 0
     for place, index in enumerate(chunk):
         if index == "vec":
@@ -420,17 +413,17 @@
                 rows[row : row + 1, 0 : source.shape[1]] = source[...].astype(FULL)
             out[offset : offset + VEC_ROWS, :] = rows[...].astype(LOW)
             continue
-        count = sub_blocks(index)
+        parts = {"low": (4, (0, 1)), "high": (4, (2, 3))}.get(index, (1, (0,)))
         rows = ins[place].shape[0]
-        for s in range(count):
-            first = pl.multiple_of((core * count + s) * LANES, LANES)
+        for s in parts[1]:
+            first = pl.multiple_of((core * parts[0] + s) * LANES, LANES)
             out[offset : offset + rows, :] = ins[place][:, pl.ds(first, LANES)]
             offset += rows
 
 
 def pack(place, shards, chunk):
     rows = sum(block_rows(i) for i in chunk)
-    ins = [shards[i] for i in chunk if i != "vec"]
+    ins = [shards[16 if i in ("low", "high") else i] for i in chunk if i != "vec"]
     scratch = ()
     if "vec" in chunk:
         ins += [shards[i].reshape(1, -1) for i in VECTORS]
@@ -447,10 +440,10 @@
     core, x, y, z = at_ref[0], at_ref[1], at_ref[2], at_ref[3]
 
     def fill(zero_s, zero_r, one_s, one_r):
-        for offset, count, is_vec, out in targets:
+        for offset, blocks, count, out in targets:
             rows = out.shape[3]
-            for s in range(count):
-                first = slice(offset + s * rows, offset + (s + 1) * rows)
+            for n, s in enumerate(blocks):
+                first = slice(offset + n * rows, offset + (n + 1) * rows)
                 left = slice(s * LANES, (s + 1) * LANES)
                 right = slice((count + s) * LANES, (count + s + 1) * LANES)
                 for far in range(4):
@@ -458,7 +451,7 @@
                     for b in range(2):
                         out[plane, y, x ^ b, :, left] = zero_s[b, far, first, :]
                         out[plane, 1 - y, x ^ b, :, left] = zero_r[b, far, first, :]
-                        if not is_vec:
+                        if count:
                             out[plane, y ^ b, x, :, right] = one_s[b, far, first, :]
                             out[plane, y ^ b, 1 - x, :, right] = one_r[b, far, first, :]
 
@@ -502,7 +495,7 @@
     unpack(
         at,
         (s8, r8, s8p, r8p),
-        ((0, 1, False, w_image), (48, 1, False, w_text), (96, 1, True, small)),
+        ((0, (0,), 1, w_image), (48, (0,), 1, w_text), (96, (0,), 0, small)),
     )
     for f in range(16):
         piece = small[f >> 2, (f >> 1) & 1, f & 1].astype(FULL)
@@ -534,7 +527,7 @@
     unpack(
         at,
         (s8, r8, s8p, r8p),
-        ((0, 1, False, wq), (48, 1, False, wk), (96, 1, False, wv)),
+        ((0, (0,), 1, wq), (48, (0,), 1, wk), (96, (0,), 1, wv)),
     )
     rows = normed[...]
     for out in (q, k, v):
@@ -558,32 +551,55 @@
     return jnp.where((position == 0) | image_live | text_live, 0.0, NEGATIVE).astype(FULL)
 
 
-QUERY_CHUNKS = ((0, 256), (256, 256), (512, 256), (768, 128))
-
-
 def one_head(ref_value, head):
     lane = lax.broadcasted_iota(jnp.int32, ref_value.shape, 1)
     keep = (lane < HEAD_DIM) if head == 0 else (lane >= HEAD_DIM)
     return jnp.where(keep, ref_value, jnp.zeros_like(ref_value))
 
 
-def attend_kernel(live, q, k, v, attended, totals):
+def across(values):
+    return jnp.transpose(values.astype(FULL))
+
+
+def fold_rows(values, op):
+    return op(values.reshape(values.shape[0] // 8, 8, values.shape[1]), 0)
+
+
+def attend_kernel(live, q, k, v, attended, totals, keys, scores, probs, mixed):
     bias = mask_column(live)
-    keys = [one_head(k[0:KEYS, :], h) for h in range(2)]
-    values_t = jnp.transpose(v[0:KEYS, :].astype(FULL)).astype(LOW)
+    for h in range(2):
+        keys[h] = one_head(k[0:KEYS, :], h)
+    values_t = to_low(across(v[0:KEYS, :]))
     totals[...] = jnp.zeros_like(totals)
-    for start, width in QUERY_CHUNKS:
-        part = q[start : start + width, :]
-        mixed = []
-        for h in range(2):
-            scores = right_product(keys[h], part) + bias
-            top = jnp.max(scores, 0, keepdims=True)
-            exps = jnp.exp(scores - top)
-            total = jnp.sum(exps, 0, keepdims=True)
-            out = matmul(values_t[h * HEAD_DIM : (h + 1) * HEAD_DIM, :], to_low(exps))
-            mixed.append(out * (1.0 / total))
-            totals[0, h : h + 1, start : start + width] = top + jnp.log(total)
-        attended[start : start + width, :] = to_low(jnp.transpose(jnp.concatenate(mixed, 0)))
+    parts = [(piece, h) for piece in row_chunks(256, PADDED) for h in range(2)]
+    tiles = row_chunks(128, KEYS)
+    tops = {}
+
+    def score(n, tile):
+        piece, h = parts[n]
+        made = right_product(keys[h, tile, :], q[piece, :]) + bias[tile, :]
+        scores[n % 2, tile, 0 : made.shape[1]] = made
+        top = fold_rows(made, jnp.max)
+        tops[n] = jnp.maximum(tops[n], top) if n in tops else top
+
+    for tile in tiles:
+        score(0, tile)
+    for n, (piece, h) in enumerate(parts):
+        width = piece.stop - piece.start
+        top = jnp.max(tops[n], 0, keepdims=True)
+        total = jnp.zeros((8, width), FULL)
+        for tile in tiles:
+            if n + 1 < len(parts):
+                score(n + 1, tile)
+            exps = jnp.exp(scores[n % 2, tile, 0:width] - top)
+            total = total + fold_rows(exps, jnp.sum)
+            probs[n % 2, tile, 0:width] = to_low(exps)
+        total = jnp.sum(total, 0, keepdims=True)
+        rows = slice(h * HEAD_DIM, (h + 1) * HEAD_DIM)
+        out = matmul(values_t[rows, :], probs[n % 2, :, 0:width])
+        mixed[rows, piece] = out * (1.0 / total)
+        totals[0, h : h + 1, piece] = top + jnp.log(total)
+    attended[...] = to_low(jnp.transpose(mixed[...]))
 
 
 def attend(live, q, k, v, first, count, earlier=()):
@@ -591,7 +607,7 @@
     anywhere = pl.BlockSpec(memory_space=pl.ANY)
 
     def kernel(live, q, k, v, *refs):
-        attend_kernel(live, q, k, v, *refs[-2:])
+        attend_kernel(live, q, k, v, *refs[len(earlier) :])
 
     return pl.pallas_call(
         kernel,
@@ -599,64 +615,72 @@
         out_shape=(shape((PADDED, WIDTH)), shape((HEADS // 2, 8, PADDED), FULL)),
         in_specs=[SCALARS] + [spec] * 3 + [anywhere] * len(earlier),
         out_specs=(spec, pl.BlockSpec((1, 8, PADDED), lambda i: (i + first, 0, 0))),
+        scratch_shapes=[
+            pltpu.VMEM((2, KEYS, 2 * HEAD_DIM), LOW),
+            pltpu.VMEM((2, KEYS, 256), FULL),
+            pltpu.VMEM((2, KEYS, 256), LOW),
+            pltpu.VMEM((2 * HEAD_DIM, PADDED), FULL),
+        ],
         input_output_aliases={4 + n: n for n in range(len(earlier))},
-        compiler_params=pltpu.CompilerParams(vmem_limit_bytes=32 * 2**20),
-        cost_estimate=cost(5 * count),
+        compiler_params=pltpu.CompilerParams(vmem_limit_bytes=60 * 2**20),
+        cost_estimate=cost(3 * count),
     )(live, q, k, v, *earlier)
 
 
-def attend_back_kernel(live, q, k, v, incoming, totals, q_grad, k_grad, v_grad):
+def attend_back_kernel(
+    live, q, k, v, incoming, attended, totals, q_grad, k_grad, v_grad,
+    keys, values, probs, score_grads, mixed,
+):
     bias = mask_column(live)
-    keys = [one_head(k[0:KEYS, :], h) for h in range(2)]
-    values = [one_head(v[0:KEYS, :], h) for h in range(2)]
-    keys_t = jnp.transpose(k[0:KEYS, :].astype(FULL)).astype(LOW)
-    k_sum, v_sum = [None, None], [None, None]
-    for start, width in QUERY_CHUNKS:
-        part = q[start : start + width, :]
-        grad = incoming[start : start + width, :]
-        mixed = []
-        for h in range(2):
-            scores = right_product(keys[h], part) + bias
-            probs = jnp.exp(scores - totals[0, h : h + 1, start : start + width])
-            prob_grad = right_product(values[h], grad)
-            along = jnp.sum(probs * prob_grad, 0, keepdims=True)
-            score_grad = to_low(probs * (prob_grad - along))
-            v_part = matmul(to_low(probs), grad)
-            k_part = matmul(score_grad, part)
-            v_sum[h] = v_part if v_sum[h] is None else v_sum[h] + v_part
-            k_sum[h] = k_part if k_sum[h] is None else k_sum[h] + k_part
-            mixed.append(matmul(keys_t[h * HEAD_DIM : (h + 1) * HEAD_DIM, :], score_grad))
-        back = jnp.transpose(jnp.concatenate(mixed, 0)) * HEAD_DIM**-0.5
-        q_grad[start : start + width, :] = to_low(back)
+    for h in range(2):
+        keys[h] = one_head(k[0:KEYS, :], h)
+        values[h] = one_head(v[0:KEYS, :], h)
+    keys_t = to_low(across(k[0:KEYS, :]))
+    product = jnp.transpose(incoming[...].astype(FULL) * attended[...].astype(FULL))
+    for h in range(2):
+        rows = slice(h * HEAD_DIM, (h + 1) * HEAD_DIM)
+        along = jnp.sum(product[rows], 0, keepdims=True)
+        for piece in row_chunks(256, PADDED):
+            for tile in row_chunks(256, KEYS):
+                made = right_product(keys[h, tile, :], q[piece, :]) + bias[tile, :]
+                prob = jnp.exp(made - totals[0, h : h + 1, piece])
+                prob_grad = right_product(values[h, tile, :], incoming[piece, :])
+                probs[h, tile, piece] = to_low(prob)
+                score_grads[h, tile, piece] = to_low(prob * (prob_grad - along[:, piece]))
+        mixed[rows, :] = matmul(keys_t[rows, :], score_grads[h])
     lane = lax.broadcasted_iota(jnp.int32, (KEYS, 2 * HEAD_DIM), 1) < HEAD_DIM
-    k_grad[0:KEYS, :] = to_low(jnp.where(lane, k_sum[0], k_sum[1]))
-    v_grad[0:KEYS, :] = to_low(jnp.where(lane, v_sum[0], v_sum[1]))
-
-
-def attend_back(live, q, k, v, incoming, totals, first, count, earlier=()):
-    spec = pl.BlockSpec((PADDED, 2 * HEAD_DIM), lambda i: (0, i + first))
-    anywhere = pl.BlockSpec(memory_space=pl.ANY)
-
-    def kernel(live, q, k, v, incoming, totals, *refs):
-        attend_back_kernel(live, q, k, v, incoming, totals, *refs[-3:])
-
+    for out, left, right in ((k_grad, score_grads, q), (v_grad, probs, incoming)):
+        right = right[...]
+        out[0:KEYS, :] = to_low(jnp.where(lane, matmul(left[0], right), matmul(left[1], right)))
+    q_grad[...] = to_low(jnp.transpose(mixed[...]) * HEAD_DIM**-0.5)
+
+
+def attend_back(live, q, k, v, incoming, attended, totals):
+    spec = pl.BlockSpec((PADDED, 2 * HEAD_DIM), lambda i: (0, i))
     return pl.pallas_call(
-        kernel,
-        grid=(count,),
+        attend_back_kernel,
+        grid=(HEADS // 2,),
         out_shape=(shape((PADDED, WIDTH)),) * 3,
-        in_specs=[SCALARS]
-        + [spec] * 4
-        + [pl.BlockSpec((1, 8, PADDED), lambda i: (i + first, 0, 0))]
-        + [anywhere] * len(earlier),
+        in_specs=[SCALARS] + [spec] * 5 + [pl.BlockSpec((1, 8, PADDED), lambda i: (i, 0, 0))],
         out_specs=(spec,) * 3,
-        input_output_aliases={6 + n: n for n in range(len(earlier))},
-        compiler_params=pltpu.CompilerParams(vmem_limit_bytes=32 * 2**20),
-        cost_estimate=cost(6.5 * count),
-    )(live, q, k, v, incoming, totals, *earlier)
-
-
-def middle_kernel(at, attended, embedded, vec, s8, r8, s8p, r8p, w_out, w_hid, middle, second):
-    unpack(at, (s8, r8, s8p, r8p), ((0, 1, False, w_out), (48, 4, False, w_hid)))
+        scratch_shapes=[
+            pltpu.VMEM((2, KEYS, 2 * HEAD_DIM), LOW),
+            pltpu.VMEM((2, KEYS, 2 * HEAD_DIM), LOW),
+            pltpu.VMEM((2, KEYS, PADDED), LOW),
+            pltpu.VMEM((2, KEYS, PADDED), LOW),
+            pltpu.VMEM((2 * HEAD_DIM, PADDED), FULL),
+        ],
+        compiler_params=pltpu.CompilerParams(vmem_limit_bytes=60 * 2**20),
+        cost_estimate=cost(28),
+    )(live, q, k, v, incoming, attended, totals)
+
+
+def middle_kernel(
+    at, attended, embedded, vec, s8, r8, s8p, r8p, s_hi, r_hi, sp_hi, rp_hi,
+    w_out, w_hid, middle, second,
+):
+    unpack(at, (s8, r8, s8p, r8p), ((0, (0,), 1, w_out), (48, (0, 1), 4, w_hid)))
+    unpack(at, (s_hi, r_hi, sp_hi, rp_hi), ((0, (2, 3), 4, w_hid),))
     middle[...] = embedded[...] + matmul(attended[0:ROWS, :], square(w_out)) + vec[7:8, :]
     for rows in row_chunks(64):
         unit, unused_scale = standard(middle[rows, :])
@@ -809,7 +833,7 @@
         feed_kernel,
         grid_spec=grid,
         out_shape=outs,
-        compiler_params=pltpu.CompilerParams(vmem_limit_bytes=56 * 2**20),
+        compiler_params=pltpu.CompilerParams(vmem_limit_bytes=60 * 2**20),
         cost_estimate=cost(40),
     )(place.scalars, second, cot, middle, vec, w_hid, hid, *pieces)
 
@@ -995,8 +1019,8 @@
     def send_second(self):
         self.got = to_chip(self.sent, 1, 2)
 
-    def send_third(self):
-        self.got = [to_chip(part, 4 * s, 4 * s) for s, part in zip((1, 2, 3), self.sent)]
+    def send_third(self, steps=(1, 2, 3)):
+        self.got = [to_chip(self.sent[s - 1], 4 * s, 4 * s) for s in steps]
 
     def sides(self):
         zero = self.place.core == 0
@@ -1028,52 +1052,51 @@
     own_one = pack(place, shards, GATHER_CHUNKS[0])
 
     z_one = all_z(own_one)
-    own_two, own_rest = (pack(place, shards, chunk) for chunk in GATHER_CHUNKS[1:])
-    z_one, own_two, own_rest = settle(z_one, own_two, own_rest)
+    owns = [pack(place, shards, chunk) for chunk in GATHER_CHUNKS[1:]]
+    z_one, owns = settle(z_one, owns)
 
     z_one = jnp.stack(z_one)
-    owns = [own_rest[n * 144 : (n + 1) * 144] for n in range(3)]
-    b_one, z_two = to_chip(z_one, 1, 2), all_z(own_two)
+    b_one, z_two = to_chip(z_one, 1, 2), all_z(owns[0])
     b_one, z_two, z_one, owns = settle(b_one, z_two, z_one, owns)
 
     s_one, z_two = jnp.stack([z_one, b_one]), jnp.stack(z_two)
-    r_one, sp_one, z_a = to_chip(s_one, 2, 1), swap_cores(s_one), all_z(owns[0])
+    r_one, sp_one, z_a = to_chip(s_one, 2, 1), swap_cores(s_one), all_z(owns[1])
     r_one, sp_one, s_one, z_a, z_two = settle(r_one, sp_one, s_one, z_a, z_two)
 
-    b_two, z_b, rp_one = to_chip(z_two, 1, 2), all_z(owns[1]), swap_cores(r_one)
+    z_a = jnp.stack(z_a)
+    b_two, rp_one, b_a, z_b = to_chip(z_two, 1, 2), swap_cores(r_one), to_chip(z_a, 1, 2), all_z(owns[2])
     w_image, w_text, vec, hid, embedded, normed = embed(
-        place, image, text, (s_one, r_one, sp_one, rp_one)
-    )
-    b_two, z_b, z_two, normed = settle(b_two, z_b, z_two, normed)
+        place, image, after(text, z_a), (s_one, r_one, sp_one, rp_one)
+    )
+    b_two, b_a, z_b, z_two, normed = settle(b_two, b_a, z_b, z_two, normed)
 
     s_two = jnp.stack([z_two, b_two])
-    r_two, sp_two, z_c = to_chip(s_two, 2, 1), swap_cores(s_two), all_z(owns[2])
-    z_ab = [jnp.concatenate(pair, 0) for pair in zip(z_a, z_b)]
-    r_two, sp_two, z_c, s_two, z_ab = settle(r_two, sp_two, z_c, s_two, z_ab)
-
-    z_rest = jnp.stack([jnp.concatenate(pair, 0) for pair in zip(z_ab, z_c)])
-    b_rest, rp_two = to_chip(z_rest, 1, 2), swap_cores(r_two)
-    wq, wk, wv, q, k, v = qkv(place, after(normed, z_rest), vec, (s_two, r_two, sp_two, rp_two))
+    r_two, sp_two, z_c = to_chip(s_two, 2, 1), swap_cores(s_two), all_z(owns[3])
+    s_a, z_b = jnp.stack([z_a, b_a]), jnp.stack(z_b)
+    r_two, sp_two, z_c, s_two, s_a, z_b = settle(r_two, sp_two, z_c, s_two, s_a, z_b)
+
+    rp_two, r_a, b_b = swap_cores(r_two), to_chip(s_a, 2, 1), to_chip(z_b, 1, 2)
+    z_c, sp_a = jnp.stack(z_c), swap_cores(s_a)
+    wq, wk, wv, q, k, v = qkv(place, after(normed, z_c), vec, (s_two, r_two, sp_two, rp_two))
     both = attend(live, q, k, v, 0, 2)
-    b_rest, z_rest, both = settle(b_rest, z_rest, both)
-
-    s_three = jnp.stack([z_rest[:, :240], b_rest[:, :240]])
-    s_four = jnp.stack([z_rest[:, 240:], b_rest[:, 240:]])
-    r_three, r_four = to_chip(s_three, 2, 1), to_chip(s_four, 2, 1)
-    sp_three, sp_four = swap_cores(s_three), swap_cores(s_four)
-    both = attend(live, after(q, s_three, s_four), k, v, 2, 2, both)
+    r_a, b_b, z_c, sp_a, both = settle(r_a, b_b, z_c, sp_a, both)
+
+    s_b = jnp.stack([z_b, b_b])
+    r_b, b_c, sp_b, rp_a = to_chip(s_b, 2, 1), to_chip(z_c, 1, 2), swap_cores(s_b), swap_cores(r_a)
+    both = attend(live, after(q, s_b), k, v, 2, 2, both)
     attended, totals = attend(live, q, k, v, 4, 2, both)
-    r_three, r_four, sp_three, sp_four, attended = settle(
-        r_three, r_four, sp_three, sp_four, attended
-    )
-
-    rp_three, rp_four = swap_cores(r_three), swap_cores(r_four)
+    r_b, b_c, sp_b, rp_a, attended = settle(r_b, b_c, sp_b, rp_a, attended)
+
+    s_c = jnp.stack([z_c, b_c])
+    r_c, sp_c, rp_b = to_chip(s_c, 2, 1), swap_cores(s_c), swap_cores(r_b)
     w_out, w_hid, middle, second = middle_of(
-        place, attended, embedded, vec, (s_three, r_three, sp_three, rp_three)
-    )
+        place, after(attended, s_c), embedded, vec, (s_a, r_a, sp_a, rp_a, s_b, r_b, sp_b, rp_b)
+    )
+    r_c, sp_c, second = settle(r_c, sp_c, second)
+
     layer_out, second_grad, ret_keep, ret_send, hid_keep, hid_send, hid_sum, ret_sum = feed(
         place, second, cot, middle, vec, w_hid.reshape(WIDTH, HIDDEN), hid,
-        (s_four, r_four, sp_four, rp_four),
+        (s_c, r_c, sp_c, swap_cores(r_c)),
     )
 
     feeding = Scatter(place, ((ret_keep, ret_send), (hid_keep, hid_send)))
@@ -1083,73 +1106,69 @@
 
     feeding.first()
     feeding.send_first()
-    ready = after(incoming, feeding.sent, feeding.kept)
-    grads = attend_back(live, q, k, v, ready, totals, 0, 2)
-    grads = attend_back(live, q, k, v, ready, totals, 2, 2, grads)
-    feeding.got, feeding.kept, incoming, grads = settle(feeding.got, feeding.kept, ready, grads)
+    incoming = after(incoming, feeding.sent, feeding.kept)
+    grads = attend_back(live, q, k, v, incoming, attended, totals)
+    feeding.got, feeding.kept, grads = settle(feeding.got, feeding.kept, grads)
 
     feeding.second()
     feeding.send_second()
-    ready = after(incoming, feeding.sent, feeding.kept)
-    grads = attend_back(live, q, k, v, ready, totals, 4, 2, grads)
-    feeding.got, feeding.kept, grads, normed = settle(feeding.got, feeding.kept, grads, normed)
+    grads = after(grads, feeding.sent, feeding.kept)
+    pair = square_grads(place, attended, branch, normed, grads)
+    feeding.got, feeding.kept, grads, pair = settle(feeding.got, feeding.kept, grads, pair)
 
     feeding.third()
-    feeding.send_third()
-    normed, grads = after((normed, grads), feeding.sent, feeding.kept)
-    pair = square_grads(place, attended, branch, normed, grads)
-    image_low, text_low, late = norm_one(grads, (wq, wk, wv), embedded, middle_grad, vec)
-    feeding.got, feeding.kept, pair, image_low, text_low = settle(
-        feeding.got, feeding.kept, pair, image_low, text_low
-    )
-
-    feeding.fourth()
-    feeding.swap()
+    feeding.send_third((1, 3))
     squares = Scatter(place, (pair,))
     squares.swap()
-    pair = last(
-        place, image, text, after(image_low, feeding.sent), text_low, sums, hid_sum, ret_sum, late
-    )
-    feeding.got, squares.got, squares.kept, pair, image_low = settle(
-        feeding.got, squares.got, squares.kept, pair, image_low
-    )
-
+    grads = after(grads, feeding.sent, feeding.kept)
+    image_low, text_low, late = norm_one(grads, (wq, wk, wv), embedded, middle_grad, vec)
+    early, feeding.sent, squares.got, squares.kept, image_low, text_low = settle(
+        feeding.got, feeding.sent, squares.got, squares.kept, image_low, text_low
+    )
+
+    feeding.send_third((2,))
     squares.first()
     squares.send_first()
+    image_low, text_low = after((image_low, text_low), squares.sent, squares.kept)
+    pair = last(place, image, text, image_low, text_low, sums, hid_sum, ret_sum, late)
+    image_grad, text_grad = input_grads(image_low, text_low, w_image, w_text)
+    feeding.got, squares.got, squares.kept, pair, image_grad, text_grad = settle(
+        feeding.got + early, squares.got, squares.kept, pair, image_grad, text_grad
+    )
+
     ending = Scatter(place, (pair,))
     ending.swap()
-    ready = after(image_low, squares.sent, squares.kept)
-    image_grad, text_grad = input_grads(ready, text_low, w_image, w_text)
-    squares.got, squares.kept, ending.got, ending.kept, image_grad, text_grad = settle(
-        squares.got, squares.kept, ending.got, ending.kept, image_grad, text_grad
-    )
-
     squares.second()
     squares.send_second()
+    feeding.fourth()
+    ending.got, ending.kept, squares.got, squares.kept, feeding.sent = settle(
+        ending.got, ending.kept, squares.got, squares.kept, feeding.sent
+    )
+
+    feeding.kept = feeding.sent
+    feeding.swap()
     ending.first()
     ending.send_first()
-    owned = owned_rows(SCATTER_CHUNKS[0], *feeding.sides())
-    squares.got, squares.kept, ending.got, ending.kept, owned = settle(
-        squares.got, squares.kept, ending.got, ending.kept, owned
-    )
-
     squares.third()
     squares.send_third()
+    ending.got, ending.kept, squares.got, squares.kept, feeding.got, image_grad, text_grad = settle(
+        ending.got, ending.kept, squares.got, squares.kept, feeding.got, image_grad, text_grad
+    )
+
     ending.second()
     ending.send_second()
-    squares.got, squares.kept, ending.got, ending.kept = settle(
-        squares.got, squares.kept, ending.got, ending.kept
-    )
+    squares.fourth()
+    squares.swap()
+    owned = owned_rows(SCATTER_CHUNKS[0], *feeding.sides())
+    ending.got, ending.kept, squares.got, owned = settle(ending.got, ending.kept, squares.got, owned)
 
     ending.third()
     ending.send_third()
-    squares.fourth()
-    squares.swap()
-    ending.got, ending.kept, squares.got = settle(ending.got, ending.kept, squares.got)
+    owned.update(owned_rows(SCATTER_CHUNKS[1], *squares.sides()))
+    ending.got, ending.kept, owned = settle(ending.got, ending.kept, owned)
 
     ending.fourth()
     ending.swap()
-    owned.update(owned_rows(SCATTER_CHUNKS[1], *squares.sides()))
     owned.update(owned_rows(SCATTER_CHUNKS[2], *ending.sides()))
     return (layer_out[None], image_grad[None], text_grad[None]) + tuple(owned[i] for i in range(20))
 

time: 377 us -> 339 us (0.90)
  Pallas kernels: 176 us -> 160 us
  local copies, waits for them, and re-layouts: 30.1 us -> 14.6 us
  waiting for transfers between devices: 76.3 us -> 69.1 us
    unnamed x99 -> x71, local copies, waits for them, and re-layouts: 27.1 us -> 11.2 us
    pallas_call x3 -> x1, Pallas kernels: 39.1 us -> 28.4 us  [attend_back(): pl.pallas_call(attend_back_kernel, grid=(HEADS // 2,), out_shape=(shape((...]
    ppermute x37 -> x40, waiting for transfers between devices: 71.8 us -> 63.1 us  [to_chip(): return lax.ppermute(values, BOTH, pairs)]
    pallas_call x3, Pallas kernels: 30.9 us -> 22.4 us  [attend(): pl.pallas_call(kernel, grid=(count,), out_shape=(shape((PADDED, WIDTH)),...]
    pallas_call x11 -> x13, Pallas kernels: 66 us -> 69.4 us  [call(): pl.pallas_call(kernel, out_shape=tuple(outs), in_specs=specs, out_specs=t...]
    convert_element_type x20 -> x18, other arithmetic: 20.3 us -> 18.6 us  [to_low(): return values.astype(jnp.bfloat16)]
    ppermute x37 -> x40, starting transfers between devices: 53.5 us -> 54.6 us  [to_chip(): return lax.ppermute(values, BOTH, pairs)]
  transfers between devices with their start and end apart: 52 -> 57, of which waited for: 16 -> 20; matrix products, arithmetic and copies ran while one was open for 5% -> 7% of each run, Pallas kernels for 36% -> 36%
where the time goes in v3:
time: 339 us; the launch traced here: 334 us
  Pallas kernels  160 us (47%)
  waiting for transfers between devices  69.1 us (20%)
  starting transfers between devices  57.6 us (17%)
  other arithmetic  29.4 us (9%)
  local copies, waits for them, and re-layouts  14.6 us (4%)
    pallas_call x13, Pallas kernels, call(): pl.pallas_call(kernel, out_shape=tuple(outs), in_specs=specs, out_specs=t...  69.4 us
    ppermute x40, waiting for transfers between devices, to_chip(): return lax.ppermute(values, BOTH, pairs)  63.1 us
    ppermute x40, starting transfers between devices, to_chip(): return lax.ppermute(values, BOTH, pairs)  54.6 us
    pallas_call x1, Pallas kernels, feed(): pl.pallas_call(feed_kernel, grid_spec=grid, out_shape=outs, compiler_para...  39.8 us
    pallas_call x1, Pallas kernels, attend_back(): pl.pallas_call(attend_back_kernel, grid=(HEADS // 2,), out_shape=(shape((...  28.4 us
    pallas_call x3, Pallas kernels, attend(): pl.pallas_call(kernel, grid=(count,), out_shape=(shape((PADDED, WIDTH)),...  22.4 us
    convert_element_type x18, other arithmetic, to_low(): return values.astype(jnp.bfloat16)  18.6 us
    unnamed x71, local copies, waits for them, and re-layouts  11.2 us
  transfers between devices with their start and end apart: 57, of which 20 were waited for; matrix products, arithmetic and copies ran while one was open for 7% of the time, Pallas kernels for 36%

profile of v3, /device:TPU:0, one launch (start us, length us, event | category | flops | bytes accessed | tf_op | source)
XLA Modules:
  0.0 333.8 jit_solution(13120219924651756805)
XLA Ops:
  2.5 1.7 shard_map.416
  4.2 3.0 collective-permute-start
  7.2 2.6 collective-permute-start.1
  9.8 1.6 shard_map.420
  11.4 1.6 shard_map.419
  13.0 1.7 shard_map.418
  14.7 1.6 shard_map.417
  17.0 1.6 collective-permute-start.3
  18.5 1.5 collective-permute-start.4
  20.0 2.4 collective-permute-start.5
  24.1 6.2 %collective-permute-done.5 = bf16[144,384]{1,0:T(8,128)(2,1)S(1)} collective-permute-done((bf16[144,384]{1,0:T(8,128)(2,1)}, bf16[144,384]{1,0:T(8,128)(2,1)S(1)}, u32[]{:S(2)}, u32[]{:S(2)}) %collective-permute-start.5) | collective-permute-done | bytes 110624 | tf_op jit(solution)/shard_map/chips_8_8/ppermute | solution.py:391
  31.0 2.6 collective-permute-start.10
  33.6 1.5 collective-permute-start.11
  35.2 7.4 %collective-permute-done.10 = bf16[144,384]{1,0:T(8,128)(2,1)S(1)} collective-permute-done((bf16[144,384]{1,0:T(8,128)(2,1)S(1)}, bf16[144,384]{1,0:T(8,128)(2,1)S(1)}, u32[]{:S(2)}, u32[]{:S(2)}) %collective-permute-start.10) | collective-permute-done | bytes 110624 | tf_op jit(solution)/shard_map/chips_8_8/ppermute | solution.py:391
  44.5 1.6 collective-permute-start.13
  46.6 1.6 collective-permute-start.14
  50.4 1.5 collective-permute-start.16
  51.9 5.7 %shard_map.421 = (bf16[4,2,2,48,768]{4,3,2,1,0:T(8,128)(2,1)}, bf16[4,2,2,48,768]{4,3,2,1,0:T(8,128)(2,1)}, f32[16,768]{1,0:T(8,128)}, f32[1,3072]{1,0:T(1,128)}...) custom-call(s32[4]{0:T(128)} %pad_add_fusion.at_ref.at, bf16[325,768]{1,0:T(8,128)(2,1)} %bitcast.207, ...), custom_call_target="tpu_custom_call" | custom-call | flops 1650000000 | bytes 1024 | tf_op jit(solution)/shard_map/pallas_call | solution.py:361
  57.7 1.6 collective-permute-start.18
  59.3 1.6 collective-permute-start.20
  62.2 1.5 collective-permute-start.22
  63.9 4.4 %collective-permute-done.20 = bf16[192,384]{1,0:T(8,128)(2,1)S(1)} collective-permute-done((bf16[192,384]{1,0:T(8,128)(2,1)S(1)}, bf16[192,384]{1,0:T(8,128)(2,1)S(1)}, u32[]{:S(2)}, u32[]{:S(2)}) %collective-permute-start.20) | collective-permute-done | bytes 147488 | tf_op jit(solution)/shard_map/chips_4_4/ppermute | solution.py:391
  68.3 6.6 %collective-permute-done.21 = bf16[192,384]{1,0:T(8,128)(2,1)S(1)} collective-permute-done((bf16[192,384]{1,0:T(8,128)(2,1)S(1)}, bf16[192,384]{1,0:T(8,128)(2,1)S(1)}, u32[]{:S(2)}, u32[]{:S(2)}) %collective-permute-start.21) | collective-permute-done | bytes 147488 | tf_op jit(solution)/shard_map/chips_8_8/ppermute | solution.py:391
  81.1 7.2 %shard_map.422 = (bf16[4,2,2,48,768]{4,3,2,1,0:T(8,128)(2,1)}, bf16[4,2,2,48,768]{4,3,2,1,0:T(8,128)(2,1)}, bf16[4,2,2,48,768]{4,3,2,1,0:T(8,128)(2,1)}, bf16[89...) custom-call(s32[4]{0:T(128)} %pad_add_fusion.at_ref.at, ...), custom_call_target="tpu_custom_call" | custom-call | flops 2100000000 | bytes 1024 | tf_op jit(solution)/shard_map/pallas_call | solution.py:361
  88.3 7.5 %shard_map.423 = (bf16[896,768]{1,0:T(8,128)(2,1)}, f32[6,8,896]{2,1,0:T(8,128)}) custom-call(s32[2]{0:T(128)} %pad_add_fusion.1.live, bf16[896,768]{1,0:T(8,128)(2,1)} %get-tuple-element.254.q, bf16[896,768]{1,0:T(8,128)(2,1)} %get-tuple-element.247.k, bf16[896,768]{1,0:T(8,128)(2,1)} %get-tuple-element.248.v), custom_call_target="tpu_custom_call" | custom-call | flops 1800000000 | bytes 1024 | tf_op jit(solution)/shard_map/pallas_call | solution.py:612
  98.3 7.4 %shard_map.424 = (bf16[896,768]{1,0:T(8,128)(2,1)}, f32[6,8,896]{2,1,0:T(8,128)}) custom-call(s32[2]{0:T(128)} %pad_add_fusion.1.live, bf16[896,768]{1,0:T(8,128)(2,1)} %get-tuple-element.254.q, bf16[896,768]{1,0:T(8,128)(2,1)} %get-tuple-element.247.k, bf16[896,768]{1,0:T(8,128)(2,1)} %get-tuple-element.248.v, ...), custom_call_target="tpu_custom_call", output_to_operand_aliasing={{0}: (4, {}), {1}: (5, {})} | custom-call | flops 1800000000 | bytes 1024 | tf_op jit(solution)/shard_map/pallas_call | solution.py:612
  105.8 7.5 %shard_map.425 = (bf16[896,768]{1,0:T(8,128)(2,1)}, f32[6,8,896]{2,1,0:T(8,128)}) custom-call(s32[2]{0:T(128)} %pad_add_fusion.1.live, bf16[896,768]{1,0:T(8,128)(2,1)} %get-tuple-element.254.q, bf16[896,768]{1,0:T(8,128)(2,1)} %get-tuple-element.247.k, bf16[896,768]{1,0:T(8,128)(2,1)} %get-tuple-element.248.v, ...), custom_call_target="tpu_custom_call", output_to_operand_aliasing={{0}: (4, {}), {1}: (5, {})} | custom-call | flops 1800000000 | bytes 1024 | tf_op jit(solution)/shard_map/pallas_call | solution.py:612
  115.4 1.3 collective-permute-start.31
  117.2 2.8 collective-permute-done.33.rp_hi
  120.8 8.4 %shard_map.426 = (bf16[4,2,2,48,768]{4,3,2,1,0:T(8,128)(2,1)}, bf16[4,2,2,48,3072]{4,3,2,1,0:T(8,128)(2,1)}, f32[839,768]{1,0:T(8,128)}, bf16[839,768]{1,0:T(8,128)(2,1)}) custom-call(s32[4]{0:T(128)} %pad_add_fusion.at_ref.at, bf16[896,768]{1,0:T(8,128)(2,1)} %get-tuple-element.262.attended, f32[839,768]{1,0:T(8,128)} %get-tuple-element.263.embedded, ...), custom_call_target="tpu_custom_call" | custom-call | flops 2400000000 | bytes 1024 | tf_op jit(solution)/shard_map/pallas_call | solution.py:361
  129.3 2.3 collective-permute-done.31.r8
  131.6 2.8 collective-permute-done.34.r8p
  135.5 39.8 %shard_map.427 = (bf16[839,768]{1,0:T(8,128)(2,1)}, f32[839,768]{1,0:T(8,128)}, bf16[16,192,384]{2,1,0:T(8,128)(2,1)}, bf16[16,192,384]{2,1,0:T(8,128)(2,1)}, bf...) custom-call(s32[4]{0:T(128)} %pad_add_fusion.at_ref.at, ...), custom_call_target="tpu_custom_call" | custom-call | flops 12000000000 | bytes 1024 | tf_op jit(solution)/shard_map/pallas_call | solution.py:832
  175.9 8.0 %shard_map.428 = (f32[839,768]{1,0:T(8,128)}, bf16[839,768]{1,0:T(8,128)(2,1)}, bf16[896,768]{1,0:T(8,128)(2,1)}, f32[8,768]{1,0:T(8,128)}) custom-call(f32[839,768]{1,0:T(8,128)} %get-tuple-element.270.middle, f32[839,768]{1,0:T(8,128)} %get-tuple-element.280.second_grad, bf16[839,768]{1,0:T(8,128)(2,1)} %bitcast.204, f32[16,768]{1,0:T(8,128)} %get-tuple-element.242.vec, ...), custom_call_target="tpu_custom_call" | custom-call | flops 2400000000 | bytes 1024 | tf_op jit(solution)/shard_map/pallas_call | solution.py:361
  183.9 2.6 add_convert_fusion.13
  186.5 1.7 maximum_maximum_fusion
  189.5 2.6 add_convert_fusion.9
  192.3 28.4 %shard_map.429 = (bf16[896,768]{1,0:T(8,128)(2,1)}, bf16[896,768]{1,0:T(8,128)(2,1)}, bf16[896,768]{1,0:T(8,128)(2,1)}) custom-call(s32[2]{0:T(128)} %pad_add_fusion.1.live, bf16[896,768]{1,0:T(8,128)(2,1)} %get-tuple-element.254.q, bf16[896,768]{1,0:T(8,128)(2,1)} %get-tuple-element.247.k, bf16[896,768]{1,0:T(8,128)(2,1)} %get-tuple-element.248.v, ...), custom_call_target="tpu_custom_call" | custom-call | flops 8400000000 | bytes 1024 | tf_op jit(solution)/shard_map/pallas_call | solution.py:660
  220.8 2.6 fusion.1
  224.1 1.6 fusion.2
  225.6 11.2 %shard_map.430 = (bf16[16,192,384]{2,1,0:T(8,128)(2,1)}, bf16[16,192,384]{2,1,0:T(8,128)(2,1)}) custom-call(s32[4]{0:T(128)} %pad_add_fusion.at_ref.at, bf16[896,768]{1,0:T(8,128)(2,1)} %get-tuple-element.262.attended, bf16[839,768]{1,0:T(8,128)(2,1)} %get-tuple-element.301.branch, bf16[839,768]{1,0:T(8,128)(2,1)} %get-tuple-element.241.normed, ...), custom_call_target="tpu_custom_call" | custom-call | flops 3300000000 | bytes 1024 | tf_op jit(solution)/shard_map/pallas_call | solution.py:361
  236.8 3.1 collective-permute-done.38
  239.9 1.6 add_convert_fusion
  242.3 3.0 collective-permute-start.39
  245.3 2.4 collective-permute-start.40
  247.6 10.9 %shard_map.431 = (bf16[325,768]{1,0:T(8,128)(2,1)}, bf16[513,768]{1,0:T(8,128)(2,1)}, f32[8,768]{1,0:T(8,128)}) custom-call(bf16[896,768]{1,0:T(8,128)(2,1)} %get-tuple-element.311.dq, bf16[896,768]{1,0:T(8,128)(2,1)} %get-tuple-element.312.dk, bf16[896,768]{1,0:T(8,128)(2,1)} %get-tuple-element.313.dv, bf16[4,2,2,48,768]{4,3,2,1,0:T(8,128)(2,1)} %get-tuple-element.314.wq, ...), custom_call_target="tpu_custom_call" | custom-call | flops 3300000000 | bytes 1024 | tf_op jit(solution)/shard_map/pallas_call | solution.py:361
  258.6 2.8 collective-permute-done.40
  261.4 1.7 add_convert_fusion.7
  264.0 1.5 add_convert_fusion.5
  265.9 4.4 %shard_map.433 = (f32[325,768]{1,0:T(8,128)}, f32[513,768]{1,0:T(8,128)}) custom-call(bf16[325,768]{1,0:T(8,128)(2,1)} %get-tuple-element.327.image_low, bf16[513,768]{1,0:T(8,128)(2,1)} %get-tuple-element.328.text_low, bf16[4,2,2,48,768]{4,3,2,1,0:T(8,128)(2,1)} %get-tuple-element.335.w_image, bf16[4,2,2,48,768]{4,3,2,1,0:T(8,128)(2,1)} %get-tuple-element.336.w_text), custom_call_target="tpu_custom_call" | custom-call | flops 1320000000 | bytes 1024 | tf_op jit(solution)/shard_map/pallas_call | solution.py:361
  270.3 5.3 %shard_map.432 = (bf16[16,112,384]{2,1,0:T(8,128)(2,1)}, bf16[16,112,384]{2,1,0:T(8,128)(2,1)}) custom-call(s32[4]{0:T(128)} %pad_add_fusion.at_ref.at, bf16[325,768]{1,0:T(8,128)(2,1)} %bitcast.208, bf16[513,768]{1,0:T(8,128)(2,1)} %bitcast.206, bf16[325,768]{1,0:T(8,128)(2,1)} %get-tuple-element.327.image_low, ...), custom_call_target="tpu_custom_call" | custom-call | flops 1650000000 | bytes 1024 | tf_op jit(solution)/shard_map/pallas_call | solution.py:361
  275.7 3.0 collective-permute-done.42
  283.9 6.8 %collective-permute-done.45 = bf16[4,192,384]{2,1,0:T(8,128)(2,1)S(1)} collective-permute-done((bf16[4,192,384]{2,1,0:T(8,128)(2,1)S(1)}, bf16[4,192,384]{2,1,0:T(8,128)(2,1)S(1)}, u32[]{:S(2)}, u32[]{:S(2)}) %collective-permute-start.45) | collective-permute-done | bytes 589856 | tf_op jit(solution)/shard_map/chips_1_2/ppermute | solution.py:391
  292.1 2.8 collective-permute-start.48
  295.0 1.5 collective-permute-start.49
  296.8 4.4 %collective-permute-done.47 = bf16[192,384]{1,0:T(8,128)(2,1)S(1)} collective-permute-done((bf16[192,384]{1,0:T(8,128)(2,1)S(1)}, bf16[192,384]{1,0:T(8,128)(2,1)S(1)}, u32[]{:S(2)}, u32[]{:S(2)}) %collective-permute-start.47) | collective-permute-done | bytes 147488 | tf_op jit(solution)/shard_map/chips_4_4/ppermute | solution.py:391
  301.2 5.0 %collective-permute-done.48 = bf16[192,384]{1,0:T(8,128)(2,1)S(1)} collective-permute-done((bf16[192,384]{1,0:T(8,128)(2,1)S(1)}, bf16[192,384]{1,0:T(8,128)(2,1)S(1)}, u32[]{:S(2)}, u32[]{:S(2)}) %collective-permute-start.48) | collective-permute-done | bytes 147488 | tf_op jit(solution)/shard_map/chips_8_8/ppermute | solution.py:391
  306.4 1.6 collective-permute-start.51
  309.5 4.2 %collective-permute-done.51 = bf16[4,112,384]{2,1,0:T(8,128)(2,1)S(1)} collective-permute-done((bf16[4,112,384]{2,1,0:T(8,128)(2,1)S(1)}, bf16[4,112,384]{2,1,0:T(8,128)(2,1)S(1)}, u32[]{:S(2)}, u32[]{:S(2)}) %collective-permute-start.51) | collective-permute-done | bytes 344096 | tf_op jit(solution)/shard_map/chips_1_2/ppermute | solution.py:391
  314.0 3.4 %collective-permute-start.53 = (bf16[112,384]{1,0:T(8,128)(2,1)S(1)}, bf16[112,384]{1,0:T(8,128)(2,1)S(1)}, u32[]{:S(2)}, u32[]{:S(2)}) collective-permute-start(bf16[112,384]{1,0:T(8,128)(2,1)S(1)} %get-tuple-element.431), channel_id=1, source_target_pairs={{0,8},{1,9},{2,10},{3,11},{4,12},{5,13},{6,14},{7,15},{8,0},{9,1},... | collective-permute-start | bytes 258056 | tf_op jit(solution)/shard_map/chips_4_4/ppermute | solution.py:391
  318.3 1.5 collective-permute-start.55
  322.5 3.4 %collective-permute-done.54 = bf16[112,384]{1,0:T(8,128)(2,1)S(1)} collective-permute-done((bf16[112,384]{1,0:T(8,128)(2,1)S(1)}, bf16[112,384]{1,0:T(8,128)(2,1)S(1)}, u32[]{:S(2)}, u32[]{:S(2)}) %collective-permute-start.54) | collective-permute-done | bytes 86048 | tf_op jit(solution)/shard_map/chips_8_8/ppermute | solution.py:391
  326.1 2.8 copy.75
  328.9 2.0 copy.74
  (198 shorter events, 42.9 us)
Async XLA Ops:
  4.2 12.2 %collective-permute-start = (bf16[112,384]{1,0:T(8,128)(2,1)}, bf16[112,384]{1,0:T(8,128)(2,1)S(1)}, u32[]{:S(2)}, u32[]{:S(2)}) collective-permute-start(bf16[112,384]{1,0:T(8,128)(2,1)} %shard_map.416), channel_id=1, source_target_pairs={{0,8},{1,9},{2,10},{3,11},{4,12},{5,13},{6,14},{7,15},{8,0},{9,1},... | collective-permute-start | bytes 258056 | tf_op jit(solution)/shard_map/chips_4_4/ppermute | solution.py:391
  7.2 9.7 %collective-permute-start.1 = (bf16[112,384]{1,0:T(8,128)(2,1)}, bf16[112,384]{1,0:T(8,128)(2,1)S(1)}, u32[]{:S(2)}, u32[]{:S(2)}) collective-permute-start(bf16[112,384]{1,0:T(8,128)(2,1)} %shard_map.416), channel_id=1, source_target_pairs={{0,16},{1,17},{2,18},{3,19},{4,20},{5,21},{6,22},{7,23},{8,24},{9,... | collective-permute-start | bytes 258056 | tf_op jit(solution)/shard_map/chips_8_8/ppermute | solution.py:391
  9.8 7.1 %collective-permute-start.2 = (bf16[112,384]{1,0:T(8,128)(2,1)}, bf16[112,384]{1,0:T(8,128)(2,1)S(1)}, u32[]{:S(2)}, u32[]{:S(2)}) collective-permute-start(bf16[112,384]{1,0:T(8,128)(2,1)} %shard_map.416), channel_id=1, source_target_pairs={{0,24},{1,25},{2,26},{3,27},{4,28},{5,29},{6,30},{7,31},{8,16},{9,... | collective-permute-start | bytes 258056 | tf_op jit(solution)/shard_map/chips_12_12/ppermute | solution.py:391
  16.4 14.6 %copy-start.19 = (bf16[144,384]{1,0:T(8,128)(2,1)S(1)}, bf16[144,384]{1,0:T(8,128)(2,1)}, u32[]{:S(2)}) copy-start(bf16[144,384]{1,0:T(8,128)(2,1)} %shard_map.418) | copy-start | bytes 331780
  16.4 18.7 %copy-start.18 = (bf16[144,384]{1,0:T(8,128)(2,1)S(1)}, bf16[144,384]{1,0:T(8,128)(2,1)}, u32[]{:S(2)}) copy-start(bf16[144,384]{1,0:T(8,128)(2,1)} %shard_map.417) | copy-start | bytes 331780
  17.0 13.3 %collective-permute-start.3 = (bf16[4,112,384]{2,1,0:T(8,128)(2,1)S(1)}, bf16[4,112,384]{2,1,0:T(8,128)(2,1)S(1)}, u32[]{:S(2)}, u32[]{:S(2)}) collective-permute-start(bf16[4,112,384]{2,1,0:T(8,128)(2,1)S(1)} %pad_maximum_fusion.13), channel_id=1, source_target_pairs={{0,2},{1,5},{2,0},{3,7},{4,6},{5,1},{6,4},{7,3},{8,10},{9,13},{10,... | collective-permute-start | bytes 1032200 | tf_op jit(solution)/shard_map/chips_1_2/ppermute | solution.py:391
  18.5 5.6 %collective-permute-start.4 = (bf16[144,384]{1,0:T(8,128)(2,1)}, bf16[144,384]{1,0:T(8,128)(2,1)S(1)}, u32[]{:S(2)}, u32[]{:S(2)}) collective-permute-start(bf16[144,384]{1,0:T(8,128)(2,1)} %shard_map.417), channel_id=1, source_target_pairs={{0,8},{1,9},{2,10},{3,11},{4,12},{5,13},{6,14},{7,15},{8,0},{9,1},... | collective-permute-start | bytes 331784 | tf_op jit(solution)/shard_map/chips_4_4/ppermute | solution.py:391
  20.0 10.3 %collective-permute-start.5 = (bf16[144,384]{1,0:T(8,128)(2,1)}, bf16[144,384]{1,0:T(8,128)(2,1)S(1)}, u32[]{:S(2)}, u32[]{:S(2)}) collective-permute-start(bf16[144,384]{1,0:T(8,128)(2,1)} %shard_map.417), channel_id=1, source_target_pairs={{0,16},{1,17},{2,18},{3,19},{4,20},{5,21},{6,22},{7,23},{8,24},{9,... | collective-permute-start | bytes 331784 | tf_op jit(solution)/shard_map/chips_8_8/ppermute | solution.py:391
  22.4 7.9 %collective-permute-start.6 = (bf16[144,384]{1,0:T(8,128)(2,1)}, bf16[144,384]{1,0:T(8,128)(2,1)S(1)}, u32[]{:S(2)}, u32[]{:S(2)}) collective-permute-start(bf16[144,384]{1,0:T(8,128)(2,1)} %shard_map.417), channel_id=1, source_target_pairs={{0,24},{1,25},{2,26},{3,27},{4,28},{5,29},{6,30},{7,31},{8,16},{9,... | collective-permute-start | bytes 331784 | tf_op jit(solution)/shard_map/chips_12_12/ppermute | solution.py:391
  30.4 21.5 %copy-start.11 = (bf16[2,4,112,384]{3,2,1,0:T(8,128)(2,1)}, bf16[2,4,112,384]{3,2,1,0:T(8,128)(2,1)S(1)}, u32[]{:S(2)}) copy-start(bf16[2,4,112,384]{3,2,1,0:T(8,128)(2,1)S(1)} %pad_maximum_fusion.5.s8) | copy-start | bytes 2064388
  30.4 16.1 %copy-start.21 = (bf16[96,384]{1,0:T(8,128)(2,1)S(1)}, bf16[96,384]{1,0:T(8,128)(2,1)}, u32[]{:S(2)}) copy-start(bf16[96,384]{1,0:T(8,128)(2,1)} %shard_map.419) | copy-start | bytes 221188
  30.4 13.1 %collective-permute-start.7 = (bf16[2,4,112,384]{3,2,1,0:T(8,128)(2,1)S(1)}, bf16[2,4,112,384]{3,2,1,0:T(8,128)(2,1)S(1)}, u32[]{:S(2)}, u32[]{:S(2)}) collective-permute-start(bf16[2,4,112,384]{3,2,1,0:T(8,128)(2,1)S(1)} %pad_maximum_fusion.5.s8), channel_id=1, source_target_pairs={{0,4},{1,3},{2,6},{3,1},{4,0},{5,7},{6,2},{7,5},{8,12},{9,11},{10,... | collective-permute-start | bytes 2064392 | tf_op jit(solution)/shard_map/chips_2_1/ppermute | solution.py:391
  31.0 12.5 %collective-permute-start.8 = (bf16[2,4,112,384]{3,2,1,0:T(8,128)(2,1)S(1)}, bf16[2,4,112,384]{3,2,1,0:T(8,128)(2,1)S(1)}, u32[]{:S(2)}, u32[]{:S(2)}) collective-permute-start(bf16[2,4,112,384]{3,2,1,0:T(8,128)(2,1)S(1)} %pad_maximum_fusion.5.s8), channel_id=1, source_target_pairs={{0,1},{1,0},{2,3},{3,2},{4,5},{5,4},{6,7},{7,6},{8,9},{9,8},{10,11... | collective-permute-start | bytes 2064392 | tf_op jit(solution)/shard_map/between_cores/ppermute | solution.py:382
  31.0 11.5 %collective-permute-start.10 = (bf16[144,384]{1,0:T(8,128)(2,1)S(1)}, bf16[144,384]{1,0:T(8,128)(2,1)S(1)}, u32[]{:S(2)}, u32[]{:S(2)}) collective-permute-start(bf16[144,384]{1,0:T(8,128)(2,1)S(1)} %copy-done.19), channel_id=1, source_target_pairs={{0,16},{1,17},{2,18},{3,19},{4,20},{5,21},{6,22},{7,23},{8,24},{9,... | collective-permute-start | bytes 331784 | tf_op jit(solution)/shard_map/chips_8_8/ppermute | solution.py:391
  33.6 8.9 %collective-permute-start.11 = (bf16[144,384]{1,0:T(8,128)(2,1)S(1)}, bf16[144,384]{1,0:T(8,128)(2,1)S(1)}, u32[]{:S(2)}, u32[]{:S(2)}) collective-permute-start(bf16[144,384]{1,0:T(8,128)(2,1)S(1)} %copy-done.19), channel_id=1, source_target_pairs={{0,24},{1,25},{2,26},{3,27},{4,28},{5,29},{6,30},{7,31},{8,16},{9,... | collective-permute-start | bytes 331784 | tf_op jit(solution)/shard_map/chips_12_12/ppermute | solution.py:391
  35.1 8.4 %collective-permute-start.9 = (bf16[144,384]{1,0:T(8,128)(2,1)S(1)}, bf16[144,384]{1,0:T(8,128)(2,1)S(1)}, u32[]{:S(2)}, u32[]{:S(2)}) collective-permute-start(bf16[144,384]{1,0:T(8,128)(2,1)S(1)} %copy-done.19), channel_id=1, source_target_pairs={{0,8},{1,9},{2,10},{3,11},{4,12},{5,13},{6,14},{7,15},{8,0},{9,1},... | collective-permute-start | bytes 331784 | tf_op jit(solution)/shard_map/chips_4_4/ppermute | solution.py:391
  43.5 6.0 %collective-permute-start.17 = (bf16[2,4,112,384]{3,2,1,0:T(8,128)(2,1)S(1)}, bf16[2,4,112,384]{3,2,1,0:T(8,128)(2,1)S(1)}, u32[]{:S(2)}, u32[]{:S(2)}) collective-permute-start(bf16[2,4,112,384]{3,2,1,0:T(8,128)(2,1)S(1)} %collective-permute-done.7.r8), channel_id=1, source_target_pairs={{0,1},{1,0},{2,3},{3,2},{4,5},{5,4},{6,7},{7,6},{8,9},{9,8},{10,11... | collective-permute-start | bytes 2064392 | tf_op jit(solution)/shard_map/between_cores/ppermute | solution.py:382
  44.5 13.1 %collective-permute-start.13 = (bf16[4,144,384]{2,1,0:T(8,128)(2,1)S(1)}, bf16[4,144,384]{2,1,0:T(8,128)(2,1)S(1)}, u32[]{:S(2)}, u32[]{:S(2)}) collective-permute-start(bf16[4,144,384]{2,1,0:T(8,128)(2,1)S(1)} %get-tuple-element.427), channel_id=1, source_target_pairs={{0,2},{1,5},{2,0},{3,7},{4,6},{5,1},{6,4},{7,3},{8,10},{9,13},{10,... | collective-permute-start | bytes 1327112 | tf_op jit(solution)/shard_map/chips_1_2/ppermute | solution.py:391
  46.0 11.6 %collective-permute-start.12 = (bf16[4,144,384]{2,1,0:T(8,128)(2,1)S(1)}, bf16[4,144,384]{2,1,0:T(8,128)(2,1)S(1)}, u32[]{:S(2)}, u32[]{:S(2)}) collective-permute-start(bf16[4,144,384]{2,1,0:T(8,128)(2,1)S(1)} %pad_maximum_fusion.11), channel_id=1, source_target_pairs={{0,2},{1,5},{2,0},{3,7},{4,6},{5,1},{6,4},{7,3},{8,10},{9,13},{10,... | collective-permute-start | bytes 1327112 | tf_op jit(solution)/shard_map/chips_1_2/ppermute | solution.py:391
  46.6 11.0 %collective-permute-start.14 = (bf16[96,384]{1,0:T(8,128)(2,1)S(1)}, bf16[96,384]{1,0:T(8,128)(2,1)S(1)}, u32[]{:S(2)}, u32[]{:S(2)}) collective-permute-start(bf16[96,384]{1,0:T(8,128)(2,1)S(1)} %copy-done.21), channel_id=1, source_target_pairs={{0,8},{1,9},{2,10},{3,11},{4,12},{5,13},{6,14},{7,15},{8,0},{9,1},... | collective-permute-start | bytes 221192 | tf_op jit(solution)/shard_map/chips_4_4/ppermute | solution.py:391
  48.2 9.4 %collective-permute-start.15 = (bf16[96,384]{1,0:T(8,128)(2,1)S(1)}, bf16[96,384]{1,0:T(8,128)(2,1)S(1)}, u32[]{:S(2)}, u32[]{:S(2)}) collective-permute-start(bf16[96,384]{1,0:T(8,128)(2,1)S(1)} %copy-done.21), channel_id=1, source_target_pairs={{0,16},{1,17},{2,18},{3,19},{4,20},{5,21},{6,22},{7,23},{8,24},{9,... | collective-permute-start | bytes 221192 | tf_op jit(solution)/shard_map/chips_8_8/ppermute | solution.py:391
  50.4 7.2 %collective-permute-start.16 = (bf16[96,384]{1,0:T(8,128)(2,1)S(1)}, bf16[96,384]{1,0:T(8,128)(2,1)S(1)}, u32[]{:S(2)}, u32[]{:S(2)}) collective-permute-start(bf16[96,384]{1,0:T(8,128)(2,1)S(1)} %copy-done.21), channel_id=1, source_target_pairs={{0,24},{1,25},{2,26},{3,27},{4,28},{5,29},{6,30},{7,31},{8,16},{9,... | collective-permute-start | bytes 221192 | tf_op jit(solution)/shard_map/chips_12_12/ppermute | solution.py:391
  57.7 21.8 %copy-start.10 = (bf16[2,4,144,384]{3,2,1,0:T(8,128)(2,1)}, bf16[2,4,144,384]{3,2,1,0:T(8,128)(2,1)S(1)}, u32[]{:S(2)}) copy-start(bf16[2,4,144,384]{3,2,1,0:T(8,128)(2,1)S(1)} %pad_maximum_fusion.3.s8) | copy-start | bytes 2654212
  57.7 17.1 %collective-permute-start.18 = (bf16[2,4,144,384]{3,2,1,0:T(8,128)(2,1)S(1)}, bf16[2,4,144,384]{3,2,1,0:T(8,128)(2,1)S(1)}, u32[]{:S(2)}, u32[]{:S(2)}) collective-permute-start(bf16[2,4,144,384]{3,2,1,0:T(8,128)(2,1)S(1)} %pad_maximum_fusion.3.s8), channel_id=1, source_target_pairs={{0,4},{1,3},{2,6},{3,1},{4,0},{5,7},{6,2},{7,5},{8,12},{9,11},{10,... | collective-permute-start | bytes 2654216 | tf_op jit(solution)/shard_map/chips_2_1/ppermute | solution.py:391
  59.3 15.5 %collective-permute-start.19 = (bf16[2,4,144,384]{3,2,1,0:T(8,128)(2,1)S(1)}, bf16[2,4,144,384]{3,2,1,0:T(8,128)(2,1)S(1)}, u32[]{:S(2)}, u32[]{:S(2)}) collective-permute-start(bf16[2,4,144,384]{3,2,1,0:T(8,128)(2,1)S(1)} %pad_maximum_fusion.3.s8), channel_id=1, source_target_pairs={{0,1},{1,0},{2,3},{3,2},{4,5},{5,4},{6,7},{7,6},{8,9},{9,8},{10,11... | collective-permute-start | bytes 2654216 | tf_op jit(solution)/shard_map/between_cores/ppermute | solution.py:382
  59.3 8.9 %collective-permute-start.20 = (bf16[192,384]{1,0:T(8,128)(2,1)S(1)}, bf16[192,384]{1,0:T(8,128)(2,1)S(1)}, u32[]{:S(2)}, u32[]{:S(2)}) collective-permute-start(bf16[192,384]{1,0:T(8,128)(2,1)S(1)} %copy-done.17), channel_id=1, source_target_pairs={{0,8},{1,9},{2,10},{3,11},{4,12},{5,13},{6,14},{7,15},{8,0},{9,1},... | collective-permute-start | bytes 442376 | tf_op jit(solution)/shard_map/chips_4_4/ppermute | solution.py:391
  60.9 13.9 %collective-permute-start.21 = (bf16[192,384]{1,0:T(8,128)(2,1)S(1)}, bf16[192,384]{1,0:T(8,128)(2,1)S(1)}, u32[]{:S(2)}, u32[]{:S(2)}) collective-permute-start(bf16[192,384]{1,0:T(8,128)(2,1)S(1)} %copy-done.17), channel_id=1, source_target_pairs={{0,16},{1,17},{2,18},{3,19},{4,20},{5,21},{6,22},{7,23},{8,24},{9,... | collective-permute-start | bytes 442376 | tf_op jit(solution)/shard_map/chips_8_8/ppermute | solution.py:391
  62.2 12.6 %collective-permute-start.22 = (bf16[192,384]{1,0:T(8,128)(2,1)S(1)}, bf16[192,384]{1,0:T(8,128)(2,1)S(1)}, u32[]{:S(2)}, u32[]{:S(2)}) collective-permute-start(bf16[192,384]{1,0:T(8,128)(2,1)S(1)} %copy-done.17), channel_id=1, source_target_pairs={{0,24},{1,25},{2,26},{3,27},{4,28},{5,29},{6,30},{7,31},{8,16},{9,... | collective-permute-start | bytes 442376 | tf_op jit(solution)/shard_map/chips_12_12/ppermute | solution.py:391
  63.9 24.4 %copy-start = (bf16[2,4,144,384]{3,2,1,0:T(8,128)(2,1)}, bf16[2,4,144,384]{3,2,1,0:T(8,128)(2,1)S(1)}, u32[]{:S(2)}) copy-start(bf16[2,4,144,384]{3,2,1,0:T(8,128)(2,1)S(1)} %pad_maximum_fusion.4.s8) | copy-start | bytes 2654212
  75.8 4.3 %collective-permute-start.26 = (bf16[2,4,144,384]{3,2,1,0:T(8,128)(2,1)S(1)}, bf16[2,4,144,384]{3,2,1,0:T(8,128)(2,1)S(1)}, u32[]{:S(2)}, u32[]{:S(2)}) collective-permute-start(bf16[2,4,144,384]{3,2,1,0:T(8,128)(2,1)S(1)} %collective-permute-done.18.r8), channel_id=1, source_target_pairs={{0,1},{1,0},{2,3},{3,2},{4,5},{5,4},{6,7},{7,6},{8,9},{9,8},{10,11... | collective-permute-start | bytes 2654216 | tf_op jit(solution)/shard_map/between_cores/ppermute | solution.py:382
  75.8 20.0 %collective-permute-start.23 = (bf16[2,4,144,384]{3,2,1,0:T(8,128)(2,1)S(1)}, bf16[2,4,144,384]{3,2,1,0:T(8,128)(2,1)S(1)}, u32[]{:S(2)}, u32[]{:S(2)}) collective-permute-start(bf16[2,4,144,384]{3,2,1,0:T(8,128)(2,1)S(1)} %pad_maximum_fusion.4.s8), channel_id=1, source_target_pairs={{0,4},{1,3},{2,6},{3,1},{4,0},{5,7},{6,2},{7,5},{8,12},{9,11},{10,... | collective-permute-start | bytes 2654216 | tf_op jit(solution)/shard_map/chips_2_1/ppermute | solution.py:391
  76.3 19.5 %collective-permute-start.25 = (bf16[2,4,144,384]{3,2,1,0:T(8,128)(2,1)S(1)}, bf16[2,4,144,384]{3,2,1,0:T(8,128)(2,1)S(1)}, u32[]{:S(2)}, u32[]{:S(2)}) collective-permute-start(bf16[2,4,144,384]{3,2,1,0:T(8,128)(2,1)S(1)} %pad_maximum_fusion.4.s8), channel_id=1, source_target_pairs={{0,1},{1,0},{2,3},{3,2},{4,5},{5,4},{6,7},{7,6},{8,9},{9,8},{10,11... | collective-permute-start | bytes 2654216 | tf_op jit(solution)/shard_map/between_cores/ppermute | solution.py:382
  79.5 16.3 %collective-permute-start.24 = (bf16[4,96,384]{2,1,0:T(8,128)(2,1)S(1)}, bf16[4,96,384]{2,1,0:T(8,128)(2,1)S(1)}, u32[]{:S(2)}, u32[]{:S(2)}) collective-permute-start(bf16[4,96,384]{2,1,0:T(8,128)(2,1)S(1)} %pad_maximum_fusion.14), channel_id=1, source_target_pairs={{0,2},{1,5},{2,0},{3,7},{4,6},{5,1},{6,4},{7,3},{8,10},{9,13},{10,... | collective-permute-start | bytes 884744 | tf_op jit(solution)/shard_map/chips_1_2/ppermute | solution.py:391
  95.8 17.5 %collective-permute-start.30 = (bf16[2,4,144,384]{3,2,1,0:T(8,128)(2,1)S(1)}, bf16[2,4,144,384]{3,2,1,0:T(8,128)(2,1)}, u32[]{:S(2)}, u32[]{:S(2)}) collective-permute-start(bf16[2,4,144,384]{3,2,1,0:T(8,128)(2,1)S(1)} %collective-permute-done.23.r8), channel_id=1, source_target_pairs={{0,1},{1,0},{2,3},{3,2},{4,5},{5,4},{6,7},{7,6},{8,9},{9,8},{10,11... | collective-permute-start | bytes 2654216 | tf_op jit(solution)/shard_map/between_cores/ppermute | solution.py:382
  96.0 17.3 %collective-permute-start.27 = (bf16[2,4,96,384]{3,2,1,0:T(8,128)(2,1)S(1)}, bf16[2,4,96,384]{3,2,1,0:T(8,128)(2,1)S(1)}, u32[]{:S(2)}, u32[]{:S(2)}) collective-permute-start(bf16[2,4,96,384]{3,2,1,0:T(8,128)(2,1)S(1)} %pad_maximum_fusion.9.s_hi), channel_id=1, source_target_pairs={{0,4},{1,3},{2,6},{3,1},{4,0},{5,7},{6,2},{7,5},{8,12},{9,11},{10,... | collective-permute-start | bytes 1769480 | tf_op jit(solution)/shard_map/chips_2_1/ppermute | solution.py:391
  97.3 16.0 %collective-permute-start.29 = (bf16[2,4,96,384]{3,2,1,0:T(8,128)(2,1)S(1)}, bf16[2,4,96,384]{3,2,1,0:T(8,128)(2,1)}, u32[]{:S(2)}, u32[]{:S(2)}) collective-permute-start(bf16[2,4,96,384]{3,2,1,0:T(8,128)(2,1)S(1)} %pad_maximum_fusion.9.s_hi), channel_id=1, source_target_pairs={{0,1},{1,0},{2,3},{3,2},{4,5},{5,4},{6,7},{7,6},{8,9},{9,8},{10,11... | collective-permute-start | bytes 1769480 | tf_op jit(solution)/shard_map/between_cores/ppermute | solution.py:382
  97.8 15.5 %collective-permute-start.28 = (bf16[4,192,384]{2,1,0:T(8,128)(2,1)S(1)}, bf16[4,192,384]{2,1,0:T(8,128)(2,1)}, u32[]{:S(2)}, u32[]{:S(2)}) collective-permute-start(bf16[4,192,384]{2,1,0:T(8,128)(2,1)S(1)} %pad_maximum_fusion.8), channel_id=1, source_target_pairs={{0,2},{1,5},{2,0},{3,7},{4,6},{5,1},{6,4},{7,3},{8,10},{9,13},{10,... | collective-permute-start | bytes 1769480 | tf_op jit(solution)/shard_map/chips_1_2/ppermute | solution.py:391
  115.3 13.9 %copy-start.6 = (bf16[2,4,192,384]{3,2,1,0:T(8,128)(2,1)}, bf16[2,4,192,384]{3,2,1,0:T(8,128)(2,1)S(1)}, u32[]{:S(2)}) copy-start(bf16[2,4,192,384]{3,2,1,0:T(8,128)(2,1)S(1)} %pad_maximum_fusion.s8) | copy-start | bytes 3538948
  115.4 16.3 %collective-permute-start.31 = (bf16[2,4,192,384]{3,2,1,0:T(8,128)(2,1)S(1)}, bf16[2,4,192,384]{3,2,1,0:T(8,128)(2,1)S(1)}, u32[]{:S(2)}, u32[]{:S(2)}) collective-permute-start(bf16[2,4,192,384]{3,2,1,0:T(8,128)(2,1)S(1)} %pad_maximum_fusion.s8), channel_id=1, source_target_pairs={{0,4},{1,3},{2,6},{3,1},{4,0},{5,7},{6,2},{7,5},{8,12},{9,11},{10,... | collective-permute-start | bytes 3538952 | tf_op jit(solution)/shard_map/chips_2_1/ppermute | solution.py:391
  116.7 14.9 %collective-permute-start.32 = (bf16[2,4,192,384]{3,2,1,0:T(8,128)(2,1)S(1)}, bf16[2,4,192,384]{3,2,1,0:T(8,128)(2,1)}, u32[]{:S(2)}, u32[]{:S(2)}) collective-permute-start(bf16[2,4,192,384]{3,2,1,0:T(8,128)(2,1)S(1)} %pad_maximum_fusion.s8), channel_id=1, source_target_pairs={{0,1},{1,0},{2,3},{3,2},{4,5},{5,4},{6,7},{7,6},{8,9},{9,8},{10,11... | collective-permute-start | bytes 3538952 | tf_op jit(solution)/shard_map/between_cores/ppermute | solution.py:382
  116.7 3.3 collective-permute-start.33
  131.6 2.8 collective-permute-start.34
  175.3 8.5 %collective-permute-start.35 = (bf16[16,192,384]{2,1,0:T(8,128)(2,1)}, bf16[16,192,384]{2,1,0:T(8,128)(2,1)}, u32[]{:S(2)}, u32[]{:S(2)}) collective-permute-start(bf16[16,192,384]{2,1,0:T(8,128)(2,1)} %get-tuple-element.276), channel_id=1, source_target_pairs={{0,1},{1,0},{2,3},{3,2},{4,5},{5,4},{6,7},{7,6},{8,9},{9,8},{10,11... | collective-permute-start | bytes 7077896 | tf_op jit(solution)/shard_map/between_cores/ppermute | solution.py:382
  175.5 8.3 %collective-permute-start.36 = (bf16[16,192,384]{2,1,0:T(8,128)(2,1)}, bf16[16,192,384]{2,1,0:T(8,128)(2,1)}, u32[]{:S(2)}, u32[]{:S(2)}) collective-permute-start(bf16[16,192,384]{2,1,0:T(8,128)(2,1)} %get-tuple-element.277), channel_id=1, source_target_pairs={{0,1},{1,0},{2,3},{3,2},{4,5},{5,4},{6,7},{7,6},{8,9},{9,8},{10,11... | collective-permute-start | bytes 7077896 | tf_op jit(solution)/shard_map/between_cores/ppermute | solution.py:382
  188.2 32.6 %collective-permute-start.37 = (bf16[4,2,384,384]{3,2,0,1:T(8,128)(2,1)}, bf16[4,2,384,384]{3,2,0,1:T(8,128)(2,1)}, u32[]{:S(2)}, u32[]{:S(2)}) collective-permute-start(bf16[4,2,384,384]{3,2,0,1:T(8,128)(2,1)} %maximum_maximum_fusion), channel_id=1, source_target_pairs={{0,4},{1,3},{2,6},{3,1},{4,0},{5,7},{6,2},{7,5},{8,12},{9,11},{10,... | collective-permute-start | bytes 7077896 | tf_op jit(solution)/shard_map/chips_2_1/ppermute | solution.py:391
  223.4 16.5 %collective-permute-start.38 = (bf16[4,384,384]{2,1,0:T(8,128)(2,1)}, bf16[4,384,384]{2,1,0:T(8,128)(2,1)}, u32[]{:S(2)}, u32[]{:S(2)}) collective-permute-start(bf16[4,384,384]{2,1,0:T(8,128)(2,1)} %fusion.1), channel_id=1, source_target_pairs={{0,2},{1,5},{2,0},{3,7},{4,6},{5,1},{6,4},{7,3},{8,10},{9,13},{10,... | collective-permute-start | bytes 3538952 | tf_op jit(solution)/shard_map/chips_1_2/ppermute | solution.py:391
  239.9 21.5 %collective-permute-start.41 = (bf16[16,192,384]{2,1,0:T(8,128)(2,1)}, bf16[16,192,384]{2,1,0:T(8,128)(2,1)}, u32[]{:S(2)}, u32[]{:S(2)}) collective-permute-start(bf16[16,192,384]{2,1,0:T(8,128)(2,1)} %get-tuple-element.306), channel_id=1, source_target_pairs={{0,1},{1,0},{2,3},{3,2},{4,5},{5,4},{6,7},{7,6},{8,9},{9,8},{10,11... | collective-permute-start | bytes 7077896 | tf_op jit(solution)/shard_map/between_cores/ppermute | solution.py:382
  242.3 16.3 %collective-permute-start.39 = (bf16[384,384]{1,0:T(8,128)(2,1)S(1)}, bf16[384,384]{1,0:T(8,128)(2,1)S(1)}, u32[]{:S(2)}, u32[]{:S(2)}) collective-permute-start(bf16[384,384]{1,0:T(8,128)(2,1)S(1)} %get-tuple-element.419), channel_id=1, source_target_pairs={{0,8},{1,9},{2,10},{3,11},{4,12},{5,13},{6,14},{7,15},{8,0},{9,1},... | collective-permute-start | bytes 884744 | tf_op jit(solution)/shard_map/chips_4_4/ppermute | solution.py:391
  245.3 16.1 %collective-permute-start.40 = (bf16[384,384]{1,0:T(8,128)(2,1)S(1)}, bf16[384,384]{1,0:T(8,128)(2,1)S(1)}, u32[]{:S(2)}, u32[]{:S(2)}) collective-permute-start(bf16[384,384]{1,0:T(8,128)(2,1)S(1)} %get-tuple-element.418), channel_id=1, source_target_pairs={{0,24},{1,25},{2,26},{3,27},{4,28},{5,29},{6,30},{7,31},{8,16},{9,... | collective-permute-start | bytes 884744 | tf_op jit(solution)/shard_map/chips_12_12/ppermute | solution.py:391
  263.2 16.4 %collective-permute-start.43 = (bf16[4,2,192,384]{3,2,0,1:T(8,128)(2,1)S(1)}, bf16[4,2,192,384]{3,2,0,1:T(8,128)(2,1)}, u32[]{:S(2)}, u32[]{:S(2)}) collective-permute-start(bf16[4,2,192,384]{3,2,0,1:T(8,128)(2,1)S(1)} %pad_maximum_fusion.1), channel_id=1, source_target_pairs={{0,4},{1,3},{2,6},{3,1},{4,0},{5,7},{6,2},{7,5},{8,12},{9,11},{10,... | collective-permute-start | bytes 3538952 | tf_op jit(solution)/shard_map/chips_2_1/ppermute | solution.py:391
  264.0 14.7 %collective-permute-start.42 = (bf16[384,384]{1,0:T(8,128)(2,1)}, bf16[384,384]{1,0:T(8,128)(2,1)}, u32[]{:S(2)}, u32[]{:S(2)}) collective-permute-start(bf16[384,384]{1,0:T(8,128)(2,1)} %get-tuple-element.320), channel_id=1, source_target_pairs={{0,16},{1,17},{2,18},{3,19},{4,20},{5,21},{6,22},{7,23},{8,24},{9,... | collective-permute-start | bytes 884744 | tf_op jit(solution)/shard_map/chips_8_8/ppermute | solution.py:391
  279.6 11.2 %collective-permute-start.44 = (bf16[16,112,384]{2,1,0:T(8,128)(2,1)}, bf16[16,112,384]{2,1,0:T(8,128)(2,1)S(1)}, u32[]{:S(2)}, u32[]{:S(2)}) collective-permute-start(bf16[16,112,384]{2,1,0:T(8,128)(2,1)} %get-tuple-element.339), channel_id=1, source_target_pairs={{0,1},{1,0},{2,3},{3,2},{4,5},{5,4},{6,7},{7,6},{8,9},{9,8},{10,11... | collective-permute-start | bytes 4128776 | tf_op jit(solution)/shard_map/between_cores/ppermute | solution.py:382
  280.8 9.9 %collective-permute-start.45 = (bf16[4,192,384]{2,1,0:T(8,128)(2,1)S(1)}, bf16[4,192,384]{2,1,0:T(8,128)(2,1)S(1)}, u32[]{:S(2)}, u32[]{:S(2)}) collective-permute-start(bf16[4,192,384]{2,1,0:T(8,128)(2,1)S(1)} %fusion.5), channel_id=1, source_target_pairs={{0,2},{1,5},{2,0},{3,7},{4,6},{5,1},{6,4},{7,3},{8,10},{9,13},{10,... | collective-permute-start | bytes 1769480 | tf_op jit(solution)/shard_map/chips_1_2/ppermute | solution.py:391
  291.0 15.1 %collective-permute-start.46 = (bf16[4,2,112,384]{3,2,0,1:T(8,128)(2,1)S(1)}, bf16[4,2,112,384]{3,2,0,1:T(8,128)(2,1)S(1)}, u32[]{:S(2)}, u32[]{:S(2)}) collective-permute-start(bf16[4,2,112,384]{3,2,0,1:T(8,128)(2,1)S(1)} %pad_maximum_fusion.6), channel_id=1, source_target_pairs={{0,4},{1,3},{2,6},{3,1},{4,0},{5,7},{6,2},{7,5},{8,12},{9,11},{10,... | collective-permute-start | bytes 2064392 | tf_op jit(solution)/shard_map/chips_2_1/ppermute | solution.py:391
  291.8 14.3 %collective-permute-start.50 = (bf16[384,384]{1,0:T(8,128)(2,1)S(1)}, bf16[384,384]{1,0:T(8,128)(2,1)S(1)}, u32[]{:S(2)}, u32[]{:S(2)}) collective-permute-start(bf16[384,384]{1,0:T(8,128)(2,1)S(1)} %add_convert_fusion.22), channel_id=1, source_target_pairs={{0,1},{1,0},{2,3},{3,2},{4,5},{5,4},{6,7},{7,6},{8,9},{9,8},{10,11... | collective-permute-start | bytes 884744 | tf_op jit(solution)/shard_map/between_cores/ppermute | solution.py:382
  292.1 9.1 %collective-permute-start.47 = (bf16[192,384]{1,0:T(8,128)(2,1)S(1)}, bf16[192,384]{1,0:T(8,128)(2,1)S(1)}, u32[]{:S(2)}, u32[]{:S(2)}) collective-permute-start(bf16[192,384]{1,0:T(8,128)(2,1)S(1)} %get-tuple-element.425), channel_id=1, source_target_pairs={{0,8},{1,9},{2,10},{3,11},{4,12},{5,13},{6,14},{7,15},{8,0},{9,1},... | collective-permute-start | bytes 442376 | tf_op jit(solution)/shard_map/chips_4_4/ppermute | solution.py:391
  292.1 14.0 %collective-permute-start.48 = (bf16[192,384]{1,0:T(8,128)(2,1)S(1)}, bf16[192,384]{1,0:T(8,128)(2,1)S(1)}, u32[]{:S(2)}, u32[]{:S(2)}) collective-permute-start(bf16[192,384]{1,0:T(8,128)(2,1)S(1)} %get-tuple-element.424), channel_id=1, source_target_pairs={{0,16},{1,17},{2,18},{3,19},{4,20},{5,21},{6,22},{7,23},{8,24},{9,... | collective-permute-start | bytes 442376 | tf_op jit(solution)/shard_map/chips_8_8/ppermute | solution.py:391
  295.0 11.1 %collective-permute-start.49 = (bf16[192,384]{1,0:T(8,128)(2,1)S(1)}, bf16[192,384]{1,0:T(8,128)(2,1)S(1)}, u32[]{:S(2)}, u32[]{:S(2)}) collective-permute-start(bf16[192,384]{1,0:T(8,128)(2,1)S(1)} %get-tuple-element.423), channel_id=1, source_target_pairs={{0,24},{1,25},{2,26},{3,27},{4,28},{5,29},{6,30},{7,31},{8,16},{9,... | collective-permute-start | bytes 442376 | tf_op jit(solution)/shard_map/chips_12_12/ppermute | solution.py:391
  306.4 7.3 %collective-permute-start.51 = (bf16[4,112,384]{2,1,0:T(8,128)(2,1)S(1)}, bf16[4,112,384]{2,1,0:T(8,128)(2,1)S(1)}, u32[]{:S(2)}, u32[]{:S(2)}) collective-permute-start(bf16[4,112,384]{2,1,0:T(8,128)(2,1)S(1)} %fusion.7), channel_id=1, source_target_pairs={{0,2},{1,5},{2,0},{3,7},{4,6},{5,1},{6,4},{7,3},{8,10},{9,13},{10,... | collective-permute-start | bytes 1032200 | tf_op jit(solution)/shard_map/chips_1_2/ppermute | solution.py:391
  308.1 1.4 collective-permute-start.52
  314.0 8.5 %collective-permute-start.53 = (bf16[112,384]{1,0:T(8,128)(2,1)S(1)}, bf16[112,384]{1,0:T(8,128)(2,1)S(1)}, u32[]{:S(2)}, u32[]{:S(2)}) collective-permute-start(bf16[112,384]{1,0:T(8,128)(2,1)S(1)} %get-tuple-element.431), channel_id=1, source_target_pairs={{0,8},{1,9},{2,10},{3,11},{4,12},{5,13},{6,14},{7,15},{8,0},{9,1},... | collective-permute-start | bytes 258056 | tf_op jit(solution)/shard_map/chips_4_4/ppermute | solution.py:391
  317.4 8.5 %collective-permute-start.54 = (bf16[112,384]{1,0:T(8,128)(2,1)S(1)}, bf16[112,384]{1,0:T(8,128)(2,1)S(1)}, u32[]{:S(2)}, u32[]{:S(2)}) collective-permute-start(bf16[112,384]{1,0:T(8,128)(2,1)S(1)} %get-tuple-element.430), channel_id=1, source_target_pairs={{0,16},{1,17},{2,18},{3,19},{4,20},{5,21},{6,22},{7,23},{8,24},{9,... | collective-permute-start | bytes 258056 | tf_op jit(solution)/shard_map/chips_8_8/ppermute | solution.py:391
  318.3 7.6 %collective-permute-start.55 = (bf16[112,384]{1,0:T(8,128)(2,1)S(1)}, bf16[112,384]{1,0:T(8,128)(2,1)S(1)}, u32[]{:S(2)}, u32[]{:S(2)}) collective-permute-start(bf16[112,384]{1,0:T(8,128)(2,1)S(1)} %get-tuple-element.429), channel_id=1, source_target_pairs={{0,24},{1,25},{2,26},{3,27},{4,28},{5,29},{6,30},{7,31},{8,16},{9,... | collective-permute-start | bytes 258056 | tf_op jit(solution)/shard_map/chips_12_12/ppermute | solution.py:391
  326.0 4.8 %collective-permute-start.56 = (bf16[112,384]{1,0:T(8,128)(2,1)S(1)}, bf16[112,384]{1,0:T(8,128)(2,1)S(1)}, u32[]{:S(2)}, u32[]{:S(2)}) collective-permute-start(bf16[112,384]{1,0:T(8,128)(2,1)S(1)} %add_convert_fusion.24), channel_id=1, source_target_pairs={{0,1},{1,0},{2,3},{3,2},{4,5},{5,4},{6,7},{7,6},{8,9},{9,8},{10,11... | collective-permute-start | bytes 258056 | tf_op jit(solution)/shard_map/between_cores/ppermute | solution.py:382
  (24 other events, 109.8 us)

commit v4 on v3

--- a/solution.py
+++ b/solution.py
@@ -321,7 +321,7 @@
 VECTORS = (1, 3, 4, 5, 6, 8, 11, 13, 14, 15, 19, 17)
 LANES = 384
 VEC_ROWS = 16
-GATHER_CHUNKS = ((0, 2, "vec"), (7, 9, 10), (12, "low"), ("high",), (18,))
+GATHER_CHUNKS = ((0, 2, "vec", 7, 9, 10), (12, "low"), ("high", 18))
 SCATTER_CHUNKS = ((18, 16), (12, 7, 9, 10), (0, 2, "vec"))
 BOTH = ("fsdp", "dp")
 WIDTH = 768
@@ -404,20 +404,23 @@
     count = len(chunk) + (11 if "vec" in chunk else 0)
     ins, out = refs[:count], refs[count]
     offset = 0
-    for place, index in enumerate(chunk):
+    order = [i for i in chunk if i != "vec"]
+    for index in chunk:
         if index == "vec":
             rows = refs[-1]
             rows[...] = jnp.zeros_like(rows)
             for row in range(12):
-                source = ins[place + row]
+                source = ins[len(order) + row]
                 rows[row : row + 1, 0 : source.shape[1]] = source[...].astype(FULL)
             out[offset : offset + VEC_ROWS, :] = rows[...].astype(LOW)
+            offset += VEC_ROWS
             continue
         parts = {"low": (4, (0, 1)), "high": (4, (2, 3))}.get(index, (1, (0,)))
-        rows = ins[place].shape[0]
+        source = ins[order.index(index)]
+        rows = source.shape[0]
         for s in parts[1]:
             first = pl.multiple_of((core * parts[0] + s) * LANES, LANES)
-            out[offset : offset + rows, :] = ins[place][:, pl.ds(first, LANES)]
+            out[offset : offset + rows, :] = source[:, pl.ds(first, LANES)]
             offset += rows
 
 
@@ -491,11 +494,21 @@
     return jnp.sum(values.astype(FULL), 0, keepdims=True)
 
 
-def embed_kernel(at, image, text, s8, r8, s8p, r8p, w_image, w_text, vec, hid, embedded, normed, small):
+def embed_kernel(
+    at, image, text, s8, r8, s8p, r8p,
+    w_image, w_text, wq, wk, wv, vec, hid, embedded, normed, q, k, v, small,
+):
     unpack(
         at,
         (s8, r8, s8p, r8p),
-        ((0, (0,), 1, w_image), (48, (0,), 1, w_text), (96, (0,), 0, small)),
+        (
+            (0, (0,), 1, w_image),
+            (48, (0,), 1, w_text),
+            (96, (0,), 0, small),
+            (112, (0,), 1, wq),
+            (160, (0,), 1, wk),
+            (208, (0,), 1, wv),
+        ),
     )
     for f in range(16):
         piece = small[f >> 2, (f >> 1) & 1, f & 1].astype(FULL)
@@ -507,40 +520,21 @@
     for rows in row_chunks(64):
         unit, unused_scale = standard(embedded[rows, :])
         normed[rows, :] = to_low(unit * vec[3:4, :] + vec[4:5, :])
-
-
-def embed(place, image, text, pieces):
-    block = (4, 2, 2, 48, WIDTH)
-    outs = [
-        shape(block),
-        shape(block),
-        shape((VEC_ROWS, WIDTH), FULL),
-        shape((1, HIDDEN), FULL),
-        shape((ROWS, WIDTH), FULL),
-        shape((ROWS, WIDTH)),
-    ]
-    scratch = (pltpu.VMEM((4, 2, 2, VEC_ROWS, LANES), LOW),)
-    return call(embed_kernel, 5.5, outs, place.scalars, image, text, *pieces, scratch=scratch)
-
-
-def qkv_kernel(at, normed, vec, s8, r8, s8p, r8p, wq, wk, wv, q, k, v):
-    unpack(
-        at,
-        (s8, r8, s8p, r8p),
-        ((0, (0,), 1, wq), (48, (0,), 1, wk), (96, (0,), 1, wv)),
-    )
-    rows = normed[...]
     for out in (q, k, v):
         out[832:PADDED, :] = jnp.zeros((PADDED - 832, WIDTH), LOW)
+    rows = normed[...]
     low = to_low(matmul(rows, square(wq)) + vec[5:6, :])
     q[0:ROWS, :] = to_low(low.astype(FULL) * HEAD_DIM**-0.5)
     k[0:ROWS, :] = to_low(matmul(rows, square(wk)))
     v[0:ROWS, :] = to_low(matmul(rows, square(wv)) + vec[6:7, :])
 
 
-def qkv(place, normed, vec, pieces):
-    outs = [shape((4, 2, 2, 48, WIDTH))] * 3 + [shape((PADDED, WIDTH))] * 3
-    return call(qkv_kernel, 7, outs, place.scalars, normed, vec, *pieces)
+def embed(place, image, text, pieces):
+    outs = [shape((4, 2, 2, 48, WIDTH))] * 5
+    outs += [shape((VEC_ROWS, WIDTH), FULL), shape((1, HIDDEN), FULL)]
+    outs += [shape((ROWS, WIDTH), FULL), shape((ROWS, WIDTH))] + [shape((PADDED, WIDTH))] * 3
+    scratch = (pltpu.VMEM((4, 2, 2, VEC_ROWS, LANES), LOW),)
+    return call(embed_kernel, 12, outs, place.scalars, image, text, *pieces, scratch=scratch)
 
 
 def mask_column(live):
@@ -864,19 +858,19 @@
     return call(branch_kernel, 8, outs, middle, second_grad, cot, vec, w_out)
 
 
-def both_halves(core, left, right_ref, first, keep, send, offset, rows):
+def both_halves(core, left_t, right_ref, first, keep, send, offset):
     for half, out in ((core, keep), (1 - core, send)):
         columns = pl.ds(pl.multiple_of(half * LANES, LANES), LANES)
-        grad = left_product(left, right_ref[first, columns])
+        grad = matmul(left_t, right_ref[first, columns])
         out[:, offset : offset + 48, :] = to_low(grad).reshape(16, 48, LANES)
 
 
 def square_grads_kernel(at, attended, branch, normed, dq, dk, dv, keep, send):
     rows = slice(0, ROWS)
-    both_halves(at[0], attended[rows, :], branch, rows, keep, send, 0, 48)
-    left = normed[...]
+    both_halves(at[0], jnp.transpose(attended[rows, :]), branch, rows, keep, send, 0)
+    left_t = jnp.transpose(normed[...])
     for n, ref in enumerate((dq, dk, dv)):
-        both_halves(at[0], left, ref, rows, keep, send, 48 * (n + 1), 48)
+        both_halves(at[0], left_t, ref, rows, keep, send, 48 * (n + 1))
 
 
 def square_grads(place, attended, branch, normed, grads):
@@ -922,8 +916,8 @@
     at, image, text, image_low, text_low, sums, hid_sum, ret_sum, late,
     keep, send, rows16, packed,
 ):
-    both_halves(at[0], image[...], image_low, slice(0, IMAGE), keep, send, 0, 48)
-    both_halves(at[0], text[...], text_low, slice(0, TEXTS), keep, send, 48, 48)
+    both_halves(at[0], jnp.transpose(image[...]), image_low, slice(0, IMAGE), keep, send, 0)
+    both_halves(at[0], jnp.transpose(text[...]), text_low, slice(0, TEXTS), keep, send, 48)
     rows16[...] = jnp.zeros_like(rows16)
     found = (
         sum_rows(image_low[...]), sum_rows(text_low[...]), late[0:1, :], late[1:2, :], late[2:3, :],
@@ -950,12 +944,12 @@
 
 
 def inputs_kernel(image_low, text_low, w_image, w_text, image_grad, text_grad):
-    image_grad[...] = right_product(image_low[...], square(w_image))
-    text_grad[...] = right_product(text_low[...], square(w_text))
+    image_grad[:, 0, :] = right_product(image_low[...], square(w_image))
+    text_grad[:, 0, :] = right_product(text_low[...], square(w_text))
 
 
 def input_grads(image_low, text_low, w_image, w_text):
-    outs = [shape((IMAGE, WIDTH), FULL), shape((TEXTS, WIDTH), FULL)]
+    outs = [shape((IMAGE, 1, WIDTH), FULL), shape((TEXTS, 1, WIDTH), FULL)]
     return call(inputs_kernel, 4.4, outs, image_low, text_low, w_image, w_text)
 
 
@@ -980,26 +974,28 @@
     def state(self):
         return self.kept, self.got
 
+    def summed(self, q):
+        parts = []
+        for keep, more in zip(self.kept, self.swapped):
+            keep, more = (pick(v.reshape(4, 4, v.shape[1], LANES), q, 1) for v in (keep, more))
+            parts.append(keep.astype(FULL) + more.astype(FULL))
+        return jnp.concatenate(parts, 1) if len(parts) > 1 else parts[0]
+
     def first(self):
         zero, x, y = self.place.core == 0, self.place.x, self.place.y
-        near = [jnp.where(zero, 2 * y + s, 2 * s + x) for s in (0, 1)]
+        self.swapped = self.got
         far = [jnp.where(zero, 2 * (1 - y) + s, 2 * s + (1 - x)) for s in (0, 1)]
-
-        def summed(places):
-            parts = []
-            for keep, more in zip(self.kept, self.got):
-                keep, more = (v.reshape(4, 4, v.shape[1], LANES) for v in (keep, more))
-                added = [add_low(pick(keep, q, 1), pick(more, q, 1)) for q in places]
-                parts.append(jnp.stack(added, 1))
-            return jnp.concatenate(parts, 2) if len(parts) > 1 else parts[0]
-
-        self.sent, self.kept = summed(far), summed(near)
+        self.sent = jnp.stack([to_low(self.summed(q)) for q in far], 1)
 
     def second(self):
-        mine = jnp.where(self.place.core == 0, self.place.x, self.place.y)
-        kept, got = self.kept, self.got
-        self.sent = add_low(pick(kept, 1 - mine, 1), pick(got, 1 - mine, 1))
-        self.kept = add_low(pick(kept, mine, 1), pick(got, mine, 1))
+        zero, x, y = self.place.core == 0, self.place.x, self.place.y
+        mine = jnp.where(zero, x, y)
+
+        def added(s):
+            near = self.summed(jnp.where(zero, 2 * y + s, 2 * s + x))
+            return to_low(near + pick(self.got, s, 1).astype(FULL))
+
+        self.sent, self.kept = added(1 - mine), added(mine)
 
     def third(self):
         z = self.place.z
@@ -1056,47 +1052,41 @@
     z_one, owns = settle(z_one, owns)
 
     z_one = jnp.stack(z_one)
-    b_one, z_two = to_chip(z_one, 1, 2), all_z(owns[0])
-    b_one, z_two, z_one, owns = settle(b_one, z_two, z_one, owns)
-
-    s_one, z_two = jnp.stack([z_one, b_one]), jnp.stack(z_two)
-    r_one, sp_one, z_a = to_chip(s_one, 2, 1), swap_cores(s_one), all_z(owns[1])
-    r_one, sp_one, s_one, z_a, z_two = settle(r_one, sp_one, s_one, z_a, z_two)
-
-    z_a = jnp.stack(z_a)
-    b_two, rp_one, b_a, z_b = to_chip(z_two, 1, 2), swap_cores(r_one), to_chip(z_a, 1, 2), all_z(owns[2])
-    w_image, w_text, vec, hid, embedded, normed = embed(
-        place, image, after(text, z_a), (s_one, r_one, sp_one, rp_one)
-    )
-    b_two, b_a, z_b, z_two, normed = settle(b_two, b_a, z_b, z_two, normed)
-
-    s_two = jnp.stack([z_two, b_two])
-    r_two, sp_two, z_c = to_chip(s_two, 2, 1), swap_cores(s_two), all_z(owns[3])
-    s_a, z_b = jnp.stack([z_a, b_a]), jnp.stack(z_b)
-    r_two, sp_two, z_c, s_two, s_a, z_b = settle(r_two, sp_two, z_c, s_two, s_a, z_b)
-
-    rp_two, r_a, b_b = swap_cores(r_two), to_chip(s_a, 2, 1), to_chip(z_b, 1, 2)
-    z_c, sp_a = jnp.stack(z_c), swap_cores(s_a)
-    wq, wk, wv, q, k, v = qkv(place, after(normed, z_c), vec, (s_two, r_two, sp_two, rp_two))
-    both = attend(live, q, k, v, 0, 2)
-    r_a, b_b, z_c, sp_a, both = settle(r_a, b_b, z_c, sp_a, both)
-
-    s_b = jnp.stack([z_b, b_b])
-    r_b, b_c, sp_b, rp_a = to_chip(s_b, 2, 1), to_chip(z_c, 1, 2), swap_cores(s_b), swap_cores(r_a)
-    both = attend(live, after(q, s_b), k, v, 2, 2, both)
-    attended, totals = attend(live, q, k, v, 4, 2, both)
-    r_b, b_c, sp_b, rp_a, attended = settle(r_b, b_c, sp_b, rp_a, attended)
-
-    s_c = jnp.stack([z_c, b_c])
-    r_c, sp_c, rp_b = to_chip(s_c, 2, 1), swap_cores(s_c), swap_cores(r_b)
+    b_one, z_a, z_one, owns = settle(to_chip(z_one, 1, 2), all_z(owns[0]), z_one, owns)
+
+    s_one, z_a = jnp.stack([z_one, b_one]), jnp.stack(z_a)
+    r_one, sp_one, z_b, s_one, z_a = settle(
+        to_chip(s_one, 2, 1), swap_cores(s_one), all_z(owns[1]), s_one, z_a
+    )
+
+    rp_one, b_a = swap_cores(r_one), to_chip(z_a, 1, 2)
+    z_b = jnp.stack(z_b)
+    b_b = to_chip(z_b, 1, 2)
+    w_image, w_text, wq, wk, wv, vec, hid, embedded, normed, q, k, v = embed(
+        place, image, after(text, z_a, z_b), (s_one, r_one, sp_one, rp_one)
+    )
+    b_a, b_b, z_a, z_b, q = settle(b_a, b_b, z_a, z_b, q)
+
+    s_a, s_b = jnp.stack([z_a, b_a]), jnp.stack([z_b[:, :96], b_b[:, :96]])
+    s_c = jnp.stack([z_b[:, 96:], b_b[:, 96:]])
+    r_a, r_b, sp_a = to_chip(s_a, 2, 1), to_chip(s_b, 2, 1), swap_cores(s_a)
+    both = attend(live, after(q, s_a, s_b, s_c), k, v, 0, 3)
+    r_a, r_b, sp_a, both, s_b, s_c = settle(r_a, r_b, sp_a, both, s_b, s_c)
+
+    r_c, sp_b, sp_c = to_chip(s_c, 2, 1), swap_cores(s_b), swap_cores(s_c)
+    rp_a, rp_b = swap_cores(r_a), swap_cores(r_b)
+    attended, totals = attend(live, q, k, v, 3, 3, both)
+    r_c, sp_b, sp_c, rp_a, rp_b, attended = settle(r_c, sp_b, sp_c, rp_a, rp_b, attended)
+
+    rp_c = swap_cores(r_c)
     w_out, w_hid, middle, second = middle_of(
-        place, after(attended, s_c), embedded, vec, (s_a, r_a, sp_a, rp_a, s_b, r_b, sp_b, rp_b)
-    )
-    r_c, sp_c, second = settle(r_c, sp_c, second)
+        place, attended, embedded, vec, (s_a, r_a, sp_a, rp_a, s_b, r_b, sp_b, rp_b)
+    )
+    rp_c, second = settle(rp_c, second)
 
     layer_out, second_grad, ret_keep, ret_send, hid_keep, hid_send, hid_sum, ret_sum = feed(
         place, second, cot, middle, vec, w_hid.reshape(WIDTH, HIDDEN), hid,
-        (s_c, r_c, sp_c, swap_cores(r_c)),
+        (s_c, r_c, sp_c, rp_c),
     )
 
     feeding = Scatter(place, ((ret_keep, ret_send), (hid_keep, hid_send)))
@@ -1170,7 +1160,8 @@
     ending.fourth()
     ending.swap()
     owned.update(owned_rows(SCATTER_CHUNKS[2], *ending.sides()))
-    return (layer_out[None], image_grad[None], text_grad[None]) + tuple(owned[i] for i in range(20))
+    image_grad, text_grad = (jnp.transpose(grad, (1, 0, 2)) for grad in (image_grad, text_grad))
+    return (layer_out[None], image_grad, text_grad) + tuple(owned[i] for i in range(20))
 
 
 def gather_any(shards):

time: 339 us -> 325 us (0.959)
  waiting for transfers between devices: 69.1 us -> 82.7 us
  starting transfers between devices: 57.6 us -> 48 us
  local copies, waits for them, and re-layouts: 14.6 us -> 8.01 us
  Pallas kernels: 160 us -> 155 us
  other arithmetic: 29.4 us -> 25.1 us
    ppermute x40 -> x31, waiting for transfers between devices: 63.1 us -> 81.1 us  [to_chip(): return lax.ppermute(values, BOTH, pairs)]
    convert_element_type x18 -> x13, other arithmetic: 18.6 us -> 8.64 us  [to_low(): return values.astype(jnp.bfloat16)]
    ppermute x40 -> x31, starting transfers between devices: 54.6 us -> 46.1 us  [to_chip(): return lax.ppermute(values, BOTH, pairs)]
    unnamed x71 -> x51, local copies, waits for them, and re-layouts: 11.2 us -> 4.39 us
    ppermute x17 -> x15, waiting for transfers between devices: 6.03 us -> 1.6 us  [swap_cores(): return lax.ppermute(values, 'dp', [(0, 1), (1, 0)])]
    add x0 -> x3, other arithmetic: none -> 4.37 us  [summed(): parts.append(keep.astype(FULL) + more.astype(FULL))]
    pallas_call x13 -> x10, Pallas kernels: 69.4 us -> 65.9 us  [call(): pl.pallas_call(kernel, out_shape=tuple(outs), in_specs=specs, out_specs=t...]
    pallas_call x3 -> x2, Pallas kernels: 22.4 us -> 20.9 us  [attend(): pl.pallas_call(kernel, grid=(count,), out_shape=(shape((PADDED, WIDTH)),...]
  transfers between devices with their start and end apart: 57 -> 46, of which waited for: 20 -> 20; matrix products, arithmetic and copies ran while one was open for 7% -> 3% of each run, Pallas kernels for 36% -> 35%
where the time goes in v4:
time: 325 us; the launch traced here: 321 us
  Pallas kernels  155 us (48%)
  waiting for transfers between devices  82.7 us (25%)
  starting transfers between devices  48 us (15%)
  other arithmetic  25.1 us (8%)
  local copies, waits for them, and re-layouts  8.01 us (2%)
    ppermute x31, waiting for transfers between devices, to_chip(): return lax.ppermute(values, BOTH, pairs)  81.1 us
    pallas_call x10, Pallas kernels, call(): pl.pallas_call(kernel, out_shape=tuple(outs), in_specs=specs, out_specs=t...  65.9 us
    ppermute x31, starting transfers between devices, to_chip(): return lax.ppermute(values, BOTH, pairs)  46.1 us
    pallas_call x1, Pallas kernels, feed(): pl.pallas_call(feed_kernel, grid_spec=grid, out_shape=outs, compiler_para...  39.6 us
    pallas_call x1, Pallas kernels, attend_back(): pl.pallas_call(attend_back_kernel, grid=(HEADS // 2,), out_shape=(shape((...  28.4 us
    pallas_call x2, Pallas kernels, attend(): pl.pallas_call(kernel, grid=(count,), out_shape=(shape((PADDED, WIDTH)),...  20.9 us
    convert_element_type x13, other arithmetic, to_low(): return values.astype(jnp.bfloat16)  8.64 us
  transfers between devices with their start and end apart: 46, of which 20 were waited for; matrix products, arithmetic and copies ran while one was open for 3% of the time, Pallas kernels for 35%

profile of v4, /device:TPU:0, one launch (start us, length us, event | category | flops | bytes accessed | tf_op | source)
XLA Modules:
  0.0 321.4 jit_solution(14793170092607416498)
XLA Ops:
  0.7 1.2 reshape.238.refs_16_
  2.5 1.9 shard_map.416
  4.3 3.0 collective-permute-start
  7.4 2.6 collective-permute-start.1
  9.9 1.8 shard_map.418
  11.7 1.7 shard_map.417
  13.4 2.6 collective-permute-done
  16.0 8.7 %collective-permute-done.1 = bf16[256,384]{1,0:T(8,128)(2,1)S(1)} collective-permute-done((bf16[256,384]{1,0:T(8,128)(2,1)}, bf16[256,384]{1,0:T(8,128)(2,1)S(1)}, u32[]{:S(2)}, u32[]{:S(2)}) %collective-permute-start.1) | collective-permute-done | bytes 196640 | tf_op jit(solution)/shard_map/chips_8_8/ppermute | solution.py:391
  24.9 1.6 collective-permute-start.3
  26.4 3.4 %collective-permute-start.4 = (bf16[144,384]{1,0:T(8,128)(2,1)S(1)}, bf16[144,384]{1,0:T(8,128)(2,1)S(1)}, u32[]{:S(2)}, u32[]{:S(2)}) collective-permute-start(bf16[144,384]{1,0:T(8,128)(2,1)S(1)} %copy-done.16), channel_id=1, source_target_pairs={{0,8},{1,9},{2,10},{3,11},{4,12},{5,13},{6,14},{7,15},{8,0},{9,1},... | collective-permute-start | bytes 331784 | tf_op jit(solution)/shard_map/chips_4_4/ppermute | solution.py:391
  30.8 1.5 collective-permute-start.6
  32.2 1.3 collective-permute-done.4
  33.6 6.2 %collective-permute-done.5 = bf16[144,384]{1,0:T(8,128)(2,1)S(1)} collective-permute-done((bf16[144,384]{1,0:T(8,128)(2,1)S(1)}, bf16[144,384]{1,0:T(8,128)(2,1)S(1)}, u32[]{:S(2)}, u32[]{:S(2)}) %collective-permute-start.5) | collective-permute-done | bytes 110624 | tf_op jit(solution)/shard_map/chips_8_8/ppermute | solution.py:391
  40.7 2.7 collective-permute-start.10
  43.4 1.4 collective-permute-start.11
  44.9 14.5 %collective-permute-done.10 = bf16[288,384]{1,0:T(8,128)(2,1)S(1)} collective-permute-done((bf16[288,384]{1,0:T(8,128)(2,1)S(1)}, bf16[288,384]{1,0:T(8,128)(2,1)S(1)}, u32[]{:S(2)}, u32[]{:S(2)}) %collective-permute-start.10) | collective-permute-done | bytes 221216 | tf_op jit(solution)/shard_map/chips_8_8/ppermute | solution.py:391
  60.5 1.1 copy-done.19
  61.8 1.6 collective-permute-start.13
  65.9 1.1 copy-done.20
  67.0 11.9 %shard_map.419 = (bf16[4,2,2,48,768]{4,3,2,1,0:T(8,128)(2,1)}, bf16[4,2,2,48,768]{4,3,2,1,0:T(8,128)(2,1)}, bf16[4,2,2,48,768]{4,3,2,1,0:T(8,128)(2,1)}, bf16[4,...) custom-call(s32[4]{0:T(128)} %pad_add_fusion.at_ref.at, ...), custom_call_target="tpu_custom_call" | custom-call | flops 3600000000 | bytes 1024 | tf_op jit(solution)/shard_map/pallas_call | solution.py:361
  79.8 1.3 collective-permute-start.15
  82.4 10.6 %shard_map.420 = (bf16[896,768]{1,0:T(8,128)(2,1)}, f32[6,8,896]{2,1,0:T(8,128)}) custom-call(s32[2]{0:T(128)} %pad_add_fusion.1.live, bf16[896,768]{1,0:T(8,128)(2,1)} %get-tuple-element.210.q, bf16[896,768]{1,0:T(8,128)(2,1)} %get-tuple-element.211.k, bf16[896,768]{1,0:T(8,128)(2,1)} %get-tuple-element.212.v), custom_call_target="tpu_custom_call" | custom-call | flops 2700000000 | bytes 1024 | tf_op jit(solution)/shard_map/pallas_call | solution.py:606
  93.0 6.3 %collective-permute-done.16.r_hi = bf16[2,4,96,384]{3,2,1,0:T(8,128)(2,1)} collective-permute-done((bf16[2,4,96,384]{3,2,1,0:T(8,128)(2,1)S(1)}, bf16[2,4,96,384]{3,2,1,0:T(8,128)(2,1)}, u32[]{:S(2)}, u32[]{:S(2)}) %collective-permute-start.16) | collective-permute-done | bytes 589856 | tf_op jit(solution)/shard_map/chips_2_1/ppermute | solution.py:391
  99.3 1.2 collective-permute-start.18
  101.5 10.2 %shard_map.421 = (bf16[896,768]{1,0:T(8,128)(2,1)}, f32[6,8,896]{2,1,0:T(8,128)}) custom-call(s32[2]{0:T(128)} %pad_add_fusion.1.live, bf16[896,768]{1,0:T(8,128)(2,1)} %get-tuple-element.210.q, bf16[896,768]{1,0:T(8,128)(2,1)} %get-tuple-element.211.k, bf16[896,768]{1,0:T(8,128)(2,1)} %get-tuple-element.212.v, ...), custom_call_target="tpu_custom_call", output_to_operand_aliasing={{0}: (4, {}), {1}: (5, {})} | custom-call | flops 2700000000 | bytes 1024 | tf_op jit(solution)/shard_map/pallas_call | solution.py:606
  111.8 3.8 %collective-permute-done.18.r8 = bf16[2,4,192,384]{3,2,1,0:T(8,128)(2,1)} collective-permute-done((bf16[2,4,192,384]{3,2,1,0:T(8,128)(2,1)S(1)}, bf16[2,4,192,384]{3,2,1,0:T(8,128)(2,1)}, u32[]{:S(2)}, u32[]{:S(2)}) %collective-permute-start.18) | collective-permute-done | bytes 1179680 | tf_op jit(solution)/shard_map/chips_2_1/ppermute | solution.py:391
  115.7 8.4 %shard_map.422 = (bf16[4,2,2,48,768]{4,3,2,1,0:T(8,128)(2,1)}, bf16[4,2,2,48,3072]{4,3,2,1,0:T(8,128)(2,1)}, f32[839,768]{1,0:T(8,128)}, bf16[839,768]{1,0:T(8,128)(2,1)}) custom-call(s32[4]{0:T(128)} %pad_add_fusion.at_ref.at, bf16[896,768]{1,0:T(8,128)(2,1)} %get-tuple-element.223.attended, f32[839,768]{1,0:T(8,128)} %get-tuple-element.224.embedded, ...), custom_call_target="tpu_custom_call" | custom-call | flops 2400000000 | bytes 1024 | tf_op jit(solution)/shard_map/pallas_call | solution.py:361
  125.1 39.6 %shard_map.423 = (bf16[839,768]{1,0:T(8,128)(2,1)}, f32[839,768]{1,0:T(8,128)}, bf16[16,192,384]{2,1,0:T(8,128)(2,1)}, bf16[16,192,384]{2,1,0:T(8,128)(2,1)}, bf...) custom-call(s32[4]{0:T(128)} %pad_add_fusion.at_ref.at, ...), custom_call_target="tpu_custom_call" | custom-call | flops 12000000000 | bytes 1024 | tf_op jit(solution)/shard_map/pallas_call | solution.py:826
  165.3 8.0 %shard_map.424 = (f32[839,768]{1,0:T(8,128)}, bf16[839,768]{1,0:T(8,128)(2,1)}, bf16[896,768]{1,0:T(8,128)(2,1)}, f32[8,768]{1,0:T(8,128)}) custom-call(f32[839,768]{1,0:T(8,128)} %get-tuple-element.232.middle, f32[839,768]{1,0:T(8,128)} %get-tuple-element.242.second_grad, bf16[839,768]{1,0:T(8,128)(2,1)} %bitcast.218, f32[16,768]{1,0:T(8,128)} %get-tuple-element.225.vec, ...), custom_call_target="tpu_custom_call" | custom-call | flops 2400000000 | bytes 1024 | tf_op jit(solution)/shard_map/pallas_call | solution.py:361
  173.3 1.7 add_convert_fusion.8
  175.3 1.6 add_convert_fusion.7
  176.9 1.6 maximum_maximum_fusion
  178.5 1.2 collective-permute-start.26
  179.7 28.4 %shard_map.425 = (bf16[896,768]{1,0:T(8,128)(2,1)}, bf16[896,768]{1,0:T(8,128)(2,1)}, bf16[896,768]{1,0:T(8,128)(2,1)}) custom-call(s32[2]{0:T(128)} %pad_add_fusion.1.live, bf16[896,768]{1,0:T(8,128)(2,1)} %get-tuple-element.210.q, bf16[896,768]{1,0:T(8,128)(2,1)} %get-tuple-element.211.k, bf16[896,768]{1,0:T(8,128)(2,1)} %get-tuple-element.212.v, ...), custom_call_target="tpu_custom_call" | custom-call | flops 8400000000 | bytes 1024 | tf_op jit(solution)/shard_map/pallas_call | solution.py:654
  208.2 1.4 add_bitcast_fusion.2
  209.6 1.5 add_bitcast_fusion
  211.6 1.5 add_bitcast_fusion.1
  213.1 1.7 fusion.1
  214.8 1.5 collective-permute-start.27
  216.3 11.4 %shard_map.426 = (bf16[16,192,384]{2,1,0:T(8,128)(2,1)}, bf16[16,192,384]{2,1,0:T(8,128)(2,1)}) custom-call(s32[4]{0:T(128)} %pad_add_fusion.at_ref.at, bf16[896,768]{1,0:T(8,128)(2,1)} %get-tuple-element.223.attended, bf16[839,768]{1,0:T(8,128)(2,1)} %get-tuple-element.264.branch, bf16[839,768]{1,0:T(8,128)(2,1)} %get-tuple-element.265.normed, ...), custom_call_target="tpu_custom_call" | custom-call | flops 3300000000 | bytes 1024 | tf_op jit(solution)/shard_map/pallas_call | solution.py:361
  227.7 3.5 %collective-permute-done.27 = bf16[4,384,384]{2,1,0:T(8,128)(2,1)S(1)} collective-permute-done((bf16[4,384,384]{2,1,0:T(8,128)(2,1)}, bf16[4,384,384]{2,1,0:T(8,128)(2,1)S(1)}, u32[]{:S(2)}, u32[]{:S(2)}) %collective-permute-start.27) | collective-permute-done | bytes 1179680 | tf_op jit(solution)/shard_map/chips_1_2/ppermute | solution.py:391
  232.3 4.0 %collective-permute-start.28 = (bf16[384,384]{1,0:T(8,128)(2,1)S(1)}, bf16[384,384]{1,0:T(8,128)(2,1)S(1)}, u32[]{:S(2)}, u32[]{:S(2)}) collective-permute-start(bf16[384,384]{1,0:T(8,128)(2,1)S(1)} %get-tuple-element.356), channel_id=1, source_target_pairs={{0,8},{1,9},{2,10},{3,11},{4,12},{5,13},{6,14},{7,15},{8,0},{9,1},... | collective-permute-start | bytes 884744 | tf_op jit(solution)/shard_map/chips_4_4/ppermute | solution.py:391
  236.3 2.0 collective-permute-start.29
  238.3 10.9 %shard_map.427 = (bf16[325,768]{1,0:T(8,128)(2,1)}, bf16[513,768]{1,0:T(8,128)(2,1)}, f32[8,768]{1,0:T(8,128)}) custom-call(bf16[896,768]{1,0:T(8,128)(2,1)} %get-tuple-element.275.dq, bf16[896,768]{1,0:T(8,128)(2,1)} %get-tuple-element.276.dk, bf16[896,768]{1,0:T(8,128)(2,1)} %get-tuple-element.277.dv, bf16[4,2,2,48,768]{4,3,2,1,0:T(8,128)(2,1)} %get-tuple-element.278.wq, ...), custom_call_target="tpu_custom_call" | custom-call | flops 3300000000 | bytes 1024 | tf_op jit(solution)/shard_map/pallas_call | solution.py:361
  249.2 2.8 collective-permute-done.29
  252.0 1.7 add_convert_fusion.4
  255.1 4.7 %shard_map.429 = (f32[325,1,768]{2,1,0:T(1,128)}, f32[513,1,768]{2,1,0:T(1,128)}) custom-call(bf16[325,768]{1,0:T(8,128)(2,1)} %get-tuple-element.291.image_low, bf16[513,768]{1,0:T(8,128)(2,1)} %get-tuple-element.292.text_low, bf16[4,2,2,48,768]{4,3,2,1,0:T(8,128)(2,1)} %get-tuple-element.299.w_image, bf16[4,2,2,48,768]{4,3,2,1,0:T(8,128)(2,1)} %get-tuple-element.300.w_text), custom_call_target="tpu_custom_call" | custom-call | flops 1320000000 | bytes 1024 | tf_op jit(solution)/shard_map/pallas_call | solution.py:361
  259.7 5.3 %shard_map.428 = (bf16[16,112,384]{2,1,0:T(8,128)(2,1)}, bf16[16,112,384]{2,1,0:T(8,128)(2,1)}) custom-call(s32[4]{0:T(128)} %pad_add_fusion.at_ref.at, bf16[325,768]{1,0:T(8,128)(2,1)} %bitcast.222, bf16[513,768]{1,0:T(8,128)(2,1)} %bitcast.220, bf16[325,768]{1,0:T(8,128)(2,1)} %get-tuple-element.291.image_low, ...), custom_call_target="tpu_custom_call" | custom-call | flops 1650000000 | bytes 1024 | tf_op jit(solution)/shard_map/pallas_call | solution.py:361
  265.0 5.7 %collective-permute-done.31 = bf16[384,384]{1,0:T(8,128)(2,1)} collective-permute-done((bf16[384,384]{1,0:T(8,128)(2,1)}, bf16[384,384]{1,0:T(8,128)(2,1)}, u32[]{:S(2)}, u32[]{:S(2)}) %collective-permute-start.31) | collective-permute-done | bytes 294944 | tf_op jit(solution)/shard_map/chips_8_8/ppermute | solution.py:391
  270.7 1.5 fusion.4
  272.2 1.1 collective-permute-start.34
  273.3 1.5 fusion.5
  274.8 1.2 add_convert_fusion.13
  276.0 6.2 %collective-permute-done.34 = bf16[4,192,384]{2,1,0:T(8,128)(2,1)S(1)} collective-permute-done((bf16[4,192,384]{2,1,0:T(8,128)(2,1)S(1)}, bf16[4,192,384]{2,1,0:T(8,128)(2,1)S(1)}, u32[]{:S(2)}, u32[]{:S(2)}) %collective-permute-start.34) | collective-permute-done | bytes 589856 | tf_op jit(solution)/shard_map/chips_1_2/ppermute | solution.py:391
  283.4 2.5 collective-permute-start.37
  285.9 1.8 collective-permute-start.38
  287.8 4.3 %collective-permute-done.36 = bf16[192,384]{1,0:T(8,128)(2,1)S(1)} collective-permute-done((bf16[192,384]{1,0:T(8,128)(2,1)S(1)}, bf16[192,384]{1,0:T(8,128)(2,1)S(1)}, u32[]{:S(2)}, u32[]{:S(2)}) %collective-permute-start.36) | collective-permute-done | bytes 147488 | tf_op jit(solution)/shard_map/chips_4_4/ppermute | solution.py:391
  292.1 5.3 %collective-permute-done.37 = bf16[192,384]{1,0:T(8,128)(2,1)S(1)} collective-permute-done((bf16[192,384]{1,0:T(8,128)(2,1)S(1)}, bf16[192,384]{1,0:T(8,128)(2,1)S(1)}, u32[]{:S(2)}, u32[]{:S(2)}) %collective-permute-start.37) | collective-permute-done | bytes 147488 | tf_op jit(solution)/shard_map/chips_8_8/ppermute | solution.py:391
  297.7 1.1 collective-permute-start.40
  300.4 4.7 %collective-permute-done.40 = bf16[4,112,384]{2,1,0:T(8,128)(2,1)S(1)} collective-permute-done((bf16[4,112,384]{2,1,0:T(8,128)(2,1)S(1)}, bf16[4,112,384]{2,1,0:T(8,128)(2,1)S(1)}, u32[]{:S(2)}, u32[]{:S(2)}) %collective-permute-start.40) | collective-permute-done | bytes 344096 | tf_op jit(solution)/shard_map/chips_1_2/ppermute | solution.py:391
  305.3 3.4 %collective-permute-start.42 = (bf16[112,384]{1,0:T(8,128)(2,1)S(1)}, bf16[112,384]{1,0:T(8,128)(2,1)S(1)}, u32[]{:S(2)}, u32[]{:S(2)}) collective-permute-start(bf16[112,384]{1,0:T(8,128)(2,1)S(1)} %get-tuple-element.366), channel_id=1, source_target_pairs={{0,8},{1,9},{2,10},{3,11},{4,12},{5,13},{6,14},{7,15},{8,0},{9,1},... | collective-permute-start | bytes 258056 | tf_op jit(solution)/shard_map/chips_4_4/ppermute | solution.py:391
  309.3 1.8 collective-permute-start.44
  313.9 3.4 %collective-permute-done.43 = bf16[112,384]{1,0:T(8,128)(2,1)S(1)} collective-permute-done((bf16[112,384]{1,0:T(8,128)(2,1)S(1)}, bf16[112,384]{1,0:T(8,128)(2,1)S(1)}, u32[]{:S(2)}, u32[]{:S(2)}) %collective-permute-start.43) | collective-permute-done | bytes 86048 | tf_op jit(solution)/shard_map/chips_8_8/ppermute | solution.py:391
  317.4 1.3 collective-permute-done.45
  (148 shorter events, 22.5 us)
Async XLA Ops:
  4.3 20.4 %copy-start.15 = (bf16[256,384]{1,0:T(8,128)(2,1)S(1)}, bf16[256,384]{1,0:T(8,128)(2,1)}, u32[]{:S(2)}) copy-start(bf16[256,384]{1,0:T(8,128)(2,1)} %shard_map.416) | copy-start | bytes 589828
  4.3 11.6 %collective-permute-start = (bf16[256,384]{1,0:T(8,128)(2,1)}, bf16[256,384]{1,0:T(8,128)(2,1)S(1)}, u32[]{:S(2)}, u32[]{:S(2)}) collective-permute-start(bf16[256,384]{1,0:T(8,128)(2,1)} %shard_map.416), channel_id=1, source_target_pairs={{0,8},{1,9},{2,10},{3,11},{4,12},{5,13},{6,14},{7,15},{8,0},{9,1},... | collective-permute-start | bytes 589832 | tf_op jit(solution)/shard_map/chips_4_4/ppermute | solution.py:391
  7.4 17.4 %collective-permute-start.1 = (bf16[256,384]{1,0:T(8,128)(2,1)}, bf16[256,384]{1,0:T(8,128)(2,1)S(1)}, u32[]{:S(2)}, u32[]{:S(2)}) collective-permute-start(bf16[256,384]{1,0:T(8,128)(2,1)} %shard_map.416), channel_id=1, source_target_pairs={{0,16},{1,17},{2,18},{3,19},{4,20},{5,21},{6,22},{7,23},{8,24},{9,... | collective-permute-start | bytes 589832 | tf_op jit(solution)/shard_map/chips_8_8/ppermute | solution.py:391
  9.9 14.8 %collective-permute-start.2 = (bf16[256,384]{1,0:T(8,128)(2,1)}, bf16[256,384]{1,0:T(8,128)(2,1)S(1)}, u32[]{:S(2)}, u32[]{:S(2)}) collective-permute-start(bf16[256,384]{1,0:T(8,128)(2,1)} %shard_map.416), channel_id=1, source_target_pairs={{0,24},{1,25},{2,26},{3,27},{4,28},{5,29},{6,30},{7,31},{8,16},{9,... | collective-permute-start | bytes 589832 | tf_op jit(solution)/shard_map/chips_12_12/ppermute | solution.py:391
  13.4 13.0 %copy-start.16 = (bf16[144,384]{1,0:T(8,128)(2,1)S(1)}, bf16[144,384]{1,0:T(8,128)(2,1)}, u32[]{:S(2)}) copy-start(bf16[144,384]{1,0:T(8,128)(2,1)} %shard_map.417) | copy-start | bytes 331780
  24.9 14.9 %collective-permute-start.3 = (bf16[4,256,384]{2,1,0:T(8,128)(2,1)S(1)}, bf16[4,256,384]{2,1,0:T(8,128)(2,1)S(1)}, u32[]{:S(2)}, u32[]{:S(2)}) collective-permute-start(bf16[4,256,384]{2,1,0:T(8,128)(2,1)S(1)} %pad_maximum_fusion.5), channel_id=1, source_target_pairs={{0,2},{1,5},{2,0},{3,7},{4,6},{5,1},{6,4},{7,3},{8,10},{9,13},{10,... | collective-permute-start | bytes 2359304 | tf_op jit(solution)/shard_map/chips_1_2/ppermute | solution.py:391
  26.4 7.2 %collective-permute-start.4 = (bf16[144,384]{1,0:T(8,128)(2,1)S(1)}, bf16[144,384]{1,0:T(8,128)(2,1)S(1)}, u32[]{:S(2)}, u32[]{:S(2)}) collective-permute-start(bf16[144,384]{1,0:T(8,128)(2,1)S(1)} %copy-done.16), channel_id=1, source_target_pairs={{0,8},{1,9},{2,10},{3,11},{4,12},{5,13},{6,14},{7,15},{8,0},{9,1},... | collective-permute-start | bytes 331784 | tf_op jit(solution)/shard_map/chips_4_4/ppermute | solution.py:391
  29.8 10.0 %collective-permute-start.5 = (bf16[144,384]{1,0:T(8,128)(2,1)S(1)}, bf16[144,384]{1,0:T(8,128)(2,1)S(1)}, u32[]{:S(2)}, u32[]{:S(2)}) collective-permute-start(bf16[144,384]{1,0:T(8,128)(2,1)S(1)} %copy-done.16), channel_id=1, source_target_pairs={{0,16},{1,17},{2,18},{3,19},{4,20},{5,21},{6,22},{7,23},{8,24},{9,... | collective-permute-start | bytes 331784 | tf_op jit(solution)/shard_map/chips_8_8/ppermute | solution.py:391
  30.8 9.0 %collective-permute-start.6 = (bf16[144,384]{1,0:T(8,128)(2,1)S(1)}, bf16[144,384]{1,0:T(8,128)(2,1)S(1)}, u32[]{:S(2)}, u32[]{:S(2)}) collective-permute-start(bf16[144,384]{1,0:T(8,128)(2,1)S(1)} %copy-done.16), channel_id=1, source_target_pairs={{0,24},{1,25},{2,26},{3,27},{4,28},{5,29},{6,30},{7,31},{8,16},{9,... | collective-permute-start | bytes 331784 | tf_op jit(solution)/shard_map/chips_12_12/ppermute | solution.py:391
  40.0 21.8 %copy-start.6 = (bf16[2,4,256,384]{3,2,1,0:T(8,128)(2,1)}, bf16[2,4,256,384]{3,2,1,0:T(8,128)(2,1)S(1)}, u32[]{:S(2)}) copy-start(bf16[2,4,256,384]{3,2,1,0:T(8,128)(2,1)S(1)} %pad_maximum_fusion.s8) | copy-start | bytes 4718596
  40.0 20.5 %collective-permute-start.7 = (bf16[2,4,256,384]{3,2,1,0:T(8,128)(2,1)S(1)}, bf16[2,4,256,384]{3,2,1,0:T(8,128)(2,1)S(1)}, u32[]{:S(2)}, u32[]{:S(2)}) collective-permute-start(bf16[2,4,256,384]{3,2,1,0:T(8,128)(2,1)S(1)} %pad_maximum_fusion.s8), channel_id=1, source_target_pairs={{0,4},{1,3},{2,6},{3,1},{4,0},{5,7},{6,2},{7,5},{8,12},{9,11},{10,... | collective-permute-start | bytes 4718600 | tf_op jit(solution)/shard_map/chips_2_1/ppermute | solution.py:391
  40.5 19.9 %collective-permute-start.8 = (bf16[2,4,256,384]{3,2,1,0:T(8,128)(2,1)S(1)}, bf16[2,4,256,384]{3,2,1,0:T(8,128)(2,1)S(1)}, u32[]{:S(2)}, u32[]{:S(2)}) collective-permute-start(bf16[2,4,256,384]{3,2,1,0:T(8,128)(2,1)S(1)} %pad_maximum_fusion.s8), channel_id=1, source_target_pairs={{0,1},{1,0},{2,3},{3,2},{4,5},{5,4},{6,7},{7,6},{8,9},{9,8},{10,11... | collective-permute-start | bytes 4718600 | tf_op jit(solution)/shard_map/between_cores/ppermute | solution.py:382
  40.7 18.7 %collective-permute-start.10 = (bf16[288,384]{1,0:T(8,128)(2,1)S(1)}, bf16[288,384]{1,0:T(8,128)(2,1)S(1)}, u32[]{:S(2)}, u32[]{:S(2)}) collective-permute-start(bf16[288,384]{1,0:T(8,128)(2,1)S(1)} %copy-done.14), channel_id=1, source_target_pairs={{0,16},{1,17},{2,18},{3,19},{4,20},{5,21},{6,22},{7,23},{8,24},{9,... | collective-permute-start | bytes 663560 | tf_op jit(solution)/shard_map/chips_8_8/ppermute | solution.py:391
  43.4 16.0 %collective-permute-start.11 = (bf16[288,384]{1,0:T(8,128)(2,1)S(1)}, bf16[288,384]{1,0:T(8,128)(2,1)S(1)}, u32[]{:S(2)}, u32[]{:S(2)}) collective-permute-start(bf16[288,384]{1,0:T(8,128)(2,1)S(1)} %copy-done.14), channel_id=1, source_target_pairs={{0,24},{1,25},{2,26},{3,27},{4,28},{5,29},{6,30},{7,31},{8,16},{9,... | collective-permute-start | bytes 663560 | tf_op jit(solution)/shard_map/chips_12_12/ppermute | solution.py:391
  44.8 15.4 %collective-permute-start.9 = (bf16[288,384]{1,0:T(8,128)(2,1)S(1)}, bf16[288,384]{1,0:T(8,128)(2,1)S(1)}, u32[]{:S(2)}, u32[]{:S(2)}) collective-permute-start(bf16[288,384]{1,0:T(8,128)(2,1)S(1)} %copy-done.14), channel_id=1, source_target_pairs={{0,8},{1,9},{2,10},{3,11},{4,12},{5,13},{6,14},{7,15},{8,0},{9,1},... | collective-permute-start | bytes 663560 | tf_op jit(solution)/shard_map/chips_4_4/ppermute | solution.py:391
  60.4 3.6 %copy-start.18 = (bf16[2,4,256,384]{3,2,1,0:T(8,128)(2,1)}, bf16[2,4,256,384]{3,2,1,0:T(8,128)(2,1)S(1)}, u32[]{:S(2)}) copy-start(bf16[2,4,256,384]{3,2,1,0:T(8,128)(2,1)S(1)} %collective-permute-done.7.r8) | copy-start | bytes 4718596
  60.5 1.2 copy-start.19
  60.5 5.4 %collective-permute-start.14 = (bf16[2,4,256,384]{3,2,1,0:T(8,128)(2,1)S(1)}, bf16[2,4,256,384]{3,2,1,0:T(8,128)(2,1)S(1)}, u32[]{:S(2)}, u32[]{:S(2)}) collective-permute-start(bf16[2,4,256,384]{3,2,1,0:T(8,128)(2,1)S(1)} %collective-permute-done.7.r8), channel_id=1, source_target_pairs={{0,1},{1,0},{2,3},{3,2},{4,5},{5,4},{6,7},{7,6},{8,9},{9,8},{10,11... | collective-permute-start | bytes 4718600 | tf_op jit(solution)/shard_map/between_cores/ppermute | solution.py:382
  61.8 17.9 %collective-permute-start.13 = (bf16[4,288,384]{2,1,0:T(8,128)(2,1)S(1)}, bf16[4,288,384]{2,1,0:T(8,128)(2,1)S(1)}, u32[]{:S(2)}, u32[]{:S(2)}) collective-permute-start(bf16[4,288,384]{2,1,0:T(8,128)(2,1)S(1)} %pad_maximum_fusion.3), channel_id=1, source_target_pairs={{0,2},{1,5},{2,0},{3,7},{4,6},{5,1},{6,4},{7,3},{8,10},{9,13},{10,... | collective-permute-start | bytes 2654216 | tf_op jit(solution)/shard_map/chips_1_2/ppermute | solution.py:391
  64.7 15.0 %collective-permute-start.12 = (bf16[4,144,384]{2,1,0:T(8,128)(2,1)S(1)}, bf16[4,144,384]{2,1,0:T(8,128)(2,1)S(1)}, u32[]{:S(2)}, u32[]{:S(2)}) collective-permute-start(bf16[4,144,384]{2,1,0:T(8,128)(2,1)S(1)} %pad_maximum_fusion.9), channel_id=1, source_target_pairs={{0,2},{1,5},{2,0},{3,7},{4,6},{5,1},{6,4},{7,3},{8,10},{9,13},{10,... | collective-permute-start | bytes 1327112 | tf_op jit(solution)/shard_map/chips_1_2/ppermute | solution.py:391
  79.8 2.5 copy-start
  79.8 19.5 %collective-permute-start.15 = (bf16[2,4,144,384]{3,2,1,0:T(8,128)(2,1)S(1)}, bf16[2,4,144,384]{3,2,1,0:T(8,128)(2,1)}, u32[]{:S(2)}, u32[]{:S(2)}) collective-permute-start(bf16[2,4,144,384]{3,2,1,0:T(8,128)(2,1)S(1)} %pad_maximum_fusion.4.s8), channel_id=1, source_target_pairs={{0,4},{1,3},{2,6},{3,1},{4,0},{5,7},{6,2},{7,5},{8,12},{9,11},{10,... | collective-permute-start | bytes 2654216 | tf_op jit(solution)/shard_map/chips_2_1/ppermute | solution.py:391
  81.0 18.3 %collective-permute-start.17 = (bf16[2,4,144,384]{3,2,1,0:T(8,128)(2,1)S(1)}, bf16[2,4,144,384]{3,2,1,0:T(8,128)(2,1)}, u32[]{:S(2)}, u32[]{:S(2)}) collective-permute-start(bf16[2,4,144,384]{3,2,1,0:T(8,128)(2,1)S(1)} %pad_maximum_fusion.4.s8), channel_id=1, source_target_pairs={{0,1},{1,0},{2,3},{3,2},{4,5},{5,4},{6,7},{7,6},{8,9},{9,8},{10,11... | collective-permute-start | bytes 2654216 | tf_op jit(solution)/shard_map/between_cores/ppermute | solution.py:382
  81.2 19.8 %copy-start.1 = (bf16[2,4,96,384]{3,2,1,0:T(8,128)(2,1)}, bf16[2,4,96,384]{3,2,1,0:T(8,128)(2,1)S(1)}, u32[]{:S(2)}) copy-start(bf16[2,4,96,384]{3,2,1,0:T(8,128)(2,1)S(1)} %pad_maximum_fusion.7.s_hi) | copy-start | bytes 1769476
  81.2 18.1 %collective-permute-start.16 = (bf16[2,4,96,384]{3,2,1,0:T(8,128)(2,1)S(1)}, bf16[2,4,96,384]{3,2,1,0:T(8,128)(2,1)}, u32[]{:S(2)}, u32[]{:S(2)}) collective-permute-start(bf16[2,4,96,384]{3,2,1,0:T(8,128)(2,1)S(1)} %pad_maximum_fusion.7.s_hi), channel_id=1, source_target_pairs={{0,4},{1,3},{2,6},{3,1},{4,0},{5,7},{6,2},{7,5},{8,12},{9,11},{10,... | collective-permute-start | bytes 1769480 | tf_op jit(solution)/shard_map/chips_2_1/ppermute | solution.py:391
  82.4 18.2 %copy-start.8 = (bf16[2,4,192,384]{3,2,1,0:T(8,128)(2,1)}, bf16[2,4,192,384]{3,2,1,0:T(8,128)(2,1)S(1)}, u32[]{:S(2)}) copy-start(bf16[2,4,192,384]{3,2,1,0:T(8,128)(2,1)S(1)} %pad_maximum_fusion.1.s8) | copy-start | bytes 3538948
  99.3 16.3 %collective-permute-start.18 = (bf16[2,4,192,384]{3,2,1,0:T(8,128)(2,1)S(1)}, bf16[2,4,192,384]{3,2,1,0:T(8,128)(2,1)}, u32[]{:S(2)}, u32[]{:S(2)}) collective-permute-start(bf16[2,4,192,384]{3,2,1,0:T(8,128)(2,1)S(1)} %pad_maximum_fusion.1.s8), channel_id=1, source_target_pairs={{0,4},{1,3},{2,6},{3,1},{4,0},{5,7},{6,2},{7,5},{8,12},{9,11},{10,... | collective-permute-start | bytes 3538952 | tf_op jit(solution)/shard_map/chips_2_1/ppermute | solution.py:391
  100.5 15.1 %collective-permute-start.20 = (bf16[2,4,192,384]{3,2,1,0:T(8,128)(2,1)S(1)}, bf16[2,4,192,384]{3,2,1,0:T(8,128)(2,1)}, u32[]{:S(2)}, u32[]{:S(2)}) collective-permute-start(bf16[2,4,192,384]{3,2,1,0:T(8,128)(2,1)S(1)} %pad_maximum_fusion.1.s8), channel_id=1, source_target_pairs={{0,1},{1,0},{2,3},{3,2},{4,5},{5,4},{6,7},{7,6},{8,9},{9,8},{10,11... | collective-permute-start | bytes 3538952 | tf_op jit(solution)/shard_map/between_cores/ppermute | solution.py:382
  100.5 11.3 %collective-permute-start.21 = (bf16[2,4,144,384]{3,2,1,0:T(8,128)(2,1)}, bf16[2,4,144,384]{3,2,1,0:T(8,128)(2,1)S(1)}, u32[]{:S(2)}, u32[]{:S(2)}) collective-permute-start(bf16[2,4,144,384]{3,2,1,0:T(8,128)(2,1)} %collective-permute-done.15.r8), channel_id=1, source_target_pairs={{0,1},{1,0},{2,3},{3,2},{4,5},{5,4},{6,7},{7,6},{8,9},{9,8},{10,11... | collective-permute-start | bytes 2654216 | tf_op jit(solution)/shard_map/between_cores/ppermute | solution.py:382
  101.0 10.7 %collective-permute-start.19 = (bf16[2,4,96,384]{3,2,1,0:T(8,128)(2,1)S(1)}, bf16[2,4,96,384]{3,2,1,0:T(8,128)(2,1)S(1)}, u32[]{:S(2)}, u32[]{:S(2)}) collective-permute-start(bf16[2,4,96,384]{3,2,1,0:T(8,128)(2,1)S(1)} %pad_maximum_fusion.7.s_hi), channel_id=1, source_target_pairs={{0,1},{1,0},{2,3},{3,2},{4,5},{5,4},{6,7},{7,6},{8,9},{9,8},{10,11... | collective-permute-start | bytes 1769480 | tf_op jit(solution)/shard_map/between_cores/ppermute | solution.py:382
  101.0 10.7 %collective-permute-start.22 = (bf16[2,4,96,384]{3,2,1,0:T(8,128)(2,1)}, bf16[2,4,96,384]{3,2,1,0:T(8,128)(2,1)S(1)}, u32[]{:S(2)}, u32[]{:S(2)}) collective-permute-start(bf16[2,4,96,384]{3,2,1,0:T(8,128)(2,1)} %collective-permute-done.16.r_hi), channel_id=1, source_target_pairs={{0,1},{1,0},{2,3},{3,2},{4,5},{5,4},{6,7},{7,6},{8,9},{9,8},{10,11... | collective-permute-start | bytes 1769480 | tf_op jit(solution)/shard_map/between_cores/ppermute | solution.py:382
  111.8 3.9 %copy-start.10 = (bf16[2,4,96,384]{3,2,1,0:T(8,128)(2,1)}, bf16[2,4,96,384]{3,2,1,0:T(8,128)(2,1)S(1)}, u32[]{:S(2)}) copy-start(bf16[2,4,96,384]{3,2,1,0:T(8,128)(2,1)S(1)} %collective-permute-done.19.sp_hi) | copy-start | bytes 1769476
  111.8 3.9 %copy-start.11 = (bf16[2,4,96,384]{3,2,1,0:T(8,128)(2,1)}, bf16[2,4,96,384]{3,2,1,0:T(8,128)(2,1)S(1)}, u32[]{:S(2)}) copy-start(bf16[2,4,96,384]{3,2,1,0:T(8,128)(2,1)S(1)} %collective-permute-done.22.rp_hi) | copy-start | bytes 1769476
  111.8 3.8 %copy-start.9 = (bf16[2,4,144,384]{3,2,1,0:T(8,128)(2,1)}, bf16[2,4,144,384]{3,2,1,0:T(8,128)(2,1)S(1)}, u32[]{:S(2)}) copy-start(bf16[2,4,144,384]{3,2,1,0:T(8,128)(2,1)S(1)} %collective-permute-done.21.r8p) | copy-start | bytes 2654212
  115.6 8.5 %collective-permute-start.23 = (bf16[2,4,192,384]{3,2,1,0:T(8,128)(2,1)}, bf16[2,4,192,384]{3,2,1,0:T(8,128)(2,1)S(1)}, u32[]{:S(2)}, u32[]{:S(2)}) collective-permute-start(bf16[2,4,192,384]{3,2,1,0:T(8,128)(2,1)} %collective-permute-done.18.r8), channel_id=1, source_target_pairs={{0,1},{1,0},{2,3},{3,2},{4,5},{5,4},{6,7},{7,6},{8,9},{9,8},{10,11... | collective-permute-start | bytes 3538952 | tf_op jit(solution)/shard_map/between_cores/ppermute | solution.py:382
  164.7 8.6 %collective-permute-start.24 = (bf16[16,192,384]{2,1,0:T(8,128)(2,1)}, bf16[16,192,384]{2,1,0:T(8,128)(2,1)}, u32[]{:S(2)}, u32[]{:S(2)}) collective-permute-start(bf16[16,192,384]{2,1,0:T(8,128)(2,1)} %get-tuple-element.238), channel_id=1, source_target_pairs={{0,1},{1,0},{2,3},{3,2},{4,5},{5,4},{6,7},{7,6},{8,9},{9,8},{10,11... | collective-permute-start | bytes 7077896 | tf_op jit(solution)/shard_map/between_cores/ppermute | solution.py:382
  165.2 8.1 %collective-permute-start.25 = (bf16[16,192,384]{2,1,0:T(8,128)(2,1)}, bf16[16,192,384]{2,1,0:T(8,128)(2,1)}, u32[]{:S(2)}, u32[]{:S(2)}) collective-permute-start(bf16[16,192,384]{2,1,0:T(8,128)(2,1)} %get-tuple-element.239), channel_id=1, source_target_pairs={{0,1},{1,0},{2,3},{3,2},{4,5},{5,4},{6,7},{7,6},{8,9},{9,8},{10,11... | collective-permute-start | bytes 7077896 | tf_op jit(solution)/shard_map/between_cores/ppermute | solution.py:382
  165.3 8.0 %copy-start.2 = (bf16[16,192,384]{2,1,0:T(8,128)(2,1)S(1)}, bf16[16,192,384]{2,1,0:T(8,128)(2,1)}, u32[]{:S(2)}) copy-start(bf16[16,192,384]{2,1,0:T(8,128)(2,1)} %get-tuple-element.255) | copy-start | bytes 7077892
  173.3 2.0 copy-start.4
  178.5 29.6 %collective-permute-start.26 = (bf16[4,2,384,384]{3,2,0,1:T(8,128)(2,1)}, bf16[4,2,384,384]{3,2,0,1:T(8,128)(2,1)S(1)}, u32[]{:S(2)}, u32[]{:S(2)}) collective-permute-start(bf16[4,2,384,384]{3,2,0,1:T(8,128)(2,1)} %maximum_maximum_fusion), channel_id=1, source_target_pairs={{0,4},{1,3},{2,6},{3,1},{4,0},{5,7},{6,2},{7,5},{8,12},{9,11},{10,... | collective-permute-start | bytes 7077896 | tf_op jit(solution)/shard_map/chips_2_1/ppermute | solution.py:391
  209.6 2.0 copy-start.3
  214.8 16.4 %collective-permute-start.27 = (bf16[4,384,384]{2,1,0:T(8,128)(2,1)}, bf16[4,384,384]{2,1,0:T(8,128)(2,1)S(1)}, u32[]{:S(2)}, u32[]{:S(2)}) collective-permute-start(bf16[4,384,384]{2,1,0:T(8,128)(2,1)} %get-tuple-element.352), channel_id=1, source_target_pairs={{0,2},{1,5},{2,0},{3,7},{4,6},{5,1},{6,4},{7,3},{8,10},{9,13},{10,... | collective-permute-start | bytes 3538952 | tf_op jit(solution)/shard_map/chips_1_2/ppermute | solution.py:391
  231.2 20.8 %collective-permute-start.30 = (bf16[16,192,384]{2,1,0:T(8,128)(2,1)}, bf16[16,192,384]{2,1,0:T(8,128)(2,1)}, u32[]{:S(2)}, u32[]{:S(2)}) collective-permute-start(bf16[16,192,384]{2,1,0:T(8,128)(2,1)} %get-tuple-element.270), channel_id=1, source_target_pairs={{0,1},{1,0},{2,3},{3,2},{4,5},{5,4},{6,7},{7,6},{8,9},{9,8},{10,11... | collective-permute-start | bytes 7077896 | tf_op jit(solution)/shard_map/between_cores/ppermute | solution.py:382
  232.3 16.9 %collective-permute-start.28 = (bf16[384,384]{1,0:T(8,128)(2,1)S(1)}, bf16[384,384]{1,0:T(8,128)(2,1)S(1)}, u32[]{:S(2)}, u32[]{:S(2)}) collective-permute-start(bf16[384,384]{1,0:T(8,128)(2,1)S(1)} %get-tuple-element.356), channel_id=1, source_target_pairs={{0,8},{1,9},{2,10},{3,11},{4,12},{5,13},{6,14},{7,15},{8,0},{9,1},... | collective-permute-start | bytes 884744 | tf_op jit(solution)/shard_map/chips_4_4/ppermute | solution.py:391
  236.3 15.7 %collective-permute-start.29 = (bf16[384,384]{1,0:T(8,128)(2,1)S(1)}, bf16[384,384]{1,0:T(8,128)(2,1)S(1)}, u32[]{:S(2)}, u32[]{:S(2)}) collective-permute-start(bf16[384,384]{1,0:T(8,128)(2,1)S(1)} %get-tuple-element.355), channel_id=1, source_target_pairs={{0,24},{1,25},{2,26},{3,27},{4,28},{5,29},{6,30},{7,31},{8,16},{9,... | collective-permute-start | bytes 884744 | tf_op jit(solution)/shard_map/chips_12_12/ppermute | solution.py:391
  238.3 13.7 %copy-start.5 = (bf16[16,192,384]{2,1,0:T(8,128)(2,1)S(1)}, bf16[16,192,384]{2,1,0:T(8,128)(2,1)}, u32[]{:S(2)}) copy-start(bf16[16,192,384]{2,1,0:T(8,128)(2,1)} %get-tuple-element.305) | copy-start | bytes 7077892
  252.0 1.7 copy-start.12
  253.9 16.9 %collective-permute-start.32 = (bf16[4,2,192,384]{3,2,0,1:T(8,128)(2,1)S(1)}, bf16[4,2,192,384]{3,2,0,1:T(8,128)(2,1)}, u32[]{:S(2)}, u32[]{:S(2)}) collective-permute-start(bf16[4,2,192,384]{3,2,0,1:T(8,128)(2,1)S(1)} %pad_maximum_fusion.2), channel_id=1, source_target_pairs={{0,4},{1,3},{2,6},{3,1},{4,0},{5,7},{6,2},{7,5},{8,12},{9,11},{10,... | collective-permute-start | bytes 3538952 | tf_op jit(solution)/shard_map/chips_2_1/ppermute | solution.py:391
  254.9 15.8 %collective-permute-start.31 = (bf16[384,384]{1,0:T(8,128)(2,1)}, bf16[384,384]{1,0:T(8,128)(2,1)}, u32[]{:S(2)}, u32[]{:S(2)}) collective-permute-start(bf16[384,384]{1,0:T(8,128)(2,1)} %get-tuple-element.284), channel_id=1, source_target_pairs={{0,16},{1,17},{2,18},{3,19},{4,20},{5,21},{6,22},{7,23},{8,24},{9,... | collective-permute-start | bytes 884744 | tf_op jit(solution)/shard_map/chips_8_8/ppermute | solution.py:391
  270.7 11.5 %collective-permute-start.33 = (bf16[16,112,384]{2,1,0:T(8,128)(2,1)}, bf16[16,112,384]{2,1,0:T(8,128)(2,1)S(1)}, u32[]{:S(2)}, u32[]{:S(2)}) collective-permute-start(bf16[16,112,384]{2,1,0:T(8,128)(2,1)} %get-tuple-element.303), channel_id=1, source_target_pairs={{0,1},{1,0},{2,3},{3,2},{4,5},{5,4},{6,7},{7,6},{8,9},{9,8},{10,11... | collective-permute-start | bytes 4128776 | tf_op jit(solution)/shard_map/between_cores/ppermute | solution.py:382
  272.2 2.5 copy-start.13
  272.2 9.9 %collective-permute-start.34 = (bf16[4,192,384]{2,1,0:T(8,128)(2,1)S(1)}, bf16[4,192,384]{2,1,0:T(8,128)(2,1)S(1)}, u32[]{:S(2)}, u32[]{:S(2)}) collective-permute-start(bf16[4,192,384]{2,1,0:T(8,128)(2,1)S(1)} %fusion.4), channel_id=1, source_target_pairs={{0,2},{1,5},{2,0},{3,7},{4,6},{5,1},{6,4},{7,3},{8,10},{9,13},{10,... | collective-permute-start | bytes 1769480 | tf_op jit(solution)/shard_map/chips_1_2/ppermute | solution.py:391
  274.8 7.4 %copy-start.7 = (bf16[16,112,384]{2,1,0:T(8,128)(2,1)S(1)}, bf16[16,112,384]{2,1,0:T(8,128)(2,1)}, u32[]{:S(2)}) copy-start(bf16[16,112,384]{2,1,0:T(8,128)(2,1)} %get-tuple-element.319) | copy-start | bytes 4128772
  282.4 15.0 %collective-permute-start.35 = (bf16[4,2,112,384]{3,2,0,1:T(8,128)(2,1)S(1)}, bf16[4,2,112,384]{3,2,0,1:T(8,128)(2,1)S(1)}, u32[]{:S(2)}, u32[]{:S(2)}) collective-permute-start(bf16[4,2,112,384]{3,2,0,1:T(8,128)(2,1)S(1)} %pad_maximum_fusion.6), channel_id=1, source_target_pairs={{0,4},{1,3},{2,6},{3,1},{4,0},{5,7},{6,2},{7,5},{8,12},{9,11},{10,... | collective-permute-start | bytes 2064392 | tf_op jit(solution)/shard_map/chips_2_1/ppermute | solution.py:391
  283.1 14.3 %collective-permute-start.39 = (bf16[384,384]{1,0:T(8,128)(2,1)S(1)}, bf16[384,384]{1,0:T(8,128)(2,1)S(1)}, u32[]{:S(2)}, u32[]{:S(2)}) collective-permute-start(bf16[384,384]{1,0:T(8,128)(2,1)S(1)} %add_convert_fusion.13), channel_id=1, source_target_pairs={{0,1},{1,0},{2,3},{3,2},{4,5},{5,4},{6,7},{7,6},{8,9},{9,8},{10,11... | collective-permute-start | bytes 884744 | tf_op jit(solution)/shard_map/between_cores/ppermute | solution.py:382
  283.3 8.8 %collective-permute-start.36 = (bf16[192,384]{1,0:T(8,128)(2,1)S(1)}, bf16[192,384]{1,0:T(8,128)(2,1)S(1)}, u32[]{:S(2)}, u32[]{:S(2)}) collective-permute-start(bf16[192,384]{1,0:T(8,128)(2,1)S(1)} %get-tuple-element.362), channel_id=1, source_target_pairs={{0,8},{1,9},{2,10},{3,11},{4,12},{5,13},{6,14},{7,15},{8,0},{9,1},... | collective-permute-start | bytes 442376 | tf_op jit(solution)/shard_map/chips_4_4/ppermute | solution.py:391
  283.4 14.0 %collective-permute-start.37 = (bf16[192,384]{1,0:T(8,128)(2,1)S(1)}, bf16[192,384]{1,0:T(8,128)(2,1)S(1)}, u32[]{:S(2)}, u32[]{:S(2)}) collective-permute-start(bf16[192,384]{1,0:T(8,128)(2,1)S(1)} %get-tuple-element.361), channel_id=1, source_target_pairs={{0,16},{1,17},{2,18},{3,19},{4,20},{5,21},{6,22},{7,23},{8,24},{9,... | collective-permute-start | bytes 442376 | tf_op jit(solution)/shard_map/chips_8_8/ppermute | solution.py:391
  285.9 11.4 %collective-permute-start.38 = (bf16[192,384]{1,0:T(8,128)(2,1)S(1)}, bf16[192,384]{1,0:T(8,128)(2,1)S(1)}, u32[]{:S(2)}, u32[]{:S(2)}) collective-permute-start(bf16[192,384]{1,0:T(8,128)(2,1)S(1)} %get-tuple-element.360), channel_id=1, source_target_pairs={{0,24},{1,25},{2,26},{3,27},{4,28},{5,29},{6,30},{7,31},{8,16},{9,... | collective-permute-start | bytes 442376 | tf_op jit(solution)/shard_map/chips_12_12/ppermute | solution.py:391
  297.7 7.3 %collective-permute-start.40 = (bf16[4,112,384]{2,1,0:T(8,128)(2,1)S(1)}, bf16[4,112,384]{2,1,0:T(8,128)(2,1)S(1)}, u32[]{:S(2)}, u32[]{:S(2)}) collective-permute-start(bf16[4,112,384]{2,1,0:T(8,128)(2,1)S(1)} %fusion.6), channel_id=1, source_target_pairs={{0,2},{1,5},{2,0},{3,7},{4,6},{5,1},{6,4},{7,3},{8,10},{9,13},{10,... | collective-permute-start | bytes 1032200 | tf_op jit(solution)/shard_map/chips_1_2/ppermute | solution.py:391
  298.9 1.4 collective-permute-start.41
  305.3 8.5 %collective-permute-start.42 = (bf16[112,384]{1,0:T(8,128)(2,1)S(1)}, bf16[112,384]{1,0:T(8,128)(2,1)S(1)}, u32[]{:S(2)}, u32[]{:S(2)}) collective-permute-start(bf16[112,384]{1,0:T(8,128)(2,1)S(1)} %get-tuple-element.366), channel_id=1, source_target_pairs={{0,8},{1,9},{2,10},{3,11},{4,12},{5,13},{6,14},{7,15},{8,0},{9,1},... | collective-permute-start | bytes 258056 | tf_op jit(solution)/shard_map/chips_4_4/ppermute | solution.py:391
  308.7 8.5 %collective-permute-start.43 = (bf16[112,384]{1,0:T(8,128)(2,1)S(1)}, bf16[112,384]{1,0:T(8,128)(2,1)S(1)}, u32[]{:S(2)}, u32[]{:S(2)}) collective-permute-start(bf16[112,384]{1,0:T(8,128)(2,1)S(1)} %get-tuple-element.365), channel_id=1, source_target_pairs={{0,16},{1,17},{2,18},{3,19},{4,20},{5,21},{6,22},{7,23},{8,24},{9,... | collective-permute-start | bytes 258056 | tf_op jit(solution)/shard_map/chips_8_8/ppermute | solution.py:391
  309.3 8.0 %collective-permute-start.44 = (bf16[112,384]{1,0:T(8,128)(2,1)S(1)}, bf16[112,384]{1,0:T(8,128)(2,1)S(1)}, u32[]{:S(2)}, u32[]{:S(2)}) collective-permute-start(bf16[112,384]{1,0:T(8,128)(2,1)S(1)} %get-tuple-element.364), channel_id=1, source_target_pairs={{0,24},{1,25},{2,26},{3,27},{4,28},{5,29},{6,30},{7,31},{8,16},{9,... | collective-permute-start | bytes 258056 | tf_op jit(solution)/shard_map/chips_12_12/ppermute | solution.py:391
  317.3 1.3 collective-permute-start.45
  (4 other events, 4.3 us)

commit v5 on v4

--- a/solution.py
+++ b/solution.py
@@ -411,7 +411,8 @@
             rows[...] = jnp.zeros_like(rows)
             for row in range(12):
                 source = ins[len(order) + row]
-                rows[row : row + 1, 0 : source.shape[1]] = source[...].astype(FULL)
+                width = source.shape[0]
+                rows[row : row + 1, 0:width] = source[...].astype(FULL).reshape(1, width)
             out[offset : offset + VEC_ROWS, :] = rows[...].astype(LOW)
             offset += VEC_ROWS
             continue
@@ -429,7 +430,7 @@
     ins = [shards[16 if i in ("low", "high") else i] for i in chunk if i != "vec"]
     scratch = ()
     if "vec" in chunk:
-        ins += [shards[i].reshape(1, -1) for i in VECTORS]
+        ins += [shards[i] for i in VECTORS]
         scratch = (pltpu.VMEM((VEC_ROWS, LANES), FULL),)
     kernel = functools.partial(pack_kernel, chunk)
     return call(kernel, 1, [shape((rows, LANES))], place.scalars, *ins, scratch=scratch)[0]
@@ -827,7 +828,7 @@
         feed_kernel,
         grid_spec=grid,
         out_shape=outs,
-        compiler_params=pltpu.CompilerParams(vmem_limit_bytes=60 * 2**20),
+        compiler_params=pltpu.CompilerParams(vmem_limit_bytes=63 * 2**20),
         cost_estimate=cost(40),
     )(place.scalars, second, cot, middle, vec, w_hid, hid, *pieces)
 

time: 325 us -> 323 us (level)
  no operation moved by 1% of the time
where the time goes in v5:
time: 323 us; the launch traced here: 319 us
  Pallas kernels  155 us (48%)
  waiting for transfers between devices  82.8 us (26%)
  starting transfers between devices  48 us (15%)
  other arithmetic  25.2 us (8%)
  local copies, waits for them, and re-layouts  5.78 us (2%)
    ppermute x31, waiting for transfers between devices, to_chip(): return lax.ppermute(values, BOTH, pairs)  81.2 us
    pallas_call x10, Pallas kernels, call(): pl.pallas_call(kernel, out_shape=tuple(outs), in_specs=specs, out_specs=t...  65.9 us
    ppermute x31, starting transfers between devices, to_chip(): return lax.ppermute(values, BOTH, pairs)  46.1 us
    pallas_call x1, Pallas kernels, feed(): pl.pallas_call(feed_kernel, grid_spec=grid, out_shape=outs, compiler_para...  39.6 us
    pallas_call x1, Pallas kernels, attend_back(): pl.pallas_call(attend_back_kernel, grid=(HEADS // 2,), out_shape=(shape((...  28.4 us
    pallas_call x2, Pallas kernels, attend(): pl.pallas_call(kernel, grid=(count,), out_shape=(shape((PADDED, WIDTH)),...  20.9 us
    convert_element_type x13, other arithmetic, to_low(): return values.astype(jnp.bfloat16)  8.65 us
  transfers between devices with their start and end apart: 46, of which 20 were waited for; matrix products, arithmetic and copies ran while one was open for 3% of the time, Pallas kernels for 35%

profile of v5, /device:TPU:0, one launch (start us, length us, event | category | flops | bytes accessed | tf_op | source)
XLA Modules:
  0.0 319.2 jit_solution(7808914337287037966)
XLA Ops:
  1.3 1.9 shard_map.416
  3.1 3.0 collective-permute-start
  6.1 2.6 collective-permute-start.1
  8.7 1.8 shard_map.418
  10.5 1.7 shard_map.417
  12.2 2.6 collective-permute-done
  14.8 8.7 %collective-permute-done.1 = bf16[256,384]{1,0:T(8,128)(2,1)S(1)} collective-permute-done((bf16[256,384]{1,0:T(8,128)(2,1)}, bf16[256,384]{1,0:T(8,128)(2,1)S(1)}, u32[]{:S(2)}, u32[]{:S(2)}) %collective-permute-start.1) | collective-permute-done | bytes 196640 | tf_op jit(solution)/shard_map/chips_8_8/ppermute | solution.py:391
  23.6 1.6 collective-permute-start.3
  25.2 3.4 %collective-permute-start.4 = (bf16[144,384]{1,0:T(8,128)(2,1)S(1)}, bf16[144,384]{1,0:T(8,128)(2,1)S(1)}, u32[]{:S(2)}, u32[]{:S(2)}) collective-permute-start(bf16[144,384]{1,0:T(8,128)(2,1)S(1)} %copy-done.16), channel_id=1, source_target_pairs={{0,8},{1,9},{2,10},{3,11},{4,12},{5,13},{6,14},{7,15},{8,0},{9,1},... | collective-permute-start | bytes 331784 | tf_op jit(solution)/shard_map/chips_4_4/ppermute | solution.py:391
  28.6 1.0 collective-permute-start.5
  29.6 1.5 collective-permute-start.6
  31.0 1.3 collective-permute-done.4
  32.4 6.2 %collective-permute-done.5 = bf16[144,384]{1,0:T(8,128)(2,1)S(1)} collective-permute-done((bf16[144,384]{1,0:T(8,128)(2,1)S(1)}, bf16[144,384]{1,0:T(8,128)(2,1)S(1)}, u32[]{:S(2)}, u32[]{:S(2)}) %collective-permute-start.5) | collective-permute-done | bytes 110624 | tf_op jit(solution)/shard_map/chips_8_8/ppermute | solution.py:391
  39.5 2.7 collective-permute-start.10
  42.1 1.4 collective-permute-start.11
  43.7 14.5 %collective-permute-done.10 = bf16[288,384]{1,0:T(8,128)(2,1)S(1)} collective-permute-done((bf16[288,384]{1,0:T(8,128)(2,1)S(1)}, bf16[288,384]{1,0:T(8,128)(2,1)S(1)}, u32[]{:S(2)}, u32[]{:S(2)}) %collective-permute-start.10) | collective-permute-done | bytes 221216 | tf_op jit(solution)/shard_map/chips_8_8/ppermute | solution.py:391
  59.3 1.1 copy-done.19
  60.6 1.6 collective-permute-start.13
  64.6 1.1 copy-done.20
  65.8 11.9 %shard_map.419 = (bf16[4,2,2,48,768]{4,3,2,1,0:T(8,128)(2,1)}, bf16[4,2,2,48,768]{4,3,2,1,0:T(8,128)(2,1)}, bf16[4,2,2,48,768]{4,3,2,1,0:T(8,128)(2,1)}, bf16[4,...) custom-call(s32[4]{0:T(128)} %pad_add_fusion.at_ref.at, ...), custom_call_target="tpu_custom_call" | custom-call | flops 3600000000 | bytes 1024 | tf_op jit(solution)/shard_map/pallas_call | solution.py:361
  78.6 1.3 collective-permute-start.15
  81.2 10.6 %shard_map.420 = (bf16[896,768]{1,0:T(8,128)(2,1)}, f32[6,8,896]{2,1,0:T(8,128)}) custom-call(s32[2]{0:T(128)} %pad_add_fusion.1.live, bf16[896,768]{1,0:T(8,128)(2,1)} %get-tuple-element.210.q, bf16[896,768]{1,0:T(8,128)(2,1)} %get-tuple-element.211.k, bf16[896,768]{1,0:T(8,128)(2,1)} %get-tuple-element.212.v), custom_call_target="tpu_custom_call" | custom-call | flops 2700000000 | bytes 1024 | tf_op jit(solution)/shard_map/pallas_call | solution.py:607
  91.8 6.3 %collective-permute-done.16.r_hi = bf16[2,4,96,384]{3,2,1,0:T(8,128)(2,1)} collective-permute-done((bf16[2,4,96,384]{3,2,1,0:T(8,128)(2,1)S(1)}, bf16[2,4,96,384]{3,2,1,0:T(8,128)(2,1)}, u32[]{:S(2)}, u32[]{:S(2)}) %collective-permute-start.16) | collective-permute-done | bytes 589856 | tf_op jit(solution)/shard_map/chips_2_1/ppermute | solution.py:391
  98.1 1.2 collective-permute-start.18
  100.3 10.2 %shard_map.421 = (bf16[896,768]{1,0:T(8,128)(2,1)}, f32[6,8,896]{2,1,0:T(8,128)}) custom-call(s32[2]{0:T(128)} %pad_add_fusion.1.live, bf16[896,768]{1,0:T(8,128)(2,1)} %get-tuple-element.210.q, bf16[896,768]{1,0:T(8,128)(2,1)} %get-tuple-element.211.k, bf16[896,768]{1,0:T(8,128)(2,1)} %get-tuple-element.212.v, ...), custom_call_target="tpu_custom_call", output_to_operand_aliasing={{0}: (4, {}), {1}: (5, {})} | custom-call | flops 2700000000 | bytes 1024 | tf_op jit(solution)/shard_map/pallas_call | solution.py:607
  110.6 3.8 %collective-permute-done.18.r8 = bf16[2,4,192,384]{3,2,1,0:T(8,128)(2,1)} collective-permute-done((bf16[2,4,192,384]{3,2,1,0:T(8,128)(2,1)S(1)}, bf16[2,4,192,384]{3,2,1,0:T(8,128)(2,1)}, u32[]{:S(2)}, u32[]{:S(2)}) %collective-permute-start.18) | collective-permute-done | bytes 1179680 | tf_op jit(solution)/shard_map/chips_2_1/ppermute | solution.py:391
  114.4 8.4 %shard_map.422 = (bf16[4,2,2,48,768]{4,3,2,1,0:T(8,128)(2,1)}, bf16[4,2,2,48,3072]{4,3,2,1,0:T(8,128)(2,1)}, f32[839,768]{1,0:T(8,128)}, bf16[839,768]{1,0:T(8,128)(2,1)}) custom-call(s32[4]{0:T(128)} %pad_add_fusion.at_ref.at, bf16[896,768]{1,0:T(8,128)(2,1)} %get-tuple-element.223.attended, f32[839,768]{1,0:T(8,128)} %get-tuple-element.224.embedded, ...), custom_call_target="tpu_custom_call" | custom-call | flops 2400000000 | bytes 1024 | tf_op jit(solution)/shard_map/pallas_call | solution.py:361
  122.9 39.6 %shard_map.423 = (bf16[839,768]{1,0:T(8,128)(2,1)}, f32[839,768]{1,0:T(8,128)}, bf16[16,192,384]{2,1,0:T(8,128)(2,1)}, bf16[16,192,384]{2,1,0:T(8,128)(2,1)}, bf...) custom-call(s32[4]{0:T(128)} %pad_add_fusion.at_ref.at, ...), custom_call_target="tpu_custom_call" | custom-call | flops 12000000000 | bytes 1024 | tf_op jit(solution)/shard_map/pallas_call | solution.py:827
  163.1 8.0 %shard_map.424 = (f32[839,768]{1,0:T(8,128)}, bf16[839,768]{1,0:T(8,128)(2,1)}, bf16[896,768]{1,0:T(8,128)(2,1)}, f32[8,768]{1,0:T(8,128)}) custom-call(f32[839,768]{1,0:T(8,128)} %get-tuple-element.232.middle, f32[839,768]{1,0:T(8,128)} %get-tuple-element.242.second_grad, bf16[839,768]{1,0:T(8,128)(2,1)} %bitcast.207, f32[16,768]{1,0:T(8,128)} %get-tuple-element.225.vec, ...), custom_call_target="tpu_custom_call" | custom-call | flops 2400000000 | bytes 1024 | tf_op jit(solution)/shard_map/pallas_call | solution.py:361
  171.1 1.7 add_convert_fusion.8
  173.1 1.6 add_convert_fusion.7
  174.7 1.6 maximum_maximum_fusion
  176.3 1.2 collective-permute-start.26
  177.5 28.4 %shard_map.425 = (bf16[896,768]{1,0:T(8,128)(2,1)}, bf16[896,768]{1,0:T(8,128)(2,1)}, bf16[896,768]{1,0:T(8,128)(2,1)}) custom-call(s32[2]{0:T(128)} %pad_add_fusion.1.live, bf16[896,768]{1,0:T(8,128)(2,1)} %get-tuple-element.210.q, bf16[896,768]{1,0:T(8,128)(2,1)} %get-tuple-element.211.k, bf16[896,768]{1,0:T(8,128)(2,1)} %get-tuple-element.212.v, ...), custom_call_target="tpu_custom_call" | custom-call | flops 8400000000 | bytes 1024 | tf_op jit(solution)/shard_map/pallas_call | solution.py:655
  205.9 1.4 add_bitcast_fusion.2
  207.3 1.5 add_bitcast_fusion
  209.3 1.5 add_bitcast_fusion.1
  210.8 1.7 fusion.1
  212.5 1.5 collective-permute-start.27
  214.0 11.4 %shard_map.426 = (bf16[16,192,384]{2,1,0:T(8,128)(2,1)}, bf16[16,192,384]{2,1,0:T(8,128)(2,1)}) custom-call(s32[4]{0:T(128)} %pad_add_fusion.at_ref.at, bf16[896,768]{1,0:T(8,128)(2,1)} %get-tuple-element.223.attended, bf16[839,768]{1,0:T(8,128)(2,1)} %get-tuple-element.264.branch, bf16[839,768]{1,0:T(8,128)(2,1)} %get-tuple-element.265.normed, ...), custom_call_target="tpu_custom_call" | custom-call | flops 3300000000 | bytes 1024 | tf_op jit(solution)/shard_map/pallas_call | solution.py:361
  225.4 3.5 %collective-permute-done.27 = bf16[4,384,384]{2,1,0:T(8,128)(2,1)S(1)} collective-permute-done((bf16[4,384,384]{2,1,0:T(8,128)(2,1)}, bf16[4,384,384]{2,1,0:T(8,128)(2,1)S(1)}, u32[]{:S(2)}, u32[]{:S(2)}) %collective-permute-start.27) | collective-permute-done | bytes 1179680 | tf_op jit(solution)/shard_map/chips_1_2/ppermute | solution.py:391
  230.1 4.0 %collective-permute-start.28 = (bf16[384,384]{1,0:T(8,128)(2,1)S(1)}, bf16[384,384]{1,0:T(8,128)(2,1)S(1)}, u32[]{:S(2)}, u32[]{:S(2)}) collective-permute-start(bf16[384,384]{1,0:T(8,128)(2,1)S(1)} %get-tuple-element.356), channel_id=1, source_target_pairs={{0,8},{1,9},{2,10},{3,11},{4,12},{5,13},{6,14},{7,15},{8,0},{9,1},... | collective-permute-start | bytes 884744 | tf_op jit(solution)/shard_map/chips_4_4/ppermute | solution.py:391
  234.1 2.0 collective-permute-start.29
  236.0 10.9 %shard_map.427 = (bf16[325,768]{1,0:T(8,128)(2,1)}, bf16[513,768]{1,0:T(8,128)(2,1)}, f32[8,768]{1,0:T(8,128)}) custom-call(bf16[896,768]{1,0:T(8,128)(2,1)} %get-tuple-element.275.dq, bf16[896,768]{1,0:T(8,128)(2,1)} %get-tuple-element.276.dk, bf16[896,768]{1,0:T(8,128)(2,1)} %get-tuple-element.277.dv, bf16[4,2,2,48,768]{4,3,2,1,0:T(8,128)(2,1)} %get-tuple-element.278.wq, ...), custom_call_target="tpu_custom_call" | custom-call | flops 3300000000 | bytes 1024 | tf_op jit(solution)/shard_map/pallas_call | solution.py:361
  246.9 2.8 collective-permute-done.29
  249.8 1.7 add_convert_fusion.4
  252.8 4.7 %shard_map.429 = (f32[325,1,768]{2,1,0:T(1,128)}, f32[513,1,768]{2,1,0:T(1,128)}) custom-call(bf16[325,768]{1,0:T(8,128)(2,1)} %get-tuple-element.291.image_low, bf16[513,768]{1,0:T(8,128)(2,1)} %get-tuple-element.292.text_low, bf16[4,2,2,48,768]{4,3,2,1,0:T(8,128)(2,1)} %get-tuple-element.299.w_image, bf16[4,2,2,48,768]{4,3,2,1,0:T(8,128)(2,1)} %get-tuple-element.300.w_text), custom_call_target="tpu_custom_call" | custom-call | flops 1320000000 | bytes 1024 | tf_op jit(solution)/shard_map/pallas_call | solution.py:361
  257.4 5.3 %shard_map.428 = (bf16[16,112,384]{2,1,0:T(8,128)(2,1)}, bf16[16,112,384]{2,1,0:T(8,128)(2,1)}) custom-call(s32[4]{0:T(128)} %pad_add_fusion.at_ref.at, bf16[325,768]{1,0:T(8,128)(2,1)} %bitcast.211, bf16[513,768]{1,0:T(8,128)(2,1)} %bitcast.209, bf16[325,768]{1,0:T(8,128)(2,1)} %get-tuple-element.291.image_low, ...), custom_call_target="tpu_custom_call" | custom-call | flops 1650000000 | bytes 1024 | tf_op jit(solution)/shard_map/pallas_call | solution.py:361
  262.7 5.7 %collective-permute-done.31 = bf16[384,384]{1,0:T(8,128)(2,1)} collective-permute-done((bf16[384,384]{1,0:T(8,128)(2,1)}, bf16[384,384]{1,0:T(8,128)(2,1)}, u32[]{:S(2)}, u32[]{:S(2)}) %collective-permute-start.31) | collective-permute-done | bytes 294944 | tf_op jit(solution)/shard_map/chips_8_8/ppermute | solution.py:391
  268.4 1.5 fusion.4
  269.9 1.1 collective-permute-start.34
  271.0 1.5 fusion.5
  272.5 1.2 add_convert_fusion.13
  273.7 6.2 %collective-permute-done.34 = bf16[4,192,384]{2,1,0:T(8,128)(2,1)S(1)} collective-permute-done((bf16[4,192,384]{2,1,0:T(8,128)(2,1)S(1)}, bf16[4,192,384]{2,1,0:T(8,128)(2,1)S(1)}, u32[]{:S(2)}, u32[]{:S(2)}) %collective-permute-start.34) | collective-permute-done | bytes 589856 | tf_op jit(solution)/shard_map/chips_1_2/ppermute | solution.py:391
  281.2 2.5 collective-permute-start.37
  283.7 1.9 collective-permute-start.38
  285.6 4.3 %collective-permute-done.36 = bf16[192,384]{1,0:T(8,128)(2,1)S(1)} collective-permute-done((bf16[192,384]{1,0:T(8,128)(2,1)S(1)}, bf16[192,384]{1,0:T(8,128)(2,1)S(1)}, u32[]{:S(2)}, u32[]{:S(2)}) %collective-permute-start.36) | collective-permute-done | bytes 147488 | tf_op jit(solution)/shard_map/chips_4_4/ppermute | solution.py:391
  289.9 5.3 %collective-permute-done.37 = bf16[192,384]{1,0:T(8,128)(2,1)S(1)} collective-permute-done((bf16[192,384]{1,0:T(8,128)(2,1)S(1)}, bf16[192,384]{1,0:T(8,128)(2,1)S(1)}, u32[]{:S(2)}, u32[]{:S(2)}) %collective-permute-start.37) | collective-permute-done | bytes 147488 | tf_op jit(solution)/shard_map/chips_8_8/ppermute | solution.py:391
  295.5 1.1 collective-permute-start.40
  298.1 4.7 %collective-permute-done.40 = bf16[4,112,384]{2,1,0:T(8,128)(2,1)S(1)} collective-permute-done((bf16[4,112,384]{2,1,0:T(8,128)(2,1)S(1)}, bf16[4,112,384]{2,1,0:T(8,128)(2,1)S(1)}, u32[]{:S(2)}, u32[]{:S(2)}) %collective-permute-start.40) | collective-permute-done | bytes 344096 | tf_op jit(solution)/shard_map/chips_1_2/ppermute | solution.py:391
  303.1 3.4 %collective-permute-start.42 = (bf16[112,384]{1,0:T(8,128)(2,1)S(1)}, bf16[112,384]{1,0:T(8,128)(2,1)S(1)}, u32[]{:S(2)}, u32[]{:S(2)}) collective-permute-start(bf16[112,384]{1,0:T(8,128)(2,1)S(1)} %get-tuple-element.366), channel_id=1, source_target_pairs={{0,8},{1,9},{2,10},{3,11},{4,12},{5,13},{6,14},{7,15},{8,0},{9,1},... | collective-permute-start | bytes 258056 | tf_op jit(solution)/shard_map/chips_4_4/ppermute | solution.py:391
  307.1 1.9 collective-permute-start.44
  311.6 3.4 %collective-permute-done.43 = bf16[112,384]{1,0:T(8,128)(2,1)S(1)} collective-permute-done((bf16[112,384]{1,0:T(8,128)(2,1)S(1)}, bf16[112,384]{1,0:T(8,128)(2,1)S(1)}, u32[]{:S(2)}, u32[]{:S(2)}) %collective-permute-start.43) | collective-permute-done | bytes 86048 | tf_op jit(solution)/shard_map/chips_8_8/ppermute | solution.py:391
  315.2 1.3 collective-permute-done.45
  (145 shorter events, 20.6 us)
Async XLA Ops:
  3.1 20.4 %copy-start.15 = (bf16[256,384]{1,0:T(8,128)(2,1)S(1)}, bf16[256,384]{1,0:T(8,128)(2,1)}, u32[]{:S(2)}) copy-start(bf16[256,384]{1,0:T(8,128)(2,1)} %shard_map.416) | copy-start | bytes 589828
  3.1 11.6 %collective-permute-start = (bf16[256,384]{1,0:T(8,128)(2,1)}, bf16[256,384]{1,0:T(8,128)(2,1)S(1)}, u32[]{:S(2)}, u32[]{:S(2)}) collective-permute-start(bf16[256,384]{1,0:T(8,128)(2,1)} %shard_map.416), channel_id=1, source_target_pairs={{0,8},{1,9},{2,10},{3,11},{4,12},{5,13},{6,14},{7,15},{8,0},{9,1},... | collective-permute-start | bytes 589832 | tf_op jit(solution)/shard_map/chips_4_4/ppermute | solution.py:391
  6.1 17.4 %collective-permute-start.1 = (bf16[256,384]{1,0:T(8,128)(2,1)}, bf16[256,384]{1,0:T(8,128)(2,1)S(1)}, u32[]{:S(2)}, u32[]{:S(2)}) collective-permute-start(bf16[256,384]{1,0:T(8,128)(2,1)} %shard_map.416), channel_id=1, source_target_pairs={{0,16},{1,17},{2,18},{3,19},{4,20},{5,21},{6,22},{7,23},{8,24},{9,... | collective-permute-start | bytes 589832 | tf_op jit(solution)/shard_map/chips_8_8/ppermute | solution.py:391
  8.7 14.8 %collective-permute-start.2 = (bf16[256,384]{1,0:T(8,128)(2,1)}, bf16[256,384]{1,0:T(8,128)(2,1)S(1)}, u32[]{:S(2)}, u32[]{:S(2)}) collective-permute-start(bf16[256,384]{1,0:T(8,128)(2,1)} %shard_map.416), channel_id=1, source_target_pairs={{0,24},{1,25},{2,26},{3,27},{4,28},{5,29},{6,30},{7,31},{8,16},{9,... | collective-permute-start | bytes 589832 | tf_op jit(solution)/shard_map/chips_12_12/ppermute | solution.py:391
  12.2 13.0 %copy-start.16 = (bf16[144,384]{1,0:T(8,128)(2,1)S(1)}, bf16[144,384]{1,0:T(8,128)(2,1)}, u32[]{:S(2)}) copy-start(bf16[144,384]{1,0:T(8,128)(2,1)} %shard_map.417) | copy-start | bytes 331780
  23.6 14.9 %collective-permute-start.3 = (bf16[4,256,384]{2,1,0:T(8,128)(2,1)S(1)}, bf16[4,256,384]{2,1,0:T(8,128)(2,1)S(1)}, u32[]{:S(2)}, u32[]{:S(2)}) collective-permute-start(bf16[4,256,384]{2,1,0:T(8,128)(2,1)S(1)} %pad_maximum_fusion.5), channel_id=1, source_target_pairs={{0,2},{1,5},{2,0},{3,7},{4,6},{5,1},{6,4},{7,3},{8,10},{9,13},{10,... | collective-permute-start | bytes 2359304 | tf_op jit(solution)/shard_map/chips_1_2/ppermute | solution.py:391
  25.2 7.2 %collective-permute-start.4 = (bf16[144,384]{1,0:T(8,128)(2,1)S(1)}, bf16[144,384]{1,0:T(8,128)(2,1)S(1)}, u32[]{:S(2)}, u32[]{:S(2)}) collective-permute-start(bf16[144,384]{1,0:T(8,128)(2,1)S(1)} %copy-done.16), channel_id=1, source_target_pairs={{0,8},{1,9},{2,10},{3,11},{4,12},{5,13},{6,14},{7,15},{8,0},{9,1},... | collective-permute-start | bytes 331784 | tf_op jit(solution)/shard_map/chips_4_4/ppermute | solution.py:391
  28.6 10.0 %collective-permute-start.5 = (bf16[144,384]{1,0:T(8,128)(2,1)S(1)}, bf16[144,384]{1,0:T(8,128)(2,1)S(1)}, u32[]{:S(2)}, u32[]{:S(2)}) collective-permute-start(bf16[144,384]{1,0:T(8,128)(2,1)S(1)} %copy-done.16), channel_id=1, source_target_pairs={{0,16},{1,17},{2,18},{3,19},{4,20},{5,21},{6,22},{7,23},{8,24},{9,... | collective-permute-start | bytes 331784 | tf_op jit(solution)/shard_map/chips_8_8/ppermute | solution.py:391
  29.6 9.0 %collective-permute-start.6 = (bf16[144,384]{1,0:T(8,128)(2,1)S(1)}, bf16[144,384]{1,0:T(8,128)(2,1)S(1)}, u32[]{:S(2)}, u32[]{:S(2)}) collective-permute-start(bf16[144,384]{1,0:T(8,128)(2,1)S(1)} %copy-done.16), channel_id=1, source_target_pairs={{0,24},{1,25},{2,26},{3,27},{4,28},{5,29},{6,30},{7,31},{8,16},{9,... | collective-permute-start | bytes 331784 | tf_op jit(solution)/shard_map/chips_12_12/ppermute | solution.py:391
  38.7 21.8 %copy-start.6 = (bf16[2,4,256,384]{3,2,1,0:T(8,128)(2,1)}, bf16[2,4,256,384]{3,2,1,0:T(8,128)(2,1)S(1)}, u32[]{:S(2)}) copy-start(bf16[2,4,256,384]{3,2,1,0:T(8,128)(2,1)S(1)} %pad_maximum_fusion.s8) | copy-start | bytes 4718596
  38.7 20.5 %collective-permute-start.7 = (bf16[2,4,256,384]{3,2,1,0:T(8,128)(2,1)S(1)}, bf16[2,4,256,384]{3,2,1,0:T(8,128)(2,1)S(1)}, u32[]{:S(2)}, u32[]{:S(2)}) collective-permute-start(bf16[2,4,256,384]{3,2,1,0:T(8,128)(2,1)S(1)} %pad_maximum_fusion.s8), channel_id=1, source_target_pairs={{0,4},{1,3},{2,6},{3,1},{4,0},{5,7},{6,2},{7,5},{8,12},{9,11},{10,... | collective-permute-start | bytes 4718600 | tf_op jit(solution)/shard_map/chips_2_1/ppermute | solution.py:391
  39.3 19.9 %collective-permute-start.8 = (bf16[2,4,256,384]{3,2,1,0:T(8,128)(2,1)S(1)}, bf16[2,4,256,384]{3,2,1,0:T(8,128)(2,1)S(1)}, u32[]{:S(2)}, u32[]{:S(2)}) collective-permute-start(bf16[2,4,256,384]{3,2,1,0:T(8,128)(2,1)S(1)} %pad_maximum_fusion.s8), channel_id=1, source_target_pairs={{0,1},{1,0},{2,3},{3,2},{4,5},{5,4},{6,7},{7,6},{8,9},{9,8},{10,11... | collective-permute-start | bytes 4718600 | tf_op jit(solution)/shard_map/between_cores/ppermute | solution.py:382
  39.5 18.7 %collective-permute-start.10 = (bf16[288,384]{1,0:T(8,128)(2,1)S(1)}, bf16[288,384]{1,0:T(8,128)(2,1)S(1)}, u32[]{:S(2)}, u32[]{:S(2)}) collective-permute-start(bf16[288,384]{1,0:T(8,128)(2,1)S(1)} %copy-done.14), channel_id=1, source_target_pairs={{0,16},{1,17},{2,18},{3,19},{4,20},{5,21},{6,22},{7,23},{8,24},{9,... | collective-permute-start | bytes 663560 | tf_op jit(solution)/shard_map/chips_8_8/ppermute | solution.py:391
  42.1 16.0 %collective-permute-start.11 = (bf16[288,384]{1,0:T(8,128)(2,1)S(1)}, bf16[288,384]{1,0:T(8,128)(2,1)S(1)}, u32[]{:S(2)}, u32[]{:S(2)}) collective-permute-start(bf16[288,384]{1,0:T(8,128)(2,1)S(1)} %copy-done.14), channel_id=1, source_target_pairs={{0,24},{1,25},{2,26},{3,27},{4,28},{5,29},{6,30},{7,31},{8,16},{9,... | collective-permute-start | bytes 663560 | tf_op jit(solution)/shard_map/chips_12_12/ppermute | solution.py:391
  43.6 15.4 %collective-permute-start.9 = (bf16[288,384]{1,0:T(8,128)(2,1)S(1)}, bf16[288,384]{1,0:T(8,128)(2,1)S(1)}, u32[]{:S(2)}, u32[]{:S(2)}) collective-permute-start(bf16[288,384]{1,0:T(8,128)(2,1)S(1)} %copy-done.14), channel_id=1, source_target_pairs={{0,8},{1,9},{2,10},{3,11},{4,12},{5,13},{6,14},{7,15},{8,0},{9,1},... | collective-permute-start | bytes 663560 | tf_op jit(solution)/shard_map/chips_4_4/ppermute | solution.py:391
  59.2 3.6 %copy-start.18 = (bf16[2,4,256,384]{3,2,1,0:T(8,128)(2,1)}, bf16[2,4,256,384]{3,2,1,0:T(8,128)(2,1)S(1)}, u32[]{:S(2)}) copy-start(bf16[2,4,256,384]{3,2,1,0:T(8,128)(2,1)S(1)} %collective-permute-done.7.r8) | copy-start | bytes 4718596
  59.2 1.2 copy-start.19
  59.2 5.4 %collective-permute-start.14 = (bf16[2,4,256,384]{3,2,1,0:T(8,128)(2,1)S(1)}, bf16[2,4,256,384]{3,2,1,0:T(8,128)(2,1)S(1)}, u32[]{:S(2)}, u32[]{:S(2)}) collective-permute-start(bf16[2,4,256,384]{3,2,1,0:T(8,128)(2,1)S(1)} %collective-permute-done.7.r8), channel_id=1, source_target_pairs={{0,1},{1,0},{2,3},{3,2},{4,5},{5,4},{6,7},{7,6},{8,9},{9,8},{10,11... | collective-permute-start | bytes 4718600 | tf_op jit(solution)/shard_map/between_cores/ppermute | solution.py:382
  60.6 17.9 %collective-permute-start.13 = (bf16[4,288,384]{2,1,0:T(8,128)(2,1)S(1)}, bf16[4,288,384]{2,1,0:T(8,128)(2,1)S(1)}, u32[]{:S(2)}, u32[]{:S(2)}) collective-permute-start(bf16[4,288,384]{2,1,0:T(8,128)(2,1)S(1)} %pad_maximum_fusion.3), channel_id=1, source_target_pairs={{0,2},{1,5},{2,0},{3,7},{4,6},{5,1},{6,4},{7,3},{8,10},{9,13},{10,... | collective-permute-start | bytes 2654216 | tf_op jit(solution)/shard_map/chips_1_2/ppermute | solution.py:391
  63.5 15.0 %collective-permute-start.12 = (bf16[4,144,384]{2,1,0:T(8,128)(2,1)S(1)}, bf16[4,144,384]{2,1,0:T(8,128)(2,1)S(1)}, u32[]{:S(2)}, u32[]{:S(2)}) collective-permute-start(bf16[4,144,384]{2,1,0:T(8,128)(2,1)S(1)} %pad_maximum_fusion.9), channel_id=1, source_target_pairs={{0,2},{1,5},{2,0},{3,7},{4,6},{5,1},{6,4},{7,3},{8,10},{9,13},{10,... | collective-permute-start | bytes 1327112 | tf_op jit(solution)/shard_map/chips_1_2/ppermute | solution.py:391
  78.5 2.5 copy-start
  78.6 19.5 %collective-permute-start.15 = (bf16[2,4,144,384]{3,2,1,0:T(8,128)(2,1)S(1)}, bf16[2,4,144,384]{3,2,1,0:T(8,128)(2,1)}, u32[]{:S(2)}, u32[]{:S(2)}) collective-permute-start(bf16[2,4,144,384]{3,2,1,0:T(8,128)(2,1)S(1)} %pad_maximum_fusion.4.s8), channel_id=1, source_target_pairs={{0,4},{1,3},{2,6},{3,1},{4,0},{5,7},{6,2},{7,5},{8,12},{9,11},{10,... | collective-permute-start | bytes 2654216 | tf_op jit(solution)/shard_map/chips_2_1/ppermute | solution.py:391
  79.8 18.3 %collective-permute-start.17 = (bf16[2,4,144,384]{3,2,1,0:T(8,128)(2,1)S(1)}, bf16[2,4,144,384]{3,2,1,0:T(8,128)(2,1)}, u32[]{:S(2)}, u32[]{:S(2)}) collective-permute-start(bf16[2,4,144,384]{3,2,1,0:T(8,128)(2,1)S(1)} %pad_maximum_fusion.4.s8), channel_id=1, source_target_pairs={{0,1},{1,0},{2,3},{3,2},{4,5},{5,4},{6,7},{7,6},{8,9},{9,8},{10,11... | collective-permute-start | bytes 2654216 | tf_op jit(solution)/shard_map/between_cores/ppermute | solution.py:382
  80.0 19.8 %copy-start.1 = (bf16[2,4,96,384]{3,2,1,0:T(8,128)(2,1)}, bf16[2,4,96,384]{3,2,1,0:T(8,128)(2,1)S(1)}, u32[]{:S(2)}) copy-start(bf16[2,4,96,384]{3,2,1,0:T(8,128)(2,1)S(1)} %pad_maximum_fusion.7.s_hi) | copy-start | bytes 1769476
  80.0 18.1 %collective-permute-start.16 = (bf16[2,4,96,384]{3,2,1,0:T(8,128)(2,1)S(1)}, bf16[2,4,96,384]{3,2,1,0:T(8,128)(2,1)}, u32[]{:S(2)}, u32[]{:S(2)}) collective-permute-start(bf16[2,4,96,384]{3,2,1,0:T(8,128)(2,1)S(1)} %pad_maximum_fusion.7.s_hi), channel_id=1, source_target_pairs={{0,4},{1,3},{2,6},{3,1},{4,0},{5,7},{6,2},{7,5},{8,12},{9,11},{10,... | collective-permute-start | bytes 1769480 | tf_op jit(solution)/shard_map/chips_2_1/ppermute | solution.py:391
  81.2 18.2 %copy-start.8 = (bf16[2,4,192,384]{3,2,1,0:T(8,128)(2,1)}, bf16[2,4,192,384]{3,2,1,0:T(8,128)(2,1)S(1)}, u32[]{:S(2)}) copy-start(bf16[2,4,192,384]{3,2,1,0:T(8,128)(2,1)S(1)} %pad_maximum_fusion.1.s8) | copy-start | bytes 3538948
  98.1 16.3 %collective-permute-start.18 = (bf16[2,4,192,384]{3,2,1,0:T(8,128)(2,1)S(1)}, bf16[2,4,192,384]{3,2,1,0:T(8,128)(2,1)}, u32[]{:S(2)}, u32[]{:S(2)}) collective-permute-start(bf16[2,4,192,384]{3,2,1,0:T(8,128)(2,1)S(1)} %pad_maximum_fusion.1.s8), channel_id=1, source_target_pairs={{0,4},{1,3},{2,6},{3,1},{4,0},{5,7},{6,2},{7,5},{8,12},{9,11},{10,... | collective-permute-start | bytes 3538952 | tf_op jit(solution)/shard_map/chips_2_1/ppermute | solution.py:391
  99.3 15.1 %collective-permute-start.20 = (bf16[2,4,192,384]{3,2,1,0:T(8,128)(2,1)S(1)}, bf16[2,4,192,384]{3,2,1,0:T(8,128)(2,1)}, u32[]{:S(2)}, u32[]{:S(2)}) collective-permute-start(bf16[2,4,192,384]{3,2,1,0:T(8,128)(2,1)S(1)} %pad_maximum_fusion.1.s8), channel_id=1, source_target_pairs={{0,1},{1,0},{2,3},{3,2},{4,5},{5,4},{6,7},{7,6},{8,9},{9,8},{10,11... | collective-permute-start | bytes 3538952 | tf_op jit(solution)/shard_map/between_cores/ppermute | solution.py:382
  99.3 11.3 %collective-permute-start.21 = (bf16[2,4,144,384]{3,2,1,0:T(8,128)(2,1)}, bf16[2,4,144,384]{3,2,1,0:T(8,128)(2,1)S(1)}, u32[]{:S(2)}, u32[]{:S(2)}) collective-permute-start(bf16[2,4,144,384]{3,2,1,0:T(8,128)(2,1)} %collective-permute-done.15.r8), channel_id=1, source_target_pairs={{0,1},{1,0},{2,3},{3,2},{4,5},{5,4},{6,7},{7,6},{8,9},{9,8},{10,11... | collective-permute-start | bytes 2654216 | tf_op jit(solution)/shard_map/between_cores/ppermute | solution.py:382
  99.8 10.7 %collective-permute-start.19 = (bf16[2,4,96,384]{3,2,1,0:T(8,128)(2,1)S(1)}, bf16[2,4,96,384]{3,2,1,0:T(8,128)(2,1)S(1)}, u32[]{:S(2)}, u32[]{:S(2)}) collective-permute-start(bf16[2,4,96,384]{3,2,1,0:T(8,128)(2,1)S(1)} %pad_maximum_fusion.7.s_hi), channel_id=1, source_target_pairs={{0,1},{1,0},{2,3},{3,2},{4,5},{5,4},{6,7},{7,6},{8,9},{9,8},{10,11... | collective-permute-start | bytes 1769480 | tf_op jit(solution)/shard_map/between_cores/ppermute | solution.py:382
  99.8 10.7 %collective-permute-start.22 = (bf16[2,4,96,384]{3,2,1,0:T(8,128)(2,1)}, bf16[2,4,96,384]{3,2,1,0:T(8,128)(2,1)S(1)}, u32[]{:S(2)}, u32[]{:S(2)}) collective-permute-start(bf16[2,4,96,384]{3,2,1,0:T(8,128)(2,1)} %collective-permute-done.16.r_hi), channel_id=1, source_target_pairs={{0,1},{1,0},{2,3},{3,2},{4,5},{5,4},{6,7},{7,6},{8,9},{9,8},{10,11... | collective-permute-start | bytes 1769480 | tf_op jit(solution)/shard_map/between_cores/ppermute | solution.py:382
  110.5 3.9 %copy-start.10 = (bf16[2,4,96,384]{3,2,1,0:T(8,128)(2,1)}, bf16[2,4,96,384]{3,2,1,0:T(8,128)(2,1)S(1)}, u32[]{:S(2)}) copy-start(bf16[2,4,96,384]{3,2,1,0:T(8,128)(2,1)S(1)} %collective-permute-done.19.sp_hi) | copy-start | bytes 1769476
  110.6 3.9 %copy-start.11 = (bf16[2,4,96,384]{3,2,1,0:T(8,128)(2,1)}, bf16[2,4,96,384]{3,2,1,0:T(8,128)(2,1)S(1)}, u32[]{:S(2)}) copy-start(bf16[2,4,96,384]{3,2,1,0:T(8,128)(2,1)S(1)} %collective-permute-done.22.rp_hi) | copy-start | bytes 1769476
  110.6 3.8 %copy-start.9 = (bf16[2,4,144,384]{3,2,1,0:T(8,128)(2,1)}, bf16[2,4,144,384]{3,2,1,0:T(8,128)(2,1)S(1)}, u32[]{:S(2)}) copy-start(bf16[2,4,144,384]{3,2,1,0:T(8,128)(2,1)S(1)} %collective-permute-done.21.r8p) | copy-start | bytes 2654212
  114.4 8.5 %collective-permute-start.23 = (bf16[2,4,192,384]{3,2,1,0:T(8,128)(2,1)}, bf16[2,4,192,384]{3,2,1,0:T(8,128)(2,1)}, u32[]{:S(2)}, u32[]{:S(2)}) collective-permute-start(bf16[2,4,192,384]{3,2,1,0:T(8,128)(2,1)} %collective-permute-done.18.r8), channel_id=1, source_target_pairs={{0,1},{1,0},{2,3},{3,2},{4,5},{5,4},{6,7},{7,6},{8,9},{9,8},{10,11... | collective-permute-start | bytes 3538952 | tf_op jit(solution)/shard_map/between_cores/ppermute | solution.py:382
  162.5 8.6 %collective-permute-start.24 = (bf16[16,192,384]{2,1,0:T(8,128)(2,1)}, bf16[16,192,384]{2,1,0:T(8,128)(2,1)}, u32[]{:S(2)}, u32[]{:S(2)}) collective-permute-start(bf16[16,192,384]{2,1,0:T(8,128)(2,1)} %get-tuple-element.238), channel_id=1, source_target_pairs={{0,1},{1,0},{2,3},{3,2},{4,5},{5,4},{6,7},{7,6},{8,9},{9,8},{10,11... | collective-permute-start | bytes 7077896 | tf_op jit(solution)/shard_map/between_cores/ppermute | solution.py:382
  163.0 8.0 %collective-permute-start.25 = (bf16[16,192,384]{2,1,0:T(8,128)(2,1)}, bf16[16,192,384]{2,1,0:T(8,128)(2,1)}, u32[]{:S(2)}, u32[]{:S(2)}) collective-permute-start(bf16[16,192,384]{2,1,0:T(8,128)(2,1)} %get-tuple-element.239), channel_id=1, source_target_pairs={{0,1},{1,0},{2,3},{3,2},{4,5},{5,4},{6,7},{7,6},{8,9},{9,8},{10,11... | collective-permute-start | bytes 7077896 | tf_op jit(solution)/shard_map/between_cores/ppermute | solution.py:382
  163.1 8.0 %copy-start.2 = (bf16[16,192,384]{2,1,0:T(8,128)(2,1)S(1)}, bf16[16,192,384]{2,1,0:T(8,128)(2,1)}, u32[]{:S(2)}) copy-start(bf16[16,192,384]{2,1,0:T(8,128)(2,1)} %get-tuple-element.255) | copy-start | bytes 7077892
  171.1 2.0 copy-start.4
  176.3 29.6 %collective-permute-start.26 = (bf16[4,2,384,384]{3,2,0,1:T(8,128)(2,1)}, bf16[4,2,384,384]{3,2,0,1:T(8,128)(2,1)S(1)}, u32[]{:S(2)}, u32[]{:S(2)}) collective-permute-start(bf16[4,2,384,384]{3,2,0,1:T(8,128)(2,1)} %maximum_maximum_fusion), channel_id=1, source_target_pairs={{0,4},{1,3},{2,6},{3,1},{4,0},{5,7},{6,2},{7,5},{8,12},{9,11},{10,... | collective-permute-start | bytes 7077896 | tf_op jit(solution)/shard_map/chips_2_1/ppermute | solution.py:391
  207.3 2.0 copy-start.3
  212.5 16.4 %collective-permute-start.27 = (bf16[4,384,384]{2,1,0:T(8,128)(2,1)}, bf16[4,384,384]{2,1,0:T(8,128)(2,1)S(1)}, u32[]{:S(2)}, u32[]{:S(2)}) collective-permute-start(bf16[4,384,384]{2,1,0:T(8,128)(2,1)} %get-tuple-element.352), channel_id=1, source_target_pairs={{0,2},{1,5},{2,0},{3,7},{4,6},{5,1},{6,4},{7,3},{8,10},{9,13},{10,... | collective-permute-start | bytes 3538952 | tf_op jit(solution)/shard_map/chips_1_2/ppermute | solution.py:391
  228.9 20.8 %collective-permute-start.30 = (bf16[16,192,384]{2,1,0:T(8,128)(2,1)}, bf16[16,192,384]{2,1,0:T(8,128)(2,1)}, u32[]{:S(2)}, u32[]{:S(2)}) collective-permute-start(bf16[16,192,384]{2,1,0:T(8,128)(2,1)} %get-tuple-element.270), channel_id=1, source_target_pairs={{0,1},{1,0},{2,3},{3,2},{4,5},{5,4},{6,7},{7,6},{8,9},{9,8},{10,11... | collective-permute-start | bytes 7077896 | tf_op jit(solution)/shard_map/between_cores/ppermute | solution.py:382
  230.1 16.9 %collective-permute-start.28 = (bf16[384,384]{1,0:T(8,128)(2,1)S(1)}, bf16[384,384]{1,0:T(8,128)(2,1)S(1)}, u32[]{:S(2)}, u32[]{:S(2)}) collective-permute-start(bf16[384,384]{1,0:T(8,128)(2,1)S(1)} %get-tuple-element.356), channel_id=1, source_target_pairs={{0,8},{1,9},{2,10},{3,11},{4,12},{5,13},{6,14},{7,15},{8,0},{9,1},... | collective-permute-start | bytes 884744 | tf_op jit(solution)/shard_map/chips_4_4/ppermute | solution.py:391
  234.1 15.7 %collective-permute-start.29 = (bf16[384,384]{1,0:T(8,128)(2,1)S(1)}, bf16[384,384]{1,0:T(8,128)(2,1)S(1)}, u32[]{:S(2)}, u32[]{:S(2)}) collective-permute-start(bf16[384,384]{1,0:T(8,128)(2,1)S(1)} %get-tuple-element.355), channel_id=1, source_target_pairs={{0,24},{1,25},{2,26},{3,27},{4,28},{5,29},{6,30},{7,31},{8,16},{9,... | collective-permute-start | bytes 884744 | tf_op jit(solution)/shard_map/chips_12_12/ppermute | solution.py:391
  236.0 13.7 %copy-start.5 = (bf16[16,192,384]{2,1,0:T(8,128)(2,1)S(1)}, bf16[16,192,384]{2,1,0:T(8,128)(2,1)}, u32[]{:S(2)}) copy-start(bf16[16,192,384]{2,1,0:T(8,128)(2,1)} %get-tuple-element.305) | copy-start | bytes 7077892
  249.8 1.7 copy-start.12
  251.6 16.9 %collective-permute-start.32 = (bf16[4,2,192,384]{3,2,0,1:T(8,128)(2,1)S(1)}, bf16[4,2,192,384]{3,2,0,1:T(8,128)(2,1)}, u32[]{:S(2)}, u32[]{:S(2)}) collective-permute-start(bf16[4,2,192,384]{3,2,0,1:T(8,128)(2,1)S(1)} %pad_maximum_fusion.2), channel_id=1, source_target_pairs={{0,4},{1,3},{2,6},{3,1},{4,0},{5,7},{6,2},{7,5},{8,12},{9,11},{10,... | collective-permute-start | bytes 3538952 | tf_op jit(solution)/shard_map/chips_2_1/ppermute | solution.py:391
  252.6 15.9 %collective-permute-start.31 = (bf16[384,384]{1,0:T(8,128)(2,1)}, bf16[384,384]{1,0:T(8,128)(2,1)}, u32[]{:S(2)}, u32[]{:S(2)}) collective-permute-start(bf16[384,384]{1,0:T(8,128)(2,1)} %get-tuple-element.284), channel_id=1, source_target_pairs={{0,16},{1,17},{2,18},{3,19},{4,20},{5,21},{6,22},{7,23},{8,24},{9,... | collective-permute-start | bytes 884744 | tf_op jit(solution)/shard_map/chips_8_8/ppermute | solution.py:391
  268.4 11.5 %collective-permute-start.33 = (bf16[16,112,384]{2,1,0:T(8,128)(2,1)}, bf16[16,112,384]{2,1,0:T(8,128)(2,1)S(1)}, u32[]{:S(2)}, u32[]{:S(2)}) collective-permute-start(bf16[16,112,384]{2,1,0:T(8,128)(2,1)} %get-tuple-element.303), channel_id=1, source_target_pairs={{0,1},{1,0},{2,3},{3,2},{4,5},{5,4},{6,7},{7,6},{8,9},{9,8},{10,11... | collective-permute-start | bytes 4128776 | tf_op jit(solution)/shard_map/between_cores/ppermute | solution.py:382
  269.9 2.5 copy-start.13
  269.9 9.9 %collective-permute-start.34 = (bf16[4,192,384]{2,1,0:T(8,128)(2,1)S(1)}, bf16[4,192,384]{2,1,0:T(8,128)(2,1)S(1)}, u32[]{:S(2)}, u32[]{:S(2)}) collective-permute-start(bf16[4,192,384]{2,1,0:T(8,128)(2,1)S(1)} %fusion.4), channel_id=1, source_target_pairs={{0,2},{1,5},{2,0},{3,7},{4,6},{5,1},{6,4},{7,3},{8,10},{9,13},{10,... | collective-permute-start | bytes 1769480 | tf_op jit(solution)/shard_map/chips_1_2/ppermute | solution.py:391
  272.5 7.4 %copy-start.7 = (bf16[16,112,384]{2,1,0:T(8,128)(2,1)S(1)}, bf16[16,112,384]{2,1,0:T(8,128)(2,1)}, u32[]{:S(2)}) copy-start(bf16[16,112,384]{2,1,0:T(8,128)(2,1)} %get-tuple-element.319) | copy-start | bytes 4128772
  280.2 15.0 %collective-permute-start.35 = (bf16[4,2,112,384]{3,2,0,1:T(8,128)(2,1)S(1)}, bf16[4,2,112,384]{3,2,0,1:T(8,128)(2,1)S(1)}, u32[]{:S(2)}, u32[]{:S(2)}) collective-permute-start(bf16[4,2,112,384]{3,2,0,1:T(8,128)(2,1)S(1)} %pad_maximum_fusion.6), channel_id=1, source_target_pairs={{0,4},{1,3},{2,6},{3,1},{4,0},{5,7},{6,2},{7,5},{8,12},{9,11},{10,... | collective-permute-start | bytes 2064392 | tf_op jit(solution)/shard_map/chips_2_1/ppermute | solution.py:391
  280.9 14.3 %collective-permute-start.39 = (bf16[384,384]{1,0:T(8,128)(2,1)S(1)}, bf16[384,384]{1,0:T(8,128)(2,1)S(1)}, u32[]{:S(2)}, u32[]{:S(2)}) collective-permute-start(bf16[384,384]{1,0:T(8,128)(2,1)S(1)} %add_convert_fusion.13), channel_id=1, source_target_pairs={{0,1},{1,0},{2,3},{3,2},{4,5},{5,4},{6,7},{7,6},{8,9},{9,8},{10,11... | collective-permute-start | bytes 884744 | tf_op jit(solution)/shard_map/between_cores/ppermute | solution.py:382
  281.1 8.8 %collective-permute-start.36 = (bf16[192,384]{1,0:T(8,128)(2,1)S(1)}, bf16[192,384]{1,0:T(8,128)(2,1)S(1)}, u32[]{:S(2)}, u32[]{:S(2)}) collective-permute-start(bf16[192,384]{1,0:T(8,128)(2,1)S(1)} %get-tuple-element.362), channel_id=1, source_target_pairs={{0,8},{1,9},{2,10},{3,11},{4,12},{5,13},{6,14},{7,15},{8,0},{9,1},... | collective-permute-start | bytes 442376 | tf_op jit(solution)/shard_map/chips_4_4/ppermute | solution.py:391
  281.2 14.0 %collective-permute-start.37 = (bf16[192,384]{1,0:T(8,128)(2,1)S(1)}, bf16[192,384]{1,0:T(8,128)(2,1)S(1)}, u32[]{:S(2)}, u32[]{:S(2)}) collective-permute-start(bf16[192,384]{1,0:T(8,128)(2,1)S(1)} %get-tuple-element.361), channel_id=1, source_target_pairs={{0,16},{1,17},{2,18},{3,19},{4,20},{5,21},{6,22},{7,23},{8,24},{9,... | collective-permute-start | bytes 442376 | tf_op jit(solution)/shard_map/chips_8_8/ppermute | solution.py:391
  283.7 11.5 %collective-permute-start.38 = (bf16[192,384]{1,0:T(8,128)(2,1)S(1)}, bf16[192,384]{1,0:T(8,128)(2,1)S(1)}, u32[]{:S(2)}, u32[]{:S(2)}) collective-permute-start(bf16[192,384]{1,0:T(8,128)(2,1)S(1)} %get-tuple-element.360), channel_id=1, source_target_pairs={{0,24},{1,25},{2,26},{3,27},{4,28},{5,29},{6,30},{7,31},{8,16},{9,... | collective-permute-start | bytes 442376 | tf_op jit(solution)/shard_map/chips_12_12/ppermute | solution.py:391
  295.5 7.3 %collective-permute-start.40 = (bf16[4,112,384]{2,1,0:T(8,128)(2,1)S(1)}, bf16[4,112,384]{2,1,0:T(8,128)(2,1)S(1)}, u32[]{:S(2)}, u32[]{:S(2)}) collective-permute-start(bf16[4,112,384]{2,1,0:T(8,128)(2,1)S(1)} %fusion.6), channel_id=1, source_target_pairs={{0,2},{1,5},{2,0},{3,7},{4,6},{5,1},{6,4},{7,3},{8,10},{9,13},{10,... | collective-permute-start | bytes 1032200 | tf_op jit(solution)/shard_map/chips_1_2/ppermute | solution.py:391
  296.7 1.4 collective-permute-start.41
  303.1 8.5 %collective-permute-start.42 = (bf16[112,384]{1,0:T(8,128)(2,1)S(1)}, bf16[112,384]{1,0:T(8,128)(2,1)S(1)}, u32[]{:S(2)}, u32[]{:S(2)}) collective-permute-start(bf16[112,384]{1,0:T(8,128)(2,1)S(1)} %get-tuple-element.366), channel_id=1, source_target_pairs={{0,8},{1,9},{2,10},{3,11},{4,12},{5,13},{6,14},{7,15},{8,0},{9,1},... | collective-permute-start | bytes 258056 | tf_op jit(solution)/shard_map/chips_4_4/ppermute | solution.py:391
  306.5 8.5 %collective-permute-start.43 = (bf16[112,384]{1,0:T(8,128)(2,1)S(1)}, bf16[112,384]{1,0:T(8,128)(2,1)S(1)}, u32[]{:S(2)}, u32[]{:S(2)}) collective-permute-start(bf16[112,384]{1,0:T(8,128)(2,1)S(1)} %get-tuple-element.365), channel_id=1, source_target_pairs={{0,16},{1,17},{2,18},{3,19},{4,20},{5,21},{6,22},{7,23},{8,24},{9,... | collective-permute-start | bytes 258056 | tf_op jit(solution)/shard_map/chips_8_8/ppermute | solution.py:391
  307.1 8.0 %collective-permute-start.44 = (bf16[112,384]{1,0:T(8,128)(2,1)S(1)}, bf16[112,384]{1,0:T(8,128)(2,1)S(1)}, u32[]{:S(2)}, u32[]{:S(2)}) collective-permute-start(bf16[112,384]{1,0:T(8,128)(2,1)S(1)} %get-tuple-element.364), channel_id=1, source_target_pairs={{0,24},{1,25},{2,26},{3,27},{4,28},{5,29},{6,30},{7,31},{8,16},{9,... | collective-permute-start | bytes 258056 | tf_op jit(solution)/shard_map/chips_12_12/ppermute | solution.py:391
  315.1 1.3 collective-permute-start.45
  (3 other events, 3.2 us)

commit v6 on v5

--- a/solution.py
+++ b/solution.py
@@ -1099,60 +1099,61 @@
     feeding.send_first()
     incoming = after(incoming, feeding.sent, feeding.kept)
     grads = attend_back(live, q, k, v, incoming, attended, totals)
-    feeding.got, feeding.kept, grads = settle(feeding.got, feeding.kept, grads)
+    pair = square_grads(place, attended, branch, normed, grads)
+    feeding.got, feeding.kept, grads, pair = settle(feeding.got, feeding.kept, grads, pair)
 
     feeding.second()
     feeding.send_second()
-    grads = after(grads, feeding.sent, feeding.kept)
-    pair = square_grads(place, attended, branch, normed, grads)
-    feeding.got, feeding.kept, grads, pair = settle(feeding.got, feeding.kept, grads, pair)
+    squares = Scatter(place, (pair,))
+    squares.swap()
+    grads = after(grads, feeding.sent, feeding.kept, squares.kept)
+    image_low, text_low, late = norm_one(grads, (wq, wk, wv), embedded, middle_grad, vec)
+    feeding.got, feeding.kept, squares.got, squares.kept, image_low, text_low = settle(
+        feeding.got, feeding.kept, squares.got, squares.kept, image_low, text_low
+    )
 
     feeding.third()
     feeding.send_third((1, 3))
-    squares = Scatter(place, (pair,))
-    squares.swap()
-    grads = after(grads, feeding.sent, feeding.kept)
-    image_low, text_low, late = norm_one(grads, (wq, wk, wv), embedded, middle_grad, vec)
-    early, feeding.sent, squares.got, squares.kept, image_low, text_low = settle(
-        feeding.got, feeding.sent, squares.got, squares.kept, image_low, text_low
-    )
-
-    feeding.send_third((2,))
     squares.first()
     squares.send_first()
-    image_low, text_low = after((image_low, text_low), squares.sent, squares.kept)
+    image_low, text_low = after(
+        (image_low, text_low), squares.sent, squares.kept, feeding.sent, feeding.kept
+    )
     pair = last(place, image, text, image_low, text_low, sums, hid_sum, ret_sum, late)
     image_grad, text_grad = input_grads(image_low, text_low, w_image, w_text)
-    feeding.got, squares.got, squares.kept, pair, image_grad, text_grad = settle(
-        feeding.got + early, squares.got, squares.kept, pair, image_grad, text_grad
-    )
-
+    early, feeding.sent, squares.got, squares.kept, pair, image_grad, text_grad = settle(
+        feeding.got, feeding.sent, squares.got, squares.kept, pair, image_grad, text_grad
+    )
+
+    feeding.send_third((2,))
     ending = Scatter(place, (pair,))
     ending.swap()
     squares.second()
     squares.send_second()
-    feeding.fourth()
-    ending.got, ending.kept, squares.got, squares.kept, feeding.sent = settle(
-        ending.got, ending.kept, squares.got, squares.kept, feeding.sent
-    )
-
-    feeding.kept = feeding.sent
-    feeding.swap()
+    feeding.got, ending.got, ending.kept, squares.got, squares.kept = settle(
+        feeding.got + early, ending.got, ending.kept, squares.got, squares.kept
+    )
+
     ending.first()
     ending.send_first()
     squares.third()
     squares.send_third()
-    ending.got, ending.kept, squares.got, squares.kept, feeding.got, image_grad, text_grad = settle(
-        ending.got, ending.kept, squares.got, squares.kept, feeding.got, image_grad, text_grad
-    )
-
+    feeding.fourth()
+    ending.got, ending.kept, squares.got, squares.kept, feeding.sent = settle(
+        ending.got, ending.kept, squares.got, squares.kept, feeding.sent
+    )
+
+    feeding.kept = feeding.sent
+    feeding.swap()
     ending.second()
     ending.send_second()
     squares.fourth()
     squares.swap()
+    ending.got, ending.kept, squares.got, feeding.got = settle(
+        ending.got, ending.kept, squares.got, feeding.got
+    )
+
     owned = owned_rows(SCATTER_CHUNKS[0], *feeding.sides())
-    ending.got, ending.kept, squares.got, owned = settle(ending.got, ending.kept, squares.got, owned)
-
     ending.third()
     ending.send_third()
     owned.update(owned_rows(SCATTER_CHUNKS[1], *squares.sides()))

time: 323 us -> 326 us (level)
  transfers between devices with their start and end apart: 46 -> 46, of which waited for: 20 -> 19; matrix products, arithmetic and copies ran while one was open for 3% -> 5% of each run, Pallas kernels for 35% -> 35%
where the time goes in v6:
time: 326 us; the launch traced here: 322 us
  Pallas kernels  155 us (48%)
  waiting for transfers between devices  84.3 us (26%)
  starting transfers between devices  47.8 us (15%)
  other arithmetic  26.3 us (8%)
  local copies, waits for them, and re-layouts  6.34 us (2%)
    ppermute x31, waiting for transfers between devices, to_chip(): return lax.ppermute(values, BOTH, pairs)  82 us
    pallas_call x10, Pallas kernels, call(): pl.pallas_call(kernel, out_shape=tuple(outs), in_specs=specs, out_specs=t...  66 us
    ppermute x31, starting transfers between devices, to_chip(): return lax.ppermute(values, BOTH, pairs)  44.9 us
    pallas_call x1, Pallas kernels, feed(): pl.pallas_call(feed_kernel, grid_spec=grid, out_shape=outs, compiler_para...  39.6 us
    pallas_call x1, Pallas kernels, attend_back(): pl.pallas_call(attend_back_kernel, grid=(HEADS // 2,), out_shape=(shape((...  28.4 us
    pallas_call x2, Pallas kernels, attend(): pl.pallas_call(kernel, grid=(count,), out_shape=(shape((PADDED, WIDTH)),...  20.9 us
    convert_element_type x13, other arithmetic, to_low(): return values.astype(jnp.bfloat16)  8.71 us
  transfers between devices with their start and end apart: 46, of which 19 were waited for; matrix products, arithmetic and copies ran while one was open for 5% of the time, Pallas kernels for 35%

profile of v6, /device:TPU:0, one launch (start us, length us, event | category | flops | bytes accessed | tf_op | source)
XLA Modules:
  0.0 322.2 jit_solution(16722666256396600062)
XLA Ops:
  1.3 1.9 shard_map.416
  3.1 3.0 collective-permute-start
  6.1 2.6 collective-permute-start.1
  8.7 1.8 shard_map.418
  10.5 1.7 shard_map.417
  12.2 2.6 collective-permute-done
  14.8 8.7 %collective-permute-done.1 = bf16[256,384]{1,0:T(8,128)(2,1)S(1)} collective-permute-done((bf16[256,384]{1,0:T(8,128)(2,1)}, bf16[256,384]{1,0:T(8,128)(2,1)S(1)}, u32[]{:S(2)}, u32[]{:S(2)}) %collective-permute-start.1) | collective-permute-done | bytes 196640 | tf_op jit(solution)/shard_map/chips_8_8/ppermute | solution.py:391
  23.6 1.6 collective-permute-start.3
  25.2 3.4 %collective-permute-start.4 = (bf16[144,384]{1,0:T(8,128)(2,1)S(1)}, bf16[144,384]{1,0:T(8,128)(2,1)S(1)}, u32[]{:S(2)}, u32[]{:S(2)}) collective-permute-start(bf16[144,384]{1,0:T(8,128)(2,1)S(1)} %copy-done.14), channel_id=1, source_target_pairs={{0,8},{1,9},{2,10},{3,11},{4,12},{5,13},{6,14},{7,15},{8,0},{9,1},... | collective-permute-start | bytes 331784 | tf_op jit(solution)/shard_map/chips_4_4/ppermute | solution.py:391
  29.6 1.5 collective-permute-start.6
  31.0 1.3 collective-permute-done.4
  32.4 6.2 %collective-permute-done.5 = bf16[144,384]{1,0:T(8,128)(2,1)S(1)} collective-permute-done((bf16[144,384]{1,0:T(8,128)(2,1)S(1)}, bf16[144,384]{1,0:T(8,128)(2,1)S(1)}, u32[]{:S(2)}, u32[]{:S(2)}) %collective-permute-start.5) | collective-permute-done | bytes 110624 | tf_op jit(solution)/shard_map/chips_8_8/ppermute | solution.py:391
  39.5 2.7 collective-permute-start.10
  42.1 1.4 collective-permute-start.11
  43.7 14.5 %collective-permute-done.10 = bf16[288,384]{1,0:T(8,128)(2,1)S(1)} collective-permute-done((bf16[288,384]{1,0:T(8,128)(2,1)S(1)}, bf16[288,384]{1,0:T(8,128)(2,1)S(1)}, u32[]{:S(2)}, u32[]{:S(2)}) %collective-permute-start.10) | collective-permute-done | bytes 221216 | tf_op jit(solution)/shard_map/chips_8_8/ppermute | solution.py:391
  59.3 1.1 copy-done.17
  60.6 1.6 collective-permute-start.13
  64.6 1.1 copy-done.18
  65.8 11.9 %shard_map.419 = (bf16[4,2,2,48,768]{4,3,2,1,0:T(8,128)(2,1)}, bf16[4,2,2,48,768]{4,3,2,1,0:T(8,128)(2,1)}, bf16[4,2,2,48,768]{4,3,2,1,0:T(8,128)(2,1)}, bf16[4,...) custom-call(s32[4]{0:T(128)} %pad_add_fusion.at_ref.at, ...), custom_call_target="tpu_custom_call" | custom-call | flops 3600000000 | bytes 1024 | tf_op jit(solution)/shard_map/pallas_call | solution.py:361
  78.6 1.3 collective-permute-start.15
  81.2 10.6 %shard_map.420 = (bf16[896,768]{1,0:T(8,128)(2,1)}, f32[6,8,896]{2,1,0:T(8,128)}) custom-call(s32[2]{0:T(128)} %pad_add_fusion.1.live, bf16[896,768]{1,0:T(8,128)(2,1)} %get-tuple-element.200.q, bf16[896,768]{1,0:T(8,128)(2,1)} %get-tuple-element.201.k, bf16[896,768]{1,0:T(8,128)(2,1)} %get-tuple-element.202.v), custom_call_target="tpu_custom_call" | custom-call | flops 2700000000 | bytes 1024 | tf_op jit(solution)/shard_map/pallas_call | solution.py:607
  91.8 6.3 %collective-permute-done.16.r_hi = bf16[2,4,96,384]{3,2,1,0:T(8,128)(2,1)} collective-permute-done((bf16[2,4,96,384]{3,2,1,0:T(8,128)(2,1)S(1)}, bf16[2,4,96,384]{3,2,1,0:T(8,128)(2,1)}, u32[]{:S(2)}, u32[]{:S(2)}) %collective-permute-start.16) | collective-permute-done | bytes 589856 | tf_op jit(solution)/shard_map/chips_2_1/ppermute | solution.py:391
  98.1 1.2 collective-permute-start.18
  100.3 10.2 %shard_map.421 = (bf16[896,768]{1,0:T(8,128)(2,1)}, f32[6,8,896]{2,1,0:T(8,128)}) custom-call(s32[2]{0:T(128)} %pad_add_fusion.1.live, bf16[896,768]{1,0:T(8,128)(2,1)} %get-tuple-element.200.q, bf16[896,768]{1,0:T(8,128)(2,1)} %get-tuple-element.201.k, bf16[896,768]{1,0:T(8,128)(2,1)} %get-tuple-element.202.v, ...), custom_call_target="tpu_custom_call", output_to_operand_aliasing={{0}: (4, {}), {1}: (5, {})} | custom-call | flops 2700000000 | bytes 1024 | tf_op jit(solution)/shard_map/pallas_call | solution.py:607
  110.6 3.8 %collective-permute-done.18.r8 = bf16[2,4,192,384]{3,2,1,0:T(8,128)(2,1)} collective-permute-done((bf16[2,4,192,384]{3,2,1,0:T(8,128)(2,1)S(1)}, bf16[2,4,192,384]{3,2,1,0:T(8,128)(2,1)}, u32[]{:S(2)}, u32[]{:S(2)}) %collective-permute-start.18) | collective-permute-done | bytes 1179680 | tf_op jit(solution)/shard_map/chips_2_1/ppermute | solution.py:391
  114.4 8.6 %shard_map.422 = (bf16[4,2,2,48,768]{4,3,2,1,0:T(8,128)(2,1)}, bf16[4,2,2,48,3072]{4,3,2,1,0:T(8,128)(2,1)}, f32[839,768]{1,0:T(8,128)}, bf16[839,768]{1,0:T(8,128)(2,1)}) custom-call(s32[4]{0:T(128)} %pad_add_fusion.at_ref.at, bf16[896,768]{1,0:T(8,128)(2,1)} %get-tuple-element.213.attended, f32[839,768]{1,0:T(8,128)} %get-tuple-element.214.embedded, ...), custom_call_target="tpu_custom_call" | custom-call | flops 2400000000 | bytes 1024 | tf_op jit(solution)/shard_map/pallas_call | solution.py:361
  123.0 39.6 %shard_map.423 = (bf16[839,768]{1,0:T(8,128)(2,1)}, f32[839,768]{1,0:T(8,128)}, bf16[16,192,384]{2,1,0:T(8,128)(2,1)}, bf16[16,192,384]{2,1,0:T(8,128)(2,1)}, bf...) custom-call(s32[4]{0:T(128)} %pad_add_fusion.at_ref.at, ...), custom_call_target="tpu_custom_call" | custom-call | flops 12000000000 | bytes 1024 | tf_op jit(solution)/shard_map/pallas_call | solution.py:827
  163.3 8.0 %shard_map.424 = (f32[839,768]{1,0:T(8,128)}, bf16[839,768]{1,0:T(8,128)(2,1)}, bf16[896,768]{1,0:T(8,128)(2,1)}, f32[8,768]{1,0:T(8,128)}) custom-call(f32[839,768]{1,0:T(8,128)} %get-tuple-element.222.middle, f32[839,768]{1,0:T(8,128)} %get-tuple-element.232.second_grad, bf16[839,768]{1,0:T(8,128)(2,1)} %bitcast.207, f32[16,768]{1,0:T(8,128)} %get-tuple-element.215.vec, ...), custom_call_target="tpu_custom_call" | custom-call | flops 2400000000 | bytes 1024 | tf_op jit(solution)/shard_map/pallas_call | solution.py:361
  171.3 1.7 add_convert_fusion.8
  173.3 1.6 add_convert_fusion.7
  174.9 1.7 maximum_maximum_fusion
  176.5 1.2 collective-permute-start.26
  177.7 28.4 %shard_map.425 = (bf16[896,768]{1,0:T(8,128)(2,1)}, bf16[896,768]{1,0:T(8,128)(2,1)}, bf16[896,768]{1,0:T(8,128)(2,1)}) custom-call(s32[2]{0:T(128)} %pad_add_fusion.1.live, bf16[896,768]{1,0:T(8,128)(2,1)} %get-tuple-element.200.q, bf16[896,768]{1,0:T(8,128)(2,1)} %get-tuple-element.201.k, bf16[896,768]{1,0:T(8,128)(2,1)} %get-tuple-element.202.v, ...), custom_call_target="tpu_custom_call" | custom-call | flops 8400000000 | bytes 1024 | tf_op jit(solution)/shard_map/pallas_call | solution.py:655
  206.1 11.1 %shard_map.426 = (bf16[16,192,384]{2,1,0:T(8,128)(2,1)}, bf16[16,192,384]{2,1,0:T(8,128)(2,1)}) custom-call(s32[4]{0:T(128)} %pad_add_fusion.at_ref.at, bf16[896,768]{1,0:T(8,128)(2,1)} %get-tuple-element.213.attended, bf16[839,768]{1,0:T(8,128)(2,1)} %get-tuple-element.245.branch, bf16[839,768]{1,0:T(8,128)(2,1)} %get-tuple-element.246.normed, ...), custom_call_target="tpu_custom_call" | custom-call | flops 3300000000 | bytes 1024 | tf_op jit(solution)/shard_map/pallas_call | solution.py:361
  217.7 1.4 add_bitcast_fusion.2
  219.1 1.5 add_bitcast_fusion
  221.1 1.5 add_bitcast_fusion.1
  222.5 1.7 fusion.1
  224.3 1.1 collective-permute-start.27
  225.3 10.9 %shard_map.427 = (bf16[325,768]{1,0:T(8,128)(2,1)}, bf16[513,768]{1,0:T(8,128)(2,1)}, f32[8,768]{1,0:T(8,128)}) custom-call(bf16[896,768]{1,0:T(8,128)(2,1)} %get-tuple-element.257.dq, bf16[896,768]{1,0:T(8,128)(2,1)} %get-tuple-element.258.dk, bf16[896,768]{1,0:T(8,128)(2,1)} %get-tuple-element.259.dv, bf16[4,2,2,48,768]{4,3,2,1,0:T(8,128)(2,1)} %get-tuple-element.260.wq, ...), custom_call_target="tpu_custom_call" | custom-call | flops 3300000000 | bytes 1024 | tf_op jit(solution)/shard_map/pallas_call | solution.py:361
  236.3 4.5 %collective-permute-done.27 = bf16[4,384,384]{2,1,0:T(8,128)(2,1)} collective-permute-done((bf16[4,384,384]{2,1,0:T(8,128)(2,1)}, bf16[4,384,384]{2,1,0:T(8,128)(2,1)}, u32[]{:S(2)}, u32[]{:S(2)}) %collective-permute-start.27) | collective-permute-done | bytes 1179680 | tf_op jit(solution)/shard_map/chips_1_2/ppermute | solution.py:391
  240.8 1.5 add_convert_fusion.4
  242.3 1.2 pad_maximum_fusion.2
  243.5 1.2 collective-permute-start.31
  244.7 1.6 add_convert_fusion
  247.1 4.0 %collective-permute-start.29 = (bf16[384,384]{1,0:T(8,128)(2,1)}, bf16[384,384]{1,0:T(8,128)(2,1)S(1)}, u32[]{:S(2)}, u32[]{:S(2)}) collective-permute-start(bf16[384,384]{1,0:T(8,128)(2,1)} %get-tuple-element.336), channel_id=1, source_target_pairs={{0,8},{1,9},{2,10},{3,11},{4,12},{5,13},{6,14},{7,15},{8,0},{9,1},... | collective-permute-start | bytes 884744 | tf_op jit(solution)/shard_map/chips_4_4/ppermute | solution.py:391
  251.1 2.0 collective-permute-start.30
  253.1 4.9 %shard_map.429 = (f32[325,1,768]{2,1,0:T(1,128)}, f32[513,1,768]{2,1,0:T(1,128)}) custom-call(bf16[325,768]{1,0:T(8,128)(2,1)} %get-tuple-element.272.image_low, bf16[513,768]{1,0:T(8,128)(2,1)} %get-tuple-element.273.text_low, bf16[4,2,2,48,768]{4,3,2,1,0:T(8,128)(2,1)} %get-tuple-element.280.w_image, bf16[4,2,2,48,768]{4,3,2,1,0:T(8,128)(2,1)} %get-tuple-element.281.w_text), custom_call_target="tpu_custom_call" | custom-call | flops 1320000000 | bytes 1024 | tf_op jit(solution)/shard_map/pallas_call | solution.py:361
  258.0 5.3 %shard_map.428 = (bf16[16,112,384]{2,1,0:T(8,128)(2,1)}, bf16[16,112,384]{2,1,0:T(8,128)(2,1)}) custom-call(s32[4]{0:T(128)} %pad_add_fusion.at_ref.at, bf16[325,768]{1,0:T(8,128)(2,1)} %bitcast.211, bf16[513,768]{1,0:T(8,128)(2,1)} %bitcast.209, bf16[325,768]{1,0:T(8,128)(2,1)} %get-tuple-element.272.image_low, ...), custom_call_target="tpu_custom_call" | custom-call | flops 1650000000 | bytes 1024 | tf_op jit(solution)/shard_map/pallas_call | solution.py:361
  263.2 2.5 collective-permute-done.30
  265.7 1.5 fusion.4
  267.8 1.5 fusion.5
  269.3 14.1 %collective-permute-done.32 = bf16[384,384]{1,0:T(8,128)(2,1)S(1)} collective-permute-done((bf16[384,384]{1,0:T(8,128)(2,1)S(1)}, bf16[384,384]{1,0:T(8,128)(2,1)S(1)}, u32[]{:S(2)}, u32[]{:S(2)}) %collective-permute-start.32) | collective-permute-done | bytes 294944 | tf_op jit(solution)/shard_map/chips_8_8/ppermute | solution.py:391
  283.7 1.6 collective-permute-start.35
  285.5 2.5 collective-permute-start.37
  288.1 1.9 collective-permute-start.38
  290.1 2.8 collective-permute-done.36
  292.8 6.6 %collective-permute-done.37 = bf16[192,384]{1,0:T(8,128)(2,1)S(1)} collective-permute-done((bf16[192,384]{1,0:T(8,128)(2,1)S(1)}, bf16[192,384]{1,0:T(8,128)(2,1)S(1)}, u32[]{:S(2)}, u32[]{:S(2)}) %collective-permute-start.37) | collective-permute-done | bytes 147488 | tf_op jit(solution)/shard_map/chips_8_8/ppermute | solution.py:391
  301.1 1.0 collective-permute-done.40
  302.1 4.7 %collective-permute-done.39 = bf16[4,112,384]{2,1,0:T(8,128)(2,1)S(1)} collective-permute-done((bf16[4,112,384]{2,1,0:T(8,128)(2,1)S(1)}, bf16[4,112,384]{2,1,0:T(8,128)(2,1)S(1)}, u32[]{:S(2)}, u32[]{:S(2)}) %collective-permute-start.39) | collective-permute-done | bytes 344096 | tf_op jit(solution)/shard_map/chips_1_2/ppermute | solution.py:391
  308.0 2.4 collective-permute-start.42
  311.0 1.9 collective-permute-start.44
  316.4 1.6 collective-permute-done.43
  318.1 1.3 collective-permute-done.45
  (141 shorter events, 22.0 us)
Async XLA Ops:
  3.1 20.4 %copy-start.13 = (bf16[256,384]{1,0:T(8,128)(2,1)S(1)}, bf16[256,384]{1,0:T(8,128)(2,1)}, u32[]{:S(2)}) copy-start(bf16[256,384]{1,0:T(8,128)(2,1)} %shard_map.416) | copy-start | bytes 589828
  3.1 11.6 %collective-permute-start = (bf16[256,384]{1,0:T(8,128)(2,1)}, bf16[256,384]{1,0:T(8,128)(2,1)S(1)}, u32[]{:S(2)}, u32[]{:S(2)}) collective-permute-start(bf16[256,384]{1,0:T(8,128)(2,1)} %shard_map.416), channel_id=1, source_target_pairs={{0,8},{1,9},{2,10},{3,11},{4,12},{5,13},{6,14},{7,15},{8,0},{9,1},... | collective-permute-start | bytes 589832 | tf_op jit(solution)/shard_map/chips_4_4/ppermute | solution.py:391
  6.1 17.4 %collective-permute-start.1 = (bf16[256,384]{1,0:T(8,128)(2,1)}, bf16[256,384]{1,0:T(8,128)(2,1)S(1)}, u32[]{:S(2)}, u32[]{:S(2)}) collective-permute-start(bf16[256,384]{1,0:T(8,128)(2,1)} %shard_map.416), channel_id=1, source_target_pairs={{0,16},{1,17},{2,18},{3,19},{4,20},{5,21},{6,22},{7,23},{8,24},{9,... | collective-permute-start | bytes 589832 | tf_op jit(solution)/shard_map/chips_8_8/ppermute | solution.py:391
  8.7 14.8 %collective-permute-start.2 = (bf16[256,384]{1,0:T(8,128)(2,1)}, bf16[256,384]{1,0:T(8,128)(2,1)S(1)}, u32[]{:S(2)}, u32[]{:S(2)}) collective-permute-start(bf16[256,384]{1,0:T(8,128)(2,1)} %shard_map.416), channel_id=1, source_target_pairs={{0,24},{1,25},{2,26},{3,27},{4,28},{5,29},{6,30},{7,31},{8,16},{9,... | collective-permute-start | bytes 589832 | tf_op jit(solution)/shard_map/chips_12_12/ppermute | solution.py:391
  12.2 13.0 %copy-start.14 = (bf16[144,384]{1,0:T(8,128)(2,1)S(1)}, bf16[144,384]{1,0:T(8,128)(2,1)}, u32[]{:S(2)}) copy-start(bf16[144,384]{1,0:T(8,128)(2,1)} %shard_map.417) | copy-start | bytes 331780
  23.6 14.9 %collective-permute-start.3 = (bf16[4,256,384]{2,1,0:T(8,128)(2,1)S(1)}, bf16[4,256,384]{2,1,0:T(8,128)(2,1)S(1)}, u32[]{:S(2)}, u32[]{:S(2)}) collective-permute-start(bf16[4,256,384]{2,1,0:T(8,128)(2,1)S(1)} %pad_maximum_fusion.5), channel_id=1, source_target_pairs={{0,2},{1,5},{2,0},{3,7},{4,6},{5,1},{6,4},{7,3},{8,10},{9,13},{10,... | collective-permute-start | bytes 2359304 | tf_op jit(solution)/shard_map/chips_1_2/ppermute | solution.py:391
  25.2 7.2 %collective-permute-start.4 = (bf16[144,384]{1,0:T(8,128)(2,1)S(1)}, bf16[144,384]{1,0:T(8,128)(2,1)S(1)}, u32[]{:S(2)}, u32[]{:S(2)}) collective-permute-start(bf16[144,384]{1,0:T(8,128)(2,1)S(1)} %copy-done.14), channel_id=1, source_target_pairs={{0,8},{1,9},{2,10},{3,11},{4,12},{5,13},{6,14},{7,15},{8,0},{9,1},... | collective-permute-start | bytes 331784 | tf_op jit(solution)/shard_map/chips_4_4/ppermute | solution.py:391
  28.6 10.0 %collective-permute-start.5 = (bf16[144,384]{1,0:T(8,128)(2,1)S(1)}, bf16[144,384]{1,0:T(8,128)(2,1)S(1)}, u32[]{:S(2)}, u32[]{:S(2)}) collective-permute-start(bf16[144,384]{1,0:T(8,128)(2,1)S(1)} %copy-done.14), channel_id=1, source_target_pairs={{0,16},{1,17},{2,18},{3,19},{4,20},{5,21},{6,22},{7,23},{8,24},{9,... | collective-permute-start | bytes 331784 | tf_op jit(solution)/shard_map/chips_8_8/ppermute | solution.py:391
  29.6 9.0 %collective-permute-start.6 = (bf16[144,384]{1,0:T(8,128)(2,1)S(1)}, bf16[144,384]{1,0:T(8,128)(2,1)S(1)}, u32[]{:S(2)}, u32[]{:S(2)}) collective-permute-start(bf16[144,384]{1,0:T(8,128)(2,1)S(1)} %copy-done.14), channel_id=1, source_target_pairs={{0,24},{1,25},{2,26},{3,27},{4,28},{5,29},{6,30},{7,31},{8,16},{9,... | collective-permute-start | bytes 331784 | tf_op jit(solution)/shard_map/chips_12_12/ppermute | solution.py:391
  38.5 0.9 copy-start.12
  38.7 21.8 %copy-start.6 = (bf16[2,4,256,384]{3,2,1,0:T(8,128)(2,1)}, bf16[2,4,256,384]{3,2,1,0:T(8,128)(2,1)S(1)}, u32[]{:S(2)}) copy-start(bf16[2,4,256,384]{3,2,1,0:T(8,128)(2,1)S(1)} %pad_maximum_fusion.s8) | copy-start | bytes 4718596
  38.7 20.5 %collective-permute-start.7 = (bf16[2,4,256,384]{3,2,1,0:T(8,128)(2,1)S(1)}, bf16[2,4,256,384]{3,2,1,0:T(8,128)(2,1)S(1)}, u32[]{:S(2)}, u32[]{:S(2)}) collective-permute-start(bf16[2,4,256,384]{3,2,1,0:T(8,128)(2,1)S(1)} %pad_maximum_fusion.s8), channel_id=1, source_target_pairs={{0,4},{1,3},{2,6},{3,1},{4,0},{5,7},{6,2},{7,5},{8,12},{9,11},{10,... | collective-permute-start | bytes 4718600 | tf_op jit(solution)/shard_map/chips_2_1/ppermute | solution.py:391
  39.3 19.9 %collective-permute-start.8 = (bf16[2,4,256,384]{3,2,1,0:T(8,128)(2,1)S(1)}, bf16[2,4,256,384]{3,2,1,0:T(8,128)(2,1)S(1)}, u32[]{:S(2)}, u32[]{:S(2)}) collective-permute-start(bf16[2,4,256,384]{3,2,1,0:T(8,128)(2,1)S(1)} %pad_maximum_fusion.s8), channel_id=1, source_target_pairs={{0,1},{1,0},{2,3},{3,2},{4,5},{5,4},{6,7},{7,6},{8,9},{9,8},{10,11... | collective-permute-start | bytes 4718600 | tf_op jit(solution)/shard_map/between_cores/ppermute | solution.py:382
  39.5 18.7 %collective-permute-start.10 = (bf16[288,384]{1,0:T(8,128)(2,1)S(1)}, bf16[288,384]{1,0:T(8,128)(2,1)S(1)}, u32[]{:S(2)}, u32[]{:S(2)}) collective-permute-start(bf16[288,384]{1,0:T(8,128)(2,1)S(1)} %copy-done.12), channel_id=1, source_target_pairs={{0,16},{1,17},{2,18},{3,19},{4,20},{5,21},{6,22},{7,23},{8,24},{9,... | collective-permute-start | bytes 663560 | tf_op jit(solution)/shard_map/chips_8_8/ppermute | solution.py:391
  42.1 16.0 %collective-permute-start.11 = (bf16[288,384]{1,0:T(8,128)(2,1)S(1)}, bf16[288,384]{1,0:T(8,128)(2,1)S(1)}, u32[]{:S(2)}, u32[]{:S(2)}) collective-permute-start(bf16[288,384]{1,0:T(8,128)(2,1)S(1)} %copy-done.12), channel_id=1, source_target_pairs={{0,24},{1,25},{2,26},{3,27},{4,28},{5,29},{6,30},{7,31},{8,16},{9,... | collective-permute-start | bytes 663560 | tf_op jit(solution)/shard_map/chips_12_12/ppermute | solution.py:391
  43.6 15.4 %collective-permute-start.9 = (bf16[288,384]{1,0:T(8,128)(2,1)S(1)}, bf16[288,384]{1,0:T(8,128)(2,1)S(1)}, u32[]{:S(2)}, u32[]{:S(2)}) collective-permute-start(bf16[288,384]{1,0:T(8,128)(2,1)S(1)} %copy-done.12), channel_id=1, source_target_pairs={{0,8},{1,9},{2,10},{3,11},{4,12},{5,13},{6,14},{7,15},{8,0},{9,1},... | collective-permute-start | bytes 663560 | tf_op jit(solution)/shard_map/chips_4_4/ppermute | solution.py:391
  59.2 3.6 %copy-start.16 = (bf16[2,4,256,384]{3,2,1,0:T(8,128)(2,1)}, bf16[2,4,256,384]{3,2,1,0:T(8,128)(2,1)S(1)}, u32[]{:S(2)}) copy-start(bf16[2,4,256,384]{3,2,1,0:T(8,128)(2,1)S(1)} %collective-permute-done.7.r8) | copy-start | bytes 4718596
  59.2 1.2 copy-start.17
  59.2 5.4 %collective-permute-start.14 = (bf16[2,4,256,384]{3,2,1,0:T(8,128)(2,1)S(1)}, bf16[2,4,256,384]{3,2,1,0:T(8,128)(2,1)S(1)}, u32[]{:S(2)}, u32[]{:S(2)}) collective-permute-start(bf16[2,4,256,384]{3,2,1,0:T(8,128)(2,1)S(1)} %collective-permute-done.7.r8), channel_id=1, source_target_pairs={{0,1},{1,0},{2,3},{3,2},{4,5},{5,4},{6,7},{7,6},{8,9},{9,8},{10,11... | collective-permute-start | bytes 4718600 | tf_op jit(solution)/shard_map/between_cores/ppermute | solution.py:382
  60.6 17.9 %collective-permute-start.13 = (bf16[4,288,384]{2,1,0:T(8,128)(2,1)S(1)}, bf16[4,288,384]{2,1,0:T(8,128)(2,1)S(1)}, u32[]{:S(2)}, u32[]{:S(2)}) collective-permute-start(bf16[4,288,384]{2,1,0:T(8,128)(2,1)S(1)} %pad_maximum_fusion.3), channel_id=1, source_target_pairs={{0,2},{1,5},{2,0},{3,7},{4,6},{5,1},{6,4},{7,3},{8,10},{9,13},{10,... | collective-permute-start | bytes 2654216 | tf_op jit(solution)/shard_map/chips_1_2/ppermute | solution.py:391
  63.4 15.0 %collective-permute-start.12 = (bf16[4,144,384]{2,1,0:T(8,128)(2,1)S(1)}, bf16[4,144,384]{2,1,0:T(8,128)(2,1)S(1)}, u32[]{:S(2)}, u32[]{:S(2)}) collective-permute-start(bf16[4,144,384]{2,1,0:T(8,128)(2,1)S(1)} %pad_maximum_fusion.9), channel_id=1, source_target_pairs={{0,2},{1,5},{2,0},{3,7},{4,6},{5,1},{6,4},{7,3},{8,10},{9,13},{10,... | collective-permute-start | bytes 1327112 | tf_op jit(solution)/shard_map/chips_1_2/ppermute | solution.py:391
  64.6 1.1 copy-start.18
  78.5 2.5 copy-start
  78.6 19.5 %collective-permute-start.15 = (bf16[2,4,144,384]{3,2,1,0:T(8,128)(2,1)S(1)}, bf16[2,4,144,384]{3,2,1,0:T(8,128)(2,1)}, u32[]{:S(2)}, u32[]{:S(2)}) collective-permute-start(bf16[2,4,144,384]{3,2,1,0:T(8,128)(2,1)S(1)} %pad_maximum_fusion.4.s8), channel_id=1, source_target_pairs={{0,4},{1,3},{2,6},{3,1},{4,0},{5,7},{6,2},{7,5},{8,12},{9,11},{10,... | collective-permute-start | bytes 2654216 | tf_op jit(solution)/shard_map/chips_2_1/ppermute | solution.py:391
  79.8 18.3 %collective-permute-start.17 = (bf16[2,4,144,384]{3,2,1,0:T(8,128)(2,1)S(1)}, bf16[2,4,144,384]{3,2,1,0:T(8,128)(2,1)}, u32[]{:S(2)}, u32[]{:S(2)}) collective-permute-start(bf16[2,4,144,384]{3,2,1,0:T(8,128)(2,1)S(1)} %pad_maximum_fusion.4.s8), channel_id=1, source_target_pairs={{0,1},{1,0},{2,3},{3,2},{4,5},{5,4},{6,7},{7,6},{8,9},{9,8},{10,11... | collective-permute-start | bytes 2654216 | tf_op jit(solution)/shard_map/between_cores/ppermute | solution.py:382
  80.0 19.8 %copy-start.1 = (bf16[2,4,96,384]{3,2,1,0:T(8,128)(2,1)}, bf16[2,4,96,384]{3,2,1,0:T(8,128)(2,1)S(1)}, u32[]{:S(2)}) copy-start(bf16[2,4,96,384]{3,2,1,0:T(8,128)(2,1)S(1)} %pad_maximum_fusion.7.s_hi) | copy-start | bytes 1769476
  80.0 18.1 %collective-permute-start.16 = (bf16[2,4,96,384]{3,2,1,0:T(8,128)(2,1)S(1)}, bf16[2,4,96,384]{3,2,1,0:T(8,128)(2,1)}, u32[]{:S(2)}, u32[]{:S(2)}) collective-permute-start(bf16[2,4,96,384]{3,2,1,0:T(8,128)(2,1)S(1)} %pad_maximum_fusion.7.s_hi), channel_id=1, source_target_pairs={{0,4},{1,3},{2,6},{3,1},{4,0},{5,7},{6,2},{7,5},{8,12},{9,11},{10,... | collective-permute-start | bytes 1769480 | tf_op jit(solution)/shard_map/chips_2_1/ppermute | solution.py:391
  81.1 18.2 %copy-start.8 = (bf16[2,4,192,384]{3,2,1,0:T(8,128)(2,1)}, bf16[2,4,192,384]{3,2,1,0:T(8,128)(2,1)S(1)}, u32[]{:S(2)}) copy-start(bf16[2,4,192,384]{3,2,1,0:T(8,128)(2,1)S(1)} %pad_maximum_fusion.1.s8) | copy-start | bytes 3538948
  98.1 16.3 %collective-permute-start.18 = (bf16[2,4,192,384]{3,2,1,0:T(8,128)(2,1)S(1)}, bf16[2,4,192,384]{3,2,1,0:T(8,128)(2,1)}, u32[]{:S(2)}, u32[]{:S(2)}) collective-permute-start(bf16[2,4,192,384]{3,2,1,0:T(8,128)(2,1)S(1)} %pad_maximum_fusion.1.s8), channel_id=1, source_target_pairs={{0,4},{1,3},{2,6},{3,1},{4,0},{5,7},{6,2},{7,5},{8,12},{9,11},{10,... | collective-permute-start | bytes 3538952 | tf_op jit(solution)/shard_map/chips_2_1/ppermute | solution.py:391
  99.3 15.1 %collective-permute-start.20 = (bf16[2,4,192,384]{3,2,1,0:T(8,128)(2,1)S(1)}, bf16[2,4,192,384]{3,2,1,0:T(8,128)(2,1)}, u32[]{:S(2)}, u32[]{:S(2)}) collective-permute-start(bf16[2,4,192,384]{3,2,1,0:T(8,128)(2,1)S(1)} %pad_maximum_fusion.1.s8), channel_id=1, source_target_pairs={{0,1},{1,0},{2,3},{3,2},{4,5},{5,4},{6,7},{7,6},{8,9},{9,8},{10,11... | collective-permute-start | bytes 3538952 | tf_op jit(solution)/shard_map/between_cores/ppermute | solution.py:382
  99.3 11.3 %collective-permute-start.21 = (bf16[2,4,144,384]{3,2,1,0:T(8,128)(2,1)}, bf16[2,4,144,384]{3,2,1,0:T(8,128)(2,1)S(1)}, u32[]{:S(2)}, u32[]{:S(2)}) collective-permute-start(bf16[2,4,144,384]{3,2,1,0:T(8,128)(2,1)} %collective-permute-done.15.r8), channel_id=1, source_target_pairs={{0,1},{1,0},{2,3},{3,2},{4,5},{5,4},{6,7},{7,6},{8,9},{9,8},{10,11... | collective-permute-start | bytes 2654216 | tf_op jit(solution)/shard_map/between_cores/ppermute | solution.py:382
  99.8 10.7 %collective-permute-start.19 = (bf16[2,4,96,384]{3,2,1,0:T(8,128)(2,1)S(1)}, bf16[2,4,96,384]{3,2,1,0:T(8,128)(2,1)S(1)}, u32[]{:S(2)}, u32[]{:S(2)}) collective-permute-start(bf16[2,4,96,384]{3,2,1,0:T(8,128)(2,1)S(1)} %pad_maximum_fusion.7.s_hi), channel_id=1, source_target_pairs={{0,1},{1,0},{2,3},{3,2},{4,5},{5,4},{6,7},{7,6},{8,9},{9,8},{10,11... | collective-permute-start | bytes 1769480 | tf_op jit(solution)/shard_map/between_cores/ppermute | solution.py:382
  99.8 10.7 %collective-permute-start.22 = (bf16[2,4,96,384]{3,2,1,0:T(8,128)(2,1)}, bf16[2,4,96,384]{3,2,1,0:T(8,128)(2,1)S(1)}, u32[]{:S(2)}, u32[]{:S(2)}) collective-permute-start(bf16[2,4,96,384]{3,2,1,0:T(8,128)(2,1)} %collective-permute-done.16.r_hi), channel_id=1, source_target_pairs={{0,1},{1,0},{2,3},{3,2},{4,5},{5,4},{6,7},{7,6},{8,9},{9,8},{10,11... | collective-permute-start | bytes 1769480 | tf_op jit(solution)/shard_map/between_cores/ppermute | solution.py:382
  110.5 3.9 %copy-start.10 = (bf16[2,4,96,384]{3,2,1,0:T(8,128)(2,1)}, bf16[2,4,96,384]{3,2,1,0:T(8,128)(2,1)S(1)}, u32[]{:S(2)}) copy-start(bf16[2,4,96,384]{3,2,1,0:T(8,128)(2,1)S(1)} %collective-permute-done.19.sp_hi) | copy-start | bytes 1769476
  110.6 3.9 %copy-start.11 = (bf16[2,4,96,384]{3,2,1,0:T(8,128)(2,1)}, bf16[2,4,96,384]{3,2,1,0:T(8,128)(2,1)S(1)}, u32[]{:S(2)}) copy-start(bf16[2,4,96,384]{3,2,1,0:T(8,128)(2,1)S(1)} %collective-permute-done.22.rp_hi) | copy-start | bytes 1769476
  110.6 3.8 %copy-start.9 = (bf16[2,4,144,384]{3,2,1,0:T(8,128)(2,1)}, bf16[2,4,144,384]{3,2,1,0:T(8,128)(2,1)S(1)}, u32[]{:S(2)}) copy-start(bf16[2,4,144,384]{3,2,1,0:T(8,128)(2,1)S(1)} %collective-permute-done.21.r8p) | copy-start | bytes 2654212
  114.4 8.6 %collective-permute-start.23 = (bf16[2,4,192,384]{3,2,1,0:T(8,128)(2,1)}, bf16[2,4,192,384]{3,2,1,0:T(8,128)(2,1)}, u32[]{:S(2)}, u32[]{:S(2)}) collective-permute-start(bf16[2,4,192,384]{3,2,1,0:T(8,128)(2,1)} %collective-permute-done.18.r8), channel_id=1, source_target_pairs={{0,1},{1,0},{2,3},{3,2},{4,5},{5,4},{6,7},{7,6},{8,9},{9,8},{10,11... | collective-permute-start | bytes 3538952 | tf_op jit(solution)/shard_map/between_cores/ppermute | solution.py:382
  162.6 8.6 %collective-permute-start.24 = (bf16[16,192,384]{2,1,0:T(8,128)(2,1)}, bf16[16,192,384]{2,1,0:T(8,128)(2,1)}, u32[]{:S(2)}, u32[]{:S(2)}) collective-permute-start(bf16[16,192,384]{2,1,0:T(8,128)(2,1)} %get-tuple-element.228), channel_id=1, source_target_pairs={{0,1},{1,0},{2,3},{3,2},{4,5},{5,4},{6,7},{7,6},{8,9},{9,8},{10,11... | collective-permute-start | bytes 7077896 | tf_op jit(solution)/shard_map/between_cores/ppermute | solution.py:382
  163.2 8.1 %collective-permute-start.25 = (bf16[16,192,384]{2,1,0:T(8,128)(2,1)}, bf16[16,192,384]{2,1,0:T(8,128)(2,1)}, u32[]{:S(2)}, u32[]{:S(2)}) collective-permute-start(bf16[16,192,384]{2,1,0:T(8,128)(2,1)} %get-tuple-element.229), channel_id=1, source_target_pairs={{0,1},{1,0},{2,3},{3,2},{4,5},{5,4},{6,7},{7,6},{8,9},{9,8},{10,11... | collective-permute-start | bytes 7077896 | tf_op jit(solution)/shard_map/between_cores/ppermute | solution.py:382
  163.3 8.0 %copy-start.2 = (bf16[16,192,384]{2,1,0:T(8,128)(2,1)S(1)}, bf16[16,192,384]{2,1,0:T(8,128)(2,1)}, u32[]{:S(2)}) copy-start(bf16[16,192,384]{2,1,0:T(8,128)(2,1)} %get-tuple-element.249) | copy-start | bytes 7077892
  171.3 2.0 copy-start.4
  176.5 40.7 %collective-permute-start.26 = (bf16[4,2,384,384]{3,2,0,1:T(8,128)(2,1)}, bf16[4,2,384,384]{3,2,0,1:T(8,128)(2,1)S(1)}, u32[]{:S(2)}, u32[]{:S(2)}) collective-permute-start(bf16[4,2,384,384]{3,2,0,1:T(8,128)(2,1)} %maximum_maximum_fusion), channel_id=1, source_target_pairs={{0,4},{1,3},{2,6},{3,1},{4,0},{5,7},{6,2},{7,5},{8,12},{9,11},{10,... | collective-permute-start | bytes 7077896 | tf_op jit(solution)/shard_map/chips_2_1/ppermute | solution.py:391
  217.2 23.6 %collective-permute-start.28 = (bf16[16,192,384]{2,1,0:T(8,128)(2,1)}, bf16[16,192,384]{2,1,0:T(8,128)(2,1)}, u32[]{:S(2)}, u32[]{:S(2)}) collective-permute-start(bf16[16,192,384]{2,1,0:T(8,128)(2,1)} %get-tuple-element.252), channel_id=1, source_target_pairs={{0,1},{1,0},{2,3},{3,2},{4,5},{5,4},{6,7},{7,6},{8,9},{9,8},{10,11... | collective-permute-start | bytes 7077896 | tf_op jit(solution)/shard_map/between_cores/ppermute | solution.py:382
  219.0 2.0 copy-start.3
  224.3 16.5 %collective-permute-start.27 = (bf16[4,384,384]{2,1,0:T(8,128)(2,1)}, bf16[4,384,384]{2,1,0:T(8,128)(2,1)}, u32[]{:S(2)}, u32[]{:S(2)}) collective-permute-start(bf16[4,384,384]{2,1,0:T(8,128)(2,1)} %get-tuple-element.332), channel_id=1, source_target_pairs={{0,2},{1,5},{2,0},{3,7},{4,6},{5,1},{6,4},{7,3},{8,10},{9,13},{10,... | collective-permute-start | bytes 3538952 | tf_op jit(solution)/shard_map/chips_1_2/ppermute | solution.py:391
  225.3 15.4 %copy-start.5 = (bf16[16,192,384]{2,1,0:T(8,128)(2,1)S(1)}, bf16[16,192,384]{2,1,0:T(8,128)(2,1)}, u32[]{:S(2)}) copy-start(bf16[16,192,384]{2,1,0:T(8,128)(2,1)} %get-tuple-element.291) | copy-start | bytes 7077892
  243.5 22.2 %collective-permute-start.31 = (bf16[4,2,192,384]{3,2,0,1:T(8,128)(2,1)}, bf16[4,2,192,384]{3,2,0,1:T(8,128)(2,1)}, u32[]{:S(2)}, u32[]{:S(2)}) collective-permute-start(bf16[4,2,192,384]{3,2,0,1:T(8,128)(2,1)} %pad_maximum_fusion.2), channel_id=1, source_target_pairs={{0,4},{1,3},{2,6},{3,1},{4,0},{5,7},{6,2},{7,5},{8,12},{9,11},{10,... | collective-permute-start | bytes 3538952 | tf_op jit(solution)/shard_map/chips_2_1/ppermute | solution.py:391
  247.1 16.1 %collective-permute-start.29 = (bf16[384,384]{1,0:T(8,128)(2,1)}, bf16[384,384]{1,0:T(8,128)(2,1)S(1)}, u32[]{:S(2)}, u32[]{:S(2)}) collective-permute-start(bf16[384,384]{1,0:T(8,128)(2,1)} %get-tuple-element.336), channel_id=1, source_target_pairs={{0,8},{1,9},{2,10},{3,11},{4,12},{5,13},{6,14},{7,15},{8,0},{9,1},... | collective-permute-start | bytes 884744 | tf_op jit(solution)/shard_map/chips_4_4/ppermute | solution.py:391
  251.1 14.6 %collective-permute-start.30 = (bf16[384,384]{1,0:T(8,128)(2,1)S(1)}, bf16[384,384]{1,0:T(8,128)(2,1)S(1)}, u32[]{:S(2)}, u32[]{:S(2)}) collective-permute-start(bf16[384,384]{1,0:T(8,128)(2,1)S(1)} %get-tuple-element.335), channel_id=1, source_target_pairs={{0,24},{1,25},{2,26},{3,27},{4,28},{5,29},{6,30},{7,31},{8,16},{9,... | collective-permute-start | bytes 884744 | tf_op jit(solution)/shard_map/chips_12_12/ppermute | solution.py:391
  265.7 17.7 %collective-permute-start.33 = (bf16[16,112,384]{2,1,0:T(8,128)(2,1)}, bf16[16,112,384]{2,1,0:T(8,128)(2,1)S(1)}, u32[]{:S(2)}, u32[]{:S(2)}) collective-permute-start(bf16[16,112,384]{2,1,0:T(8,128)(2,1)} %get-tuple-element.289), channel_id=1, source_target_pairs={{0,1},{1,0},{2,3},{3,2},{4,5},{5,4},{6,7},{7,6},{8,9},{9,8},{10,11... | collective-permute-start | bytes 4128776 | tf_op jit(solution)/shard_map/between_cores/ppermute | solution.py:382
  267.2 16.2 %copy-start.7 = (bf16[16,112,384]{2,1,0:T(8,128)(2,1)S(1)}, bf16[16,112,384]{2,1,0:T(8,128)(2,1)}, u32[]{:S(2)}) copy-start(bf16[16,112,384]{2,1,0:T(8,128)(2,1)} %get-tuple-element.300) | copy-start | bytes 4128772
  267.2 16.2 %collective-permute-start.34 = (bf16[4,192,384]{2,1,0:T(8,128)(2,1)S(1)}, bf16[4,192,384]{2,1,0:T(8,128)(2,1)S(1)}, u32[]{:S(2)}, u32[]{:S(2)}) collective-permute-start(bf16[4,192,384]{2,1,0:T(8,128)(2,1)S(1)} %fusion.4), channel_id=1, source_target_pairs={{0,2},{1,5},{2,0},{3,7},{4,6},{5,1},{6,4},{7,3},{8,10},{9,13},{10,... | collective-permute-start | bytes 1769480 | tf_op jit(solution)/shard_map/chips_1_2/ppermute | solution.py:391
  267.8 15.5 %collective-permute-start.32 = (bf16[384,384]{1,0:T(8,128)(2,1)S(1)}, bf16[384,384]{1,0:T(8,128)(2,1)S(1)}, u32[]{:S(2)}, u32[]{:S(2)}) collective-permute-start(bf16[384,384]{1,0:T(8,128)(2,1)S(1)} %get-tuple-element.286), channel_id=1, source_target_pairs={{0,16},{1,17},{2,18},{3,19},{4,20},{5,21},{6,22},{7,23},{8,24},{9,... | collective-permute-start | bytes 884744 | tf_op jit(solution)/shard_map/chips_8_8/ppermute | solution.py:391
  283.7 15.7 %collective-permute-start.35 = (bf16[4,2,112,384]{3,2,0,1:T(8,128)(2,1)S(1)}, bf16[4,2,112,384]{3,2,0,1:T(8,128)(2,1)S(1)}, u32[]{:S(2)}, u32[]{:S(2)}) collective-permute-start(bf16[4,2,112,384]{3,2,0,1:T(8,128)(2,1)S(1)} %pad_maximum_fusion.6), channel_id=1, source_target_pairs={{0,4},{1,3},{2,6},{3,1},{4,0},{5,7},{6,2},{7,5},{8,12},{9,11},{10,... | collective-permute-start | bytes 2064392 | tf_op jit(solution)/shard_map/chips_2_1/ppermute | solution.py:391
  285.5 7.4 %collective-permute-start.36 = (bf16[192,384]{1,0:T(8,128)(2,1)S(1)}, bf16[192,384]{1,0:T(8,128)(2,1)S(1)}, u32[]{:S(2)}, u32[]{:S(2)}) collective-permute-start(bf16[192,384]{1,0:T(8,128)(2,1)S(1)} %get-tuple-element.342), channel_id=1, source_target_pairs={{0,8},{1,9},{2,10},{3,11},{4,12},{5,13},{6,14},{7,15},{8,0},{9,1},... | collective-permute-start | bytes 442376 | tf_op jit(solution)/shard_map/chips_4_4/ppermute | solution.py:391
  285.5 13.8 %collective-permute-start.37 = (bf16[192,384]{1,0:T(8,128)(2,1)S(1)}, bf16[192,384]{1,0:T(8,128)(2,1)S(1)}, u32[]{:S(2)}, u32[]{:S(2)}) collective-permute-start(bf16[192,384]{1,0:T(8,128)(2,1)S(1)} %get-tuple-element.341), channel_id=1, source_target_pairs={{0,16},{1,17},{2,18},{3,19},{4,20},{5,21},{6,22},{7,23},{8,24},{9,... | collective-permute-start | bytes 442376 | tf_op jit(solution)/shard_map/chips_8_8/ppermute | solution.py:391
  288.1 11.3 %collective-permute-start.38 = (bf16[192,384]{1,0:T(8,128)(2,1)S(1)}, bf16[192,384]{1,0:T(8,128)(2,1)S(1)}, u32[]{:S(2)}, u32[]{:S(2)}) collective-permute-start(bf16[192,384]{1,0:T(8,128)(2,1)S(1)} %get-tuple-element.340), channel_id=1, source_target_pairs={{0,24},{1,25},{2,26},{3,27},{4,28},{5,29},{6,30},{7,31},{8,16},{9,... | collective-permute-start | bytes 442376 | tf_op jit(solution)/shard_map/chips_12_12/ppermute | solution.py:391
  299.5 7.3 %collective-permute-start.39 = (bf16[4,112,384]{2,1,0:T(8,128)(2,1)S(1)}, bf16[4,112,384]{2,1,0:T(8,128)(2,1)S(1)}, u32[]{:S(2)}, u32[]{:S(2)}) collective-permute-start(bf16[4,112,384]{2,1,0:T(8,128)(2,1)S(1)} %fusion.6), channel_id=1, source_target_pairs={{0,2},{1,5},{2,0},{3,7},{4,6},{5,1},{6,4},{7,3},{8,10},{9,13},{10,... | collective-permute-start | bytes 1032200 | tf_op jit(solution)/shard_map/chips_1_2/ppermute | solution.py:391
  300.3 1.8 collective-permute-start.41
  300.4 1.7 collective-permute-start.40
  308.0 8.4 %collective-permute-start.42 = (bf16[112,384]{1,0:T(8,128)(2,1)S(1)}, bf16[112,384]{1,0:T(8,128)(2,1)S(1)}, u32[]{:S(2)}, u32[]{:S(2)}) collective-permute-start(bf16[112,384]{1,0:T(8,128)(2,1)S(1)} %get-tuple-element.346), channel_id=1, source_target_pairs={{0,8},{1,9},{2,10},{3,11},{4,12},{5,13},{6,14},{7,15},{8,0},{9,1},... | collective-permute-start | bytes 258056 | tf_op jit(solution)/shard_map/chips_4_4/ppermute | solution.py:391
  310.4 7.6 %collective-permute-start.43 = (bf16[112,384]{1,0:T(8,128)(2,1)S(1)}, bf16[112,384]{1,0:T(8,128)(2,1)S(1)}, u32[]{:S(2)}, u32[]{:S(2)}) collective-permute-start(bf16[112,384]{1,0:T(8,128)(2,1)S(1)} %get-tuple-element.345), channel_id=1, source_target_pairs={{0,16},{1,17},{2,18},{3,19},{4,20},{5,21},{6,22},{7,23},{8,24},{9,... | collective-permute-start | bytes 258056 | tf_op jit(solution)/shard_map/chips_8_8/ppermute | solution.py:391
  311.0 7.0 %collective-permute-start.44 = (bf16[112,384]{1,0:T(8,128)(2,1)S(1)}, bf16[112,384]{1,0:T(8,128)(2,1)S(1)}, u32[]{:S(2)}, u32[]{:S(2)}) collective-permute-start(bf16[112,384]{1,0:T(8,128)(2,1)S(1)} %get-tuple-element.344), channel_id=1, source_target_pairs={{0,24},{1,25},{2,26},{3,27},{4,28},{5,29},{6,30},{7,31},{8,16},{9,... | collective-permute-start | bytes 258056 | tf_op jit(solution)/shard_map/chips_12_12/ppermute | solution.py:391
  318.1 1.3 collective-permute-start.45
  (1 other events, 0.8 us)
